TPU v7x, 32 devices: a whole 2x2x4 slice. The times are simulated.
32 devices in a mesh: batch: 2 (over x), chan: 16 (over z, y, core).
Axes of the slice: x: 2, y: 2, z: 4, core: 2. Of those that a mesh axis runs over, the one named last changes fastest.
Arguments:
- layer_in: bfloat16 [4, 768, 4096], P('batch', 'chan'), may hold values from -6 to 6
- seq_lengths: int32 [4], P('batch'), may hold values from 256 to 4096, as said below
- ln1_gain: bfloat16 [768], P('chan'), may hold values from 0.5 to 1.5
- first_norm_bias: bfloat16 [768], P('chan'), may hold values from -1.75 to 1.75
- in_weight: bfloat16 [768, 3, 768], P(None, None, 'chan'), may hold values from -0.21875 to 0.21875
- in_bias: bfloat16 [3, 768], P(None, 'chan'), may hold values from -1.75 to 1.75
- short_weight: bfloat16 [3, 3, 768], P(None, None, 'chan'), may hold values from -3.5 to 3.5
- short_bias: bfloat16 [3, 768], P(None, 'chan'), may hold values from -1.75 to 1.75
- filt_in: float32 [33, 64], replicated, may hold values from -1 to 1
- filt_in_bias: float32 [64], replicated, may hold values from -3 to 3
- filt_mid: float32 [64, 64], replicated, may hold values from -0.75 to 0.75
- filt_mid_bias: float32 [64], replicated, may hold values from -3 to 3
- sine_freq: float32 [64], replicated, may hold values from 1 to 8
- filt_out: float32 [64, 768], P(None, 'chan'), may hold values from -0.0625 to 0.0625
- decay_rate: float32 [768], P('chan'), may hold values from 0.5 to 100
- conv_bias: float32 [768], P('chan'), may hold values from -6 to 6
- out_weight: bfloat16 [768, 768], P('chan'), may hold values from -0.21875 to 0.21875
- out_bias: bfloat16 [768], P('chan'), may hold values from -1.75 to 1.75
- ln2_gain: bfloat16 [768], P('chan'), may hold values from 0.5 to 1.5
- second_norm_bias: bfloat16 [768], P('chan'), may hold values from -1.75 to 1.75
- up_weight: bfloat16 [3072, 768], P('chan'), may hold values from -0.21875 to 0.21875
- up_bias: bfloat16 [3072], P('chan'), may hold values from -1.75 to 1.75
- down_weight: bfloat16 [3072, 768], P('chan'), may hold values from -0.109375 to 0.109375
- down_bias: bfloat16 [768], P('chan'), may hold values from -1.75 to 1.75
- cotangent: bfloat16 [4, 768, 4096], P('batch', 'chan'), may hold values from -6 to 6
Outputs:
- layer_out: bfloat16 [4, 768, 4096], P('batch', 'chan')
- grad_layer_in: float32 [4, 768, 4096], P('batch', 'chan')
- grad_ln1_gain: float32 [768], P('chan')
- grad_ln1_bias: float32 [768], P('chan')
- grad_in_weight: float32 [768, 3, 768], P('batch', None, 'chan')
- grad_in_bias: float32 [3, 768], P(None, 'chan')
- grad_short_weight: float32 [3, 3, 768], P(None, None, 'chan')
- grad_short_bias: float32 [3, 768], P(None, 'chan')
- grad_filt_in: float32 [33, 64], replicated
- grad_filt_in_bias: float32 [64], replicated
- grad_filt_mid: float32 [64, 64], replicated
- grad_filt_mid_bias: float32 [64], replicated
- grad_sine_freq: float32 [64], replicated
- grad_filt_out: float32 [64, 768], P(None, 'chan')
- grad_decay_rate: float32 [768], P('chan')
- grad_conv_bias: float32 [768], P('chan')
- grad_out_weight: float32 [768, 768], P('chan', 'batch')
- grad_out_bias: float32 [768], P('chan')
- grad_ln2_gain: float32 [768], P('chan')
- grad_ln2_bias: float32 [768], P('chan')
- grad_up_weight: float32 [3072, 768], P('chan', 'batch')
- grad_up_bias: float32 [3072], P('chan')
- grad_down_weight: float32 [3072, 768], P('chan', 'batch')
- grad_down_bias: float32 [768], P('chan')
Inputs may be any that keep to these rules, and one draw needn't show every extreme that they name: `seq_lengths`: among the 2 consecutive rows of one index of batch, at least one has length 4096.
All inputs are finite; a program needn't handle non-finite values.
Results may differ from a plain program's by a relative error of at most 0.0093.
Values may be sent and summed in bfloat16 or wider, within the bound.
No kernel may reach another device: no remote copies, remote signals or barrier semaphores. Data moves between devices by JAX's collectives and lax.ppermute only.
A program may use at most 256 MiB of HBM per device.

v0:
```python
import math

import jax
import jax.numpy as jnp
from jax import lax
from jax.sharding import PartitionSpec as P

EMB = 33
KS = 3
LMAX = 4096


epsilon = 1e-05
decay_floor = 0.05
highest = lax.Precision.HIGHEST
tile_width = 128


def position_table(begin_at, row_count, length):
    places = begin_at + lax.iota(jnp.int32, row_count)
    orders = lax.iota(jnp.int32, (EMB - 1) // 2) + 1
    turn_count = places[:, None] * orders[None, :] % length
    phases = turn_count.astype(jnp.float32) * (2.0 * math.pi / length)
    ramp_pos = places.astype(jnp.float32) / (length - 1)
    return (
        jnp.concatenate([ramp_pos[:, None], jnp.cos(phases), -jnp.sin(phases)], axis=1),
        ramp_pos,
    )


def make_filter(
    pos_table, ramp_pos, w_first, b_first, w_second, b_second, sine_rate, w_last, decay_rates
):
    first_hidden = jnp.sin(sine_rate * (jnp.dot(pos_table, w_first, precision=highest) + b_first))
    second_hidden = jnp.sin(
        sine_rate * (jnp.dot(first_hidden, w_second, precision=highest) + b_second)
    )
    raw_filter = jnp.dot(second_hidden, w_last, precision=highest)
    return raw_filter * (jnp.exp(-ramp_pos[:, None] * decay_rates[None, :]) + decay_floor)


def phase_table(rows_n, cols_n, period):
    turn_count = (
        lax.iota(jnp.int32, rows_n)[:, None] * lax.iota(jnp.int32, cols_n)[None, :] % period
    )
    phases = turn_count.astype(jnp.float32) * (2.0 * math.pi / period)
    return (jnp.cos(phases), -jnp.sin(phases))


def dft_tables(length):
    row_blocks = 2 * length // tile_width
    return (
        phase_table(row_blocks, length // tile_width, row_blocks),
        phase_table(row_blocks, tile_width, 2 * length),
        phase_table(tile_width, tile_width, tile_width),
    )


def forward_dft(signal, tables):
    (outer_re, outer_im), (twist_re, twist_im), (inner_re, inner_im) = tables
    lead_dims = signal.shape[:-2]
    grid_in = signal.reshape(lead_dims + (outer_re.shape[1], tile_width, signal.shape[-1]))
    first_re = jnp.einsum("kn,...nbc->...kbc", outer_re, grid_in, precision=highest)
    first_im = jnp.einsum("kn,...nbc->...kbc", outer_im, grid_in, precision=highest)
    turned_re = first_re * twist_re[:, :, None] - first_im * twist_im[:, :, None]
    turned_im = first_re * twist_im[:, :, None] + first_im * twist_re[:, :, None]
    spec_re = jnp.einsum("...kbc,bj->...kjc", turned_re, inner_re, precision=highest) - jnp.einsum(
        "...kbc,bj->...kjc", turned_im, inner_im, precision=highest
    )
    spec_im = jnp.einsum("...kbc,bj->...kjc", turned_re, inner_im, precision=highest) + jnp.einsum(
        "...kbc,bj->...kjc", turned_im, inner_re, precision=highest
    )
    return (spec_re, spec_im)


def inverse_dft(spec_pair, tables):
    (outer_re, outer_im), (twist_re, twist_im), (inner_re, inner_im) = tables
    spec_re, spec_im = spec_pair
    back_re = jnp.einsum("...kjc,bj->...kbc", spec_re, inner_re, precision=highest) + jnp.einsum(
        "...kjc,bj->...kbc", spec_im, inner_im, precision=highest
    )
    back_im = jnp.einsum("...kjc,bj->...kbc", spec_im, inner_re, precision=highest) - jnp.einsum(
        "...kjc,bj->...kbc", spec_re, inner_im, precision=highest
    )
    turned_re = back_re * twist_re[:, :, None] + back_im * twist_im[:, :, None]
    turned_im = back_im * twist_re[:, :, None] - back_re * twist_im[:, :, None]
    grid_out = jnp.einsum("kn,...kbc->...nbc", outer_re, turned_re, precision=highest) + jnp.einsum(
        "kn,...kbc->...nbc", outer_im, turned_im, precision=highest
    )
    lead_dims = spec_re.shape[:-3]
    return grid_out.reshape(lead_dims + (-1, spec_re.shape[-1])) / (
        2 * grid_out.shape[-3] * tile_width
    )


def complex_product(left_pair, right_pair):
    return (
        left_pair[0] * right_pair[0] - left_pair[1] * right_pair[1],
        left_pair[0] * right_pair[1] + left_pair[1] * right_pair[0],
    )


def conj_product(left_pair, right_pair):
    return (
        left_pair[0] * right_pair[0] + left_pair[1] * right_pair[1],
        left_pair[1] * right_pair[0] - left_pair[0] * right_pair[1],
    )


def smooth_gate(values):
    return jax.nn.gelu(values, approximate=True)


def local_totals(linear_term, square_term):
    return (jnp.sum(linear_term, axis=1), jnp.sum(square_term, axis=1))


def layer_norm_forward(values, column_totals, feature_width):
    linear_total, square_sum = column_totals(values, values * values)
    row_mean = linear_total / feature_width
    row_var = square_sum / feature_width - row_mean * row_mean
    inverse_deviation = lax.rsqrt(row_var + epsilon)[:, None]
    return ((values - row_mean[:, None]) * inverse_deviation, inverse_deviation)


def layer_norm_backward(
    scaled_gradient, centered_scaled, inverse_deviation, column_totals, feature_width
):
    linear_total, cross_term_total = column_totals(
        scaled_gradient, scaled_gradient * centered_scaled
    )
    return inverse_deviation * (
        scaled_gradient
        - linear_total[:, None] / feature_width
        - centered_scaled * (cross_term_total[:, None] / feature_width)
    )


def rows_exact(first, second):
    return (
        lax.all_to_all(
            first.astype(jnp.bfloat16), "chan", split_axis=0, concat_axis=2, tiled=True
        ).astype(first.dtype),
        lax.all_to_all(
            second.astype(jnp.bfloat16), "chan", split_axis=0, concat_axis=2, tiled=True
        ).astype(second.dtype),
    )


def rows_low(values):
    return lax.all_to_all(values, "chan", split_axis=0, concat_axis=2, tiled=True)


def to_channels(values):
    return lax.all_to_all(values, "chan", split_axis=2, concat_axis=0, tiled=True)


def to_rows(values):
    return jnp.transpose(values, (0, 2, 1)).reshape(-1, values.shape[1])


def to_columns(values, seq_count):
    return jnp.transpose(values.reshape(seq_count, LMAX, values.shape[1]), (0, 2, 1))


def on_device(
    layer_in,
    seq_lengths,
    ln1_gain,
    first_norm_bias,
    in_weight,
    in_bias,
    short_weight,
    short_bias,
    filt_in,
    filt_in_bias,
    filt_mid,
    filt_mid_bias,
    sine_freq,
    filt_out,
    decay_rate,
    conv_bias,
    out_weight,
    out_bias,
    ln2_gain,
    second_norm_bias,
    up_weight,
    up_bias,
    down_weight,
    down_bias,
    cotangent,
):
    seq_count = seq_lengths.shape[0]
    cols_n = layer_in.shape[1]
    rows_n = seq_count * LMAX
    chan_count = lax.axis_size("chan")
    hidden_width = cols_n * chan_count
    positions = lax.iota(jnp.int32, LMAX)
    live_mask = (positions[None, :] < seq_lengths[:, None]).astype(jnp.float32).reshape(rows_n, 1)
    widened_input = to_rows(layer_in.astype(jnp.float32))
    cot_wide = to_rows(cotangent.astype(jnp.float32))
    part_rows = rows_n // chan_count
    mask_rows = lax.dynamic_slice_in_dim(
        live_mask, lax.axis_index("chan") * part_rows, part_rows, 0
    )
    x_three, cot_three = rows_exact(widened_input[:, None, :], cot_wide[:, None, :])
    x_rows = x_three[:, 0, :]
    cot_rows = cot_three[:, 0, :]
    (
        in_all,
        out_all,
        out_bias_all,
        up_all,
        down_all,
        up_bias_all,
        down_bias_all,
        gain_one_all,
        shift_one_all,
        gain_two_all,
        shift_two_all,
    ) = (
        lax.all_gather(in_weight, "chan", axis=2, tiled=True),
        lax.all_gather(out_weight, "chan", axis=0, tiled=True),
        lax.all_gather(out_bias, "chan", axis=0, tiled=True),
        lax.all_gather(up_weight, "chan", axis=0, tiled=True),
        lax.all_gather(down_weight, "chan", axis=0, tiled=True),
        lax.all_gather(up_bias, "chan", axis=0, tiled=True),
        lax.all_gather(down_bias, "chan", axis=0, tiled=True),
        lax.all_gather(ln1_gain, "chan", axis=0, tiled=True),
        lax.all_gather(first_norm_bias, "chan", axis=0, tiled=True),
        lax.all_gather(ln2_gain, "chan", axis=0, tiled=True),
        lax.all_gather(second_norm_bias, "chan", axis=0, tiled=True),
    )
    first_centered_scaled, first_inverse_deviation = layer_norm_forward(
        x_rows, local_totals, hidden_width
    )
    first_norm_gain = gain_one_all.astype(jnp.float32)
    normed_reduced_precision = (
        first_centered_scaled * first_norm_gain + shift_one_all.astype(jnp.float32)
    ).astype(jnp.bfloat16)
    in_flat = in_all.reshape(hidden_width, -1)
    proj_rows = jnp.dot(normed_reduced_precision, in_flat, preferred_element_type=jnp.float32)
    proj_sum = to_channels(proj_rows.reshape(part_rows, 3, hidden_width)).reshape(rows_n, -1)
    projected = proj_sum.reshape(seq_count, LMAX, 3, cols_n) + in_bias.astype(jnp.float32)
    short_w = short_weight.astype(jnp.float32)
    padded = jnp.pad(projected, ((0, 0), (KS - 1, 0), (0, 0), (0, 0)))
    shorted = short_bias.astype(jnp.float32) + jnp.zeros_like(projected)
    for offset in range(KS):
        shorted = shorted + short_w[offset] * padded[:, KS - 1 - offset : KS - 1 - offset + LMAX]
    gate_out = shorted[:, :, 0]
    gate_in = shorted[:, :, 1]
    value_in = shorted[:, :, 2]
    mixed_in = value_in * gate_in
    filter_count = LMAX // lax.axis_size("batch")
    filter_start = lax.axis_index("batch") * filter_count
    pos_table, ramp_pos = position_table(filter_start, filter_count, LMAX)

    def filter_piece(w_first, b_first, w_second, b_second, sine_rate, w_last, decay_rates):
        return make_filter(
            pos_table,
            ramp_pos,
            w_first,
            b_first,
            w_second,
            b_second,
            sine_rate,
            w_last,
            decay_rates,
        )

    filter_part, filter_pull = jax.vjp(
        filter_piece,
        filt_in,
        filt_in_bias,
        filt_mid,
        filt_mid_bias,
        sine_freq,
        filt_out,
        decay_rate,
    )
    kernel = lax.all_gather(filter_part, "batch", axis=0, tiled=True)
    tables = dft_tables(LMAX)
    mixed_spec = forward_dft(mixed_in, tables)
    kernel_spec = forward_dft(kernel, tables)
    convolved = inverse_dft(complex_product(mixed_spec, kernel_spec), tables) + conv_bias * mixed_in
    gated_low = (convolved * gate_out).reshape(rows_n, cols_n).astype(jnp.bfloat16)
    gated_rows = rows_low(gated_low[:, None, :])[:, 0, :]
    residual_stream = (
        x_rows
        + jnp.dot(gated_rows, out_all, preferred_element_type=jnp.float32)
        + out_bias_all.astype(jnp.float32)
    )
    second_centered_scaled, second_inverse_deviation = layer_norm_forward(
        residual_stream, local_totals, hidden_width
    )
    second_norm_gain = gain_two_all.astype(jnp.float32)
    second_normed_rows = (
        second_centered_scaled * second_norm_gain + shift_two_all.astype(jnp.float32)
    ).astype(jnp.bfloat16)
    activated, gelu_pull = jax.vjp(
        smooth_gate,
        lax.dot_general(
            second_normed_rows, up_all, (((1,), (1,)), ((), ())), preferred_element_type=jnp.float32
        )
        + up_bias_all.astype(jnp.float32),
    )
    act_low = activated.astype(jnp.bfloat16)
    mlp_rows = jnp.dot(
        act_low, down_all, preferred_element_type=jnp.float32
    ) + down_bias_all.astype(jnp.float32)
    result_rows = mask_rows * (residual_stream + mlp_rows)
    layer_out = to_channels(result_rows[:, None, :])[:, 0, :].astype(jnp.bfloat16)
    d_final_rows = mask_rows * cot_rows
    final_low = d_final_rows.astype(jnp.bfloat16)
    d_act = lax.dot_general(
        final_low, down_all, (((1,), (1,)), ((), ())), preferred_element_type=jnp.float32
    )
    down_full = lax.dot_general(
        act_low, final_low, (((0,), (0,)), ((), ())), preferred_element_type=jnp.float32
    )
    d_hidden = gelu_pull(d_act)[0]
    hidden_low = d_hidden.astype(jnp.bfloat16)
    up_full = lax.dot_general(
        hidden_low, second_normed_rows, (((0,), (0,)), ((), ())), preferred_element_type=jnp.float32
    )
    normed_gradient = jnp.dot(hidden_low, up_all, preferred_element_type=jnp.float32)
    second_norm_gain_gradient = jnp.sum(normed_gradient * second_centered_scaled, axis=0)
    g_ln2_bias = jnp.sum(normed_gradient, axis=0)
    g_up_bias = jnp.sum(d_hidden, axis=0)
    g_down_bias = jnp.sum(d_final_rows, axis=0)
    d_residual = d_final_rows + layer_norm_backward(
        normed_gradient * second_norm_gain,
        second_centered_scaled,
        second_inverse_deviation,
        local_totals,
        hidden_width,
    )
    g_out_bias = jnp.sum(d_residual, axis=0)
    branch_low = d_residual.astype(jnp.bfloat16)
    out_full = lax.dot_general(
        gated_rows, branch_low, (((0,), (0,)), ((), ())), preferred_element_type=jnp.float32
    )
    d_gated_rows = lax.dot_general(
        branch_low, out_all, (((1,), (1,)), ((), ())), preferred_element_type=jnp.float32
    )
    d_gated = to_channels(d_gated_rows[:, None, :])[:, 0, :]
    d_gated = d_gated.reshape(seq_count, LMAX, cols_n)
    d_conv = d_gated * gate_out
    d_gate_out = d_gated * convolved
    d_spec = forward_dft(d_conv, tables)
    d_mixed = inverse_dft(conj_product(d_spec, kernel_spec), tables) + conv_bias * d_conv
    cross_spec = conj_product(d_spec, mixed_spec)
    d_kernel = inverse_dft((jnp.sum(cross_spec[0], axis=0), jnp.sum(cross_spec[1], axis=0)), tables)
    g_conv_bias = jnp.sum(d_conv * mixed_in, axis=(0, 1))
    d_short = jnp.stack([d_gate_out, d_mixed * value_in, d_mixed * gate_in], axis=2)
    g_short_bias = jnp.sum(d_short, axis=(0, 1))
    g_short_weight = jnp.stack(
        [
            jnp.sum(d_short * padded[:, KS - 1 - offset : KS - 1 - offset + LMAX], axis=(0, 1))
            for offset in range(KS)
        ]
    )
    d_pad = jnp.pad(d_short, ((0, 0), (0, KS - 1), (0, 0), (0, 0)))
    d_proj = jnp.zeros_like(d_short)
    for offset in range(KS):
        d_proj = d_proj + short_w[offset] * d_pad[:, offset : offset + LMAX]
    g_in_bias = jnp.sum(d_proj, axis=(0, 1))
    proj_low = d_proj.reshape(rows_n, -1).astype(jnp.bfloat16)
    proj_rows_low = rows_low(proj_low.reshape(rows_n, 3, cols_n)).reshape(part_rows, -1)
    in_full = lax.dot_general(
        normed_reduced_precision,
        proj_rows_low,
        (((0,), (0,)), ((), ())),
        preferred_element_type=jnp.float32,
    )
    first_normed_gradient = lax.dot_general(
        proj_rows_low, in_flat, (((1,), (1,)), ((), ())), preferred_element_type=jnp.float32
    )
    first_norm_gain_gradient = jnp.sum(first_normed_gradient * first_centered_scaled, axis=0)
    g_ln1_bias = jnp.sum(first_normed_gradient, axis=0)
    grad_rows = d_residual + layer_norm_backward(
        first_normed_gradient * first_norm_gain,
        first_centered_scaled,
        first_inverse_deviation,
        local_totals,
        hidden_width,
    )
    grad_in = to_channels(grad_rows[:, None, :])[:, 0, :]
    (
        in_part,
        out_table,
        up_table,
        down_table,
        first_norm_gain_gradient,
        g_ln1_bias,
        g_out_bias,
        second_norm_gain_gradient,
        g_ln2_bias,
        g_up_bias,
        g_down_bias,
    ) = (
        lax.psum_scatter(
            in_full.reshape(hidden_width, 3, hidden_width), "chan", scatter_dimension=2, tiled=True
        ),
        lax.psum_scatter(out_full, "chan", scatter_dimension=0, tiled=True),
        lax.psum_scatter(up_full, "chan", scatter_dimension=0, tiled=True),
        lax.psum_scatter(down_full, "chan", scatter_dimension=0, tiled=True),
        lax.psum_scatter(first_norm_gain_gradient, "chan", scatter_dimension=0, tiled=True),
        lax.psum_scatter(g_ln1_bias, "chan", scatter_dimension=0, tiled=True),
        lax.psum_scatter(g_out_bias, "chan", scatter_dimension=0, tiled=True),
        lax.psum_scatter(second_norm_gain_gradient, "chan", scatter_dimension=0, tiled=True),
        lax.psum_scatter(g_ln2_bias, "chan", scatter_dimension=0, tiled=True),
        lax.psum_scatter(g_up_bias, "chan", scatter_dimension=0, tiled=True),
        lax.psum_scatter(g_down_bias, "chan", scatter_dimension=0, tiled=True),
    )
    in_table = in_part.reshape(hidden_width, -1)
    kernel_grad = lax.psum_scatter(d_kernel, "batch", scatter_dimension=0, tiled=True)
    filter_grads = filter_pull(kernel_grad)
    g_filt_in, g_filt_in_bias, g_filt_mid, g_filt_mid_bias, g_sine_freq = lax.psum(
        (filter_grads[0], filter_grads[1], filter_grads[2], filter_grads[3], filter_grads[4]),
        ("batch", "chan"),
    )
    (
        first_norm_gain_gradient,
        g_ln1_bias,
        g_in_bias,
        g_short_weight,
        g_short_bias,
        g_filt_out,
        g_decay_rate,
        g_conv_bias,
        g_out_bias,
        second_norm_gain_gradient,
        g_ln2_bias,
        g_up_bias,
        g_down_bias,
    ) = lax.psum(
        (
            first_norm_gain_gradient,
            g_ln1_bias,
            g_in_bias,
            g_short_weight,
            g_short_bias,
            filter_grads[5],
            filter_grads[6],
            g_conv_bias,
            g_out_bias,
            second_norm_gain_gradient,
            g_ln2_bias,
            g_up_bias,
            g_down_bias,
        ),
        "batch",
    )
    in_grad, out_grad, up_grad, down_grad = (
        lax.psum_scatter(in_table, "batch", scatter_dimension=0, tiled=True),
        lax.psum_scatter(out_table, "batch", scatter_dimension=1, tiled=True),
        lax.psum_scatter(up_table, "batch", scatter_dimension=1, tiled=True),
        lax.psum_scatter(down_table, "batch", scatter_dimension=1, tiled=True),
    )
    return (
        to_columns(layer_out, seq_count),
        to_columns(grad_in, seq_count),
        first_norm_gain_gradient,
        g_ln1_bias,
        in_grad.reshape(in_grad.shape[0], 3, cols_n),
        g_in_bias,
        g_short_weight,
        g_short_bias,
        g_filt_in,
        g_filt_in_bias,
        g_filt_mid,
        g_filt_mid_bias,
        g_sine_freq,
        g_filt_out,
        g_decay_rate,
        g_conv_bias,
        out_grad,
        g_out_bias,
        second_norm_gain_gradient,
        g_ln2_bias,
        up_grad,
        g_up_bias,
        down_grad,
        g_down_bias,
    )


def solution(mesh):
    in_specs = (
        P("batch", "chan", None),
        P("batch"),
        P("chan"),
        P("chan"),
        P(None, None, "chan"),
        P(None, "chan"),
        P(None, None, "chan"),
        P(None, "chan"),
        P(),
        P(),
        P(),
        P(),
        P(),
        P(None, "chan"),
        P("chan"),
        P("chan"),
        P("chan", None),
        P("chan"),
        P("chan"),
        P("chan"),
        P("chan", None),
        P("chan"),
        P("chan", None),
        P("chan"),
        P("batch", "chan", None),
    )
    out_specs = (
        P("batch", "chan", None),
        P("batch", "chan", None),
        P("chan"),
        P("chan"),
        P("batch", None, "chan"),
        P(None, "chan"),
        P(None, None, "chan"),
        P(None, "chan"),
        P(),
        P(),
        P(),
        P(),
        P(),
        P(None, "chan"),
        P("chan"),
        P("chan"),
        P("chan", "batch"),
        P("chan"),
        P("chan"),
        P("chan"),
        P("chan", "batch"),
        P("chan"),
        P("chan", "batch"),
        P("chan"),
    )
    return jax.shard_map(
        on_device, mesh=mesh, in_specs=in_specs, out_specs=out_specs, check_vma=False
    )
```

profile of v0, /device:TPU:0, one launch (start us, length us, event | category | flops | bytes accessed | tf_op | source)
XLA Modules:
  0.0 1236.6 jit_solution(8126092752366958704)
XLA Ops:
  18.1 45.2 %reduce.10 = bf16[8192,48]{1,0:T(8,128)(2,1)S(1)} reduce(bf16[8192,1,48]{2,1,0:T(2,128)(2,1)} %reshape.579, bf16[]{:T(256)} %broadcast.552), dimensions={1}, to_apply=%reshape.579.reduce_sub_computation | reduce | bytes 1572866 | tf_op jit(solution)/shard_map/convert_element_type | solution.py:142
  78.2 66.7 %all-reduce.19 = (bf16[768]{0:T(1024)(128)(2,1)S(1)}, bf16[768]{0:T(1024)(128)(2,1)S(1)}, bf16[768]{0:T(1024)(128)(2,1)S(1)}, bf16[768]{0:T(1024)(128)(2,1)}, bf...) all-reduce(bf16[768]{0:T(1024)(128)(2,1)S(1)} %dynamic-update-slice, ...), channel_id=1, replica_groups=mesh['batch'=2,'chan'=16] {'chan'}, use_global_device_ids=true, to_apply=%add.3 | all-reduce | flops 7680 | bytes 30720
  153.6 8.5 convert_element_type.382
  165.3 62.4 %convert_reduce_fusion = f32[8192]{0:T(1024)S(1)} fusion(bf16[8192,1,48]{2,1,0:T(2,128)(2,1)} %reshape.589), kind=kLoop, calls=%fused_computation.339 | loop fusion | flops 778240 | bytes 819200 | tf_op jit(solution)/shard_map/reduce_sum | solution.py:115
  256.8 12.2 all_gather.39
  277.2 45.2 %reduce.13 = bf16[8192,48]{1,0:T(8,128)(2,1)S(1)} reduce(bf16[8192,1,48]{2,1,0:T(2,128)(2,1)} %reshape.580, bf16[]{:T(256)} %broadcast.552), dimensions={1}, to_apply=%reshape.580.reduce_sub_computation | reduce | bytes 1572866 | tf_op jit(solution)/shard_map/convert_element_type | solution.py:145
  336.7 53.8 %all-to-all-done.1 = f32[512,3,768]{0,1,2:T(4,128)} async-done(((f32[512,3,768]{0,1,2:T(4,128)}), f32[512,3,768]{0,1,2:T(4,128)}, u32[]{:S(2)}, u32[]{:S(2)}) %all-to-all-start.1) | async-done | bytes 4718624 | tf_op jit(solution)/shard_map/all_to_all | solution.py:155
  390.5 28.3 %all-to-all-start.4 = ((bf16[16,2,12288]{2,1,0:T(2,128)(2,1)}), bf16[16,2,12288]{2,1,0:T(2,128)(2,1)}, u32[]{:S(2)}, u32[]{:S(2)}) async-start(bf16[16,2,12288]{2,1,0:T(2,128)(2,1)} %reshape.594), calls=%async_computation.4 | async-start | bytes 1572864 | tf_op jit(solution)/shard_map/all_to_all | solution.py:144
  442.5 12.7 %multiply_add_fusion.1 = f32[2,4096,3,48]{1,0,3,2:T(2,128)S(1)} fusion(f32[2,4096,3,48]{1,0,3,2:T(2,128)S(1)} %broadcast_add_fusion, f32[3,48]{1,0:T(4,128)S(1)} %get-tuple-element.232, f32[3,48]{1,0:T(4,128)S(1)} %get-tuple-element.233, f32[3,48]{1,0:T(4,128)S(1)} %get-tuple-element.231, f32[3,48]{1,0:T(4,128)S(1)} %convert_element_type.338), kind=kLoop, calls=%fused_computation.15 | loop fusion | flops 7077888 | bytes 9439488 | tf_op jit(solution)/shard_map/add | solution.py:249
  544.5 10.5 reshape.595
  555.0 8.8 copy.286
  572.2 10.5 reshape.591
  582.7 8.8 copy.278
  606.4 10.6 fusion.368
  624.2 10.4 fusion.353
  655.7 8.8 fusion.41
  664.6 26.3 %all-to-all-done.5 = f32[512,1,768]{0,1,2:T(1,128)} async-done(((f32[512,1,768]{0,1,2:T(1,128)}), f32[512,1,768]{0,1,2:T(1,128)}, u32[]{:S(2)}, u32[]{:S(2)}) %all-to-all-start.5) | async-done | bytes 1572896 | tf_op jit(solution)/shard_map/all_to_all | solution.py:155
  753.7 8.5 slice_multiply_fusion.2
  765.8 13.3 %multiply_reduce_fusion.1 = (f32[3,48]{1,0:T(4,128)S(1)}, f32[3,48]{1,0:T(4,128)S(1)}, f32[3,48]{1,0:T(4,128)S(1)}, f32[2,4096,3,48]{1,0,3,2:T(2,128)S(1)}) fusion(f32[2,4096,3,48]{1,0,3,2:T(2,128)S(1)} %bitcast.457, f32[2,4096,1,48]{1,0,3,2:T(2,128)S(1)} %slice_multiply_fusion, f32[2,4096,1,48]{1,0,3,2:T(2,128)S(1)} %get-tuple-element.224, ...), kind=kLoop, calls=%fused_computation.13 | loop fusion | flops 8257104 | bytes 14157504 | tf_op jit(solution)/shard_map/reduce_sum | solution.py:359
  779.2 16.8 %fusion.365 = (f32[3,48]{1,0:T(4,128)S(1)}, bf16[2,4096,3,48]{1,0,3,2:T(2,128)(2,1)}) fusion(f32[3,48]{1,0:T(4,128)S(1)} %copy-done.68, f32[2,4096,3,48]{1,0,3,2:T(2,128)S(1)} %get-tuple-element.219, f32[3,48]{1,0:T(4,128)S(1)} %copy-done.70, f32[3,48]{1,0:T(4,128)S(1)} %copy-done.66), kind=kLoop, calls=%fused_computation.454 | loop fusion | flops 8257392 | bytes 7080192 | tf_op jit(solution)/shard_map/reduce_sum | solution.py:367
  796.0 21.6 %copy.321 = bf16[2,4096,3,48]{3,2,1,0:T(4,128)(2,1)} copy(bf16[2,4096,3,48]{1,0,3,2:T(2,128)(2,1)} %get-tuple-element.221) | data formatting | bytes 4718592 | tf_op jit(solution)/shard_map/convert_element_type | solution.py:368
  817.6 14.9 %reshape.596 = bf16[16,2,36864]{2,1,0:T(2,128)(2,1)} reshape(bf16[8192,3,48]{2,1,0:T(4,128)(2,1)} %bitcast.458) | data formatting | bytes 4718592
  832.5 11.5 all-to-all-start.6
  857.9 61.1 %all-to-all-done.6 = bf16[16,2,36864]{2,1,0:T(2,128)(2,1)} async-done(((bf16[16,2,36864]{2,1,0:T(2,128)(2,1)}), bf16[16,2,36864]{2,1,0:T(2,128)(2,1)}, u32[]{:S(2)}, u32[]{:S(2)}) %all-to-all-start.6) | async-done | bytes 2359328 | tf_op jit(solution)/shard_map/all_to_all | solution.py:151
  919.0 15.7 %reshape.597 = bf16[8192,3,48]{2,1,0:T(4,128)(2,1)} reshape(bf16[16,2,36864]{2,1,0:T(2,128)(2,1)} %all-to-all-done.6) | data formatting | bytes 4718592
  934.7 12.1 copy.323
  954.2 8.8 multiply_bitcast_fusion.1
  973.8 20.6 %all-to-all-start.3 = ((bf16[16,2,12288]{2,1,0:T(2,128)(2,1)}), bf16[16,2,12288]{2,1,0:T(2,128)(2,1)S(1)}, u32[]{:S(2)}, u32[]{:S(2)}) async-start(bf16[16,2,12288]{2,1,0:T(2,128)(2,1)} %reshape.592), calls=%async_computation.3 | async-start | bytes 1572864 | tf_op jit(solution)/shard_map/all_to_all | solution.py:155
  1059.1 49.2 %reduce-scatter.10.cloned.1.call-done = f32[768,3,48]{0,2,1:T(8,128)} async-done(((f32[768,3,768]{0,2,1:T(8,128)}), f32[768,3,48]{0,2,1:T(8,128)}) %reduce-scatter.10.cloned.1.call-update) | async-done | bytes 442384 | tf_op jit(solution)/shard_map/reduce_scatter | solution.py:402
  1111.4 41.6 %all-reduce.16 = (f32[33,64]{1,0:T(8,128)}, f32[64]{0:T(128)}, f32[64,64]{1,0:T(8,128)}, f32[64]{0:T(128)}, f32[64]{0:T(128)}) all-reduce(f32[33,64]{1,0:T(8,128)S(1)} %fusion.88, f32[64]{0:T(128)S(1)} %get-tuple-element.238, f32[64,64]{1,0:T(8,128)S(1)} %fusion.92, ...), channel_id=1, replica_groups=mesh['batch'=2,'chan'=16] {'batch','chan'}, use_global_device_ids=true, to_apply=%region_28.29 | all-reduce | flops 6400 | bytes 51200 | tf_op jit(solution)/shard_map/psum | solution.py:419
  1155.6 58.8 %all-reduce.17 = (f32[768]{0:T(1024)S(1)}, f32[768]{0:T(1024)S(1)}, f32[768]{0:T(1024)S(1)}, f32[768]{0:T(1024)S(1)}, f32[768]{0:T(1024)S(1)}, /*index=5*/f32[3072]{0:T(1024)S(1)}, f32[768]{0:T(1024)S(1)}) all-reduce(f32[768]{0:T(1024)S(1)} %get-tuple-element.175, ...), channel_id=2, replica_groups=mesh['batch'=2,'chan'=16] {'chan'}, use_global_device_ids=true, to_apply=%region_10.11.clone | all-reduce | flops 7680 | bytes 61440
  1214.9 9.0 all-reduce.18
  (423 shorter events, 424.9 us)
Async XLA Ops:
  7.2 243.3 %copy-start = (f32[64,64]{1,0:T(8,128)S(1)}, f32[64,64]{1,0:T(8,128)}, u32[]{:S(2)}) copy-start(f32[64,64]{1,0:T(8,128)} %param.35) | copy-start | bytes 49156
  7.2 222.0 %all-gather.5.cloned.1.call-start = ((), (), s32[]{:S(2)}) async-start(), calls=%async_computation.17 | async-start | bytes 3760128 | tf_op jit(solution)/shard_map/all_gather | solution.py:222
  7.9 586.3 %all-gather.7.cloned.1.call-start = ((), (), s32[]{:S(2)}) async-start(), calls=%async_computation.18 | async-start | bytes 1253376 | tf_op jit(solution)/shard_map/all_gather | solution.py:223
  8.7 589.6 %all-gather.9.cloned.1.call-start = ((), (), s32[]{:S(2)}) async-start(), calls=%async_computation.19 | async-start | bytes 5013504 | tf_op jit(solution)/shard_map/all_gather | solution.py:225
  67.2 78.5 %all-to-all-start = ((bf16[16,2,12288]{2,1,0:T(2,128)(2,1)}), bf16[16,2,12288]{2,1,0:T(2,128)(2,1)S(1)}, u32[]{:S(2)}, u32[]{:S(2)}) async-start(bf16[16,2,12288]{2,1,0:T(2,128)(2,1)} %reshape.588), calls=%async_computation | async-start | bytes 1572864 | tf_op jit(solution)/shard_map/all_to_all | solution.py:141
  165.3 63.5 %copy-start.13 = (f32[16,512,1,48]{1,0,3,2:T(8,128)}, f32[16,512,1,48]{1,0,3,2:T(8,128)S(1)}, u32[]{:S(2)}) copy-start(f32[16,512,1,48]{1,0,3,2:T(8,128)S(1)} %copy.318) | copy-start | bytes 4718596
  243.1 147.4 %all-to-all-start.1 = ((f32[512,3,768]{0,1,2:T(4,128)}), f32[512,3,768]{0,1,2:T(4,128)}, u32[]{:S(2)}, u32[]{:S(2)}) async-start(f32[512,3,768]{0,1,2:T(4,128)} %copy.271), calls=%async_computation.1 | async-start | bytes 12582912 | tf_op jit(solution)/shard_map/all_to_all | solution.py:155
  247.9 358.6 %all-gather.11.cloned.1.call-start = ((), (), s32[]{:S(2)}) async-start(), calls=%async_computation.20 | async-start | bytes 5013504 | tf_op jit(solution)/shard_map/all_gather | solution.py:226
  248.5 189.0 %copy-start.63 = (f32[3,48]{1,0:T(4,128)}, f32[3,48]{1,0:T(4,128)S(1)}, u32[]{:S(2)}) copy-start(f32[3,48]{1,0:T(4,128)S(1)} %convert_element_type.345) | copy-start | bytes 1732
  326.9 115.6 %copy-start.65 = (f32[3,48]{1,0:T(4,128)}, f32[3,48]{1,0:T(4,128)S(1)}, u32[]{:S(2)}) copy-start(f32[3,48]{1,0:T(4,128)S(1)} %get-tuple-element.231) | copy-start | bytes 1732
  326.9 115.6 %copy-start.67 = (f32[3,48]{1,0:T(4,128)}, f32[3,48]{1,0:T(4,128)S(1)}, u32[]{:S(2)}) copy-start(f32[3,48]{1,0:T(4,128)S(1)} %get-tuple-element.232) | copy-start | bytes 1732
  326.9 115.6 %copy-start.69 = (f32[3,48]{1,0:T(4,128)}, f32[3,48]{1,0:T(4,128)S(1)}, u32[]{:S(2)}) copy-start(f32[3,48]{1,0:T(4,128)S(1)} %get-tuple-element.233) | copy-start | bytes 1732
  390.5 141.1 %all-to-all-start.4 = ((bf16[16,2,12288]{2,1,0:T(2,128)(2,1)}), bf16[16,2,12288]{2,1,0:T(2,128)(2,1)}, u32[]{:S(2)}, u32[]{:S(2)}) async-start(bf16[16,2,12288]{2,1,0:T(2,128)(2,1)} %reshape.594), calls=%async_computation.4 | async-start | bytes 1572864 | tf_op jit(solution)/shard_map/all_to_all | solution.py:144
  531.5 40.7 %all-to-all-start.2 = ((bf16[16,2,12288]{2,1,0:T(2,128)(2,1)}), bf16[16,2,12288]{2,1,0:T(2,128)(2,1)}, u32[]{:S(2)}, u32[]{:S(2)}) async-start(bf16[16,2,12288]{2,1,0:T(2,128)(2,1)} %reshape.590), calls=%async_computation.2 | async-start | bytes 1572864 | tf_op jit(solution)/shard_map/all_to_all | solution.py:151
  537.7 456.9 %reduce-scatter.16.cloned.1.call-start = ((), (), s32[]{:S(2)}) async-start(), calls=%async_computation.24 | async-start | bytes 2506752 | tf_op jit(solution)/shard_map/reduce_scatter | solution.py:405
  624.1 378.2 %reduce-scatter.24.cloned.1.call-start = ((), (), s32[]{:S(2)}) async-start(), calls=%async_computation.28 | async-start | bytes 10027008 | tf_op jit(solution)/shard_map/reduce_scatter | solution.py:407
  643.4 47.5 %all-to-all-start.5 = ((f32[512,1,768]{0,1,2:T(1,128)}), f32[512,1,768]{0,1,2:T(1,128)}, u32[]{:S(2)}, u32[]{:S(2)}) async-start(f32[512,1,768]{0,1,2:T(1,128)} %copy.289), calls=%async_computation.5 | async-start | bytes 3145728 | tf_op jit(solution)/shard_map/all_to_all | solution.py:155
  649.4 396.9 %reduce-scatter.20.cloned.1.call-start = ((), (), s32[]{:S(2)}) async-start(), calls=%async_computation.26 | async-start | bytes 10027008 | tf_op jit(solution)/shard_map/reduce_scatter | solution.py:406
  832.5 86.5 %all-to-all-start.6 = ((bf16[16,2,36864]{2,1,0:T(2,128)(2,1)}), bf16[16,2,36864]{2,1,0:T(2,128)(2,1)}, u32[]{:S(2)}, u32[]{:S(2)}) async-start(bf16[16,2,36864]{2,1,0:T(2,128)(2,1)} %reshape.596), calls=%async_computation.6 | async-start | bytes 4718592 | tf_op jit(solution)/shard_map/all_to_all | solution.py:151
  844.0 209.0 %reduce-scatter.14.cloned.1.call-start = ((), (), s32[]{:S(2)}) async-start(), calls=%async_computation.23 | async-start | bytes 1179648 | tf_op jit(solution)/shard_map/reduce_scatter | solution.py:417
  857.9 250.5 %reduce-scatter.10.cloned.1.call-start = ((), (), s32[]{:S(2)}) async-start(), calls=%async_computation.21 | async-start | bytes 7520256 | tf_op jit(solution)/shard_map/reduce_scatter | solution.py:402
  973.8 39.3 %all-to-all-start.3 = ((bf16[16,2,12288]{2,1,0:T(2,128)(2,1)}), bf16[16,2,12288]{2,1,0:T(2,128)(2,1)S(1)}, u32[]{:S(2)}, u32[]{:S(2)}) async-start(bf16[16,2,12288]{2,1,0:T(2,128)(2,1)} %reshape.592), calls=%async_computation.3 | async-start | bytes 1572864 | tf_op jit(solution)/shard_map/all_to_all | solution.py:155
  994.5 235.4 %reduce-scatter.18.cloned.1.call-start = ((), (), s32[]{:S(2)}) async-start(), calls=%async_computation.25 | async-start | bytes 221184 | tf_op jit(solution)/shard_map/reduce_scatter | solution.py:457
  995.1 234.8 %reduce-scatter.26.cloned.1.call-start = ((), (), s32[]{:S(2)}) async-start(), calls=%async_computation.29 | async-start | bytes 884736 | tf_op jit(solution)/shard_map/reduce_scatter | solution.py:459
  1013.2 210.8 %all-to-all-start.7 = ((f32[512,1,768]{0,1,2:T(1,128)}), f32[512,1,768]{0,1,2:T(1,128)}, u32[]{:S(2)}, u32[]{:S(2)}) async-start(f32[512,1,768]{0,1,2:T(1,128)} %copy.300), calls=%async_computation.7 | async-start | bytes 3145728 | tf_op jit(solution)/shard_map/all_to_all | solution.py:155
  1018.7 211.1 %reduce-scatter.22.cloned.1.call-start = ((), (), s32[]{:S(2)}) async-start(), calls=%async_computation.27 | async-start | bytes 884736 | tf_op jit(solution)/shard_map/reduce_scatter | solution.py:458
  1046.3 183.6 %reduce-scatter.12.cloned.1.call-start = ((), (), s32[]{:S(2)}) async-start(), calls=%async_computation.22 | async-start | bytes 663552 | tf_op jit(solution)/shard_map/reduce_scatter | solution.py:456
  1052.9 55.4 %copy-start.49 = (f32[2048,16]{0,1:T(8,128)S(1)}, f32[2048,16]{0,1:T(8,128)}, u32[]{:S(2)}) copy-start(f32[2048,16]{0,1:T(8,128)} %copy-done.48) | copy-start | bytes 393220
  1052.9 55.4 %copy-start.55 = (f32[2048,1]{0,1:T(1,128)S(1)}, f32[2048,1]{0,1:T(1,128)}, u32[]{:S(2)}) copy-start(f32[2048,1]{0,1:T(1,128)} %copy-done.54) | copy-start | bytes 24580
  1053.0 100.0 %copy-start.44 = (f32[2048,48]{0,1:T(8,128)S(1)}, f32[2048,48]{0,1:T(8,128)}, u32[]{:S(2)}) copy-start(f32[2048,48]{0,1:T(8,128)} %get-tuple-element.243) | copy-start | bytes 1179652
  1053.1 99.9 %copy-start.40 = (f32[2048,48]{0,1:T(8,128)S(1)}, f32[2048,48]{0,1:T(8,128)}, u32[]{:S(2)}) copy-start(f32[2048,48]{0,1:T(8,128)} %reduce-scatter.14.cloned.1.call-done) | copy-start | bytes 1179652
  1056.5 99.1 %copy-start.71 = (f32[3072]{0:T(1024)S(1)}, f32[3072]{0:T(1024)}, u32[]{:S(2)}) copy-start(f32[3072]{0:T(1024)} %get-tuple-element.247) | copy-start | bytes 36868
  (85 other events, 676.4 us)
Sparse Core Ops, SparseCore 0:
  10.3 49.9 all-gather.4
  62.6 42.7 all-gather.6
  107.6 52.4 all-gather.8
  250.7 124.0 all-gather.10
  624.3 81.2 reduce-scatter.15
  710.1 110.7 reduce-scatter.23
  824.9 152.1 reduce-scatter.19
  979.4 17.1 reduce-scatter.13
  1000.6 107.6 reduce-scatter.9
  1111.1 10.1 reduce-scatter.17
  1124.2 15.2 reduce-scatter.25
  1142.2 15.7 reduce-scatter.21
  1160.8 13.4 reduce-scatter.11
where the time goes:
time: 1250 us; the launch traced here: 1240 us
  local copies, waits for them, and re-layouts  280 us (22%)
  other arithmetic  252 us (20%)
  matrix products  210 us (17%)
  waiting for transfers between devices  195 us (16%)
  blocking collectives  188 us (15%)
  starting transfers between devices  91.6 us (7%)
  between operations  18.5 us (1%)
    unnamed x2, blocking collectives  125 us
    unnamed x234, local copies, waits for them, and re-layouts  103 us
    all_to_all x4, waiting for transfers between devices, to_channels(): lax.all_to_all(values, 'chan', split_axis=2, concat_axis=0, tiled=True)  82 us
    reduce_sum x3, other arithmetic, local_totals(): return (jnp.sum(linear_term, axis=1), jnp.sum(square_term, axis=1))  62.6 us
    all_to_all x2, waiting for transfers between devices, rows_low(): lax.all_to_all(values, 'chan', split_axis=0, concat_axis=2, tiled=True)  61.1 us
    reduce_scatter x1, waiting for transfers between devices, on_device(): lax.psum_scatter(in_full.reshape(hidden_width, 3, hidden_width), 'chan',...  49.2 us
    convert_element_type x1, other arithmetic, rows_exact(): first.astype(jnp.bfloat16)  45.2 us
    convert_element_type x1, other arithmetic, rows_exact(): second.astype(jnp.bfloat16)  45.2 us
  transfers between devices with their start and end apart: 21, of which 5 were waited for; matrix products, arithmetic and copies ran while one was open for 58% of the time, Pallas kernels for 0%

commit v1 on v0

v1 whole, which is shorter than its diff:
```python
import math

import jax
import jax.numpy as jnp
import numpy as np
from jax import lax
from jax.experimental import pallas as pl
from jax.experimental.pallas import tpu as pltpu
from jax.sharding import PartitionSpec as P

EMB = 33
KS = 3
LMAX = 4096
LANE = 128
COARSE = LMAX // LANE
REPS = tuple(ka + 8 * kb for ka, count in ((0, 5), (1, 8), (2, 8), (3, 8), (4, 4)) for kb in range(count))
PLACE = {k1: i for i, k1 in enumerate(REPS)}
epsilon = 1e-05
decay_floor = 0.05
highest = lax.Precision.HIGHEST
f32 = jnp.float32
bf16 = jnp.bfloat16
vmem_limit = 56 * 1024 * 1024


def unit(turns):
    angle = 2.0 * math.pi * turns
    return math.cos(angle), math.sin(angle)


def scaled(z, c, s):
    re, im = z
    if im is None:
        return re * c, re * s
    return re * c - im * s, re * s + im * c


def plus(a, b):
    return a[0] + b[0], a[1] + b[1]


def minus(a, b):
    return a[0] - b[0], a[1] - b[1]


def dft4(z, sign):
    s0, d0 = plus(z[0], z[2]), minus(z[0], z[2])
    s1, d1 = plus(z[1], z[3]), minus(z[1], z[3])
    turned = (-d1[1], d1[0]) if sign > 0 else (d1[1], -d1[0])
    return [plus(s0, s1), plus(d0, turned), minus(s0, s1), minus(d0, turned)]


def dft8(z, sign):
    even, odd = dft4(z[0::2], sign), dft4(z[1::2], sign)
    c = math.sqrt(0.5)
    o1 = odd[1]
    o3 = odd[3]
    if sign > 0:
        odd1 = ((o1[0] - o1[1]) * c, (o1[0] + o1[1]) * c)
        odd2 = (-odd[2][1], odd[2][0])
        odd3 = ((-o3[0] - o3[1]) * c, (o3[0] - o3[1]) * c)
    else:
        odd1 = ((o1[0] + o1[1]) * c, (o1[1] - o1[0]) * c)
        odd2 = (odd[2][1], -odd[2][0])
        odd3 = ((o3[1] - o3[0]) * c, (-o3[0] - o3[1]) * c)
    turned = [odd[0], odd1, odd2, odd3]
    return [plus(even[i], turned[i]) for i in range(4)] + [minus(even[i], turned[i]) for i in range(4)]


def coarse_forward(xs, put):
    c = math.sqrt(0.5)
    cols = {ka: [None] * 8 for ka in range(5)}
    for b in range(8):
        x0, x1, x2, x3 = xs[b], xs[8 + b], xs[16 + b], xs[24 + b]
        s02, d02, s13, d13 = x0 + x2, x0 - x2, x1 + x3, x1 - x3
        d13c, s13c = d13 * c, s13 * c
        cols[0][b] = s02 + s13
        cols[4][b] = scaled((s02 - s13, None), *unit(-4 * b / 64))
        cols[2][b] = scaled((d02, -d13), *unit(-2 * b / 64))
        cols[1][b] = scaled((x0 + d13c, -s13c - x2), *unit(-b / 64))
        cols[3][b] = scaled((x0 - d13c, x2 - s13c), *unit(-3 * b / 64))
    for ka in (1, 2, 3):
        for kb, z in enumerate(dft8(cols[ka], -1)):
            put(ka + 8 * kb, z)
    for kb, z in enumerate(dft8(cols[4], -1)[:4]):
        put(4 + 8 * kb, z)
    r = cols[0]
    s04, d04, s26, d26 = r[0] + r[4], r[0] - r[4], r[2] + r[6], r[2] - r[6]
    s15, d15, s37, d37 = r[1] + r[5], r[1] - r[5], r[3] + r[7], r[3] - r[7]
    p, q = (d15 - d37) * c, (d15 + d37) * c
    even, odd = s04 + s26, s15 + s37
    put(0, (even + odd, None))
    put(32, (even - odd, None))
    put(16, (s04 - s26, s37 - s15))
    put(8, (d04 + p, -d26 - q))
    put(24, (d04 - p, d26 - q))


def coarse_inverse(get):
    c = math.sqrt(0.5)
    u = {}
    for ka in (1, 2, 3):
        back = dft8([get(ka + 8 * kb) for kb in range(8)], 1)
        u[ka] = [scaled(back[b], *unit(b * ka / 64)) for b in range(8)]
    v0, v32 = get(0)[0], get(32)[0]
    v8, v16, v24 = get(8), get(16), get(24)
    flat = []
    for b in range(8):
        total = v0 + v32 if b % 2 == 0 else v0 - v32
        for kb, v in ((1, v8), (2, v16), (3, v24)):
            co, si = unit(b * kb / 8)
            if abs(co) > 1e-9:
                total = total + v[0] * (2.0 * co)
            if abs(si) > 1e-9:
                total = total - v[1] * (2.0 * si)
        flat.append(total)
    odd = [get(4 + 8 * kb) for kb in range(4)]
    odd = odd + [(z[0], -z[1]) for z in odd[::-1]]
    half = dft8(odd, 1)
    quarter = []
    for b in range(8):
        co, si = unit(4 * b / 64)
        quarter.append(half[b][0] * co - half[b][1] * si)
    out = [None] * COARSE
    for b in range(8):
        u1, u2, u3 = u[1][b], u[2][b], u[3][b]
        s, d = flat[b] + quarter[b], flat[b] - quarter[b]
        dr, sr = (u1[0] - u3[0]) * c, u1[0] + u3[0]
        si_, di = (u1[1] + u3[1]) * c, u1[1] - u3[1]
        out[b] = s + 2.0 * (sr + u2[0])
        out[16 + b] = s - 2.0 * (di + u2[0])
        out[8 + b] = d + 2.0 * (dr - si_ - u2[1])
        out[24 + b] = d + 2.0 * (u2[1] - dr - si_)
    return out


def transform_tables():
    fine = np.arange(LANE)
    angle = 2.0 * math.pi * ((fine[:, None] * fine[None, :]) % LANE) / LANE
    co, si = np.cos(angle), np.sin(angle)
    ahead = np.block([[co, -si], [si, co]])
    back = ahead.T / (2.0 * LMAX)
    reps = np.array(REPS)
    turn = 2.0 * math.pi * ((reps[:, None] * fine[None, :]) % (2 * LMAX)) / (2 * LMAX)
    twist = np.concatenate([np.cos(turn), -np.sin(turn)], axis=1)[:, None, :]

    def pieces(table):
        table = table.astype(np.float32)
        upper = table.astype(jnp.bfloat16)
        lower = (table - upper.astype(np.float32)).astype(jnp.bfloat16)
        return np.stack([upper, lower])

    return pieces(ahead), pieces(back), twist.astype(np.float32)


AHEAD, BACK, TWIST = transform_tables()


def three_pass(values, table_ref):
    upper = values.astype(bf16)
    lower = (values - upper.astype(f32)).astype(bf16)
    t0, t1 = table_ref[0], table_ref[1]
    return (
        jnp.dot(upper, t0, preferred_element_type=f32)
        + jnp.dot(lower, t0, preferred_element_type=f32)
        + jnp.dot(upper, t1, preferred_element_type=f32)
    )


def rows_forward(xs_ref, spec_ref, rows):
    def step(g, carry):
        at = pl.ds(pl.multiple_of(g * 8, 8), 8)
        xs = [xs_ref[n, at, :] for n in range(COARSE)]

        def put(k1, z):
            i = PLACE[k1]
            spec_ref[i, at, 0:LANE] = z[0]
            spec_ref[i, at, LANE : 2 * LANE] = jnp.zeros_like(z[0]) if z[1] is None else z[1]

        coarse_forward(xs, put)
        return carry

    lax.fori_loop(0, rows // 8, step, 0)


def rows_inverse(spec_ref, ys_ref, rows):
    def step(g, carry):
        at = pl.ds(pl.multiple_of(g * 8, 8), 8)

        def get(k1):
            i = PLACE[k1]
            return spec_ref[i, at, 0:LANE], spec_ref[i, at, LANE : 2 * LANE]

        for n, y in enumerate(coarse_inverse(get)):
            ys_ref[n, at, :] = y
        return carry

    lax.fori_loop(0, rows // 8, step, 0)


def fine_forward(spec, twist, ahead_ref):
    re, im = spec[:, :LANE], spec[:, LANE:]
    tr, ti = twist[:, :LANE], twist[:, LANE:]
    return three_pass(jnp.concatenate([re * tr - im * ti, re * ti + im * tr], axis=1), ahead_ref)


def fine_inverse(spec, twist, back_ref):
    v = three_pass(spec, back_ref)
    re, im = v[:, :LANE], v[:, LANE:]
    tr, ti = twist[:, :LANE], twist[:, LANE:]
    return jnp.concatenate([re * tr + im * ti, im * tr - re * ti], axis=1)


def times(a, b):
    ar, ai, br, bi = a[:, :LANE], a[:, LANE:], b[:, :LANE], b[:, LANE:]
    return jnp.concatenate([ar * br - ai * bi, ar * bi + ai * br], axis=1)


def times_conj(a, b):
    ar, ai, br, bi = a[:, :LANE], a[:, LANE:], b[:, :LANE], b[:, LANE:]
    return jnp.concatenate([ar * br + ai * bi, ai * br - ar * bi], axis=1)


def spread(blocks_ref, xs_ref):
    per = blocks_ref.shape[2] // LANE
    for n in range(COARSE):
        r = n % per
        xs_ref[n] = blocks_ref[n // per, :, r * LANE : (r + 1) * LANE].astype(f32)


def filter_spectrum_body(filter_ref, twist_ref, ahead_ref, out_ref, xs_ref):
    rows = filter_ref.shape[0]
    for n in range(COARSE):
        xs_ref[n] = filter_ref[:, n * LANE : (n + 1) * LANE]
    rows_forward(xs_ref, out_ref, rows)

    def step(i, carry):
        out_ref[i] = fine_forward(out_ref[i], twist_ref[i], ahead_ref)
        return carry

    lax.fori_loop(0, len(REPS), step, 0)


def conv_forward_body(seqs, mixed_ref, filt_ref, bias_ref, twist_ref, ahead_ref, back_ref, out_ref, spec_ref, xs_ref, work_ref):
    rows = mixed_ref.shape[1]
    spread(mixed_ref, xs_ref)
    rows_forward(xs_ref, spec_ref, rows)

    def step(i, carry):
        z = fine_forward(spec_ref[i], twist_ref[i], ahead_ref)
        spec_ref[i] = z
        k = filt_ref[i]
        work_ref[i] = fine_inverse(times(z, jnp.concatenate([k] * seqs, axis=0)), twist_ref[i], back_ref)
        return carry

    lax.fori_loop(0, len(REPS), step, 0)
    ys_ref = xs_ref
    rows_inverse(work_ref, ys_ref, rows)
    per = mixed_ref.shape[2] // LANE
    bias = jnp.concatenate([bias_ref[...]] * seqs, axis=0)
    for n in range(COARSE):
        at = (n // per, slice(None), slice((n % per) * LANE, (n % per + 1) * LANE))
        out_ref[at] = (ys_ref[n] + bias * mixed_ref[at].astype(f32)).astype(bf16)


def conv_backward_body(
    seqs, d_ref, mixed_ref, mixed_spec_ref, filt_ref, bias_ref, twist_ref, ahead_ref, back_ref, out_ref, dfilt_ref, dbias_ref, xs_ref, spec_ref, work_ref, ys_ref
):
    rows = d_ref.shape[1]
    chans = rows // seqs
    spread(d_ref, xs_ref)
    rows_forward(xs_ref, spec_ref, rows)

    def step(i, carry):
        z = fine_forward(spec_ref[i], twist_ref[i], ahead_ref)
        k = jnp.concatenate([filt_ref[i]] * seqs, axis=0)
        cross = times_conj(z, mixed_spec_ref[i])
        cross = sum(cross[s * chans : (s + 1) * chans] for s in range(seqs))
        both = jnp.concatenate([times_conj(z, k), cross], axis=0)
        work_ref[i] = fine_inverse(both, twist_ref[i], back_ref)
        return carry

    lax.fori_loop(0, len(REPS), step, 0)
    rows_inverse(work_ref, ys_ref, rows + chans)
    per = d_ref.shape[2] // LANE
    bias = jnp.concatenate([bias_ref[...]] * seqs, axis=0)
    total = jnp.zeros((rows, LANE), f32)
    for n in range(COARSE):
        at = (n // per, slice(None), slice((n % per) * LANE, (n % per + 1) * LANE))
        d = xs_ref[n]
        out_ref[at] = (ys_ref[n, :rows, :] + bias * d).astype(bf16)
        total = total + d * mixed_ref[at].astype(f32)
        dfilt_ref[:, n * LANE : (n + 1) * LANE] = ys_ref[n, rows:, :]
    total = sum(total[s * chans : (s + 1) * chans] for s in range(seqs))
    dbias_ref[...] = jnp.sum(total, axis=1, keepdims=True)


def whole_call(body, out_shape, scratch, *args):
    return pl.pallas_call(
        body,
        out_shape=out_shape,
        in_specs=[pl.BlockSpec(memory_space=pltpu.VMEM)] * len(args),
        out_specs=jax.tree.map(lambda _: pl.BlockSpec(memory_space=pltpu.VMEM), out_shape),
        scratch_shapes=scratch,
        compiler_params=pltpu.CompilerParams(vmem_limit_bytes=vmem_limit),
    )(*args)


def filter_spectrum(filt):
    rows = filt.shape[0]
    return whole_call(
        filter_spectrum_body,
        jax.ShapeDtypeStruct((len(REPS), rows, 2 * LANE), f32),
        [pltpu.VMEM((COARSE, rows, LANE), f32)],
        filt,
        jnp.asarray(TWIST),
        jnp.asarray(AHEAD),
    )


def conv_forward(mixed, filt_spec, bias, seqs):
    blocks, rows, width = mixed.shape
    n = len(REPS)
    return whole_call(
        lambda *refs: conv_forward_body(seqs, *refs),
        (jax.ShapeDtypeStruct(mixed.shape, bf16), jax.ShapeDtypeStruct((n, rows, 2 * LANE), f32)),
        [pltpu.VMEM((COARSE, rows, LANE), f32), pltpu.VMEM((n, rows, 2 * LANE), f32)],
        mixed,
        filt_spec,
        bias,
        jnp.asarray(TWIST),
        jnp.asarray(AHEAD),
        jnp.asarray(BACK),
    )


def conv_backward(d_conv, mixed, mixed_spec, filt_spec, bias, seqs):
    blocks, rows, width = mixed.shape
    chans = rows // seqs
    n = len(REPS)
    return whole_call(
        lambda *refs: conv_backward_body(seqs, *refs),
        (
            jax.ShapeDtypeStruct(mixed.shape, bf16),
            jax.ShapeDtypeStruct((chans, LMAX), f32),
            jax.ShapeDtypeStruct((chans, 1), f32),
        ),
        [
            pltpu.VMEM((COARSE, rows, LANE), f32),
            pltpu.VMEM((n, rows, 2 * LANE), f32),
            pltpu.VMEM((n, rows + chans, 2 * LANE), f32),
            pltpu.VMEM((COARSE, rows + chans, LANE), f32),
        ],
        d_conv,
        mixed,
        mixed_spec,
        filt_spec,
        bias,
        jnp.asarray(TWIST),
        jnp.asarray(AHEAD),
        jnp.asarray(BACK),
    )


def earlier(values, halo, by):
    lane = lax.broadcasted_iota(jnp.int32, values.shape, 1)
    moved = pltpu.roll(values, by, 1)
    for i in range(by):
        moved = jnp.where(lane == i, halo[:, KS - 1 - by + i : KS - by + i], moved)
    return moved


def later(values, halo, by):
    width = values.shape[1]
    lane = lax.broadcasted_iota(jnp.int32, values.shape, 1)
    moved = pltpu.roll(values, width - by, 1)
    for i in range(by):
        moved = jnp.where(lane == width - by + i, halo[:, i : i + 1], moved)
    return moved


def short_forward_body(seqs, proj_ref, halo_ref, prm_ref, short_ref, mixed_ref):
    width = proj_ref.shape[3] // seqs
    mixed = []
    for s in range(seqs):
        part = slice(s * width, (s + 1) * width)
        parts = []
        for i in range(3):
            prm = prm_ref[0, i]
            x = proj_ref[0, i, :, part] + prm[:, 0:1]
            halo = halo_ref[0, i][:, s * (KS - 1) : (s + 1) * (KS - 1)]
            y = prm[:, 1:2] + prm[:, 2:3] * x
            for j in range(1, KS):
                y = y + prm[:, 2 + j : 3 + j] * earlier(x, halo, j)
            short_ref[0, i, :, part] = y
            parts.append(y)
        mixed.append(parts[1] * parts[2])
    mixed_ref[0] = jnp.concatenate(mixed, axis=0).astype(bf16)


def short_forward(proj, halo, prm, seqs):
    devices, _, chans, cols = proj.shape
    block = lambda a: pl.BlockSpec((1,) + a.shape[1:], lambda d: (d,) + (0,) * (len(a.shape) - 1))
    out = (
        jax.ShapeDtypeStruct(proj.shape, f32),
        jax.ShapeDtypeStruct((devices, seqs * chans, cols // seqs), bf16),
    )
    return pl.pallas_call(
        lambda *refs: short_forward_body(seqs, *refs),
        grid=(devices,),
        out_shape=out,
        in_specs=[block(proj), block(halo), block(prm)],
        out_specs=tuple(block(o) for o in out),
        compiler_params=pltpu.CompilerParams(vmem_limit_bytes=vmem_limit),
    )(proj, halo, prm)


def short_backward_body(seqs, d_gated_ref, conv_ref, d_mixed_ref, proj_ref, halo_ref, short_ref, head_ref, prm_ref, out_ref, sums_ref):
    width = proj_ref.shape[3] // seqs
    sums = [[0.0] * (2 + KS) for _ in range(3)]
    for s in range(seqs):
        part = slice(s * width, (s + 1) * width)
        d_mixed = d_mixed_ref[0, :, part]
        d_short = (
            d_gated_ref[0, :, part] * conv_ref[0, :, part],
            d_mixed * short_ref[0, 2, :, part],
            d_mixed * short_ref[0, 1, :, part],
        )
        for i in range(3):
            prm = prm_ref[0, i]
            d = d_short[i]
            x = proj_ref[0, i, :, part] + prm[:, 0:1]
            halo = halo_ref[0, i][:, s * (KS - 1) : (s + 1) * (KS - 1)]
            head = head_ref[0, i][:, s * (KS - 1) : (s + 1) * (KS - 1)]
            back = prm[:, 2:3] * d
            sums[i][1] = sums[i][1] + jnp.sum(d, axis=1, keepdims=True)
            sums[i][2] = sums[i][2] + jnp.sum(d * x, axis=1, keepdims=True)
            for j in range(1, KS):
                back = back + prm[:, 2 + j : 3 + j] * later(d, head, j)
                sums[i][2 + j] = sums[i][2 + j] + jnp.sum(d * earlier(x, halo, j), axis=1, keepdims=True)
            sums[i][0] = sums[i][0] + jnp.sum(back, axis=1, keepdims=True)
            out_ref[0, i, :, part] = back
    for i in range(3):
        lane = lax.broadcasted_iota(jnp.int32, sums_ref.shape[2:], 1)
        total = jnp.zeros(sums_ref.shape[2:], f32)
        for k in range(2 + KS):
            total = jnp.where(lane == k, sums[i][k], total)
        sums_ref[0, i] = total


def short_backward(d_gated, conv, d_mixed, proj, halo, short, head, prm, seqs):
    devices, _, chans, cols = proj.shape
    block = lambda a: pl.BlockSpec((1,) + a.shape[1:], lambda d: (d,) + (0,) * (len(a.shape) - 1))
    args = (d_gated, conv, d_mixed, proj, halo, short, head, prm)
    out = (jax.ShapeDtypeStruct(proj.shape, f32), jax.ShapeDtypeStruct(prm.shape, f32))
    return pl.pallas_call(
        lambda *refs: short_backward_body(seqs, *refs),
        grid=(devices,),
        out_shape=out,
        in_specs=[block(a) for a in args],
        out_specs=tuple(block(o) for o in out),
        compiler_params=pltpu.CompilerParams(vmem_limit_bytes=vmem_limit),
    )(*args)


def position_table():
    places = np.arange(LMAX)
    orders = np.arange(1, (EMB - 1) // 2 + 1)
    turns = 2.0 * math.pi * ((orders[:, None] * places[None, :]) % LMAX) / LMAX
    ramp = places[None, :] / (LMAX - 1)
    return np.concatenate([ramp, np.cos(turns), -np.sin(turns)], axis=0).astype(np.float32)


FEAT = position_table()


def mm(a, b, dims):
    return lax.dot_general(a, b, (dims, ((), ())), precision=highest, preferred_element_type=f32)


NN = ((1,), (0,))
TN = ((0,), (0,))
NT = ((1,), (1,))


def mm16(a, b, dims):
    return lax.dot_general(a, b, (dims, ((), ())), preferred_element_type=f32)


def exchange(values):
    return lax.all_to_all(values, "chan", split_axis=0, concat_axis=0, tiled=True)


def norm_forward(values):
    mean = jnp.mean(values, axis=0, keepdims=True)
    centered = values - mean
    var = jnp.mean(centered * centered, axis=0, keepdims=True)
    inverse = lax.rsqrt(var + epsilon)
    return centered * inverse, inverse


def norm_backward(scaled_grad, normed, inverse):
    return inverse * (
        scaled_grad
        - jnp.mean(scaled_grad, axis=0, keepdims=True)
        - normed * jnp.mean(scaled_grad * normed, axis=0, keepdims=True)
    )


def on_device(
    layer_in,
    seq_lengths,
    ln1_gain,
    first_norm_bias,
    in_weight,
    in_bias,
    short_weight,
    short_bias,
    filt_in,
    filt_in_bias,
    filt_mid,
    filt_mid_bias,
    sine_freq,
    filt_out,
    decay_rate,
    conv_bias,
    out_weight,
    out_bias,
    ln2_gain,
    second_norm_bias,
    up_weight,
    up_bias,
    down_weight,
    down_bias,
    cotangent,
):
    seqs, chans, _ = layer_in.shape
    devices = lax.axis_size("chan")
    groups = lax.axis_size("batch")
    width = LMAX // devices
    dim = chans * devices
    cols = seqs * width
    hid = up_weight.shape[0]
    place = lax.axis_index("chan")

    def to_blocks(values):
        return (
            values.reshape(seqs, chans, devices, width)
            .transpose(2, 0, 1, 3)
            .reshape(devices, seqs * chans, width)
        )

    def from_blocks(blocks):
        return (
            blocks.reshape(devices, seqs, chans, width)
            .transpose(1, 2, 0, 3)
            .reshape(seqs, chans, LMAX)
        )

    def rows_of(blocks):
        return (
            blocks.reshape(devices, seqs, chans, width)
            .transpose(0, 2, 1, 3)
            .reshape(dim, cols)
        )

    def blocks_of(values):
        return (
            values.reshape(devices, chans, seqs, width)
            .transpose(0, 2, 1, 3)
            .reshape(devices, seqs * chans, width)
        )

    x_blocks = exchange(to_blocks(layer_in))
    small = jnp.concatenate(
        [
            in_bias.reshape(-1),
            short_bias.reshape(-1),
            short_weight.reshape(-1),
            ln1_gain,
            first_norm_bias,
            ln2_gain,
            second_norm_bias,
            out_bias,
            down_bias,
            up_bias,
        ]
    )
    small_rows = -(-small.shape[0] // (16 * dim)) * 16
    small = jnp.pad(small, (0, small_rows * dim - small.shape[0])).reshape(small_rows, dim)
    in_rows = in_weight.transpose(1, 2, 0).reshape(3 * chans, dim)
    gathered = lax.all_gather(jnp.concatenate([in_rows, small], axis=0), "chan", axis=0)
    cot_blocks = exchange(to_blocks(cotangent))
    out_all = lax.all_gather(out_weight, "chan", axis=0, tiled=True)
    up_all = lax.all_gather(up_weight, "chan", axis=0, tiled=True)
    down_all = lax.all_gather(down_weight, "chan", axis=0, tiled=True)

    in_all = gathered[:, : 3 * chans].reshape(3 * dim, dim)
    small_all = gathered[:, 3 * chans :].reshape(devices, small_rows * dim).astype(f32)
    by_chan = small_all[:, : 21 * chans].reshape(devices, 21, chans)
    up_bias_all = small_all[:, 21 * chans : 21 * chans + hid].reshape(devices * hid, 1)
    prm = jnp.concatenate(
        [
            by_chan[:, 0:3, None],
            by_chan[:, 3:6, None],
            by_chan[:, 6:15].reshape(devices, KS, 3, chans).transpose(0, 2, 1, 3),
            jnp.zeros((devices, 3, 8 - 2 - KS, chans), f32),
        ],
        axis=2,
    ).transpose(0, 1, 3, 2)
    wide = by_chan[:, 15:21].transpose(1, 0, 2).reshape(6, dim, 1)
    gain1, shift1, gain2, shift2, out_b, down_b = (wide[i] for i in range(6))

    feat = jnp.asarray(FEAT)
    ramp = feat[0:1]
    rate = sine_freq[:, None]
    pre1 = mm(filt_in, feat, TN) + filt_in_bias[:, None]
    h1 = jnp.sin(rate * pre1)
    pre2 = mm(filt_mid, h1, TN) + filt_mid_bias[:, None]
    h2 = jnp.sin(rate * pre2)
    raw = mm(filt_out, h2, TN)
    falling = jnp.exp(-ramp * decay_rate[:, None])
    env = falling + decay_floor
    filt_spec = filter_spectrum(raw * env)
    bias_col = conv_bias[:, None]

    x = rows_of(x_blocks).astype(f32)
    xhat1, rstd1 = norm_forward(x)
    xn1 = (xhat1 * gain1 + shift1).astype(bf16)
    proj = mm16(in_all, xn1, NN).reshape(devices, 3, chans, cols)
    tails = jnp.concatenate(
        [proj[..., (s + 1) * width - (KS - 1) : (s + 1) * width] for s in range(seqs)], axis=-1
    ).reshape(3 * dim, seqs * (KS - 1)).T + prm[..., 0].reshape(1, 3 * dim)
    halo = lax.ppermute(tails, "chan", [(i, i + 1) for i in range(devices - 1)])
    halo = halo.T.reshape(devices, 3, chans, seqs * (KS - 1))
    short, mixed = short_forward(proj, halo, prm, seqs)

    mixed_chan = exchange(mixed)
    conv_chan, mixed_spec = conv_forward(mixed_chan, filt_spec, bias_col, seqs)
    conv = rows_of(exchange(conv_chan)).astype(f32)

    gate_out = short[:, 0].reshape(dim, cols)
    gated = (conv * gate_out).astype(bf16)
    residual = x + mm16(out_all, gated, TN) + out_b
    xhat2, rstd2 = norm_forward(residual)
    xn2 = (xhat2 * gain2 + shift2).astype(bf16)
    hidden = mm16(up_all, xn2, NN) + up_bias_all
    act, gelu_pull = jax.vjp(lambda v: jax.nn.gelu(v, approximate=True), hidden)
    act = act.astype(bf16)
    positions = place * width + lax.iota(jnp.int32, width)
    live = (positions[None, :] < seq_lengths[:, None]).astype(f32).reshape(1, cols)
    result = live * (residual + mm16(down_all, act, TN) + down_b)
    out_blocks = exchange(blocks_of(result.astype(bf16)))
    d_final = live * rows_of(cot_blocks).astype(f32)
    d_mlp = d_final.astype(bf16)
    d_hidden = gelu_pull(mm16(down_all, d_mlp, NN))[0]
    d_hidden_low = d_hidden.astype(bf16)
    g_up_bias = jnp.sum(d_hidden, axis=1)
    g_down = mm16(act, d_mlp, NT)
    g_up = mm16(d_hidden_low, xn2, NT)
    d_xn2 = mm16(up_all, d_hidden_low, TN)
    d_residual = d_final + norm_backward(d_xn2 * gain2, xhat2, rstd2)
    d_branch = d_residual.astype(bf16)
    g_out = mm16(gated, d_branch, NT)
    d_gated = mm16(out_all, d_branch, NN)
    d_conv = exchange(blocks_of((d_gated * gate_out).astype(bf16)))

    def scatter(table):
        rows = table.shape[0] // devices
        table = table.astype(bf16).reshape(devices, rows, groups, dim // groups).transpose(2, 0, 1, 3)
        return lax.psum_scatter(
            table.reshape(groups * devices, rows, dim // groups),
            ("batch", "chan"),
            scatter_dimension=0,
            tiled=True,
        )[0].astype(f32)

    early = scatter(
        jnp.concatenate(
            [
                g_up.reshape(devices, hid, dim),
                g_down.reshape(devices, hid, dim),
                g_out.reshape(devices, chans, dim),
            ],
            axis=1,
        ).reshape(devices * (2 * hid + chans), dim)
    )
    up_grad, down_grad, out_grad = early[:hid], early[hid : 2 * hid], early[2 * hid :]

    d_mixed_chan, d_filter, g_conv_bias = conv_backward(
        d_conv, mixed_chan, mixed_spec, filt_spec, bias_col, seqs
    )
    d_mixed = rows_of(exchange(d_mixed_chan)).astype(f32)

    q = d_filter * env
    g_filt_out = mm(h2, q, NT)
    g_decay = -jnp.sum(d_filter * raw * falling * ramp, axis=1)
    u2 = mm(filt_out, q, NN) * jnp.cos(rate * pre2)
    fu2 = rate * u2
    u1 = mm(filt_mid, fu2, NN) * jnp.cos(rate * pre1)
    fu1 = rate * u1
    filt_grads = jnp.concatenate(
        [
            mm(feat, fu1, NT).reshape(-1),
            jnp.sum(fu1, axis=1),
            mm(h1, fu2, NT).reshape(-1),
            jnp.sum(fu2, axis=1),
            jnp.sum(u2 * pre2 + u1 * pre1, axis=1),
        ]
    )

    def split(values):
        return values.reshape(devices, chans, cols)

    starts = [slice(s * width, s * width + KS - 1) for s in range(seqs)]
    pick = lambda v: jnp.concatenate([v[..., at] for at in starts], axis=-1)
    hd = pick(split(d_mixed))
    hs = pick(short)
    heads = jnp.stack([pick(split(d_gated)) * pick(split(conv)), hd * hs[:, 2], hd * hs[:, 1]], axis=1)
    heads = heads.reshape(3 * dim, seqs * (KS - 1)).T
    head = lax.ppermute(heads, "chan", [(i + 1, i) for i in range(devices - 1)])
    head = head.T.reshape(devices, 3, chans, seqs * (KS - 1))
    d_proj, sums = short_backward(
        split(d_gated), split(conv), split(d_mixed), proj, halo, short, head, prm, seqs
    )
    d_proj_low = d_proj.reshape(3 * dim, cols).astype(bf16)
    d_xn1 = mm16(in_all, d_proj_low, TN)
    in_grad = scatter(mm16(d_proj_low, xn1, NT))
    grad_in = d_residual + norm_backward(d_xn1 * gain1, xhat1, rstd1)
    grad_blocks = exchange(blocks_of(grad_in.astype(bf16)))

    tokens = jnp.concatenate(
        [
            sums[..., : 2 + KS].transpose(0, 3, 1, 2).reshape(devices, 3 * (2 + KS) * chans),
            jnp.sum(d_xn1 * xhat1, axis=1).reshape(devices, chans),
            jnp.sum(d_xn1, axis=1).reshape(devices, chans),
            jnp.sum(d_residual, axis=1).reshape(devices, chans),
            jnp.sum(d_xn2 * xhat2, axis=1).reshape(devices, chans),
            jnp.sum(d_xn2, axis=1).reshape(devices, chans),
            jnp.sum(d_final, axis=1).reshape(devices, chans),
            g_up_bias.reshape(devices, hid),
            jnp.broadcast_to(filt_grads[None], (devices, filt_grads.shape[0])),
        ],
        axis=1,
    )
    count = tokens.shape[1]
    tokens = jnp.pad(tokens, ((0, 0), (0, -count % 1024))).reshape(devices, -1, LANE)
    totals = jnp.sum(exchange(tokens), axis=0).reshape(-1)[:count]
    own = jnp.concatenate([totals, g_conv_bias[:, 0], g_decay, g_filt_out.reshape(-1)])
    own = lax.psum(own, "batch")
    cut = [0]

    def take(*shape):
        n = math.prod(shape)
        part = own[cut[0] : cut[0] + n].reshape(shape)
        cut[0] += n
        return part

    g_in_bias = take(3, chans)
    g_short_bias = take(3, chans)
    g_short_weight = take(KS, 3, chans)
    g_gain1, g_shift1, g_out_b, g_gain2, g_shift2, g_down_b = (take(chans) for _ in range(6))
    g_up_b = take(hid)
    ford = filt_mid.shape[0]
    g_filt_in, g_filt_in_bias = take(EMB, ford), take(ford)
    g_filt_mid, g_filt_mid_bias, g_sine = take(ford, ford), take(ford), take(ford)
    g_conv_b, g_decay_rate, g_filt_last = take(chans), take(chans), take(ford, chans)

    return (
        from_blocks(out_blocks),
        from_blocks(grad_blocks).astype(f32),
        g_gain1,
        g_shift1,
        in_grad.reshape(3, chans, dim // groups).transpose(2, 0, 1),
        g_in_bias,
        g_short_weight,
        g_short_bias,
        g_filt_in,
        g_filt_in_bias,
        g_filt_mid,
        g_filt_mid_bias,
        g_sine,
        g_filt_last,
        g_decay_rate,
        g_conv_b,
        out_grad,
        g_out_b,
        g_gain2,
        g_shift2,
        up_grad,
        g_up_b,
        down_grad,
        g_down_b,
    )


def solution(mesh):
    token = P("batch", "chan", None)
    chan = P("chan")
    rows = P("chan", None)
    two = P(None, "chan")
    three = P(None, None, "chan")
    in_specs = (
        token, P("batch"), chan, chan, three, two, three, two, P(), P(), P(), P(), P(), two, chan, chan,
        rows, chan, chan, chan, rows, chan, rows, chan, token,
    )
    table = P("chan", "batch")
    out_specs = (
        token, token, chan, chan, P("batch", None, "chan"), two, three, two, P(), P(), P(), P(), P(), two,
        chan, chan, table, chan, chan, chan, table, chan, table, chan,
    )
    return jax.shard_map(
        on_device, mesh=mesh, in_specs=in_specs, out_specs=out_specs, check_vma=False
    )
```

time: 1250 us -> 739 us (0.59)
  other arithmetic: 252 us -> 36.5 us
  blocking collectives: 188 us -> 34.5 us
  Pallas kernels: 0 us -> 114 us
  matrix products: 210 us -> 97.4 us
  local copies, waits for them, and re-layouts: 280 us -> 192 us
  starting transfers between devices: 91.6 us -> 62.6 us
  waiting for transfers between devices: 195 us -> 174 us
    unnamed x2 -> x0, blocking collectives: 125 us -> none
    pallas_call x0 -> x5, Pallas kernels: none -> 114 us  [the longest x3 52.8 us: whole_call(): pl.pallas_call(body, out_shape=out_shape, in_specs=[pl.BlockSpec(memory_s...]
    dot_general x56 -> x20, matrix products: 210 us -> 97.4 us  [the longest x12 64.5 us: mm16(): return lax.dot_general(a, b, (dims, ((), ())), preferred_element_type=f32)]
    convert_element_type x16 -> x10, other arithmetic: 107 us -> 9.91 us  [the longest x1 3.45 us: on_device(): grad_blocks = exchange(blocks_of(grad_in.astype(bf16)))]
    reduce_sum x10 -> x9, other arithmetic: 101 us -> 8.4 us  [the longest x1 2.68 us: on_device(): jnp.sum(d_xn1 * xhat1, axis=1).reshape(devices, chans)]
    unnamed x234 -> x149, local copies, waits for them, and re-layouts: 103 us -> 20.1 us
    all_to_all x8, waiting for transfers between devices: 143 us -> 66.3 us  [exchange(): lax.all_to_all(values, 'chan', split_axis=0, concat_axis=0, tiled=True)]
    all_to_all x9 -> x0, local copies, waits for them, and re-layouts: 43.4 us -> none  [the longest x3 22.2 us: rows_low(): lax.all_to_all(values, 'chan', split_axis=0, concat_axis=2, tiled=True)]
  transfers between devices with their start and end apart: 21 -> 16, of which waited for: 5 -> 7; matrix products, arithmetic and copies ran while one was open for 58% -> 34% of each run, Pallas kernels for 0% -> 7%
where the time goes in v1:
time: 739 us; the launch traced here: 727 us
  local copies, waits for them, and re-layouts  192 us (26%)
  waiting for transfers between devices  174 us (24%)
  Pallas kernels  114 us (15%)
  matrix products  97.4 us (13%)
  starting transfers between devices  62.6 us (8%)
  other arithmetic  36.5 us (5%)
  blocking collectives  34.5 us (5%)
  between operations  15.4 us (2%)
    reduce_scatter x2, waiting for transfers between devices, scatter(): lax.psum_scatter(table.reshape(groups * devices, rows, dim // groups), ('...  81.4 us
    all_to_all x8, waiting for transfers between devices, exchange(): lax.all_to_all(values, 'chan', split_axis=0, concat_axis=0, tiled=True)  66.3 us
    dot_general x12, matrix products, mm16(): return lax.dot_general(a, b, (dims, ((), ())), preferred_element_type=f32)  64.5 us
    all_to_all x8, starting transfers between devices, exchange(): lax.all_to_all(values, 'chan', split_axis=0, concat_axis=0, tiled=True)  58.9 us
    pallas_call x3, Pallas kernels, whole_call(): pl.pallas_call(body, out_shape=out_shape, in_specs=[pl.BlockSpec(memory_s...  52.8 us
    pallas_call x1, Pallas kernels, short_backward(): pl.pallas_call(lambda *refs: short_backward_body(seqs, *refs), grid=(devi...  43.5 us
    dot_general x8, matrix products, mm(): lax.dot_general(a, b, (dims, ((), ())), precision=highest, preferred_elem...  32.8 us
    all_to_all x1, blocking collectives, exchange(): lax.all_to_all(values, 'chan', split_axis=0, concat_axis=0, tiled=True)  25.9 us
  transfers between devices with their start and end apart: 16, of which 7 were waited for; matrix products, arithmetic and copies ran while one was open for 34% of the time, Pallas kernels for 7%

profile of v1, /device:TPU:0, one launch (start us, length us, event | category | flops | bytes accessed | tf_op | source)
XLA Modules:
  0.0 727.2 jit_solution(1270771396411559319)
XLA Ops:
  9.6 4.8 concatenate.68
  18.6 7.4 %all-to-all-start = ((bf16[16,96,256]{2,1,0:T(8,128)(2,1)}), bf16[16,96,256]{2,1,0:T(8,128)(2,1)S(1)}, u32[]{:S(2)}, u32[]{:S(2)}) async-start(bf16[16,96,256]{2,1,0:T(8,128)(2,1)} %bitcast.1), calls=%async_computation | async-start | bytes 1572864 | tf_op jit(solution)/shard_map/all_to_all | solution.py:491
  26.6 25.9 %all-to-all-done = bf16[16,96,256]{2,1,0:T(8,128)(2,1)S(1)} async-done(((bf16[16,96,256]{2,1,0:T(8,128)(2,1)}), bf16[16,96,256]{2,1,0:T(8,128)(2,1)S(1)}, u32[]{:S(2)}, u32[]{:S(2)}) %all-to-all-start) | async-done | bytes 786464 | tf_op jit(solution)/shard_map/all_to_all | solution.py:491
  54.1 23.8 %all-gather.12.cloned.1.call-done = bf16[2560,768]{1,0:T(8,128)(2,1)} async-done(((bf16[160,768]{1,0:T(8,128)(2,1)}), bf16[2560,768]{1,0:T(8,128)(2,1)}) %all-gather.12.cloned.1.call-update) | async-done | bytes 3932176 | tf_op jit(solution)/shard_map/all_gather | solution.py:592
  108.5 17.9 %shard_map.460 = (f32[16,3,48,512]{3,2,1,0:T(8,128)}, bf16[16,96,256]{2,1,0:T(8,128)(2,1)}) custom-call(f32[16,3,48,512]{3,2,1,0:T(8,128)} %copy-done.1, f32[16,3,48,4]{3,2,1,0:T(8,128)} %bitcast.274, f32[16,3,48,8]{3,2,1,0:T(8,128)} %copy-done.2), custom_call_target="tpu_custom_call" | custom-call | tf_op jit(solution)/shard_map/pallas_call | solution.py:408
  126.4 7.8 %all-to-all-start.1 = ((bf16[16,96,256]{2,1,0:T(8,128)(2,1)}), bf16[16,96,256]{2,1,0:T(8,128)(2,1)S(1)}, u32[]{:S(2)}, u32[]{:S(2)}) async-start(bf16[16,96,256]{2,1,0:T(8,128)(2,1)} %get-tuple-element.33), calls=%async_computation.1 | async-start | bytes 1572864 | tf_op jit(solution)/shard_map/all_to_all | solution.py:491
  135.2 20.4 %all-to-all-done.1.refs_0_.refs_1_ = bf16[16,96,256]{2,1,0:T(8,128)(2,1)S(1)} async-done(((bf16[16,96,256]{2,1,0:T(8,128)(2,1)}), bf16[16,96,256]{2,1,0:T(8,128)(2,1)S(1)}, u32[]{:S(2)}, u32[]{:S(2)}) %all-to-all-start.1) | async-done | bytes 786464 | tf_op jit(solution)/shard_map/all_to_all | solution.py:491
  155.7 14.7 %all-to-all-start.4 = ((bf16[16,96,256]{2,1,0:T(8,128)(2,1)}), bf16[16,96,256]{2,1,0:T(8,128)(2,1)S(1)}, u32[]{:S(2)}, u32[]{:S(2)}) async-start(bf16[16,96,256]{2,1,0:T(8,128)(2,1)} %bitcast.37), calls=%async_computation.4 | async-start | bytes 1572864 | tf_op jit(solution)/shard_map/all_to_all | solution.py:491
  177.7 5.5 fusion.39
  183.1 9.6 %shard_map.461.refs_1_.refs_3_ = f32[33,48,256]{2,1,0:T(8,128)} custom-call(f32[48,4096]{1,0:T(8,128)} %get-tuple-element.215.filter_ref, f32[33,1,256]{2,1,0:T(1,128)} %constant.48.clone.twist_ref.refs_3_.refs_5_, bf16[2,256,256]{2,1,0:T(8,128)(2,1)} %constant.49.clone.ahead_ref.refs_4_.refs_6_), custom_call_target="tpu_custom_call" | custom-call | tf_op jit(solution)/shard_map/pallas_call | solution.py:299
  192.7 20.7 %shard_map.462 = (bf16[16,96,256]{2,1,0:T(8,128)(2,1)}, f32[33,96,256]{2,1,0:T(8,128)}) custom-call(bf16[16,96,256]{2,1,0:T(8,128)(2,1)} %copy-done.12, f32[33,48,256]{2,1,0:T(8,128)} %shard_map.461.refs_1_.refs_3_, f32[48,1]{1,0:T(8,128)} %copy.271.refs_2_.refs_4_, f32[33,1,256]{2,1,0:T(1,128)} %constant.48.clone.twist_ref.refs_3_.refs_5_, ...), custom_call_target="tpu_custom_call" | custom-call | tf_op jit(solution)/shard_map/pallas_call | solution.py:299
  213.4 6.6 all-to-all-start.2
  237.9 11.7 %all-to-all-done.2 = bf16[16,96,256]{2,1,0:T(8,128)(2,1)} async-done(((bf16[16,96,256]{2,1,0:T(8,128)(2,1)}), bf16[16,96,256]{2,1,0:T(8,128)(2,1)}, u32[]{:S(2)}, u32[]{:S(2)}) %all-to-all-start.2) | async-done | bytes 786464 | tf_op jit(solution)/shard_map/all_to_all | solution.py:491
  257.3 10.1 %fusion.9 = (bf16[3072,512]{0,1:T(8,128)(2,1)}, f32[512,3072]{1,0:T(8,128)}) fusion(f32[3072]{0:T(1024)S(1)} %add.178, bf16[3072,768]{1,0:T(8,128)(2,1)} %all-gather.8.cloned.1.call-done, f32[768,512]{0,1:T(8,128)} %copy-done.6, f32[768]{0:T(1024)S(1)} %add.175, f32[768]{0:T(1024)S(1)} %mul.308, f32[512]{0:T(512)S(1)} %add_rsqrt_fusion, ...), kind=kOutput, calls=%fused_computation.15 | convolution fusion | flops 2433613824 | bytes 15751168 | tf_op jit(solution)/shard_map/dot_general | solution.py:487
  267.4 10.3 %fusion.71 = (f32[3072]{0:T(1024)}, bf16[3072,512]{0,1:T(8,128)(2,1)S(1)}) fusion(f32[512,3072]{1,0:T(8,128)} %get-tuple-element.220, f32[3072]{0:T(1024)S(1)} %add.178, bf16[3072,768]{1,0:T(8,128)(2,1)} %all-gather.10.cloned.1.call-done, f32[768,512]{0,1:T(8,128)} %copy.279, f32[512]{0:T(512)S(1)} %bitcast.323), kind=kOutput, calls=%fused_computation.160 | convolution fusion | flops 2451305472 | bytes 15755264 | tf_op jit(solution)/shard_map/dot_general | solution.py:487
  293.2 25.9 %all_to_all.45.refs_0_ = bf16[16,96,256]{2,1,0:T(8,128)(2,1)} all-to-all(bf16[16,96,256]{2,1,0:T(8,128)(2,1)S(1)} %bitcast.297), channel_id=1, replica_groups=mesh['batch'=2,'chan'=16] {'chan'}, dimensions={0} | all-to-all | bytes 1572864 | tf_op jit(solution)/shard_map/all_to_all | solution.py:491
  319.1 22.6 %shard_map.463 = (bf16[16,96,256]{2,1,0:T(8,128)(2,1)}, f32[48,4096]{1,0:T(8,128)}, f32[48,1]{1,0:T(8,128)}) custom-call(bf16[16,96,256]{2,1,0:T(8,128)(2,1)} %all_to_all.45.refs_0_, bf16[16,96,256]{2,1,0:T(8,128)(2,1)} %copy-done.12, f32[33,96,256]{2,1,0:T(8,128)} %get-tuple-element.36.refs_2_, f32[33,48,256]{2,1,0:T(8,128)} %shard_map.461.refs_1_.refs_3_, ...), custom_call_target="tpu_custom_call" | custom-call | tf_op jit(solution)/shard_map/pallas_call | solution.py:299
  395.0 43.5 %shard_map.464 = (f32[16,3,48,512]{3,2,1,0:T(8,128)}, f32[16,3,48,8]{3,2,1,0:T(8,128)}) custom-call(f32[16,48,512]{2,1,0:T(8,128)} %bitcast.277, f32[16,48,512]{2,1,0:T(8,128)} %reshape.554.refs_1_, f32[16,48,512]{2,1,0:T(8,128)} %reshape.555.refs_2_, f32[16,3,48,512]{3,2,1,0:T(8,128)} %copy-done.1, f32[16,3,48,4]{3,2,1,0:T(8,128)} %bitcast.275, ...), custom_call_target="tpu_custom_call" | custom-call | tf_op jit(solution)/shard_map/pallas_call | solution.py:456
  446.6 7.9 %reshape.540 = bf16[16,144,2,384]{3,2,1,0:T(2,128)(2,1)} reshape(bf16[2304,768]{1,0:T(8,128)(2,1)} %convolution_convert_fusion.1) | data formatting | bytes 7077888 | tf_op jit(solution)/shard_map/reshape | solution.py:670
  470.1 4.7 copy.305
  474.9 7.4 %convolution_convert_fusion = bf16[3072,768]{1,0:T(8,128)(2,1)} fusion(bf16[3072,512]{0,1:T(8,128)(2,1)} %copy-done.68, f32[768,512]{0,1:T(8,128)} %copy-done.6, f32[768]{0:T(1024)S(1)} %copy-done.62, f32[768]{0:T(1024)S(1)} %copy-done.47, f32[512]{0:T(512)S(1)} %copy-done.52, f32[512]{0:T(512)S(1)} %copy-done.40), kind=kOutput, calls=%fused_computation.16 | convolution fusion | flops 2420244480 | bytes 9447424 | tf_op jit(solution)/shard_map/dot_general | solution.py:487
  482.3 10.2 %concatenate.85 = bf16[16,192,2,384]{3,2,1,0:T(2,128)(2,1)} reshape(bf16[3072,768]{1,0:T(8,128)(2,1)} %convolution_convert_fusion) | data formatting | bytes 9437184 | tf_op jit(solution)/shard_map/concatenate | solution.py:679
  502.4 6.5 maximum_bitcast_fusion
  517.9 7.3 %fusion.20 = bf16[768,512]{0,1:T(8,128)(2,1)} fusion(f32[768,512]{0,1:T(8,128)} %copy-done.6, bf16[3072,512]{0,1:T(8,128)(2,1)} %get-tuple-element.219, bf16[3072,768]{1,0:T(8,128)(2,1)} %all-gather.10.cloned.1.call-done, f32[768]{0:T(1024)S(1)} %add.185, f32[512]{0:T(512)S(1)} %bitcast.325), kind=kOutput, calls=%fused_computation.40 | convolution fusion | flops 2417491968 | bytes 10228736 | tf_op jit(solution)/shard_map/dot_general | solution.py:487
  530.0 7.8 %all-to-all-start.3 = ((bf16[16,96,256]{2,1,0:T(8,128)(2,1)}), bf16[16,96,256]{2,1,0:T(8,128)(2,1)}, u32[]{:S(2)}, u32[]{:S(2)}) async-start(bf16[16,96,256]{2,1,0:T(8,128)(2,1)} %bitcast.295), calls=%async_computation.3 | async-start | bytes 1572864 | tf_op jit(solution)/shard_map/all_to_all | solution.py:491
  544.5 5.4 add_reduce_fusion
  551.6 6.4 fusion.29
  558.9 6.5 fusion.70
  584.7 6.0 all-to-all-start.8
  596.8 8.4 %all-to-all-done.8 = f32[16,64,128]{2,1,0:T(8,128)} async-done(((f32[16,64,128]{2,1,0:T(8,128)}), f32[16,64,128]{2,1,0:T(8,128)}, u32[]{:S(2)}, u32[]{:S(2)}) %all-to-all-start.8) | async-done | bytes 524320 | tf_op jit(solution)/shard_map/all_to_all | solution.py:491
  618.1 8.7 %psum.7 = f32[10768]{0:T(1024)S(1)} all-reduce(f32[10768]{0:T(1024)S(1)} %concatenate.84), channel_id=1, replica_groups=mesh['batch'=2,'chan'=16] {'batch'}, use_global_device_ids=true, to_apply=%region_20.21 | all-reduce | flops 10768 | bytes 86144 | tf_op jit(solution)/shard_map/psum | solution.py:750
  636.2 81.4 %reduce-scatter.5.cloned.1.call-done = bf16[1,432,384]{2,1,0:T(8,128)(2,1)} async-done(((bf16[32,432,384]{2,1,0:T(8,128)(2,1)}), bf16[1,432,384]{2,1,0:T(8,128)(2,1)}) %reduce-scatter.5.cloned.1.call-update) | async-done | bytes 331792 | tf_op jit(solution)/shard_map/reduce_scatter | solution.py:671
  (338 shorter events, 248.5 us)
Async XLA Ops:
  7.2 165.9 %copy-start = (f32[64,64]{1,0:T(8,128)S(1)}, f32[64,64]{1,0:T(8,128)}, u32[]{:S(2)}) copy-start(f32[64,64]{1,0:T(8,128)} %param.39) | copy-start | bytes 49156
  7.2 70.6 %all-gather.12.cloned.1.call-start = ((), (), s32[]{:S(2)}) async-start(), calls=%async_computation.16 | async-start | bytes 4177920 | tf_op jit(solution)/shard_map/all_gather | solution.py:592
  16.1 236.4 %all-gather.6.cloned.1.call-start = ((), (), s32[]{:S(2)}) async-start(), calls=%async_computation.11 | async-start | bytes 1253376 | tf_op jit(solution)/shard_map/all_gather | solution.py:594
  16.9 240.4 %all-gather.8.cloned.1.call-start = ((), (), s32[]{:S(2)}) async-start(), calls=%async_computation.12 | async-start | bytes 5013504 | tf_op jit(solution)/shard_map/all_gather | solution.py:595
  18.6 34.0 %all-to-all-start = ((bf16[16,96,256]{2,1,0:T(8,128)(2,1)}), bf16[16,96,256]{2,1,0:T(8,128)(2,1)S(1)}, u32[]{:S(2)}, u32[]{:S(2)}) async-start(bf16[16,96,256]{2,1,0:T(8,128)(2,1)} %bitcast.1), calls=%async_computation | async-start | bytes 1572864 | tf_op jit(solution)/shard_map/all_to_all | solution.py:491
  26.0 241.4 %all-gather.10.cloned.1.call-start = ((), (), s32[]{:S(2)}) async-start(), calls=%async_computation.13 | async-start | bytes 5013504 | tf_op jit(solution)/shard_map/all_gather | solution.py:596
  104.1 3.0 collective-permute-start
  126.4 29.3 %all-to-all-start.1 = ((bf16[16,96,256]{2,1,0:T(8,128)(2,1)}), bf16[16,96,256]{2,1,0:T(8,128)(2,1)S(1)}, u32[]{:S(2)}, u32[]{:S(2)}) async-start(bf16[16,96,256]{2,1,0:T(8,128)(2,1)} %get-tuple-element.33), calls=%async_computation.1 | async-start | bytes 1572864 | tf_op jit(solution)/shard_map/all_to_all | solution.py:491
  134.2 36.1 %copy-start.64 = (f32[48]{0:T(128)S(1)}, f32[48]{0:T(128)}, u32[]{:S(2)}) copy-start(f32[48]{0:T(128)} %param.44) | copy-start | bytes 580
  134.2 36.8 %copy-start.22 = (f32[33,4096]{1,0:T(8,128)S(1)}, f32[33,4096]{1,0:T(8,128)}, u32[]{:S(2)}) copy-start(f32[33,4096]{1,0:T(8,128)} %constant.47.clone) | copy-start | bytes 1622020
  134.2 36.8 %copy-start.38 = (f32[33,64]{1,0:T(8,128)S(1)}, f32[33,64]{1,0:T(8,128)}, u32[]{:S(2)}) copy-start(f32[33,64]{1,0:T(8,128)} %param.37) | copy-start | bytes 25348
  134.2 36.8 %copy-start.63 = (f32[64]{0:T(128)S(1)}, f32[64]{0:T(128)}, u32[]{:S(2)}) copy-start(f32[64]{0:T(128)} %param.38) | copy-start | bytes 772
  155.6 16.5 %copy-start.12 = (bf16[16,96,256]{2,1,0:T(8,128)(2,1)}, bf16[16,96,256]{2,1,0:T(8,128)(2,1)S(1)}, u32[]{:S(2)}) copy-start(bf16[16,96,256]{2,1,0:T(8,128)(2,1)S(1)} %all-to-all-done.1.refs_0_.refs_1_) | copy-start | bytes 2359300
  155.6 17.5 %copy-start.34 = (f32[64]{0:T(128)S(1)}, f32[64]{0:T(128)}, u32[]{:S(2)}) copy-start(f32[64]{0:T(128)} %param.41) | copy-start | bytes 772
  155.6 17.5 %copy-start.66 = (f32[64]{0:T(128)S(1)}, f32[64]{0:T(128)}, u32[]{:S(2)}) copy-start(f32[64]{0:T(128)} %param.40) | copy-start | bytes 772
  155.7 57.7 %all-to-all-start.4 = ((bf16[16,96,256]{2,1,0:T(8,128)(2,1)}), bf16[16,96,256]{2,1,0:T(8,128)(2,1)S(1)}, u32[]{:S(2)}, u32[]{:S(2)}) async-start(bf16[16,96,256]{2,1,0:T(8,128)(2,1)} %bitcast.37), calls=%async_computation.4 | async-start | bytes 1572864 | tf_op jit(solution)/shard_map/all_to_all | solution.py:491
  192.7 27.3 %copy-start.65 = (s32[2]{0:T(128)S(1)}, s32[2]{0:T(128)}, u32[]{:S(2)}) copy-start(s32[2]{0:T(128)} %param.30) | copy-start | bytes 28
  213.4 36.2 %all-to-all-start.2 = ((bf16[16,96,256]{2,1,0:T(8,128)(2,1)}), bf16[16,96,256]{2,1,0:T(8,128)(2,1)}, u32[]{:S(2)}, u32[]{:S(2)}) async-start(bf16[16,96,256]{2,1,0:T(8,128)(2,1)} %get-tuple-element.34), calls=%async_computation.2 | async-start | bytes 1572864 | tf_op jit(solution)/shard_map/all_to_all | solution.py:491
  220.7 60.5 %copy-start.49 = (f32[1,2,2,128]{3,1,2,0:T(2,128)}, f32[1,2,2,128]{3,1,2,0:T(2,128)S(1)}, u32[]{:S(2)}) copy-start(f32[1,2,2,128]{3,1,2,0:T(2,128)S(1)} %copy.325) | copy-start | bytes 6148
  232.0 25.3 %copy-start.61 = (f32[768]{0:T(1024)}, f32[768]{0:T(1024)S(1)}, u32[]{:S(2)}) copy-start(f32[768]{0:T(1024)S(1)} %add.175) | copy-start | bytes 9220
  232.1 49.1 %copy-start.46 = (f32[768]{0:T(1024)}, f32[768]{0:T(1024)S(1)}, u32[]{:S(2)}) copy-start(f32[768]{0:T(1024)S(1)} %mul.308) | copy-start | bytes 9220
  255.8 25.4 %copy-start.39 = (f32[512]{0:T(512)}, f32[512]{0:T(512)S(1)}, u32[]{:S(2)}) copy-start(f32[512]{0:T(512)S(1)} %broadcast_multiply_fusion.4) | copy-start | bytes 6148
  257.2 23.9 %copy-start.51 = (f32[512]{0:T(512)}, f32[512]{0:T(512)S(1)}, u32[]{:S(2)}) copy-start(f32[512]{0:T(512)S(1)} %add_rsqrt_fusion) | copy-start | bytes 6148
  341.7 33.3 %all-to-all-start.6 = ((bf16[16,96,256]{2,1,0:T(8,128)(2,1)}), bf16[16,96,256]{2,1,0:T(8,128)(2,1)}, u32[]{:S(2)}, u32[]{:S(2)}) async-start(bf16[16,96,256]{2,1,0:T(8,128)(2,1)} %get-tuple-element.37), calls=%async_computation.6 | async-start | bytes 1572864 | tf_op jit(solution)/shard_map/all_to_all | solution.py:491
  346.0 288.7 %reduce-scatter.3.cloned.1.call-start = ((), (), s32[]{:S(2)}) async-start(), calls=%async_computation.14 | async-start | bytes 3649536 | tf_op jit(solution)/shard_map/reduce_scatter | solution.py:671
  390.1 3.5 collective-permute-start.1
  458.8 258.8 %reduce-scatter.5.cloned.1.call-start = ((), (), s32[]{:S(2)}) async-start(), calls=%async_computation.15 | async-start | bytes 10948608 | tf_op jit(solution)/shard_map/reduce_scatter | solution.py:671
  527.7 12.1 %copy-start.11 = (f32[48,4096]{1,0:T(8,128)S(1)}, f32[48,4096]{1,0:T(8,128)}, u32[]{:S(2)}) copy-start(f32[48,4096]{1,0:T(8,128)} %get-tuple-element.40) | copy-start | bytes 2359300
  527.8 12.1 %copy-start.31 = (f32[64,48]{0,1:T(8,128)S(1)}, f32[64,48]{0,1:T(8,128)}, u32[]{:S(2)}) copy-start(f32[64,48]{0,1:T(8,128)} %param.42) | copy-start | bytes 36868
  530.0 54.7 %all-to-all-start.3 = ((bf16[16,96,256]{2,1,0:T(8,128)(2,1)}), bf16[16,96,256]{2,1,0:T(8,128)(2,1)}, u32[]{:S(2)}, u32[]{:S(2)}) async-start(bf16[16,96,256]{2,1,0:T(8,128)(2,1)} %bitcast.295), calls=%async_computation.3 | async-start | bytes 1572864 | tf_op jit(solution)/shard_map/all_to_all | solution.py:491
  584.7 20.5 %all-to-all-start.8 = ((f32[16,64,128]{2,1,0:T(8,128)}), f32[16,64,128]{2,1,0:T(8,128)}, u32[]{:S(2)}, u32[]{:S(2)}) async-start(f32[16,64,128]{2,1,0:T(8,128)} %bitcast.302), calls=%async_computation.8 | async-start | bytes 1048576 | tf_op jit(solution)/shard_map/all_to_all | solution.py:491
  605.2 27.9 %all-to-all-start.7 = ((bf16[16,96,256]{2,1,0:T(8,128)(2,1)}), bf16[16,96,256]{2,1,0:T(8,128)(2,1)S(1)}, u32[]{:S(2)}, u32[]{:S(2)}) async-start(bf16[16,96,256]{2,1,0:T(8,128)(2,1)} %bitcast.60), calls=%async_computation.7 | async-start | bytes 1572864 | tf_op jit(solution)/shard_map/all_to_all | solution.py:491
  (53 other events, 265.3 us)
Sparse Core Ops, SparseCore 0:
  16.2 61.5 all-gather.11
  80.1 37.4 all-gather.5
  119.9 65.7 all-gather.7
  187.8 62.7 all-gather.9
  458.9 110.2 reduce-scatter.2
  575.1 142.4 reduce-scatter.4

commit v2 on v1

v2 whole, which is shorter than its diff:
```python
import math

import jax
import jax.numpy as jnp
import numpy as np
from jax import lax
from jax.experimental import pallas as pl
from jax.experimental.pallas import tpu as pltpu
from jax.sharding import PartitionSpec as P

EMB = 33
KS = 3
LMAX = 4096
LANE = 128
COARSE = LMAX // LANE
REPS = tuple(ka + 8 * kb for ka, count in ((0, 5), (1, 8), (2, 8), (3, 8), (4, 4)) for kb in range(count))
PLACE = {k1: i for i, k1 in enumerate(REPS)}
epsilon = 1e-05
decay_floor = 0.05
highest = lax.Precision.HIGHEST
f32 = jnp.float32
bf16 = jnp.bfloat16
vmem_limit = 56 * 1024 * 1024
HEAD_ROWS = 16
SUM_ROWS = 16
BATCH = 3
PRM = 32


def unit(turns):
    angle = 2.0 * math.pi * turns
    return math.cos(angle), math.sin(angle)


def scaled(z, c, s):
    re, im = z
    if im is None:
        return re * c, re * s
    return re * c - im * s, re * s + im * c


def plus(a, b):
    return a[0] + b[0], a[1] + b[1]


def minus(a, b):
    return a[0] - b[0], a[1] - b[1]


def dft4(z, sign):
    s0, d0 = plus(z[0], z[2]), minus(z[0], z[2])
    s1, d1 = plus(z[1], z[3]), minus(z[1], z[3])
    turned = (-d1[1], d1[0]) if sign > 0 else (d1[1], -d1[0])
    return [plus(s0, s1), plus(d0, turned), minus(s0, s1), minus(d0, turned)]


def dft8(z, sign):
    even, odd = dft4(z[0::2], sign), dft4(z[1::2], sign)
    c = math.sqrt(0.5)
    o1 = odd[1]
    o3 = odd[3]
    if sign > 0:
        odd1 = ((o1[0] - o1[1]) * c, (o1[0] + o1[1]) * c)
        odd2 = (-odd[2][1], odd[2][0])
        odd3 = ((-o3[0] - o3[1]) * c, (o3[0] - o3[1]) * c)
    else:
        odd1 = ((o1[0] + o1[1]) * c, (o1[1] - o1[0]) * c)
        odd2 = (odd[2][1], -odd[2][0])
        odd3 = ((o3[1] - o3[0]) * c, (-o3[0] - o3[1]) * c)
    turned = [odd[0], odd1, odd2, odd3]
    return [plus(even[i], turned[i]) for i in range(4)] + [minus(even[i], turned[i]) for i in range(4)]


def coarse_forward(xs, put):
    c = math.sqrt(0.5)
    cols = {ka: [None] * 8 for ka in range(5)}
    for b in range(8):
        x0, x1, x2, x3 = xs[b], xs[8 + b], xs[16 + b], xs[24 + b]
        s02, d02, s13, d13 = x0 + x2, x0 - x2, x1 + x3, x1 - x3
        d13c, s13c = d13 * c, s13 * c
        cols[0][b] = s02 + s13
        cols[4][b] = scaled((s02 - s13, None), *unit(-4 * b / 64))
        cols[2][b] = scaled((d02, -d13), *unit(-2 * b / 64))
        cols[1][b] = scaled((x0 + d13c, -s13c - x2), *unit(-b / 64))
        cols[3][b] = scaled((x0 - d13c, x2 - s13c), *unit(-3 * b / 64))
    for ka in (1, 2, 3):
        for kb, z in enumerate(dft8(cols[ka], -1)):
            put(ka + 8 * kb, z)
    for kb, z in enumerate(dft8(cols[4], -1)[:4]):
        put(4 + 8 * kb, z)
    r = cols[0]
    s04, d04, s26, d26 = r[0] + r[4], r[0] - r[4], r[2] + r[6], r[2] - r[6]
    s15, d15, s37, d37 = r[1] + r[5], r[1] - r[5], r[3] + r[7], r[3] - r[7]
    p, q = (d15 - d37) * c, (d15 + d37) * c
    even, odd = s04 + s26, s15 + s37
    put(0, (even + odd, None))
    put(32, (even - odd, None))
    put(16, (s04 - s26, s37 - s15))
    put(8, (d04 + p, -d26 - q))
    put(24, (d04 - p, d26 - q))


def coarse_inverse(get):
    c = math.sqrt(0.5)
    u = {}
    for ka in (1, 2, 3):
        back = dft8([get(ka + 8 * kb) for kb in range(8)], 1)
        u[ka] = [scaled(back[b], *unit(b * ka / 64)) for b in range(8)]
    v0, v32 = get(0)[0], get(32)[0]
    v8, v16, v24 = get(8), get(16), get(24)
    flat = []
    for b in range(8):
        total = v0 + v32 if b % 2 == 0 else v0 - v32
        for kb, v in ((1, v8), (2, v16), (3, v24)):
            co, si = unit(b * kb / 8)
            if abs(co) > 1e-9:
                total = total + v[0] * (2.0 * co)
            if abs(si) > 1e-9:
                total = total - v[1] * (2.0 * si)
        flat.append(total)
    odd = [get(4 + 8 * kb) for kb in range(4)]
    odd = odd + [(z[0], -z[1]) for z in odd[::-1]]
    half = dft8(odd, 1)
    quarter = []
    for b in range(8):
        co, si = unit(4 * b / 64)
        quarter.append(half[b][0] * co - half[b][1] * si)
    out = [None] * COARSE
    for b in range(8):
        u1, u2, u3 = u[1][b], u[2][b], u[3][b]
        s, d = flat[b] + quarter[b], flat[b] - quarter[b]
        dr, sr = (u1[0] - u3[0]) * c, u1[0] + u3[0]
        si_, di = (u1[1] + u3[1]) * c, u1[1] - u3[1]
        out[b] = s + 2.0 * (sr + u2[0])
        out[16 + b] = s - 2.0 * (di + u2[0])
        out[8 + b] = d + 2.0 * (dr - si_ - u2[1])
        out[24 + b] = d + 2.0 * (u2[1] - dr - si_)
    return out


def transform_tables():
    fine = np.arange(LANE)
    angle = 2.0 * math.pi * ((fine[:, None] * fine[None, :]) % LANE) / LANE
    co, si = np.cos(angle), np.sin(angle)
    ahead = np.block([[co, -si], [si, co]])
    back = ahead.T / (2.0 * LMAX)
    reps = np.array(REPS)
    turn = 2.0 * math.pi * ((reps[:, None] * fine[None, :]) % (2 * LMAX)) / (2 * LMAX)
    twist = np.concatenate([np.cos(turn), -np.sin(turn)], axis=1)[:, None, :]

    def pieces(table):
        table = table.astype(np.float32)
        upper = table.astype(jnp.bfloat16)
        lower = (table - upper.astype(np.float32)).astype(jnp.bfloat16)
        return np.stack([upper, lower])

    return pieces(ahead), pieces(back), twist.astype(np.float32)


AHEAD, BACK, TWIST = transform_tables()


def three_pass(values, table_ref):
    upper = values.astype(bf16)
    lower = (values - upper.astype(f32)).astype(bf16)
    t0, t1 = table_ref[0], table_ref[1]
    return (
        jnp.dot(upper, t0, preferred_element_type=f32)
        + jnp.dot(lower, t0, preferred_element_type=f32)
        + jnp.dot(upper, t1, preferred_element_type=f32)
    )


def rows_forward(xs_ref, spec_ref, rows):
    def step(g, carry):
        at = pl.ds(pl.multiple_of(g * 8, 8), 8)
        xs = [xs_ref[n, at, :] for n in range(COARSE)]

        def put(k1, z):
            i = PLACE[k1]
            spec_ref[i, at, 0:LANE] = z[0]
            spec_ref[i, at, LANE : 2 * LANE] = jnp.zeros_like(z[0]) if z[1] is None else z[1]

        coarse_forward(xs, put)
        return carry

    lax.fori_loop(0, rows // 8, step, 0)


def rows_inverse(spec_ref, ys_ref, rows):
    def step(g, carry):
        at = pl.ds(pl.multiple_of(g * 8, 8), 8)

        def get(k1):
            i = PLACE[k1]
            return spec_ref[i, at, 0:LANE], spec_ref[i, at, LANE : 2 * LANE]

        for n, y in enumerate(coarse_inverse(get)):
            ys_ref[n, at, :] = y
        return carry

    lax.fori_loop(0, rows // 8, step, 0)


def fine_forward(spec, twist, ahead_ref):
    re, im = spec[:, :LANE], spec[:, LANE:]
    tr, ti = twist[:, :LANE], twist[:, LANE:]
    return three_pass(jnp.concatenate([re * tr - im * ti, re * ti + im * tr], axis=1), ahead_ref)


def fine_inverse(spec, twist, back_ref):
    v = three_pass(spec, back_ref)
    re, im = v[:, :LANE], v[:, LANE:]
    tr, ti = twist[:, :LANE], twist[:, LANE:]
    return jnp.concatenate([re * tr + im * ti, im * tr - re * ti], axis=1)


def times(a, b):
    ar, ai, br, bi = a[:, :LANE], a[:, LANE:], b[:, :LANE], b[:, LANE:]
    return jnp.concatenate([ar * br - ai * bi, ar * bi + ai * br], axis=1)


def times_conj(a, b):
    ar, ai, br, bi = a[:, :LANE], a[:, LANE:], b[:, :LANE], b[:, LANE:]
    return jnp.concatenate([ar * br + ai * bi, ai * br - ar * bi], axis=1)


def together(values):
    return values.reshape(values.shape[0] * values.shape[1], values.shape[2])


def apart(values):
    return values.reshape(BATCH, values.shape[0] // BATCH, values.shape[1])


def twists(twist_ref, at, rows):
    return together(jnp.broadcast_to(twist_ref[at], (BATCH, rows, 2 * LANE)))


def spread(blocks_ref, xs_ref):
    per = blocks_ref.shape[2] // LANE
    for n in range(COARSE):
        r = n % per
        xs_ref[n] = blocks_ref[n // per, :, r * LANE : (r + 1) * LANE].astype(f32)


def filter_spectrum_body(filter_ref, twist_ref, ahead_ref, out_ref, xs_ref):
    rows = filter_ref.shape[0]
    for n in range(COARSE):
        xs_ref[n] = filter_ref[:, n * LANE : (n + 1) * LANE]
    rows_forward(xs_ref, out_ref, rows)

    def step(i, carry):
        at = pl.ds(i * BATCH, BATCH)
        out_ref[at] = apart(fine_forward(together(out_ref[at]), twists(twist_ref, at, rows), ahead_ref))
        return carry

    lax.fori_loop(0, len(REPS) // BATCH, step, 0)


def conv_forward_body(seqs, mixed_ref, filt_ref, bias_ref, twist_ref, ahead_ref, back_ref, out_ref, spec_ref, xs_ref, work_ref):
    rows = mixed_ref.shape[1]
    spread(mixed_ref, xs_ref)
    rows_forward(xs_ref, spec_ref, rows)

    def step(i, carry):
        at = pl.ds(i * BATCH, BATCH)
        twist = twists(twist_ref, at, rows)
        z = fine_forward(together(spec_ref[at]), twist, ahead_ref)
        spec_ref[at] = apart(z)
        k = together(jnp.concatenate([filt_ref[at]] * seqs, axis=1))
        work_ref[at] = apart(fine_inverse(times(z, k), twist, back_ref))
        return carry

    lax.fori_loop(0, len(REPS) // BATCH, step, 0)
    ys_ref = xs_ref
    rows_inverse(work_ref, ys_ref, rows)
    per = mixed_ref.shape[2] // LANE
    bias = jnp.concatenate([bias_ref[...]] * seqs, axis=0)
    for n in range(COARSE):
        at = (n // per, slice(None), slice((n % per) * LANE, (n % per + 1) * LANE))
        out_ref[at] = (ys_ref[n] + bias * mixed_ref[at].astype(f32)).astype(bf16)


def heads_out(out_ref, block, y):
    rows, width = y.shape[0], out_ref.shape[2]
    square = jnp.concatenate([y, jnp.zeros((LANE - rows, LANE), f32)], axis=0) if rows < LANE else y
    head = square.T[:HEAD_ROWS]
    if width > LANE:
        head = jnp.concatenate([head, jnp.zeros((HEAD_ROWS, width - LANE), f32)], axis=1)
    out_ref[block, rows:, :] = head.astype(bf16)


def conv_backward_body(
    seqs, d_ref, mixed_ref, mixed_spec_ref, filt_ref, bias_ref, twist_ref, ahead_ref, back_ref, out_ref, dfilt_ref, dbias_ref, xs_ref, spec_ref, work_ref, ys_ref
):
    rows = d_ref.shape[1]
    chans = rows // seqs
    spread(d_ref, xs_ref)
    rows_forward(xs_ref, spec_ref, rows)

    def step(i, carry):
        at = pl.ds(i * BATCH, BATCH)
        z = fine_forward(together(spec_ref[at]), twists(twist_ref, at, rows), ahead_ref)
        k = together(jnp.concatenate([filt_ref[at]] * seqs, axis=1))
        cross = apart(times_conj(z, together(mixed_spec_ref[at])))
        cross = sum(cross[:, s * chans : (s + 1) * chans] for s in range(seqs))
        both = together(jnp.concatenate([apart(times_conj(z, k)), cross], axis=1))
        work_ref[at] = apart(fine_inverse(both, twists(twist_ref, at, rows + chans), back_ref))
        return carry

    lax.fori_loop(0, len(REPS) // BATCH, step, 0)
    rows_inverse(work_ref, ys_ref, rows + chans)
    per = d_ref.shape[2] // LANE
    bias = jnp.concatenate([bias_ref[...]] * seqs, axis=0)
    total = jnp.zeros((rows, LANE), f32)
    out_ref[out_ref.shape[0] - 1, rows:, :] = jnp.zeros((HEAD_ROWS, d_ref.shape[2]), bf16)
    for n in range(COARSE):
        at = (n // per, slice(0, rows), slice((n % per) * LANE, (n % per + 1) * LANE))
        d = xs_ref[n]
        y = ys_ref[n, :rows, :] + bias * d
        out_ref[at] = y.astype(bf16)
        if n % per == 0 and n > 0:
            heads_out(out_ref, n // per - 1, y)
        total = total + d * mixed_ref[at].astype(f32)
        dfilt_ref[:, n * LANE : (n + 1) * LANE] = ys_ref[n, rows:, :]
    total = sum(total[s * chans : (s + 1) * chans] for s in range(seqs))
    dbias_ref[...] = jnp.sum(total, axis=1, keepdims=True)


def takes(us):
    return pl.CostEstimate(flops=int(us * 1e9), bytes_accessed=int(us * 3e6), transcendentals=0)


def whole_call(us, body, out_shape, scratch, *args):
    return pl.pallas_call(
        body,
        cost_estimate=takes(us),
        out_shape=out_shape,
        in_specs=[pl.BlockSpec(memory_space=pltpu.VMEM)] * len(args),
        out_specs=jax.tree.map(lambda _: pl.BlockSpec(memory_space=pltpu.VMEM), out_shape),
        scratch_shapes=scratch,
        compiler_params=pltpu.CompilerParams(vmem_limit_bytes=vmem_limit),
    )(*args)


def filter_spectrum(filt):
    rows = filt.shape[0]
    return whole_call(
        8,
        filter_spectrum_body,
        jax.ShapeDtypeStruct((len(REPS), rows, 2 * LANE), f32),
        [pltpu.VMEM((COARSE, rows, LANE), f32)],
        filt,
        jnp.asarray(TWIST),
        jnp.asarray(AHEAD),
    )


def conv_forward(mixed, filt_spec, bias, seqs):
    blocks, rows, width = mixed.shape
    n = len(REPS)
    return whole_call(
        14,
        lambda *refs: conv_forward_body(seqs, *refs),
        (jax.ShapeDtypeStruct(mixed.shape, bf16), jax.ShapeDtypeStruct((n, rows, 2 * LANE), f32)),
        [pltpu.VMEM((COARSE, rows, LANE), f32), pltpu.VMEM((n, rows, 2 * LANE), f32)],
        mixed,
        filt_spec,
        bias,
        jnp.asarray(TWIST),
        jnp.asarray(AHEAD),
        jnp.asarray(BACK),
    )


def conv_backward(d_conv, mixed, mixed_spec, filt_spec, bias, seqs):
    blocks, rows, width = mixed.shape
    chans = rows // seqs
    n = len(REPS)
    return whole_call(
        16,
        lambda *refs: conv_backward_body(seqs, *refs),
        (
            jax.ShapeDtypeStruct((blocks, rows + HEAD_ROWS, width), bf16),
            jax.ShapeDtypeStruct((chans, LMAX), f32),
            jax.ShapeDtypeStruct((chans, 1), f32),
        ),
        [
            pltpu.VMEM((COARSE, rows, LANE), f32),
            pltpu.VMEM((n, rows, 2 * LANE), f32),
            pltpu.VMEM((n, rows + chans, 2 * LANE), f32),
            pltpu.VMEM((COARSE, rows + chans, LANE), f32),
        ],
        d_conv,
        mixed,
        mixed_spec,
        filt_spec,
        bias,
        jnp.asarray(TWIST),
        jnp.asarray(AHEAD),
        jnp.asarray(BACK),
    )


CHUNK = 48


def lanes_of(shape):
    return lax.broadcasted_iota(jnp.int32, shape, 1)


def side_by_side(block, seqs):
    chans = block.shape[0] // seqs
    return jnp.concatenate([block[s * chans : (s + 1) * chans] for s in range(seqs)], axis=1)


def stacked(values, seqs):
    width = values.shape[1] // seqs
    return jnp.concatenate([values[:, s * width : (s + 1) * width] for s in range(seqs)], axis=0)


def eights(values):
    return jnp.sum(values.reshape(values.shape[0] // 8, 8, values.shape[1]), axis=0)


def folded(values):
    return sum(values[:, i * LANE : (i + 1) * LANE] for i in range(values.shape[1] // LANE))


def row_totals(values):
    ones = jnp.ones((8, LANE), bf16)
    upper = values.astype(bf16)
    lower = (values - upper.astype(f32)).astype(bf16)
    return mm16(ones, upper, NT) + mm16(ones, lower, NT)


def padded_totals(values, width):
    extra = -values.shape[0] % width
    if extra:
        values = jnp.concatenate([values, jnp.zeros((extra, LANE), f32)], axis=0)
    totals = row_totals(values)
    return [totals[:, i * width : (i + 1) * width] for i in range(totals.shape[1] // width)]


def as_rows(totals, rows):
    halves = []
    for t in totals:
        upper = t.astype(bf16).astype(f32)
        halves += [upper, t - upper]
    place = lax.broadcasted_iota(jnp.int32, halves[0].shape, 0)
    tiles = []
    for first in range(0, rows, 8):
        tile = jnp.zeros_like(halves[0])
        for i, h in enumerate(halves[first : first + 8]):
            tile = jnp.where(place == i, h, tile)
        tiles.append(tile)
    return jnp.concatenate(tiles, axis=0).astype(bf16)


def chunk_rows(i):
    return pl.ds(pl.multiple_of(i * CHUNK, CHUNK), CHUNK)


def norm_stats(ref, dim):
    cols = ref.shape[1]
    zero = jnp.zeros((8, cols), f32)
    total = lax.fori_loop(0, dim // CHUNK, lambda i, t: t + eights(ref[chunk_rows(i), :]), zero)
    mean = jnp.sum(total, axis=0, keepdims=True) / dim

    def spread_sq(i, t):
        v = ref[chunk_rows(i), :] - mean
        return t + eights(v * v)

    var = jnp.sum(lax.fori_loop(0, dim // CHUNK, spread_sq, zero), axis=0, keepdims=True) / dim
    return mean, lax.rsqrt(var + epsilon)


def front_body(seqs, group, flag_ref, x_ref, xh_ref, w_ref, prm_ref, after_ref, xn_ref, stat_ref, gate_ref, pair_ref, projx0_ref, projx_ref, mixed_ref, heads_ref, xs, xb):
    devices, _, width = x_ref.shape
    dim, cols = xn_ref.shape
    chans = dim // devices
    step = pl.program_id(0)

    @pl.when(step == 0)
    def _():
        def gather(d, carry):
            at = pl.ds(pl.multiple_of(d * chans, 8), chans)
            row = side_by_side(x_ref[d].astype(f32), seqs)
            tail = xh_ref[d].astype(f32)
            tail = jnp.where(
                lanes_of((chans, LANE)) < LANE // 2, pltpu.roll(tail[chans : 2 * chans], LANE // 2, 1), tail[:chans]
            )
            xs[at, :] = jnp.concatenate([row, tail], axis=1)
            return carry

        lax.fori_loop(0, devices, gather, 0)
        mean, inverse = norm_stats(xs, dim)

        def scale(i, carry):
            at = chunk_rows(i)
            prm = prm_ref[at, :]
            v = (xs[at, :] - mean) * inverse * prm[:, 15:16] + prm[:, 16:17]
            xb[at, :] = v.astype(bf16)
            xn_ref[at, :] = v[:, :cols].astype(bf16)
            return carry

        lax.fori_loop(0, dim // CHUNK, scale, 0)
        stat_ref[0:8, :] = jnp.broadcast_to(mean[:, :cols], (8, cols))
        stat_ref[8:16, :] = jnp.broadcast_to(inverse[:, :cols], (8, cols))

    keep = (flag_ref[0] > 0).astype(f32)
    for g in range(group):
        prm = prm_ref[pl.ds(pl.multiple_of((step * group + g) * chans, 8), chans), :]
        proj = mm16(w_ref[g, PRM:, :], xb[...], NN)
        ys = []
        px = []
        for i in range(3):
            x = proj[i * chans : (i + 1) * chans] + prm[:, i : i + 1]
            tail = x[:, cols:] * keep
            px += [jnp.concatenate([x[:, :cols], tail], axis=1)]
            weights = [jnp.broadcast_to(prm[:, 6 + 3 * j + i : 7 + 3 * j + i], (chans, width)) for j in range(KS)]
            bias = jnp.broadcast_to(prm[:, 3 + i : 4 + i], (chans, width))
            parts = []
            for s in range(seqs):
                v = x[:, s * width : (s + 1) * width]
                wide = jnp.concatenate([tail if s == 0 else pltpu.roll(tail, LANE // 2, 1), v], axis=1)
                y = bias + weights[0] * v
                for j in range(1, KS):
                    y = y + weights[j] * pltpu.roll(wide, j, 1)[:, LANE:]
                parts.append(y)
            ys.append(jnp.concatenate(parts, axis=1))
        projx0_ref[g] = px[0].astype(bf16)
        projx_ref[g] = jnp.concatenate(px[1:], axis=0).astype(bf16)
        gate_ref[g] = ys[0]
        pair = jnp.concatenate(ys[1:], axis=0)
        pair_ref[g] = pair
        mixed_ref[g] = stacked(ys[1] * ys[2], seqs).astype(bf16)
        heads_ref[g] = first_tokens(pair, seqs).astype(bf16)


def first_tokens(values, seqs):
    width = values.shape[1] // seqs
    second = pltpu.roll(values[:, width : width + LANE], LANE // 2, 1)
    return jnp.where(lanes_of((values.shape[0], LANE)) < LANE // 2, values[:, :LANE], second)


def params(kind):
    return pltpu.CompilerParams(vmem_limit_bytes=vmem_limit, dimension_semantics=("arbitrary",))


def whole(a):
    return pl.BlockSpec(a.shape, lambda i: (0,) * len(a.shape), pipeline_mode=pl.Buffered(1))


def half(a, which):
    return pl.BlockSpec(
        (a.shape[0], a.shape[1] // 2, a.shape[2]), lambda i: (0, which, 0), pipeline_mode=pl.Buffered(1)
    )


def untouched():
    return pl.BlockSpec(memory_space=pl.ANY)


def by_group(a, group):
    return pl.BlockSpec((group,) + a.shape[1:], lambda i: (i,) + (0,) * (len(a.shape) - 1))


def smem():
    return pl.BlockSpec(memory_space=pltpu.SMEM)


def front(flag, x_cot, xh, weights, prm, after, seqs):
    devices, rows, width = x_cot.shape
    rows = rows // 2
    chans = rows // seqs
    dim = devices * chans
    cols = seqs * width
    group = 2
    sd = jax.ShapeDtypeStruct
    out = (
        sd((dim, cols), bf16),
        sd((16, cols), f32),
        sd((devices, chans, cols), f32),
        sd((devices, 2 * chans, cols), f32),
        sd((devices, chans, cols + LANE), bf16),
        sd((devices, 2 * chans, cols + LANE), bf16),
        sd((devices, rows, width), bf16),
        sd((devices, 2 * chans, LANE), bf16),
    )
    return pl.pallas_call(
        lambda *refs: front_body(seqs, group, *refs),
        cost_estimate=takes(16),
        grid=(devices // group,),
        out_shape=out,
        in_specs=[smem(), half(x_cot, 0), whole(xh), by_group(weights, group), whole(prm), untouched()],
        out_specs=(whole(out[0]), whole(out[1])) + tuple(by_group(o, group) for o in out[2:]),
        scratch_shapes=[pltpu.VMEM((dim, cols + LANE), f32), pltpu.VMEM((dim, cols + LANE), bf16)],
        compiler_params=params(0),
    )(flag, x_cot, xh, weights, prm, after)


def middle_body(
    seqs, group, lens_ref, conv_ref, x_ref, cot_ref, gate_ref, w_ref, out_w_ref, prm_ref,
    layer_ref, d_conv_ref, d_res_ref, p0_ref, p0h_ref, g_ref,
    cs, res, ds, xb, db, gb, acc_out, acc_in, folds, up_folds, stats,
):
    devices, _, width = x_ref.shape
    dim, cols = d_res_ref.shape
    chans = dim // devices
    hid = w_ref.shape[1] // 2
    step = pl.program_id(0)
    last = pl.num_programs(0) - 1
    lane = lanes_of((1, cols))
    live = jnp.zeros((1, cols), f32)
    for s in range(seqs):
        inside = (lane >= s * width) & (lane < (s + 1) * width) & (lens_ref[seqs] * width + lane - s * width < lens_ref[s])
        live = jnp.where(inside, 1.0, live)

    def device_rows(d):
        return pl.ds(pl.multiple_of(d * chans, 8), chans)

    @pl.when(step == 0)
    def _():
        def gather(d, carry):
            at = device_rows(d)
            cs[at, :] = side_by_side(conv_ref[d].astype(f32), seqs)
            res[at, :] = side_by_side(x_ref[d].astype(f32), seqs)
            ds[at, :] = live * side_by_side(cot_ref[d].astype(f32), seqs)
            return carry

        lax.fori_loop(0, devices, gather, 0)

        def gated(i, carry):
            at = chunk_rows(i)
            gb[at, :] = (cs[at, :] * gate_ref[at, :]).astype(bf16)
            d = ds[at, :]
            db[at, :] = d.astype(bf16)
            folds[3, at, :] = folded(d)
            acc_in[at, :] = jnp.zeros((CHUNK, cols), f32)
            return carry

        lax.fori_loop(0, dim // CHUNK, gated, 0)
        for n in range(dim // 256):
            at = slice(n * 256, (n + 1) * 256)
            acc_out[at, :] = mm16(out_w_ref[:, at], gb[...], TN)

        def add(i, carry):
            at = chunk_rows(i)
            res[at, :] = res[at, :] + acc_out[at, :] + prm_ref[at, 19:20]
            acc_out[at, :] = jnp.zeros((CHUNK, cols), f32)
            return carry

        lax.fori_loop(0, dim // CHUNK, add, 0)
        mean, inverse = norm_stats(res, dim)

        def scale(i, carry):
            at = chunk_rows(i)
            normed = (res[at, :] - mean) * inverse
            cs_norm = normed * prm_ref[at, 17:18] + prm_ref[at, 18:19]
            xb[at, :] = cs_norm.astype(bf16)
            return carry

        lax.fori_loop(0, dim // CHUNK, scale, 0)
        stats[0:8, :] = jnp.broadcast_to(mean, (8, cols))
        stats[8:16, :] = jnp.broadcast_to(inverse, (8, cols))

    up_b = []
    for g in range(group):
        prm = prm_ref[device_rows(step * group + g), :]
        up_b += [prm[:, 21 + m : 22 + m] for m in range(hid // chans)]
    up_b = jnp.concatenate(up_b, axis=0)
    up = w_ref[:, :hid, :].reshape(group * hid, dim)
    down = w_ref[:, hid:, :].reshape(group * hid, dim)
    u = mm16(up, xb[...], NN) + up_b
    d_act = mm16(down, db[...], NN)
    a, k = 0.044715, math.sqrt(2.0 / math.pi)
    sq = u * u
    t = jnp.tanh(u * (k + (k * a) * sq))
    half = 0.5 * (1.0 + t)
    act = (u * half).astype(bf16)
    d_u = d_act * (half + 0.5 * u * (1.0 - t * t) * (k + (3.0 * k * a) * sq))
    d_low = d_u.astype(bf16)
    up_folds[pl.ds(pl.multiple_of(step * group * hid, 8), group * hid), :] = folded(d_u)
    acc_out[...] += mm16(down, act, TN)
    acc_in[...] += mm16(up, d_low, TN)
    mine = pl.ds(step * group, group)
    g_ref[mine, :hid, :] = mm16(d_low, xb[...], NT).astype(bf16).reshape(group, hid, dim)
    g_ref[mine, hid : 2 * hid, :] = mm16(act, db[...], NT).astype(bf16).reshape(group, hid, dim)

    @pl.when(step == last)
    def _():
        mean, inverse = stats[0:1, :], stats[8:9, :]

        def result(i, t):
            at = chunk_rows(i)
            r = res[at, :]
            acc_out[at, :] = live * (r + acc_out[at, :] + prm_ref[at, 20:21])
            normed = (r - mean) * inverse
            d = acc_in[at, :]
            both = d * normed
            folds[0, at, :] = folded(both)
            folds[1, at, :] = folded(d)
            gain = prm_ref[at, 17:18]
            return t[0] + eights(d * gain), t[1] + eights(both * gain)

        zero = jnp.zeros((8, cols), f32)
        m1, m2 = lax.fori_loop(0, dim // CHUNK, result, (zero, zero))
        m1 = jnp.sum(m1, axis=0, keepdims=True) / dim
        m2 = jnp.sum(m2, axis=0, keepdims=True) / dim

        def residual(i, carry):
            at = chunk_rows(i)
            normed = (res[at, :] - mean) * inverse
            d = ds[at, :] + inverse * (acc_in[at, :] * prm_ref[at, 17:18] - m1 - normed * m2)
            d_res_ref[at, :] = d
            folds[2, at, :] = folded(d)
            db[at, :] = d.astype(bf16)
            return carry

        lax.fori_loop(0, dim // CHUNK, residual, 0)
        for n in range(dim // 256):
            at = slice(n * 256, (n + 1) * 256)
            acc_in[at, :] = mm16(out_w_ref[at, :], db[...], NN)
        some = 192 // chans
        for n in range(devices // some):
            g_out = mm16(gb[n * 192 : (n + 1) * 192, :], db[...], NT).reshape(some, chans, dim)
            g_ref[n * some : (n + 1) * some, 2 * hid :, :] = g_out.astype(bf16)

        def products(i, carry):
            at = chunk_rows(i)
            d = acc_in[at, :]
            p0 = d * cs[at, :]
            p0_ref[at, :] = p0
            p0h_ref[at, :] = first_tokens(p0, seqs)
            acc_in[at, :] = d * gate_ref[at, :]
            return carry

        lax.fori_loop(0, dim // CHUNK, products, 0)

        def scatter(d, carry):
            at = device_rows(d)
            layer_ref[d, : seqs * chans, :] = stacked(acc_out[at, :], seqs).astype(bf16)
            d_conv_ref[d] = stacked(acc_in[at, :], seqs).astype(bf16)
            totals = [padded_totals(folds[q, at, :], width)[0] for q in range(4)]
            totals += padded_totals(up_folds[pl.ds(pl.multiple_of(d * hid, 8), hid), :], width)
            layer_ref[d, seqs * chans :, :] = as_rows(totals, SUM_ROWS)
            return carry

        lax.fori_loop(0, devices, scatter, 0)


def middle(lens, conv, x_cot, gate, weights, out_w, prm, hid, seqs):
    devices, rows, width = conv.shape
    dim, cols = gate.shape
    chans = dim // devices
    group = 2
    sd = jax.ShapeDtypeStruct
    out = (
        sd((devices, rows + SUM_ROWS, width), bf16),
        sd((devices, rows, width), bf16),
        sd((dim, cols), f32),
        sd((dim, cols), f32),
        sd((dim, LANE), f32),
        sd((devices, 2 * hid + chans, dim), bf16),
    )
    big = pltpu.VMEM((dim, cols), f32)
    low = pltpu.VMEM((dim, cols), bf16)
    return pl.pallas_call(
        lambda *refs: middle_body(seqs, group, *refs),
        cost_estimate=takes(40),
        grid=(devices // group,),
        out_shape=out,
        in_specs=[
            smem(), whole(conv), half(x_cot, 0), half(x_cot, 1), whole(gate),
            pl.BlockSpec((group, 2 * hid, dim), lambda i: (i, 0, 0)), whole(out_w), whole(prm),
        ],
        out_specs=tuple(whole(o) for o in out),
        scratch_shapes=[
            big, big, big, low, low, low, big, big, pltpu.VMEM((4, dim, LANE), f32),
            pltpu.VMEM((devices * hid, LANE), f32), pltpu.VMEM((16, cols), f32),
        ],
        compiler_params=params(0),
    )(lens, conv, x_cot, x_cot, gate, weights, out_w, prm)


def short_back(seqs, prm, kinds, d_short, head, projx, width, cols):
    chans = prm.shape[0]
    d_proj = []
    totals = [[] for _ in range(2 + KS)]
    for n, i in enumerate(kinds):
        px = projx[n * chans : (n + 1) * chans]
        weights = [jnp.broadcast_to(prm[:, 6 + 3 * j + i : 7 + 3 * j + i], (chans, width)) for j in range(KS)]
        parts = []
        sums = [0.0] * (2 + KS)
        for s in range(seqs):
            at = slice(s * width, (s + 1) * width)
            d = d_short[n][:, at]
            x = px[:, at]
            tail = px[:, cols:]
            wide = jnp.concatenate([tail if s == 0 else pltpu.roll(tail, LANE // 2, 1), x], axis=1)
            after = jnp.concatenate([d, head[n] if s == 0 else pltpu.roll(head[n], LANE // 2, 1)], axis=1)
            y = weights[0] * d
            sums[1] = sums[1] + folded(d)
            sums[2] = sums[2] + folded(d * x)
            for j in range(1, KS):
                y = y + weights[j] * pltpu.roll(after, width + LANE - j, 1)[:, :width]
                sums[2 + j] = sums[2 + j] + folded(d * pltpu.roll(wide, j, 1)[:, LANE:])
            sums[0] = sums[0] + folded(y)
            parts.append(y)
        d_proj.append(jnp.concatenate(parts, axis=1))
        for k in range(2 + KS):
            totals[k].append(sums[k])
    d_low = jnp.concatenate(d_proj, axis=0).astype(bf16)
    return d_low, padded_totals(jnp.concatenate(sum(totals, []), axis=0), width)


def back_gate_body(seqs, group, p0_ref, p0h_ref, projx_ref, w_ref, prm_ref, xn_ref, g_ref, sums_ref, acc):
    dim, cols = xn_ref.shape
    chans = p0_ref.shape[1]
    step = pl.program_id(0)

    @pl.when(step == 0)
    def _():
        acc[...] = jnp.zeros_like(acc)

    for g in range(group):
        prm = prm_ref[pl.ds(pl.multiple_of((step * group + g) * chans, 8), chans), :]
        d_low, totals = short_back(
            seqs, prm, (0,), (p0_ref[g],), (p0h_ref[g],), projx_ref[g].astype(f32), cols // seqs, cols
        )
        sums_ref[g] = totals[0]
        acc[...] += mm16(w_ref[g, PRM : PRM + chans, :], d_low, TN)
        g_ref[g] = mm16(d_low, xn_ref[...], NT).astype(bf16)


def back_gate(p0, p0h, projx, weights, prm, xn, seqs):
    devices, chans, cols = p0.shape
    dim = xn.shape[0]
    group = 4
    sd = jax.ShapeDtypeStruct
    out = (
        sd((devices, chans, dim), bf16),
        sd((devices, 8, cols // seqs), f32),
        sd((dim, cols), f32),
    )
    return pl.pallas_call(
        lambda *refs: back_gate_body(seqs, group, *refs),
        cost_estimate=takes(12),
        grid=(devices // group,),
        out_shape=out,
        in_specs=[by_group(a, group) for a in (p0, p0h, projx, weights)] + [whole(prm), whole(xn)],
        out_specs=(by_group(out[0], group), by_group(out[1], group), whole(out[2])),
        compiler_params=params(0),
    )(p0, p0h, projx, weights, prm, xn)


def back_body(
    seqs, group, d_mixed_ref, pair_ref, heads_ref, projx_ref, w_ref, prm_ref, xn_ref, x_ref, stat_ref, d_res_ref, acc0_ref,
    sums0_ref, layer_ref, shared_ref, tail_ref, g_ref, acc, xs, folds, sums,
):
    devices, _, width = x_ref.shape
    dim, cols = xn_ref.shape
    chans = dim // devices
    step = pl.program_id(0)
    last = pl.num_programs(0) - 1

    @pl.when(step == 0)
    def _():
        acc[...] = acc0_ref[...]

    for g in range(group):
        prm = prm_ref[pl.ds(pl.multiple_of((step * group + g) * chans, 8), chans), :]
        block = d_mixed_ref[g].astype(f32)
        d_mixed = side_by_side(block[: seqs * chans], seqs)
        square = jnp.concatenate([block[seqs * chans :, :LANE], jnp.zeros((LANE - HEAD_ROWS, LANE), f32)], axis=0).T
        second = pltpu.roll(square[chans : 2 * chans], LANE // 2, 1)
        d_head = jnp.where(lanes_of((chans, LANE)) < LANE // 2, square[:chans], second)
        pair = pair_ref[g]
        pair_head = heads_ref[g].astype(f32)
        d_short = (d_mixed * pair[chans:], d_mixed * pair[:chans])
        head = (d_head * pair_head[chans:], d_head * pair_head[:chans])
        d_low, totals = short_back(seqs, prm, (1, 2), d_short, head, projx_ref[g].astype(f32), width, cols)
        for n, t in enumerate(totals):
            sums[n, step * group + g] = t
        acc[...] += mm16(w_ref[g, PRM + chans :, :], d_low, TN)
        g_ref[g] = mm16(d_low, xn_ref[...], NT).astype(bf16)

    @pl.when(step == last)
    def _():
        def gather(d, carry):
            xs[pl.ds(pl.multiple_of(d * chans, 8), chans), :] = side_by_side(x_ref[d].astype(f32), seqs)
            return carry

        lax.fori_loop(0, devices, gather, 0)
        mean, inverse = stat_ref[0:1, :], stat_ref[8:9, :]

        def first(i, t):
            at = chunk_rows(i)
            normed = (xs[at, :] - mean) * inverse
            d = acc[at, :]
            both = d * normed
            folds[0, at, :] = folded(both)
            folds[1, at, :] = folded(d)
            gain = prm_ref[at, 15:16]
            return t[0] + eights(d * gain), t[1] + eights(both * gain)

        zero = jnp.zeros((8, cols), f32)
        m1, m2 = lax.fori_loop(0, dim // CHUNK, first, (zero, zero))
        m1 = jnp.sum(m1, axis=0, keepdims=True) / dim
        m2 = jnp.sum(m2, axis=0, keepdims=True) / dim

        def second(i, carry):
            at = chunk_rows(i)
            normed = (xs[at, :] - mean) * inverse
            acc[at, :] = d_res_ref[at, :] + inverse * (acc[at, :] * prm_ref[at, 15:16] - m1 - normed * m2)
            return carry

        lax.fori_loop(0, dim // CHUNK, second, 0)

        rows = seqs * chans
        ends = [rows, 2 * rows + SUM_ROWS, 2 * rows + 2 * SUM_ROWS]

        def scatter(d, carry):
            at = pl.ds(pl.multiple_of(d * chans, 8), chans)
            tail_ref[d, : ends[0], :] = stacked(acc[at, :], seqs).astype(bf16)
            tail_ref[d, ends[0] : ends[1], :] = layer_ref[d]
            totals = [sums0_ref[d]] + [sums[n, d] for n in range(sums.shape[0])]
            totals += [padded_totals(folds[q, at, :], width)[0] for q in range(2)]
            tail_ref[d, ends[1] : ends[2], :] = as_rows(totals, SUM_ROWS)
            tail_ref[d, ends[2] :, :] = shared_ref[...]
            return carry

        lax.fori_loop(0, devices, scatter, 0)


def back(d_mixed, pair, heads, projx, weights, prm, xn, x_cot, stat, d_res, acc0, sums0, layer, shared, seqs):
    devices, rows, width = x_cot.shape
    rows = rows // 2
    dim, cols = xn.shape
    chans = dim // devices
    group = 2
    sd = jax.ShapeDtypeStruct
    pieces = -(-2 * (2 + KS) * chans // width)
    out = (
        sd((devices, 2 * rows + 2 * SUM_ROWS + shared.shape[0], width), bf16),
        sd((devices, 2 * chans, dim), bf16),
    )
    return pl.pallas_call(
        lambda *refs: back_body(seqs, group, *refs),
        cost_estimate=takes(20),
        grid=(devices // group,),
        out_shape=out,
        in_specs=[by_group(a, group) for a in (d_mixed, pair, heads, projx, weights)]
        + [whole(prm), whole(xn), half(x_cot, 0)]
        + [whole(a) for a in (stat, d_res, acc0, sums0, layer, shared)],
        out_specs=(whole(out[0]), by_group(out[1], group)),
        scratch_shapes=[
            pltpu.VMEM((dim, cols), f32), pltpu.VMEM((dim, cols), f32), pltpu.VMEM((2, dim, LANE), f32),
            pltpu.VMEM((pieces, devices, 8, width), f32),
        ],
        compiler_params=params(0),
    )(d_mixed, pair, heads, projx, weights, prm, xn, x_cot, stat, d_res, acc0, sums0, layer, shared)


def position_table():
    places = np.arange(LMAX)
    orders = np.arange(1, (EMB - 1) // 2 + 1)
    turns = 2.0 * math.pi * ((orders[:, None] * places[None, :]) % LMAX) / LMAX
    ramp = places[None, :] / (LMAX - 1)
    return np.concatenate([ramp, np.cos(turns), -np.sin(turns)], axis=0).astype(np.float32)


FEAT = position_table()


def mm(a, b, dims):
    return lax.dot_general(a, b, (dims, ((), ())), precision=highest, preferred_element_type=f32)


NN = ((1,), (0,))
TN = ((0,), (0,))
NT = ((1,), (1,))


def mm16(a, b, dims):
    return lax.dot_general(a, b, (dims, ((), ())), preferred_element_type=f32)


def exchange(values):
    return lax.all_to_all(values, "chan", split_axis=0, concat_axis=0, tiled=True)


def on_device(
    layer_in,
    seq_lengths,
    ln1_gain,
    first_norm_bias,
    in_weight,
    in_bias,
    short_weight,
    short_bias,
    filt_in,
    filt_in_bias,
    filt_mid,
    filt_mid_bias,
    sine_freq,
    filt_out,
    decay_rate,
    conv_bias,
    out_weight,
    out_bias,
    ln2_gain,
    second_norm_bias,
    up_weight,
    up_bias,
    down_weight,
    down_bias,
    cotangent,
):
    seqs, chans, _ = layer_in.shape
    devices = lax.axis_size("chan")
    groups = lax.axis_size("batch")
    width = LMAX // devices
    dim = chans * devices
    cols = seqs * width
    hid = up_weight.shape[0]
    ford = filt_mid.shape[0]
    place = lax.axis_index("chan")

    def to_blocks(values):
        return (
            values.reshape(seqs, chans, devices, width)
            .transpose(2, 0, 1, 3)
            .reshape(devices, seqs * chans, width)
        )

    def from_blocks(blocks):
        return (
            blocks.reshape(devices, seqs, chans, width)
            .transpose(1, 2, 0, 3)
            .reshape(seqs, chans, LMAX)
        )

    small = jnp.concatenate(
        [
            in_bias,
            short_bias,
            short_weight.reshape(3 * KS, chans),
            jnp.stack([ln1_gain, first_norm_bias, ln2_gain, second_norm_bias, out_bias, down_bias]),
            up_bias.reshape(hid // chans, chans),
        ],
        axis=0,
    )
    small = jnp.pad(small, ((0, PRM - small.shape[0]), (0, dim - chans)))
    in_rows = in_weight.transpose(1, 2, 0).reshape(3 * chans, dim)
    in_all = lax.all_gather(jnp.concatenate([small, in_rows], axis=0), "chan", axis=0)
    x = exchange(jnp.concatenate([to_blocks(layer_in), to_blocks(cotangent)], axis=1))
    rows = seqs * chans
    xh = lax.ppermute(x[:, :rows, width - LANE :], "chan", [(i, i + 1) for i in range(devices - 1)])
    rest = lax.all_gather(jnp.concatenate([up_weight, down_weight, out_weight], axis=0), "chan", axis=0)
    prm = in_all[:, :PRM, :chans].astype(f32).transpose(0, 2, 1).reshape(dim, PRM)
    out_w = rest[:, 2 * hid :].reshape(dim, dim)

    feat = jnp.asarray(FEAT)
    ramp = feat[0:1]
    rate = sine_freq[:, None]
    pre1 = mm(filt_in, feat, TN) + filt_in_bias[:, None]
    h1 = jnp.sin(rate * pre1)
    pre2 = mm(filt_mid, h1, TN) + filt_mid_bias[:, None]
    h2 = jnp.sin(rate * pre2)
    raw = mm(filt_out, h2, TN)
    falling = jnp.exp(-ramp * decay_rate[:, None])
    env = falling + decay_floor
    filt_spec = filter_spectrum(raw * env)
    bias_col = conv_bias[:, None]

    xn1, stat1, gate, pair, projx0, projx, mixed, heads = front(
        jnp.minimum(place, 1).reshape(1), x, xh, in_all, prm, filt_spec, seqs
    )
    mixed_chan = exchange(mixed)
    backward_hop = [(i + 1, i) for i in range(devices - 1)]
    heads = lax.ppermute(heads, "chan", backward_hop)
    conv_chan, mixed_spec = conv_forward(mixed_chan, filt_spec, bias_col, seqs)
    conv = exchange(conv_chan)

    lens = jnp.concatenate([seq_lengths, place.astype(jnp.int32).reshape(1)])
    layer, d_conv, d_res, p0, p0h, early = middle(
        lens, conv, x, gate.reshape(dim, cols), rest, out_w, prm, hid, seqs
    )
    d_conv_chan = exchange(d_conv)
    p0h = lax.ppermute(p0h, "chan", backward_hop)
    early = lax.psum_scatter(early, "chan", scatter_dimension=0, tiled=True)[0]

    swap = [(0, 1), (1, 0)]
    core = place % 2
    partner = [(i, i ^ 1) for i in range(devices)]
    same_core = [[b * devices + c for b in range(groups) for c in range(q, devices, 2)] for q in range(2)]

    def batch_total(values):
        return values + lax.ppermute(values, "batch", swap) if groups == 2 else lax.psum(values, "batch")

    def over_batch(table):
        if groups != 2:
            return lax.psum_scatter(table.astype(f32), "batch", scatter_dimension=1, tiled=True)
        half = dim // 2
        mine = lax.axis_index("batch") * half
        theirs = lax.dynamic_slice_in_dim(table, half - mine, half, 1)
        own = lax.dynamic_slice_in_dim(table, mine, half, 1)
        return own.astype(f32) + lax.ppermute(theirs, "batch", swap).astype(f32)

    def over_chip(table):
        table = table.reshape((devices // 2, 2) + table.shape[1:])
        own = lax.dynamic_index_in_dim(table, core, 1, False)
        theirs = lax.dynamic_index_in_dim(table, 1 - core, 1, False)
        return (own.astype(f32) + lax.ppermute(theirs, "chan", partner).astype(f32)).astype(bf16)

    def over_chips(both):
        rows = both.shape[1]
        both = both.reshape(devices // 2, rows, groups, dim // groups).transpose(2, 0, 1, 3)
        both = lax.all_to_all(
            both.reshape(groups * devices // 2, rows, dim // groups),
            ("batch", "chan"), split_axis=0, concat_axis=0, tiled=True, axis_index_groups=same_core,
        )
        return jnp.sum(both.astype(f32), axis=0)

    g_in0, sums0, acc0 = back_gate(
        p0.reshape(devices, chans, cols), p0h.reshape(devices, chans, LANE), projx0, in_all, prm, xn1, seqs
    )
    d_mixed_chan, d_filter, g_conv_bias = conv_backward(
        d_conv_chan, mixed_chan, mixed_spec, filt_spec, bias_col, seqs
    )
    g_in0 = over_chip(g_in0)
    d_mixed = exchange(d_mixed_chan)

    q = d_filter * env
    g_filt_out = mm(h2, q, NT)
    g_decay = -jnp.sum(d_filter * raw * falling * ramp, axis=1)
    u2 = mm(filt_out, q, NN) * jnp.cos(rate * pre2)
    fu2 = rate * u2
    u1 = mm(filt_mid, fu2, NN) * jnp.cos(rate * pre1)
    fu1 = rate * u1
    shared = [
        mm(feat, fu1, NT).reshape(-1),
        jnp.sum(fu1, axis=1),
        mm(h1, fu2, NT).reshape(-1),
        jnp.sum(fu2, axis=1),
        jnp.sum(u2 * pre2 + u1 * pre1, axis=1),
    ]
    apart_totals = [g_conv_bias[:, 0], g_decay, g_filt_out.reshape(-1)]
    total = batch_total(jnp.concatenate(shared + apart_totals))
    cut = [0]

    def take(*shape):
        n = math.prod(shape)
        part = total[cut[0] : cut[0] + n].reshape(shape)
        cut[0] += n
        return part

    shared = take(sum(v.shape[0] for v in shared)).astype(bf16)
    g_conv_b, g_decay_rate, g_filt_last = take(chans), take(chans), take(ford, chans)
    shared = jnp.pad(shared, (0, -shared.shape[0] % (32 * width))).reshape(-1, width)

    tail, g_in = back(
        d_mixed, pair, heads, projx, in_all, prm, xn1, x, stat1, d_res, acc0, sums0, layer, shared, seqs
    )
    tail = exchange(tail)
    in_grad = over_chips(jnp.concatenate([g_in0, over_chip(g_in)], axis=1))
    early = over_batch(early)
    up_grad, down_grad, out_grad = early[:hid], early[hid : 2 * hid], early[2 * hid :]

    grad_blocks, out_blocks = tail[:, :rows], tail[:, rows : 2 * rows]
    sums = jnp.sum(tail[:, 2 * rows : 2 * rows + SUM_ROWS].astype(f32), axis=0)
    sums2 = jnp.sum(tail[:, 2 * rows + SUM_ROWS : 2 * rows + 2 * SUM_ROWS].astype(f32), axis=0)
    sums = batch_total(jnp.concatenate([sums, sums2], axis=0))
    sums = sums[0::2] + sums[1::2]
    g_gain2, g_shift2, g_out_b, g_down_b = (sums[i, :chans] for i in range(4))
    g_up_b = sums[4, :hid]
    at = SUM_ROWS // 2
    count = (2 + KS) * chans
    pieces = -(-2 * count // width)
    short0 = sums[at, :count].reshape(2 + KS, 1, chans)
    short = sums[at + 1 : at + 1 + pieces].reshape(-1)[: 2 * count].reshape(2 + KS, 2, chans)
    short = jnp.concatenate([short0, short], axis=1)
    g_in_bias, g_short_bias, g_short_weight = short[0], short[1], short[2:]
    g_gain1, g_shift1 = (sums[at + 1 + pieces + i, :chans] for i in range(2))
    total = jnp.sum(tail[:, 2 * rows + 2 * SUM_ROWS :].astype(f32), axis=0).reshape(-1)
    cut[0] = 0
    g_filt_in, g_filt_in_bias = take(EMB, ford), take(ford)
    g_filt_mid, g_filt_mid_bias, g_sine = take(ford, ford), take(ford), take(ford)

    return (
        from_blocks(out_blocks),
        from_blocks(grad_blocks).astype(f32),
        g_gain1,
        g_shift1,
        in_grad.reshape(3, chans, dim // groups).transpose(2, 0, 1),
        g_in_bias,
        g_short_weight,
        g_short_bias,
        g_filt_in,
        g_filt_in_bias,
        g_filt_mid,
        g_filt_mid_bias,
        g_sine,
        g_filt_last,
        g_decay_rate,
        g_conv_b,
        out_grad,
        g_out_b,
        g_gain2,
        g_shift2,
        up_grad,
        g_up_b,
        down_grad,
        g_down_b,
    )


def solution(mesh):
    token = P("batch", "chan", None)
    chan = P("chan")
    rows = P("chan", None)
    two = P(None, "chan")
    three = P(None, None, "chan")
    in_specs = (
        token, P("batch"), chan, chan, three, two, three, two, P(), P(), P(), P(), P(), two, chan, chan,
        rows, chan, chan, chan, rows, chan, rows, chan, token,
    )
    table = P("chan", "batch")
    out_specs = (
        token, token, chan, chan, P("batch", None, "chan"), two, three, two, P(), P(), P(), P(), P(), two,
        chan, chan, table, chan, chan, chan, table, chan, table, chan,
    )
    return jax.shard_map(
        on_device, mesh=mesh, in_specs=in_specs, out_specs=out_specs, check_vma=False
    )
```

time: 739 us -> 491 us (0.66)
  local copies, waits for them, and re-layouts: 192 us -> 33.7 us
  matrix products: 97.4 us -> 31.8 us
  blocking collectives: 34.5 us -> 0 us
  other arithmetic: 36.5 us -> 15.5 us
  Pallas kernels: 114 us -> 129 us
  starting transfers between devices: 62.6 us -> 73.5 us
  waiting for transfers between devices: 174 us -> 183 us
    reduce_scatter x2 -> x1, waiting for transfers between devices: 81.4 us -> 0.01 us  [on_device(): early = lax.psum_scatter(early, 'chan', scatter_dimension=0, tiled=True)[0]]
    dot_general x12 -> x0, matrix products: 64.5 us -> none  [mm16(): return lax.dot_general(a, b, (dims, ((), ())), preferred_element_type=f32)]
    all_to_all x8 -> x6, waiting for transfers between devices: 66.3 us -> 123 us  [exchange(): lax.all_to_all(values, 'chan', split_axis=0, concat_axis=0, tiled=True)]
    convert_element_type x17 -> x0, local copies, waits for them, and re-layouts: 38 us -> none  [the longest x4 11.7 us: on_device(): conv = rows_of(exchange(conv_chan)).astype(f32)]
    concatenate x16 -> x2, local copies, waits for them, and re-layouts: 38.4 us -> 2.38 us  [the longest x1 2.29 us: on_device(): jnp.concatenate([in_bias, short_bias, short_weight.reshape(3 * KS, chans)...]
    all_to_all x1 -> x0, blocking collectives: 25.9 us -> none  [exchange(): lax.all_to_all(values, 'chan', split_axis=0, concat_axis=0, tiled=True)]
    reshape x27 -> x8, local copies, waits for them, and re-layouts: 32.4 us -> 7.8 us  [the longest x1 4.53 us: over_chips(): both.reshape(devices // 2, rows, groups, dim // groups)]
    all_to_all x0 -> x1, waiting for transfers between devices: none -> 23.6 us  [over_chips(): lax.all_to_all(both.reshape(groups * devices // 2, rows, dim // groups),...]
  transfers between devices with their start and end apart: 16 -> 18, of which waited for: 7 -> 10; matrix products, arithmetic and copies ran while one was open for 34% -> 15% of each run, Pallas kernels for 7% -> 18%
where the time goes in v2:
time: 491 us; the launch traced here: 481 us
  waiting for transfers between devices  183 us (37%)
  Pallas kernels  129 us (26%)
  starting transfers between devices  73.5 us (15%)
  local copies, waits for them, and re-layouts  33.7 us (7%)
  matrix products  31.8 us (6%)
  other arithmetic  15.5 us (3%)
  between operations  14.8 us (3%)
    all_to_all x6, waiting for transfers between devices, exchange(): lax.all_to_all(values, 'chan', split_axis=0, concat_axis=0, tiled=True)  123 us
    all_to_all x6, starting transfers between devices, exchange(): lax.all_to_all(values, 'chan', split_axis=0, concat_axis=0, tiled=True)  51.9 us
    pallas_call x1, Pallas kernels, middle(): pl.pallas_call(lambda *refs: middle_body(seqs, group, *refs), cost_estima...  42.3 us
    pallas_call x3, Pallas kernels, whole_call(): pl.pallas_call(body, cost_estimate=takes(us), out_shape=out_shape, in_spe...  34.9 us
    dot_general x8, matrix products, mm(): lax.dot_general(a, b, (dims, ((), ())), precision=highest, preferred_elem...  31.8 us
    all_gather x1, waiting for transfers between devices, on_device(): lax.all_gather(jnp.concatenate([up_weight, down_weight, out_weight], axis...  24.7 us
    pallas_call x1, Pallas kernels, back(): pl.pallas_call(lambda *refs: back_body(seqs, group, *refs), cost_estimate...  24.5 us
    all_to_all x1, waiting for transfers between devices, over_chips(): lax.all_to_all(both.reshape(groups * devices // 2, rows, dim // groups),...  23.6 us
  transfers between devices with their start and end apart: 18, of which 10 were waited for; matrix products, arithmetic and copies ran while one was open for 15% of the time, Pallas kernels for 18%

profile of v2, /device:TPU:0, one launch (start us, length us, event | category | flops | bytes accessed | tf_op | source)
XLA Modules:
  0.0 481.5 jit_solution(873426670499628569)
XLA Ops:
  16.4 7.6 %all-to-all-start = ((bf16[16,192,256]{2,1,0:T(8,128)(2,1)}), bf16[16,192,256]{2,1,0:T(8,128)(2,1)}, u32[]{:S(2)}, u32[]{:S(2)}) async-start(bf16[16,192,256]{2,1,0:T(8,128)(2,1)} %pad_maximum_fusion.1), calls=%async_computation | async-start | bytes 3145728 | tf_op jit(solution)/shard_map/all_to_all | solution.py:992
  25.1 4.5 fusion.3
  29.6 5.5 %fusion.14 = (f32[48,4096]{1,0:T(8,128)}, f32[48,4096]{1,0:T(8,128)}) fusion(f32[48]{0:T(128)S(1)} %copy-done.18, f32[4096]{0:T(1024)S(1)} %copy-done.11, f32[64,48]{0,1:T(8,128)S(1)} %copy-done.12, f32[64,4096]{1,0:T(8,128)S(1)} %fusion.3, f32[64]{0:T(128)S(1)} %copy-done.13), kind=kOutput, calls=%fused_computation.35 | convolution fusion | flops 151846912 | bytes 2650560 | tf_op jit(solution)/shard_map/dot_general | solution.py:979
  35.0 38.4 %all-to-all-done.refs_1_.refs_2_.refs_3_.refs_7_ = bf16[16,192,256]{2,1,0:T(8,128)(2,1)} async-done(((bf16[16,192,256]{2,1,0:T(8,128)(2,1)}), bf16[16,192,256]{2,1,0:T(8,128)(2,1)}, u32[]{:S(2)}, u32[]{:S(2)}) %all-to-all-start) | async-done | bytes 1572896 | tf_op jit(solution)/shard_map/all_to_all | solution.py:992
  74.4 2.5 collective-permute-start
  77.0 5.4 %shard_map.460.refs_5_.refs_1_.refs_3_ = f32[33,48,256]{2,1,0:T(8,128)} custom-call(f32[48,4096]{1,0:T(8,128)} %get-tuple-element.142.filter_ref, f32[33,1,256]{2,1,0:T(1,128)} %constant.63.clone.twist_ref.refs_3_.refs_5_, bf16[2,256,256]{2,1,0:T(8,128)(2,1)} %constant.64.clone.ahead_ref.refs_4_.refs_6_), custom_call_target="tpu_custom_call" | custom-call | flops 8000000000 | bytes 24000000 | tf_op jit(solution)/shard_map/pallas_call | solution.py:336
  82.4 4.1 all-gather.5.cloned.1.call-done
  89.1 15.9 %shard_map.461 = (bf16[768,512]{1,0:T(8,128)(2,1)}, f32[16,512]{1,0:T(8,128)}, f32[16,48,512]{2,1,0:T(8,128)}, f32[16,96,512]{2,1,0:T(8,128)}, bf16[16,48,640]{2...) custom-call(s32[1]{0:T(128)} %bitcast.1.refs_0_, ...), custom_call_target="tpu_custom_call" | custom-call | flops 16000000000 | bytes 48000000 | tf_op jit(solution)/shard_map/pallas_call | solution.py:592
  105.0 13.3 %all-to-all-start.1 = ((bf16[16,96,256]{2,1,0:T(8,128)(2,1)}), bf16[16,96,256]{2,1,0:T(8,128)(2,1)S(1)}, u32[]{:S(2)}, u32[]{:S(2)}) async-start(bf16[16,96,256]{2,1,0:T(8,128)(2,1)} %get-tuple-element.48), calls=%async_computation.1 | async-start | bytes 1572864 | tf_op jit(solution)/shard_map/all_to_all | solution.py:992
  119.0 24.5 %all-to-all-done.1.refs_0_.refs_1_ = bf16[16,96,256]{2,1,0:T(8,128)(2,1)S(1)} async-done(((bf16[16,96,256]{2,1,0:T(8,128)(2,1)}), bf16[16,96,256]{2,1,0:T(8,128)(2,1)S(1)}, u32[]{:S(2)}, u32[]{:S(2)}) %all-to-all-start.1) | async-done | bytes 786464 | tf_op jit(solution)/shard_map/all_to_all | solution.py:992
  144.4 13.2 %shard_map.462 = (bf16[16,96,256]{2,1,0:T(8,128)(2,1)}, f32[33,96,256]{2,1,0:T(8,128)}) custom-call(bf16[16,96,256]{2,1,0:T(8,128)(2,1)} %copy-done.7, f32[33,48,256]{2,1,0:T(8,128)} %shard_map.460.refs_5_.refs_1_.refs_3_, f32[48,1]{1,0:T(8,128)} %copy.74.refs_2_.refs_4_, f32[33,1,256]{2,1,0:T(1,128)} %constant.63.clone.twist_ref.refs_3_.refs_5_, ...), custom_call_target="tpu_custom_call" | custom-call | flops 14000000000 | bytes 42000000 | tf_op jit(solution)/shard_map/pallas_call | solution.py:336
  157.6 15.0 %all-to-all-start.2 = ((bf16[16,96,256]{2,1,0:T(8,128)(2,1)}), bf16[16,96,256]{2,1,0:T(8,128)(2,1)S(1)}, u32[]{:S(2)}, u32[]{:S(2)}) async-start(bf16[16,96,256]{2,1,0:T(8,128)(2,1)} %get-tuple-element.49), calls=%async_computation.2 | async-start | bytes 1572864 | tf_op jit(solution)/shard_map/all_to_all | solution.py:992
  173.3 24.7 %all-gather.7.cloned.1.call-done = bf16[6912,768]{1,0:T(8,128)(2,1)} async-done(((bf16[432,768]{1,0:T(8,128)(2,1)}), bf16[6912,768]{1,0:T(8,128)(2,1)}) %all-gather.7.cloned.1.call-update) | async-done | bytes 10616848 | tf_op jit(solution)/shard_map/all_gather | solution.py:1062
  201.2 42.3 %shard_map.463 = (bf16[16,112,256]{2,1,0:T(8,128)(2,1)}, bf16[16,96,256]{2,1,0:T(8,128)(2,1)}, f32[768,512]{1,0:T(8,128)}, f32[768,512]{1,0:T(8,128)}, f32[768,1...) custom-call(s32[3]{0:T(128)} %pad_add_fusion.refs_0_, bf16[16,96,256]{2,1,0:T(8,128)(2,1)} %copy-done.9, ...), custom_call_target="tpu_custom_call" | custom-call | flops 40000000000 | bytes 120000000 | tf_op jit(solution)/shard_map/pallas_call | solution.py:770
  243.6 4.0 all-to-all-start.3
  250.2 16.2 %all-to-all-done.3.refs_0_ = bf16[16,96,256]{2,1,0:T(8,128)(2,1)S(1)} async-done(((bf16[16,96,256]{2,1,0:T(8,128)(2,1)}), bf16[16,96,256]{2,1,0:T(8,128)(2,1)S(1)}, u32[]{:S(2)}, u32[]{:S(2)}) %all-to-all-start.3) | async-done | bytes 786464 | tf_op jit(solution)/shard_map/all_to_all | solution.py:992
  267.2 16.3 %shard_map.464 = (bf16[16,112,256]{2,1,0:T(8,128)(2,1)}, f32[48,4096]{1,0:T(8,128)}, f32[48,1]{1,0:T(8,128)}) custom-call(bf16[16,96,256]{2,1,0:T(8,128)(2,1)} %copy-done.8, bf16[16,96,256]{2,1,0:T(8,128)(2,1)} %copy-done.7, f32[33,96,256]{2,1,0:T(8,128)} %get-tuple-element.52.refs_2_, f32[33,48,256]{2,1,0:T(8,128)} %shard_map.460.refs_5_.refs_1_.refs_3_, ...), custom_call_target="tpu_custom_call" | custom-call | flops 16000000000 | bytes 48000000 | tf_op jit(solution)/shard_map/pallas_call | solution.py:336
  283.5 5.9 %fusion.2 = f32[64,4096]{1,0:T(8,128)S(1)} fusion(f32[64,48]{0,1:T(8,128)S(1)} %copy-done.12, f32[64,4096]{1,0:T(8,128)S(1)} %fusion.3, f32[48,4096]{1,0:T(8,128)} %get-tuple-element.66, f32[64]{0:T(128)S(1)} %copy-done.13, f32[48]{0:T(128)S(1)} %copy-done.18, f32[4096]{0:T(1024)S(1)} %copy-done.11), kind=kOutput, calls=%fused_computation.6 | convolution fusion | flops 152109056 | bytes 2912704 | tf_op jit(solution)/shard_map/dot_general | solution.py:979
  289.4 4.9 %add_reduce_fusion = (f32[64]{0:T(128)S(1)}, f32[64]{0:T(128)S(1)}, f32[64]{0:T(128)S(1)}, f32[64,4096]{1,0:T(8,128)S(1)}) fusion(f32[64,4096]{1,0:T(8,128)S(1)} %fusion, f32[64,4096]{1,0:T(8,128)S(1)} %fusion.2, f32[64,4096]{1,0:T(8,128)S(1)} %fusion.3, f32[64]{0:T(128)S(1)} %copy-done.13, f32[64,64]{1,0:T(8,128)S(1)} %copy-done), kind=kOutput, calls=%fused_computation.18 | convolution fusion | flops 204209984 | bytes 4211712 | tf_op jit(solution)/shard_map/dot_general | solution.py:979
  295.4 4.5 fusion.8
  300.0 5.9 %all-to-all-start.4 = ((bf16[16,112,256]{2,1,0:T(8,128)(2,1)}), bf16[16,112,256]{2,1,0:T(8,128)(2,1)}, u32[]{:S(2)}, u32[]{:S(2)}) async-start(bf16[16,112,256]{2,1,0:T(8,128)(2,1)} %get-tuple-element.53), calls=%async_computation.4 | async-start | bytes 1835008 | tf_op jit(solution)/shard_map/all_to_all | solution.py:992
  306.3 4.5 fusion.9
  312.7 11.7 %shard_map.465 = (bf16[16,48,768]{2,1,0:T(8,128)(2,1)}, f32[16,8,256]{2,1,0:T(8,128)}, f32[768,512]{1,0:T(8,128)}) custom-call(f32[16,48,512]{2,1,0:T(8,128)} %bitcast.154, f32[16,48,128]{2,1,0:T(8,128)} %bitcast.25.refs_1_, bf16[16,48,640]{2,1,0:T(8,128)(2,1)} %get-tuple-element.62.refs_2_, bf16[16,176,768]{2,1,0:T(8,128)(2,1)} %bitcast.144, ...), custom_call_target="tpu_custom_call" | custom-call | flops 12000000000 | bytes 36000000 | tf_op jit(solution)/shard_map/pallas_call | solution.py:848
  325.0 14.5 %all-to-all-done.4.refs_0_ = bf16[16,112,256]{2,1,0:T(8,128)(2,1)} async-done(((bf16[16,112,256]{2,1,0:T(8,128)(2,1)}), bf16[16,112,256]{2,1,0:T(8,128)(2,1)}, u32[]{:S(2)}, u32[]{:S(2)}) %all-to-all-start.4) | async-done | bytes 917536 | tf_op jit(solution)/shard_map/all_to_all | solution.py:992
  339.5 24.5 %shard_map.466 = (bf16[16,256,256]{2,1,0:T(8,128)(2,1)}, bf16[16,96,768]{2,1,0:T(8,128)(2,1)}) custom-call(bf16[16,112,256]{2,1,0:T(8,128)(2,1)} %all-to-all-done.4.refs_0_, f32[16,96,512]{2,1,0:T(8,128)} %get-tuple-element.54.refs_1_, bf16[16,96,128]{2,1,0:T(8,128)(2,1)} %collective-permute-done.1.refs_2_, bf16[16,96,640]{2,1,0:T(8,128)(2,1)} %get-tuple-element.56.refs_3_, ...), custom_call_target="tpu_custom_call" | custom-call | flops 20000000000 | bytes 60000000 | tf_op jit(solution)/shard_map/pallas_call | solution.py:950
  364.0 6.1 %all-to-all-start.5 = ((bf16[16,256,256]{2,1,0:T(8,128)(2,1)}), bf16[16,256,256]{2,1,0:T(8,128)(2,1)S(1)}, u32[]{:S(2)}, u32[]{:S(2)}) async-start(bf16[16,256,256]{2,1,0:T(8,128)(2,1)} %get-tuple-element.68), calls=%async_computation.5 | async-start | bytes 4194304 | tf_op jit(solution)/shard_map/all_to_all | solution.py:992
  380.8 4.5 reshape.184
  385.4 2.9 copy.81
  388.3 29.2 %all-to-all-done.5 = bf16[16,256,256]{2,1,0:T(8,128)(2,1)S(1)} async-done(((bf16[16,256,256]{2,1,0:T(8,128)(2,1)}), bf16[16,256,256]{2,1,0:T(8,128)(2,1)S(1)}, u32[]{:S(2)}, u32[]{:S(2)}) %all-to-all-start.5) | async-done | bytes 2097184 | tf_op jit(solution)/shard_map/all_to_all | solution.py:992
  417.5 12.1 %all-to-all-start.6 = ((bf16[16,144,384]{2,1,0:T(8,128)(2,1)}), bf16[16,144,384]{2,1,0:T(8,128)(2,1)}, u32[]{:S(2)}, u32[]{:S(2)}) async-start(bf16[16,144,384]{2,1,0:T(8,128)(2,1)} %bitcast.116), calls=%async_computation.6 | async-start | bytes 3538944 | tf_op jit(solution)/shard_map/all_to_all | solution.py:1122
  437.5 5.5 %collective-permute-done.4 = f32[32,256]{1,0:T(8,128)S(1)} collective-permute-done((f32[32,256]{1,0:T(8,128)S(1)}, f32[32,256]{1,0:T(8,128)S(1)}, u32[]{:S(2)}, u32[]{:S(2)}) %collective-permute-start.4) | collective-permute-done | bytes 32800 | tf_op jit(solution)/shard_map/ppermute | solution.py:1102
  446.9 23.6 %all-to-all-done.6 = bf16[16,144,384]{2,1,0:T(8,128)(2,1)} async-done(((bf16[16,144,384]{2,1,0:T(8,128)(2,1)}), bf16[16,144,384]{2,1,0:T(8,128)(2,1)}, u32[]{:S(2)}, u32[]{:S(2)}) %all-to-all-start.6) | async-done | bytes 1769504 | tf_op jit(solution)/shard_map/all_to_all | solution.py:1122
  (135 shorter events, 53.2 us)
Async XLA Ops:
  7.2 17.8 %copy-start = (f32[64,64]{1,0:T(8,128)S(1)}, f32[64,64]{1,0:T(8,128)}, u32[]{:S(2)}) copy-start(f32[64,64]{1,0:T(8,128)} %param.39) | copy-start | bytes 49156
  7.2 7.7 %copy-start.5 = (bf16[2,48,4096]{2,1,0:T(8,128)(2,1)S(1)}, bf16[2,48,4096]{2,1,0:T(8,128)(2,1)}, u32[]{:S(2)}) copy-start(bf16[2,48,4096]{2,1,0:T(8,128)(2,1)} %param.29) | copy-start | bytes 2359300
  7.2 79.2 %all-gather.5.cloned.1.call-start = ((), (), s32[]{:S(2)}) async-start(), calls=%async_computation.9 | async-start | bytes 4595712 | tf_op jit(solution)/shard_map/all_gather | solution.py:1058
  12.8 185.2 %all-gather.7.cloned.1.call-start = ((), (), s32[]{:S(2)}) async-start(), calls=%async_computation.10 | async-start | bytes 11280384 | tf_op jit(solution)/shard_map/all_gather | solution.py:1062
  16.3 7.6 %copy-start.3 = (f32[33,4096]{1,0:T(8,128)S(1)}, f32[33,4096]{1,0:T(8,128)}, u32[]{:S(2)}) copy-start(f32[33,4096]{1,0:T(8,128)} %constant.62.clone) | copy-start | bytes 1622020
  16.3 7.6 %copy-start.15 = (f32[33,64]{1,0:T(8,128)S(1)}, f32[33,64]{1,0:T(8,128)}, u32[]{:S(2)}) copy-start(f32[33,64]{1,0:T(8,128)} %param.37) | copy-start | bytes 25348
  16.3 7.6 %copy-start.19 = (f32[64]{0:T(128)S(1)}, f32[64]{0:T(128)}, u32[]{:S(2)}) copy-start(f32[64]{0:T(128)} %param.38) | copy-start | bytes 772
  16.3 8.7 %copy-start.13 = (f32[64]{0:T(128)S(1)}, f32[64]{0:T(128)}, u32[]{:S(2)}) copy-start(f32[64]{0:T(128)} %param.41) | copy-start | bytes 772
  16.3 8.7 %copy-start.21 = (f32[64]{0:T(128)S(1)}, f32[64]{0:T(128)}, u32[]{:S(2)}) copy-start(f32[64]{0:T(128)} %param.40) | copy-start | bytes 772
  16.4 57.1 %all-to-all-start = ((bf16[16,192,256]{2,1,0:T(8,128)(2,1)}), bf16[16,192,256]{2,1,0:T(8,128)(2,1)}, u32[]{:S(2)}, u32[]{:S(2)}) async-start(bf16[16,192,256]{2,1,0:T(8,128)(2,1)} %pad_maximum_fusion.1), calls=%async_computation | async-start | bytes 3145728 | tf_op jit(solution)/shard_map/all_to_all | solution.py:992
  74.4 13.9 %collective-permute-start = (bf16[16,96,128]{2,1,0:T(8,128)(2,1)S(1)}, bf16[16,96,128]{2,1,0:T(8,128)(2,1)S(1)}, u32[]{:S(2)}, u32[]{:S(2)}) collective-permute-start(bf16[16,96,128]{2,1,0:T(8,128)(2,1)S(1)} %slice.151), channel_id=1, source_target_pairs={{0,1},{1,2},{2,3},{3,4},{4,5},{5,6},{6,7},{7,8},{8,9},{9,10},{10,1... | collective-permute-start | bytes 1179656 | tf_op jit(solution)/shard_map/ppermute | solution.py:1061
  89.1 29.2 %copy-start.20 = (f32[48]{0:T(128)S(1)}, f32[48]{0:T(128)}, u32[]{:S(2)}) copy-start(f32[48]{0:T(128)} %param.44) | copy-start | bytes 580
  105.0 38.5 %all-to-all-start.1 = ((bf16[16,96,256]{2,1,0:T(8,128)(2,1)}), bf16[16,96,256]{2,1,0:T(8,128)(2,1)S(1)}, u32[]{:S(2)}, u32[]{:S(2)}) async-start(bf16[16,96,256]{2,1,0:T(8,128)(2,1)} %get-tuple-element.48), calls=%async_computation.1 | async-start | bytes 1572864 | tf_op jit(solution)/shard_map/all_to_all | solution.py:992
  119.0 53.7 %copy-start.23 = (s32[2]{0:T(128)S(1)}, s32[2]{0:T(128)}, u32[]{:S(2)}) copy-start(s32[2]{0:T(128)} %param.30) | copy-start | bytes 28
  157.6 42.8 %all-to-all-start.2 = ((bf16[16,96,256]{2,1,0:T(8,128)(2,1)}), bf16[16,96,256]{2,1,0:T(8,128)(2,1)S(1)}, u32[]{:S(2)}, u32[]{:S(2)}) async-start(bf16[16,96,256]{2,1,0:T(8,128)(2,1)} %get-tuple-element.49), calls=%async_computation.2 | async-start | bytes 1572864 | tf_op jit(solution)/shard_map/all_to_all | solution.py:992
  172.6 271.2 %reduce-scatter.2.cloned.1.call-start = ((), (), s32[]{:S(2)}) async-start(), calls=%async_computation.8 | async-start | bytes 11280384 | tf_op jit(solution)/shard_map/reduce_scatter | solution.py:1094
  243.6 22.8 %all-to-all-start.3 = ((bf16[16,96,256]{2,1,0:T(8,128)(2,1)}), bf16[16,96,256]{2,1,0:T(8,128)(2,1)S(1)}, u32[]{:S(2)}, u32[]{:S(2)}) async-start(bf16[16,96,256]{2,1,0:T(8,128)(2,1)} %get-tuple-element.51), calls=%async_computation.3 | async-start | bytes 1572864 | tf_op jit(solution)/shard_map/all_to_all | solution.py:992
  247.6 77.4 %collective-permute-start.1 = (bf16[16,96,128]{2,1,0:T(8,128)(2,1)}, bf16[16,96,128]{2,1,0:T(8,128)(2,1)}, u32[]{:S(2)}, u32[]{:S(2)}) collective-permute-start(bf16[16,96,128]{2,1,0:T(8,128)(2,1)} %get-tuple-element.55), channel_id=1, source_target_pairs={{1,0},{2,1},{3,2},{4,3},{5,4},{6,5},{7,6},{8,7},{9,8},{10,9},{11,1... | collective-permute-start | bytes 1179656 | tf_op jit(solution)/shard_map/ppermute | solution.py:1084
  248.9 63.8 %collective-permute-start.2 = (f32[768,128]{1,0:T(8,128)}, f32[768,128]{1,0:T(8,128)}, u32[]{:S(2)}, u32[]{:S(2)}) collective-permute-start(f32[768,128]{1,0:T(8,128)} %get-tuple-element.61), channel_id=1, source_target_pairs={{1,0},{2,1},{3,2},{4,3},{5,4},{6,5},{7,6},{8,7},{9,8},{10,9},{11,1... | collective-permute-start | bytes 1179656 | tf_op jit(solution)/shard_map/ppermute | solution.py:1093
  295.4 10.5 %copy-start.16 = (f32[4096]{0:T(1024)S(1)}, f32[4096]{0:T(1024)}, u32[]{:S(2)}) copy-start(f32[4096]{0:T(1024)} %constant.71) | copy-start | bytes 49156
  299.9 6.0 %copy-start.1 = (f32[48,4096]{1,0:T(8,128)S(1)}, f32[48,4096]{1,0:T(8,128)}, u32[]{:S(2)}) copy-start(f32[48,4096]{1,0:T(8,128)} %get-tuple-element.66) | copy-start | bytes 2359300
  299.9 6.0 %copy-start.2 = (f32[48,4096]{1,0:T(8,128)S(1)}, f32[48,4096]{1,0:T(8,128)}, u32[]{:S(2)}) copy-start(f32[48,4096]{1,0:T(8,128)} %get-tuple-element.143) | copy-start | bytes 2359300
  300.0 39.5 %all-to-all-start.4 = ((bf16[16,112,256]{2,1,0:T(8,128)(2,1)}), bf16[16,112,256]{2,1,0:T(8,128)(2,1)}, u32[]{:S(2)}, u32[]{:S(2)}) async-start(bf16[16,112,256]{2,1,0:T(8,128)(2,1)} %get-tuple-element.53), calls=%async_computation.4 | async-start | bytes 1835008 | tf_op jit(solution)/shard_map/all_to_all | solution.py:992
  311.1 13.2 %collective-permute-start.3 = (f32[9568]{0:T(1024)S(1)}, f32[9568]{0:T(1024)S(1)}, u32[]{:S(2)}, u32[]{:S(2)}) collective-permute-start(f32[9568]{0:T(1024)S(1)} %concatenate.32), channel_id=1, source_target_pairs={{0,16},{16,0},{1,17},{17,1},{2,18},{18,2},{3,19},{19,3},{4,20},{20... | collective-permute-start | bytes 114824 | tf_op jit(solution)/shard_map/ppermute | solution.py:1102
  312.7 11.7 %copy-start.17 = (pred[8192]{0:T(1024)(128)(4,1)S(1)}, pred[8192]{0:T(1024)(128)(4,1)}, u32[]{:S(2)}) copy-start(pred[8192]{0:T(1024)(128)(4,1)} %constant.52.clone.1) | copy-start | bytes 24580
  364.0 53.5 %all-to-all-start.5 = ((bf16[16,256,256]{2,1,0:T(8,128)(2,1)}), bf16[16,256,256]{2,1,0:T(8,128)(2,1)S(1)}, u32[]{:S(2)}, u32[]{:S(2)}) async-start(bf16[16,256,256]{2,1,0:T(8,128)(2,1)} %get-tuple-element.68), calls=%async_computation.5 | async-start | bytes 4194304 | tf_op jit(solution)/shard_map/all_to_all | solution.py:992
  371.5 6.1 %collective-permute-start.6 = (bf16[8,96,768]{2,1,0:T(8,128)(2,1)S(1)}, bf16[8,96,768]{2,1,0:T(8,128)(2,1)}, u32[]{:S(2)}, u32[]{:S(2)}) collective-permute-start(bf16[8,96,768]{2,1,0:T(8,128)(2,1)S(1)} %dynamic-slice_bitcast_fusion), channel_id=1, source_target_pairs={{0,1},{1,0},{2,3},{3,2},{4,5},{5,4},{6,7},{7,6},{8,9},{9,8},{10,11... | collective-permute-start | bytes 3538952 | tf_op jit(solution)/shard_map/ppermute | solution.py:1117
  373.9 2.3 collective-permute-start.5
  417.5 53.0 %all-to-all-start.6 = ((bf16[16,144,384]{2,1,0:T(8,128)(2,1)}), bf16[16,144,384]{2,1,0:T(8,128)(2,1)}, u32[]{:S(2)}, u32[]{:S(2)}) async-start(bf16[16,144,384]{2,1,0:T(8,128)(2,1)} %bitcast.116), calls=%async_computation.6 | async-start | bytes 3538944 | tf_op jit(solution)/shard_map/all_to_all | solution.py:1122
  431.0 11.9 %collective-permute-start.4 = (f32[32,256]{1,0:T(8,128)S(1)}, f32[32,256]{1,0:T(8,128)S(1)}, u32[]{:S(2)}, u32[]{:S(2)}) collective-permute-start(f32[32,256]{1,0:T(8,128)S(1)} %pad_maximum_fusion.3), channel_id=1, source_target_pairs={{0,16},{16,0},{1,17},{17,1},{2,18},{18,2},{3,19},{19,3},{4,20},{20... | collective-permute-start | bytes 98312 | tf_op jit(solution)/shard_map/ppermute | solution.py:1102
  443.8 29.2 %copy-start.10 = (bf16[1,432,768]{2,1,0:T(8,128)(2,1)S(1)}, bf16[1,432,768]{2,1,0:T(8,128)(2,1)}, u32[]{:S(2)}) copy-start(bf16[1,432,768]{2,1,0:T(8,128)(2,1)} %reduce-scatter.2.cloned.1.call-done) | copy-start | bytes 1990660
  444.9 28.1 %collective-permute-start.7 = (bf16[432,384]{1,0:T(8,128)(2,1)S(1)}, bf16[432,384]{1,0:T(8,128)(2,1)S(1)}, u32[]{:S(2)}, u32[]{:S(2)}) collective-permute-start(bf16[432,384]{1,0:T(8,128)(2,1)S(1)} %dynamic-slice_bitcast_fusion.2), channel_id=1, source_target_pairs={{0,16},{16,0},{1,17},{17,1},{2,18},{18,2},{3,19},{19,3},{4,20},{20... | collective-permute-start | bytes 995336 | tf_op jit(solution)/shard_map/ppermute | solution.py:1111
  (10 other events, 32.3 us)
Sparse Core Ops, SparseCore 0:
  12.9 73.5 all-gather.4
  88.7 109.1 all-gather.6
  243.7 151.4 reduce-scatter.1

commit v3 on v2

--- a/solution.py
+++ b/solution.py
@@ -361,7 +361,7 @@
     blocks, rows, width = mixed.shape
     n = len(REPS)
     return whole_call(
-        14,
+        100,
         lambda *refs: conv_forward_body(seqs, *refs),
         (jax.ShapeDtypeStruct(mixed.shape, bf16), jax.ShapeDtypeStruct((n, rows, 2 * LANE), f32)),
         [pltpu.VMEM((COARSE, rows, LANE), f32), pltpu.VMEM((n, rows, 2 * LANE), f32)],
@@ -379,7 +379,7 @@
     chans = rows // seqs
     n = len(REPS)
     return whole_call(
-        16,
+        100,
         lambda *refs: conv_backward_body(seqs, *refs),
         (
             jax.ShapeDtypeStruct((blocks, rows + HEAD_ROWS, width), bf16),
@@ -476,14 +476,23 @@
     return mean, lax.rsqrt(var + epsilon)
 
 
-def front_body(seqs, group, flag_ref, x_ref, xh_ref, w_ref, prm_ref, after_ref, xn_ref, stat_ref, gate_ref, pair_ref, projx0_ref, projx_ref, mixed_ref, heads_ref, xs, xb):
+def front_body(
+    seqs, table_ref, x_ref, xh_ref, own_ref, other_ref, own_small, other_small, after_ref,
+    prm_ref, xn_ref, stat_ref, gate_ref, pair_ref, projx0_ref, projx_ref, mixed_ref, heads_ref, xs, xb,
+):
     devices, _, width = x_ref.shape
     dim, cols = xn_ref.shape
     chans = dim // devices
+    turns = devices // 2
     step = pl.program_id(0)
 
     @pl.when(step == 0)
     def _():
+        for turn in range(turns):
+            for ref, (device, _) in zip((own_small, other_small), slots(table_ref, turns, turn)):
+                small = jnp.concatenate([ref[turn].astype(f32), jnp.zeros((LANE - PRM, LANE), f32)], axis=0)
+                prm_ref[pl.ds(pl.multiple_of(device * chans, 8), chans), :] = small.T[:chans, :PRM]
+
         def gather(d, carry):
             at = pl.ds(pl.multiple_of(d * chans, 8), chans)
             row = side_by_side(x_ref[d].astype(f32), seqs)
@@ -509,10 +518,10 @@
         stat_ref[0:8, :] = jnp.broadcast_to(mean[:, :cols], (8, cols))
         stat_ref[8:16, :] = jnp.broadcast_to(inverse[:, :cols], (8, cols))
 
-    keep = (flag_ref[0] > 0).astype(f32)
-    for g in range(group):
-        prm = prm_ref[pl.ds(pl.multiple_of((step * group + g) * chans, 8), chans), :]
-        proj = mm16(w_ref[g, PRM:, :], xb[...], NN)
+    keep = (table_ref[turns + 1] > 0).astype(f32)
+    for w_ref, (device, g) in zip((own_ref, other_ref), slots(table_ref, turns, step)):
+        prm = prm_ref[pl.ds(pl.multiple_of(device * chans, 8), chans), :]
+        proj = mm16(w_ref[0, PRM:, :], xb[...], NN)
         ys = []
         px = []
         for i in range(3):
@@ -545,41 +554,53 @@
     return jnp.where(lanes_of((values.shape[0], LANE)) < LANE // 2, values[:, :LANE], second)
 
 
-def params(kind):
-    return pltpu.CompilerParams(vmem_limit_bytes=vmem_limit, dimension_semantics=("arbitrary",))
-
-
 def whole(a):
-    return pl.BlockSpec(a.shape, lambda i: (0,) * len(a.shape), pipeline_mode=pl.Buffered(1))
-
-
-def half(a, which):
-    return pl.BlockSpec(
-        (a.shape[0], a.shape[1] // 2, a.shape[2]), lambda i: (0, which, 0), pipeline_mode=pl.Buffered(1)
-    )
+    return pl.BlockSpec(a.shape, lambda i, t: (0,) * len(a.shape), pipeline_mode=pl.Buffered(1))
 
 
 def untouched():
     return pl.BlockSpec(memory_space=pl.ANY)
 
 
-def by_group(a, group):
-    return pl.BlockSpec((group,) + a.shape[1:], lambda i: (i,) + (0,) * (len(a.shape) - 1))
-
-
-def smem():
-    return pl.BlockSpec(memory_space=pltpu.SMEM)
-
-
-def front(flag, x_cot, xh, weights, prm, after, seqs):
-    devices, rows, width = x_cot.shape
-    rows = rows // 2
+def by_chip(a):
+    return pl.BlockSpec((2,) + a.shape[1:], lambda i, t: (t[i],) + (0,) * (len(a.shape) - 1))
+
+
+def by_turn(a, rows=None):
+    return pl.BlockSpec((1, a.shape[1] if rows is None else rows, a.shape[2]), lambda i, t: (i, 0, 0))
+
+
+def chip_call(us, body, table, turns, args, in_specs, out, out_specs, scratch):
+    return pl.pallas_call(
+        body,
+        cost_estimate=takes(us),
+        out_shape=out,
+        grid_spec=pltpu.PrefetchScalarGridSpec(
+            num_scalar_prefetch=1,
+            grid=(turns,),
+            in_specs=in_specs,
+            out_specs=out_specs,
+            scratch_shapes=scratch,
+        ),
+        compiler_params=pltpu.CompilerParams(vmem_limit_bytes=vmem_limit, dimension_semantics=("arbitrary",)),
+    )(table, *args)
+
+
+def slots(table_ref, turns, step):
+    core = table_ref[turns]
+    chip = table_ref[step]
+    return ((2 * chip + core, core), (2 * chip + 1 - core, 1 - core))
+
+
+def front(table, x, xh, own, other, before, seqs):
+    devices, rows, width = x.shape
     chans = rows // seqs
     dim = devices * chans
     cols = seqs * width
-    group = 2
+    turns = devices // 2
     sd = jax.ShapeDtypeStruct
     out = (
+        sd((dim, PRM), f32),
         sd((dim, cols), bf16),
         sd((16, cols), f32),
         sd((devices, chans, cols), f32),
@@ -589,33 +610,44 @@
         sd((devices, rows, width), bf16),
         sd((devices, 2 * chans, LANE), bf16),
     )
-    return pl.pallas_call(
-        lambda *refs: front_body(seqs, group, *refs),
-        cost_estimate=takes(16),
-        grid=(devices // group,),
-        out_shape=out,
-        in_specs=[smem(), half(x_cot, 0), whole(xh), by_group(weights, group), whole(prm), untouched()],
-        out_specs=(whole(out[0]), whole(out[1])) + tuple(by_group(o, group) for o in out[2:]),
-        scratch_shapes=[pltpu.VMEM((dim, cols + LANE), f32), pltpu.VMEM((dim, cols + LANE), bf16)],
-        compiler_params=params(0),
-    )(flag, x_cot, xh, weights, prm, after)
-
-
-def middle_body(
-    seqs, group, lens_ref, conv_ref, x_ref, cot_ref, gate_ref, w_ref, out_w_ref, prm_ref,
-    layer_ref, d_conv_ref, d_res_ref, p0_ref, p0h_ref, g_ref,
-    cs, res, ds, xb, db, gb, acc_out, acc_in, folds, up_folds, stats,
-):
+    small = pl.BlockSpec((turns, PRM, LANE), lambda i, t: (0, 0, 0), pipeline_mode=pl.Buffered(1))
+    return chip_call(
+        100,
+        lambda *refs: front_body(seqs, *refs),
+        table,
+        turns,
+        (x, xh, own, other, own, other, before),
+        [whole(x), whole(xh), by_turn(own), by_turn(other), small, small, untouched()],
+        out,
+        tuple(whole(o) for o in out[:3]) + tuple(by_chip(o) for o in out[3:]),
+        [pltpu.VMEM((dim, cols + LANE), f32), pltpu.VMEM((dim, cols + LANE), bf16)],
+    )
+
+
+def middle_body(seqs, pieces, segments, table_ref, conv_ref, x_ref, cot_ref, gate_ref, prm_ref, *refs):
+    weights = []
+    for _ in range(pieces):
+        weights.append([[refs[2 * (segments * core + n) : 2 * (segments * core + n) + 2] for n in range(segments)] for core in range(2)])
+        refs = refs[4 * segments :]
+    layer_ref, d_conv_ref, d_res_ref, p0_ref, p0h_ref = refs[:5]
+    grads, refs = [refs[5 + 2 * p : 7 + 2 * p] for p in range(pieces)], refs[5 + 2 * pieces :]
+    cs, res, ds, xb, db, gb, acc_out, acc_in, folds, up_folds, stats, out_w32 = refs[:12]
+    out_w_refs = refs[12:]
     devices, _, width = x_ref.shape
     dim, cols = d_res_ref.shape
     chans = dim // devices
-    hid = w_ref.shape[1] // 2
+    hid = weights[0][0][0][0].shape[1] // 2
+    turns = devices // 2
+    part = dim // pieces
+    group = table_ref[turns + 2 + seqs] if pieces == 2 else 0
+    columns = [pl.ds(pl.multiple_of((group if p == 0 else 1 - group) * part, LANE), part) for p in range(pieces)]
     step = pl.program_id(0)
     last = pl.num_programs(0) - 1
     lane = lanes_of((1, cols))
     live = jnp.zeros((1, cols), f32)
     for s in range(seqs):
-        inside = (lane >= s * width) & (lane < (s + 1) * width) & (lens_ref[seqs] * width + lane - s * width < lens_ref[s])
+        position = table_ref[turns + 1] * width + lane - s * width
+        inside = (lane >= s * width) & (lane < (s + 1) * width) & (position < table_ref[turns + 2 + s])
         live = jnp.where(inside, 1.0, live)
 
     def device_rows(d):
@@ -631,6 +663,21 @@
             return carry
 
         lax.fori_loop(0, devices, gather, 0)
+        for piece, out_w_ref in zip(weights, out_w_refs):
+            for core, parts in enumerate(piece):
+                turn = 0
+                for _, out_rows in parts:
+                    for n in range(out_rows.shape[0]):
+                        device, _ = slots(table_ref, turns, turn)[core]
+                        out_w32[device_rows(device), :] = out_rows[n].astype(f32)
+                        turn += 1
+
+            def narrow(i, carry):
+                at = chunk_rows(i)
+                out_w_ref[at, :] = out_w32[at, :].astype(bf16)
+                return carry
+
+            lax.fori_loop(0, dim // CHUNK, narrow, 0)
 
         def gated(i, carry):
             at = chunk_rows(i)
@@ -642,9 +689,8 @@
             return carry
 
         lax.fori_loop(0, dim // CHUNK, gated, 0)
-        for n in range(dim // 256):
-            at = slice(n * 256, (n + 1) * 256)
-            acc_out[at, :] = mm16(out_w_ref[:, at], gb[...], TN)
+        for at, out_w_ref in zip(columns, out_w_refs):
+            acc_out[at, :] = mm16(out_w_ref[...], gb[...], TN)
 
         def add(i, carry):
             at = chunk_rows(i)
@@ -666,15 +712,21 @@
         stats[0:8, :] = jnp.broadcast_to(mean, (8, cols))
         stats[8:16, :] = jnp.broadcast_to(inverse, (8, cols))
 
+    pair = slots(table_ref, turns, step)
     up_b = []
-    for g in range(group):
-        prm = prm_ref[device_rows(step * group + g), :]
+    for device, _ in pair:
+        prm = prm_ref[device_rows(device), :]
         up_b += [prm[:, 21 + m : 22 + m] for m in range(hid // chans)]
     up_b = jnp.concatenate(up_b, axis=0)
-    up = w_ref[:, :hid, :].reshape(group * hid, dim)
-    down = w_ref[:, hid:, :].reshape(group * hid, dim)
-    u = mm16(up, xb[...], NN) + up_b
-    d_act = mm16(down, db[...], NN)
+
+    def now(parts, rows):
+        blocks = [ref[0, rows, :] for ref, _ in parts]
+        return blocks[0] if len(blocks) == 1 else jnp.where(step < turns // 2, blocks[0], blocks[1])
+
+    ups = [jnp.concatenate([now(parts, slice(0, hid)) for parts in piece], axis=0) for piece in weights]
+    downs = [jnp.concatenate([now(parts, slice(hid, 2 * hid)) for parts in piece], axis=0) for piece in weights]
+    u = sum(mm16(up, xb[at, :], NN) for up, at in zip(ups, columns)) + up_b
+    d_act = sum(mm16(down, db[at, :], NN) for down, at in zip(downs, columns))
     a, k = 0.044715, math.sqrt(2.0 / math.pi)
     sq = u * u
     t = jnp.tanh(u * (k + (k * a) * sq))
@@ -682,12 +734,18 @@
     act = (u * half).astype(bf16)
     d_u = d_act * (half + 0.5 * u * (1.0 - t * t) * (k + (3.0 * k * a) * sq))
     d_low = d_u.astype(bf16)
-    up_folds[pl.ds(pl.multiple_of(step * group * hid, 8), group * hid), :] = folded(d_u)
-    acc_out[...] += mm16(down, act, TN)
-    acc_in[...] += mm16(up, d_low, TN)
-    mine = pl.ds(step * group, group)
-    g_ref[mine, :hid, :] = mm16(d_low, xb[...], NT).astype(bf16).reshape(group, hid, dim)
-    g_ref[mine, hid : 2 * hid, :] = mm16(act, db[...], NT).astype(bf16).reshape(group, hid, dim)
+    fold = folded(d_u)
+    for n, (device, _) in enumerate(pair):
+        up_folds[pl.ds(pl.multiple_of(device * hid, 8), hid), :] = fold[n * hid : (n + 1) * hid]
+    for up, down, at, g_refs in zip(ups, downs, columns, grads):
+        g_up = mm16(d_low, xb[at, :], NT).astype(bf16)
+        g_down = mm16(act, db[at, :], NT).astype(bf16)
+        for n, g_ref in enumerate(g_refs):
+            mine = slice(n * hid, (n + 1) * hid)
+            g_ref[step, :hid, :] = g_up[mine]
+            g_ref[step, hid : 2 * hid, :] = g_down[mine]
+        acc_out[at, :] += mm16(down, act, TN)
+        acc_in[at, :] += mm16(up, d_low, TN)
 
     @pl.when(step == last)
     def _():
@@ -721,12 +779,15 @@
 
         lax.fori_loop(0, dim // CHUNK, residual, 0)
         for n in range(dim // 256):
-            at = slice(n * 256, (n + 1) * 256)
-            acc_in[at, :] = mm16(out_w_ref[at, :], db[...], NN)
-        some = 192 // chans
-        for n in range(devices // some):
-            g_out = mm16(gb[n * 192 : (n + 1) * 192, :], db[...], NT).reshape(some, chans, dim)
-            g_ref[n * some : (n + 1) * some, 2 * hid :, :] = g_out.astype(bf16)
+            some = slice(n * 256, (n + 1) * 256)
+            acc_in[some, :] = sum(mm16(w[some, :], db[at, :], NN) for w, at in zip(out_w_refs, columns))
+        for at, g_refs in zip(columns, grads):
+            for n in range(dim // 256):
+                some = slice(n * 256, (n + 1) * 256)
+                out_w32[some, :] = mm16(gb[some, :], db[at, :], NT)
+            for turn in range(turns):
+                for g_ref, (device, _) in zip(g_refs, slots(table_ref, turns, turn)):
+                    g_ref[turn, 2 * hid :, :] = out_w32[device_rows(device), :].astype(bf16)
 
         def products(i, carry):
             at = chunk_rows(i)
@@ -751,11 +812,13 @@
         lax.fori_loop(0, devices, scatter, 0)
 
 
-def middle(lens, conv, x_cot, gate, weights, out_w, prm, hid, seqs):
+def middle(table, conv, x, cot, gate, matrices, prm, hid, seqs):
     devices, rows, width = conv.shape
     dim, cols = gate.shape
     chans = dim // devices
-    group = 2
+    turns = devices // 2
+    pieces = len(matrices)
+    part = dim // pieces
     sd = jax.ShapeDtypeStruct
     out = (
         sd((devices, rows + SUM_ROWS, width), bf16),
@@ -763,26 +826,39 @@
         sd((dim, cols), f32),
         sd((dim, cols), f32),
         sd((dim, LANE), f32),
-        sd((devices, 2 * hid + chans, dim), bf16),
-    )
+    ) + (sd((turns, 2 * hid + chans, part), bf16),) * (2 * pieces)
     big = pltpu.VMEM((dim, cols), f32)
     low = pltpu.VMEM((dim, cols), bf16)
-    return pl.pallas_call(
-        lambda *refs: middle_body(seqs, group, *refs),
-        cost_estimate=takes(40),
-        grid=(devices // group,),
-        out_shape=out,
-        in_specs=[
-            smem(), whole(conv), half(x_cot, 0), half(x_cot, 1), whole(gate),
-            pl.BlockSpec((group, 2 * hid, dim), lambda i: (i, 0, 0)), whole(out_w), whole(prm),
-        ],
-        out_specs=tuple(whole(o) for o in out),
-        scratch_shapes=[
+    args, specs = [conv, x, cot, gate, prm], [whole(conv), whole(x), whole(cot), whole(gate), whole(prm)]
+    segments = len(matrices[0][0])
+    for piece in matrices:
+        for parts in piece:
+            first = 0
+            for a in parts:
+                count = a.shape[0]
+                args += [a, a]
+                specs += [
+                    pl.BlockSpec((1, 2 * hid, part), lambda i, t, f=first, c=count: (jnp.clip(i - f, 0, c - 1), 0, 0)),
+                    pl.BlockSpec(
+                        (count, chans, part), lambda i, t: (0, 2 * hid // chans, 0), pipeline_mode=pl.Buffered(1)
+                    ),
+                ]
+                first += count
+    return chip_call(
+        36,
+        lambda *refs: middle_body(seqs, pieces, segments, *refs),
+        table,
+        turns,
+        args,
+        specs,
+        out,
+        tuple(whole(o) for o in out),
+        [
             big, big, big, low, low, low, big, big, pltpu.VMEM((4, dim, LANE), f32),
-            pltpu.VMEM((devices * hid, LANE), f32), pltpu.VMEM((16, cols), f32),
-        ],
-        compiler_params=params(0),
-    )(lens, conv, x_cot, x_cot, gate, weights, out_w, prm)
+            pltpu.VMEM((devices * hid, LANE), f32), pltpu.VMEM((16, cols), f32), pltpu.VMEM((dim, part), f32),
+        ]
+        + [pltpu.VMEM((dim, part), bf16)] * pieces,
+    )
 
 
 def short_back(seqs, prm, kinds, d_short, head, projx, width, cols):
@@ -816,7 +892,7 @@
     return d_low, padded_totals(jnp.concatenate(sum(totals, []), axis=0), width)
 
 
-def back_gate_body(seqs, group, p0_ref, p0h_ref, projx_ref, w_ref, prm_ref, xn_ref, g_ref, sums_ref, acc):
+def back_gate_body(seqs, table_ref, p0_ref, p0h_ref, projx_ref, own_ref, other_ref, prm_ref, xn_ref, g_ref, sums_ref, acc):
     dim, cols = xn_ref.shape
     chans = p0_ref.shape[1]
     step = pl.program_id(0)
@@ -825,40 +901,42 @@
     def _():
         acc[...] = jnp.zeros_like(acc)
 
-    for g in range(group):
-        prm = prm_ref[pl.ds(pl.multiple_of((step * group + g) * chans, 8), chans), :]
+    turns = prm_ref.shape[0] // chans // 2
+    for w_ref, (device, g) in zip((own_ref, other_ref), slots(table_ref, turns, step)):
+        prm = prm_ref[pl.ds(pl.multiple_of(device * chans, 8), chans), :]
         d_low, totals = short_back(
             seqs, prm, (0,), (p0_ref[g],), (p0h_ref[g],), projx_ref[g].astype(f32), cols // seqs, cols
         )
         sums_ref[g] = totals[0]
-        acc[...] += mm16(w_ref[g, PRM : PRM + chans, :], d_low, TN)
+        acc[...] += mm16(w_ref[0, PRM : PRM + chans, :], d_low, TN)
         g_ref[g] = mm16(d_low, xn_ref[...], NT).astype(bf16)
 
 
-def back_gate(p0, p0h, projx, weights, prm, xn, seqs):
+def back_gate(table, p0, p0h, projx, own, other, prm, xn, seqs):
     devices, chans, cols = p0.shape
     dim = xn.shape[0]
-    group = 4
     sd = jax.ShapeDtypeStruct
     out = (
         sd((devices, chans, dim), bf16),
         sd((devices, 8, cols // seqs), f32),
         sd((dim, cols), f32),
     )
-    return pl.pallas_call(
-        lambda *refs: back_gate_body(seqs, group, *refs),
-        cost_estimate=takes(12),
-        grid=(devices // group,),
-        out_shape=out,
-        in_specs=[by_group(a, group) for a in (p0, p0h, projx, weights)] + [whole(prm), whole(xn)],
-        out_specs=(by_group(out[0], group), by_group(out[1], group), whole(out[2])),
-        compiler_params=params(0),
-    )(p0, p0h, projx, weights, prm, xn)
+    return chip_call(
+        2,
+        lambda *refs: back_gate_body(seqs, *refs),
+        table,
+        devices // 2,
+        (p0, p0h, projx, own, other, prm, xn),
+        [by_chip(a) for a in (p0, p0h, projx)] + [by_turn(own), by_turn(other), whole(prm), whole(xn)],
+        out,
+        (by_chip(out[0]), by_chip(out[1]), whole(out[2])),
+        [],
+    )
 
 
 def back_body(
-    seqs, group, d_mixed_ref, pair_ref, heads_ref, projx_ref, w_ref, prm_ref, xn_ref, x_ref, stat_ref, d_res_ref, acc0_ref,
-    sums0_ref, layer_ref, shared_ref, tail_ref, g_ref, acc, xs, folds, sums,
+    seqs, table_ref, d_mixed_ref, pair_ref, heads_ref, projx_ref, own_ref, other_ref, prm_ref, xn_ref, x_ref, stat_ref, d_res_ref,
+    acc0_ref, sums0_ref, layer_ref, tail_ref, g_ref, acc, xs, folds, sums,
 ):
     devices, _, width = x_ref.shape
     dim, cols = xn_ref.shape
@@ -870,8 +948,9 @@
     def _():
         acc[...] = acc0_ref[...]
 
-    for g in range(group):
-        prm = prm_ref[pl.ds(pl.multiple_of((step * group + g) * chans, 8), chans), :]
+    turns = devices // 2
+    for w_ref, (device, g) in zip((own_ref, other_ref), slots(table_ref, turns, step)):
+        prm = prm_ref[pl.ds(pl.multiple_of(device * chans, 8), chans), :]
         block = d_mixed_ref[g].astype(f32)
         d_mixed = side_by_side(block[: seqs * chans], seqs)
         square = jnp.concatenate([block[seqs * chans :, :LANE], jnp.zeros((LANE - HEAD_ROWS, LANE), f32)], axis=0).T
@@ -883,8 +962,8 @@
         head = (d_head * pair_head[chans:], d_head * pair_head[:chans])
         d_low, totals = short_back(seqs, prm, (1, 2), d_short, head, projx_ref[g].astype(f32), width, cols)
         for n, t in enumerate(totals):
-            sums[n, step * group + g] = t
-        acc[...] += mm16(w_ref[g, PRM + chans :, :], d_low, TN)
+            sums[n, device] = t
+        acc[...] += mm16(w_ref[0, PRM + chans :, :], d_low, TN)
         g_ref[g] = mm16(d_low, xn_ref[...], NT).astype(bf16)
 
     @pl.when(step == last)
@@ -920,48 +999,45 @@
         lax.fori_loop(0, dim // CHUNK, second, 0)
 
         rows = seqs * chans
-        ends = [rows, 2 * rows + SUM_ROWS, 2 * rows + 2 * SUM_ROWS]
 
         def scatter(d, carry):
             at = pl.ds(pl.multiple_of(d * chans, 8), chans)
-            tail_ref[d, : ends[0], :] = stacked(acc[at, :], seqs).astype(bf16)
-            tail_ref[d, ends[0] : ends[1], :] = layer_ref[d]
+            tail_ref[d, :rows, :] = stacked(acc[at, :], seqs).astype(bf16)
             totals = [sums0_ref[d]] + [sums[n, d] for n in range(sums.shape[0])]
             totals += [padded_totals(folds[q, at, :], width)[0] for q in range(2)]
-            tail_ref[d, ends[1] : ends[2], :] = as_rows(totals, SUM_ROWS)
-            tail_ref[d, ends[2] :, :] = shared_ref[...]
+            tail_ref[d, rows : rows + SUM_ROWS, :] = as_rows(totals, SUM_ROWS)
+            tail_ref[d, rows + SUM_ROWS :, :] = layer_ref[d]
             return carry
 
         lax.fori_loop(0, devices, scatter, 0)
 
 
-def back(d_mixed, pair, heads, projx, weights, prm, xn, x_cot, stat, d_res, acc0, sums0, layer, shared, seqs):
-    devices, rows, width = x_cot.shape
-    rows = rows // 2
+def back(table, d_mixed, pair, heads, projx, own, other, prm, xn, x, stat, d_res, acc0, sums0, layer, seqs):
+    devices, rows, width = x.shape
     dim, cols = xn.shape
     chans = dim // devices
-    group = 2
     sd = jax.ShapeDtypeStruct
     pieces = -(-2 * (2 + KS) * chans // width)
     out = (
-        sd((devices, 2 * rows + 2 * SUM_ROWS + shared.shape[0], width), bf16),
+        sd((devices, 2 * rows + 2 * SUM_ROWS, width), bf16),
         sd((devices, 2 * chans, dim), bf16),
     )
-    return pl.pallas_call(
-        lambda *refs: back_body(seqs, group, *refs),
-        cost_estimate=takes(20),
-        grid=(devices // group,),
-        out_shape=out,
-        in_specs=[by_group(a, group) for a in (d_mixed, pair, heads, projx, weights)]
-        + [whole(prm), whole(xn), half(x_cot, 0)]
-        + [whole(a) for a in (stat, d_res, acc0, sums0, layer, shared)],
-        out_specs=(whole(out[0]), by_group(out[1], group)),
-        scratch_shapes=[
+    return chip_call(
+        100,
+        lambda *refs: back_body(seqs, *refs),
+        table,
+        devices // 2,
+        (d_mixed, pair, heads, projx, own, other, prm, xn, x, stat, d_res, acc0, sums0, layer),
+        [by_chip(a) for a in (d_mixed, pair, heads, projx)]
+        + [by_turn(own), by_turn(other), whole(prm), whole(xn), whole(x)]
+        + [whole(a) for a in (stat, d_res, acc0, sums0, layer)],
+        out,
+        (whole(out[0]), by_chip(out[1])),
+        [
             pltpu.VMEM((dim, cols), f32), pltpu.VMEM((dim, cols), f32), pltpu.VMEM((2, dim, LANE), f32),
             pltpu.VMEM((pieces, devices, 8, width), f32),
         ],
-        compiler_params=params(0),
-    )(d_mixed, pair, heads, projx, weights, prm, xn, x_cot, stat, d_res, acc0, sums0, layer, shared)
+    )
 
 
 def position_table():
@@ -984,8 +1060,103 @@
 NT = ((1,), (1,))
 
 
+def filter_back_body(d_ref, raw_ref, fall_ref, h1_ref, h2_ref, c1_ref, c2_ref, pre1_ref, pre2_ref, feat_ref, mid_ref, last_ref, rate_ref,
+                     g_in_ref, g_mid_ref, g_last_ref, g_rows_ref, g_decay_ref):
+    chans = d_ref.shape[0]
+    d = d_ref[...]
+    q = d * (fall_ref[...] + decay_floor)
+    g_last_ref[...] = mm(h2_ref[...], q, NT)
+    decay = folded(d * raw_ref[...] * fall_ref[...] * feat_ref[0:1, :])
+    g_decay_ref[...] = -jnp.sum(decay, axis=1, keepdims=True)
+    u2 = mm(last_ref[...], q, NN) * c2_ref[...]
+    rate = rate_ref[...]
+    fu2 = rate * u2
+    u1 = mm(mid_ref[...], fu2, NN) * c1_ref[...]
+    fu1 = rate * u1
+    g_in_ref[...] = mm(feat_ref[...], fu1, NT)
+    g_mid_ref[...] = mm(h1_ref[...], fu2, NT)
+    rows = jnp.concatenate([folded(fu1), folded(fu2), folded(u2 * pre2_ref[...] + u1 * pre1_ref[...])], axis=0)
+    extra = jnp.zeros((-rows.shape[0] % LANE, LANE), f32)
+    g_rows_ref[...] = row_totals(jnp.concatenate([rows, extra], axis=0))
+
+
+def filter_back(*args):
+    chans, ford, taps = args[0].shape[0], args[3].shape[0], args[9].shape[0]
+    sd = jax.ShapeDtypeStruct
+    out = (sd((taps, ford), f32), sd((ford, ford), f32), sd((ford, chans), f32), sd((8, -(-3 * ford // LANE) * LANE), f32), sd((chans, 1), f32))
+    return whole_call(0.01, filter_back_body, out, [], *args)
+
+
 def mm16(a, b, dims):
     return lax.dot_general(a, b, (dims, ((), ())), preferred_element_type=f32)
+
+
+def ring_of(chips):
+    zs = 4
+    ys = chips // zs
+    order = [(z, 0) for z in range(zs)]
+    for y in range(1, ys):
+        order += [(z, y) for z in (range(zs - 1, 0, -1) if y % 2 else range(1, zs))]
+    order += [(0, y) for y in range(ys - 1, 0, -1)]
+    return [z * ys + y for z, y in order]
+
+
+def after(values, *others):
+    return lax.optimization_barrier((values,) + others)[0]
+
+
+def ring_hop(values, ring, by):
+    chips = len(ring)
+    moves = [(2 * ring[p] + q, 2 * ring[(p + by) % chips] + q) for p in range(chips) for q in range(2)]
+    return lax.ppermute(values, "chan", moves)
+
+
+class RingGather:
+    def __init__(self, shard, ring):
+        self.ring, self.hops = ring, len(ring) // 2
+        self.cut = shard.shape[0] // 32 * 16
+        self.behind, self.ahead = [shard], [shard]
+        self.far = None
+
+    def advance(self, upto, *others):
+        while len(self.behind) <= min(upto, self.hops - 1):
+            first, second = self.behind[-1], self.ahead[-1]
+            if others:
+                first, second = after(first, *others), after(second, *others)
+            self.behind.append(ring_hop(first, self.ring, 1))
+            self.ahead.append(ring_hop(second, self.ring, -1))
+        if upto == self.hops:
+            first, second = self.behind[-1][: self.cut], self.ahead[-1][self.cut :]
+            if others:
+                first, second = after(first, *others), after(second, *others)
+            self.far = jnp.concatenate([ring_hop(first, self.ring, 1), ring_hop(second, self.ring, -1)], axis=0)
+
+    def shards(self):
+        return self.behind + self.ahead[1:] + [self.far]
+
+
+def both_cores(shards):
+    own = stack(shards)
+    return own, lax.ppermute(own, "chan", [(i, i ^ 1) for i in range(2 * len(shards))])
+
+
+def stack_body(*refs):
+    for i, ref in enumerate(refs[:-1]):
+        refs[-1][i] = ref[...]
+
+
+def stack(shards):
+    out = jax.ShapeDtypeStruct((len(shards),) + shards[0].shape, shards[0].dtype)
+    return whole_call(0.01, stack_body, out, [], *shards)
+
+
+def turn_table(ring):
+    chips = len(ring)
+    steps = [0] + [-k for k in range(1, chips // 2)] + [k for k in range(1, chips // 2)] + [chips // 2]
+    table = np.zeros((chips, chips), np.int32)
+    for p, chip in enumerate(ring):
+        table[chip] = [ring[(p + k) % chips] for k in steps]
+    return table
 
 
 def exchange(values):
@@ -1055,48 +1226,108 @@
     )
     small = jnp.pad(small, ((0, PRM - small.shape[0]), (0, dim - chans)))
     in_rows = in_weight.transpose(1, 2, 0).reshape(3 * chans, dim)
-    in_all = lax.all_gather(jnp.concatenate([small, in_rows], axis=0), "chan", axis=0)
-    x = exchange(jnp.concatenate([to_blocks(layer_in), to_blocks(cotangent)], axis=1))
+    ring = ring_of(devices // 2)
+    chips = devices // 2
+    core = place % 2
+    batch = lax.axis_index("batch")
+    swap = [(0, 1), (1, 0)]
+    partner = [(i, i ^ 1) for i in range(devices)]
+    turns = lax.dynamic_index_in_dim(jnp.asarray(turn_table(ring)), place // 2, 0, False)
+    table = jnp.concatenate(
+        [turns, jnp.stack([core, place]).astype(jnp.int32), seq_lengths, batch.astype(jnp.int32).reshape(1)]
+    )
+    first = RingGather(jnp.concatenate([small, in_rows], axis=0), ring)
+    first.advance(chips // 8)
+    x = exchange(to_blocks(layer_in))
     rows = seqs * chans
     xh = lax.ppermute(x[:, :rows, width - LANE :], "chan", [(i, i + 1) for i in range(devices - 1)])
-    rest = lax.all_gather(jnp.concatenate([up_weight, down_weight, out_weight], axis=0), "chan", axis=0)
-    prm = in_all[:, :PRM, :chans].astype(f32).transpose(0, 2, 1).reshape(dim, PRM)
-    out_w = rest[:, 2 * hid :].reshape(dim, dim)
 
     feat = jnp.asarray(FEAT)
     ramp = feat[0:1]
     rate = sine_freq[:, None]
     pre1 = mm(filt_in, feat, TN) + filt_in_bias[:, None]
-    h1 = jnp.sin(rate * pre1)
+    h1, c1 = jnp.sin(rate * pre1), jnp.cos(rate * pre1)
     pre2 = mm(filt_mid, h1, TN) + filt_mid_bias[:, None]
-    h2 = jnp.sin(rate * pre2)
+    h2, c2 = jnp.sin(rate * pre2), jnp.cos(rate * pre2)
     raw = mm(filt_out, h2, TN)
     falling = jnp.exp(-ramp * decay_rate[:, None])
-    env = falling + decay_floor
-    filt_spec = filter_spectrum(raw * env)
+    first.advance(chips // 4, h1)
+    filt = raw * (falling + decay_floor)
+    first.advance(3 * chips // 8, filt, x)
+    filt_spec = filter_spectrum(filt)
+    first.advance(chips // 2, filt_spec)
+    in_own, in_other = both_cores(first.shards())
     bias_col = conv_bias[:, None]
 
-    xn1, stat1, gate, pair, projx0, projx, mixed, heads = front(
-        jnp.minimum(place, 1).reshape(1), x, xh, in_all, prm, filt_spec, seqs
+    late = jnp.concatenate([up_weight, down_weight, out_weight], axis=0)
+    stepped = groups == 2 and chips == 8 and dim % (2 * LANE) == 0
+    beside = [(i, i ^ 2) for i in range(devices)]
+    along = [list(range(k, devices, 4)) for k in range(4)]
+
+    def to_partner(values):
+        return lax.ppermute(values, "chan", partner)
+
+    if stepped:
+        part = dim // 2
+        late = lax.dynamic_slice_in_dim(late, batch * part, part, 1)
+        near = lax.all_gather(late, "chan", axis=0, axis_index_groups=along)
+    else:
+        late = lax.all_gather(late, "chan", axis=0).reshape((chips, 2) + late.shape)
+    prm, xn1, stat1, gate, pair, projx0, projx, mixed, heads = front(
+        table, x, xh, in_own, in_other, filt_spec, seqs
     )
     mixed_chan = exchange(mixed)
+    cot = exchange(after(to_blocks(cotangent), mixed_chan))
+    if stepped:
+        near = after(near, mixed)
+        far = lax.ppermute(near, "chan", beside)
+        near_across = lax.ppermute(near, "batch", swap)
+        near_other = to_partner(near)
     backward_hop = [(i + 1, i) for i in range(devices - 1)]
     heads = lax.ppermute(heads, "chan", backward_hop)
     conv_chan, mixed_spec = conv_forward(mixed_chan, filt_spec, bias_col, seqs)
-    conv = exchange(conv_chan)
-
-    lens = jnp.concatenate([seq_lengths, place.astype(jnp.int32).reshape(1)])
-    layer, d_conv, d_res, p0, p0h, early = middle(
-        lens, conv, x, gate.reshape(dim, cols), rest, out_w, prm, hid, seqs
-    )
+    conv = exchange(after(conv_chan, near_across, cot) if stepped else conv_chan)
+    if stepped:
+        far, near_across = after(far, conv_chan), after(near_across, conv_chan)
+        far_across = lax.ppermute(far, "batch", swap)
+        far_other, near_across_other = to_partner(far), to_partner(near_across)
+        far_across_other = to_partner(far_across)
+        matrices = [
+            [[near, far], [near_other, far_other]],
+            [[near_across, far_across], [near_across_other, far_across_other]],
+        ]
+        z = lax.iota(jnp.int32, 4) * 2
+        y = (place // 2 % 2).astype(jnp.int32)
+        order = jnp.concatenate([z + y, z + 1 - y])
+    else:
+        matrices = [[[lax.dynamic_index_in_dim(late, core, 1, False)], [lax.dynamic_index_in_dim(late, 1 - core, 1, False)]]]
+        order = lax.iota(jnp.int32, chips)
+    order = jnp.concatenate([order, table[chips:]])
+
+    results = middle(order, conv, x, cot, gate.reshape(dim, cols), matrices, prm, hid, seqs)
+    layer, d_conv, d_res, p0, p0h = results[:5]
     d_conv_chan = exchange(d_conv)
     p0h = lax.ppermute(p0h, "chan", backward_hop)
-    early = lax.psum_scatter(early, "chan", scatter_dimension=0, tiled=True)[0]
-
-    swap = [(0, 1), (1, 0)]
-    core = place % 2
-    partner = [(i, i ^ 1) for i in range(devices)]
-    same_core = [[b * devices + c for b in range(groups) for c in range(q, devices, 2)] for q in range(2)]
+
+    def added(*values):
+        return sum(v.astype(f32) for v in values).astype(bf16)
+
+    if stepped:
+        mine, mine_in = results[5], to_partner(results[6])
+        theirs, theirs_in = results[7], to_partner(results[8])
+        half = chips // 2
+        far_theirs = added(theirs[half:], theirs_in[half:])
+        near_theirs = added(theirs[:half], theirs_in[:half])
+        d_conv_chan = after(d_conv_chan, far_theirs, near_theirs)
+        far_theirs = lax.ppermute(far_theirs, "batch", swap)
+        near_theirs = lax.ppermute(after(near_theirs, far_theirs), "batch", swap)
+    else:
+        early = added(results[5], to_partner(results[6]))
+
+    if groups == 2:
+        same_core = [list(range(q, devices, 2)) for q in range(2)]
+    else:
+        same_core = [[b * devices + c for b in range(groups) for c in range(q, devices, 2)] for q in range(2)]
 
     def batch_total(values):
         return values + lax.ppermute(values, "batch", swap) if groups == 2 else lax.psum(values, "batch")
@@ -1104,11 +1335,12 @@
     def over_batch(table):
         if groups != 2:
             return lax.psum_scatter(table.astype(f32), "batch", scatter_dimension=1, tiled=True)
-        half = dim // 2
-        mine = lax.axis_index("batch") * half
-        theirs = lax.dynamic_slice_in_dim(table, half - mine, half, 1)
-        own = lax.dynamic_slice_in_dim(table, mine, half, 1)
-        return own.astype(f32) + lax.ppermute(theirs, "batch", swap).astype(f32)
+        part = dim // 2
+        axis = table.ndim - 1
+        mine = lax.axis_index("batch") * part
+        theirs = lax.dynamic_slice_in_dim(table, part - mine, part, axis)
+        kept = lax.dynamic_slice_in_dim(table, mine, part, axis)
+        return kept.astype(f32) + lax.ppermute(theirs, "batch", swap).astype(f32)
 
     def over_chip(table):
         table = table.reshape((devices // 2, 2) + table.shape[1:])
@@ -1116,40 +1348,61 @@
         theirs = lax.dynamic_index_in_dim(table, 1 - core, 1, False)
         return (own.astype(f32) + lax.ppermute(theirs, "chan", partner).astype(f32)).astype(bf16)
 
+    def over_groups(both):
+        return over_batch(both).astype(bf16) if groups == 2 else both
+
     def over_chips(both):
         rows = both.shape[1]
-        both = both.reshape(devices // 2, rows, groups, dim // groups).transpose(2, 0, 1, 3)
-        both = lax.all_to_all(
-            both.reshape(groups * devices // 2, rows, dim // groups),
-            ("batch", "chan"), split_axis=0, concat_axis=0, tiled=True, axis_index_groups=same_core,
-        )
+        if groups == 2:
+            both = lax.all_to_all(
+                both, "chan", split_axis=0, concat_axis=0, tiled=True, axis_index_groups=same_core
+            )
+        else:
+            both = both.reshape(devices // 2, rows, groups, dim // groups).transpose(2, 0, 1, 3)
+            both = lax.all_to_all(
+                both.reshape(groups * devices // 2, rows, dim // groups),
+                ("batch", "chan"), split_axis=0, concat_axis=0, tiled=True, axis_index_groups=same_core,
+            )
         return jnp.sum(both.astype(f32), axis=0)
 
-    g_in0, sums0, acc0 = back_gate(
-        p0.reshape(devices, chans, cols), p0h.reshape(devices, chans, LANE), projx0, in_all, prm, xn1, seqs
-    )
     d_mixed_chan, d_filter, g_conv_bias = conv_backward(
         d_conv_chan, mixed_chan, mixed_spec, filt_spec, bias_col, seqs
     )
+    if stepped:
+        d_mixed_chan = after(d_mixed_chan, far_theirs)
+        far_mine = added(mine[half:], mine_in[half:], far_theirs)
+        p0h = after(p0h, far_mine)
+    g_in0, sums0, acc0 = back_gate(
+        table, p0.reshape(devices, chans, cols), p0h.reshape(devices, chans, LANE), projx0, in_own, in_other, prm, xn1, seqs
+    )
     g_in0 = over_chip(g_in0)
     d_mixed = exchange(d_mixed_chan)
-
-    q = d_filter * env
-    g_filt_out = mm(h2, q, NT)
-    g_decay = -jnp.sum(d_filter * raw * falling * ramp, axis=1)
-    u2 = mm(filt_out, q, NN) * jnp.cos(rate * pre2)
-    fu2 = rate * u2
-    u1 = mm(filt_mid, fu2, NN) * jnp.cos(rate * pre1)
-    fu1 = rate * u1
-    shared = [
-        mm(feat, fu1, NT).reshape(-1),
-        jnp.sum(fu1, axis=1),
-        mm(h1, fu2, NT).reshape(-1),
-        jnp.sum(fu2, axis=1),
-        jnp.sum(u2 * pre2 + u1 * pre1, axis=1),
-    ]
-    apart_totals = [g_conv_bias[:, 0], g_decay, g_filt_out.reshape(-1)]
-    total = batch_total(jnp.concatenate(shared + apart_totals))
+    g_filt_in, g_filt_mid, g_filt_out, g_rows, g_decay = filter_back(
+        d_filter, raw, falling, h1, h2, c1, c2, pre1, pre2, feat, filt_mid, filt_out, rate
+    )
+    shared = [g_filt_in.reshape(-1), g_filt_mid.reshape(-1), g_rows[0, : 3 * ford]]
+    total = batch_total(
+        jnp.concatenate(shared + [g_conv_bias[:, 0], g_decay[:, 0], g_filt_out.reshape(-1)])
+    )
+    if stepped:
+        d_mixed = after(d_mixed, near_theirs)
+        far_mine = lax.ppermute(far_mine, "chan", beside)
+    else:
+        chan_groups = [list(range(q, devices, 2)) for q in range(2)]
+        early = lax.psum_scatter(early, "chan", scatter_dimension=0, tiled=True, axis_index_groups=chan_groups)[0]
+
+    tail, g_in = back(
+        table, d_mixed, pair, heads, projx, in_own, in_other, prm, xn1, x, stat1, d_res, acc0, sums0, layer, seqs
+    )
+    if stepped:
+        tail = after(tail, far_mine)
+        early = added(mine[:half], mine_in[:half], near_theirs, far_mine)
+        g_in = after(g_in, early)
+    tail = exchange(tail)
+    g_in = over_groups(jnp.concatenate([g_in0, over_chip(g_in)], axis=1))
+    if stepped:
+        early = lax.psum_scatter(early, "chan", scatter_dimension=0, tiled=True, axis_index_groups=along)[0]
+
     cut = [0]
 
     def take(*shape):
@@ -1158,22 +1411,33 @@
         cut[0] += n
         return part
 
-    shared = take(sum(v.shape[0] for v in shared)).astype(bf16)
+    shared = take(sum(v.shape[0] for v in shared))
+    shared = shared + lax.ppermute(shared, "chan", partner)
     g_conv_b, g_decay_rate, g_filt_last = take(chans), take(chans), take(ford, chans)
-    shared = jnp.pad(shared, (0, -shared.shape[0] % (32 * width))).reshape(-1, width)
-
-    tail, g_in = back(
-        d_mixed, pair, heads, projx, in_all, prm, xn1, x, stat1, d_res, acc0, sums0, layer, shared, seqs
-    )
-    tail = exchange(tail)
-    in_grad = over_chips(jnp.concatenate([g_in0, over_chip(g_in)], axis=1))
-    early = over_batch(early)
+    n_shared = shared.shape[0]
+    if groups != 2:
+        shared = shared / groups
+    line = g_in.shape[2]
+    shared = jnp.pad(shared.astype(bf16), (0, -n_shared % (16 * line))).reshape(1, -1, line)
+    shared = jnp.broadcast_to(shared, (devices // 2,) + shared.shape[1:])
+    mine = 3 * chans
+    in_grad = over_chips(jnp.concatenate([g_in, shared], axis=1))
+    if groups == 2:
+        total = in_grad[mine:].reshape(-1)
+    else:
+        total = lax.all_gather(in_grad[mine:], "batch", axis=1, tiled=True).reshape(-1)
+    in_grad = in_grad[:mine]
+    cut[0] = 0
+    g_filt_in, g_filt_mid = take(EMB, ford), take(ford, ford)
+    g_filt_in_bias, g_filt_mid_bias, g_sine = take(ford), take(ford), take(ford)
+
+    early = after(early, in_grad)
+    early = early.astype(f32) if stepped else over_batch(early)
     up_grad, down_grad, out_grad = early[:hid], early[hid : 2 * hid], early[2 * hid :]
 
-    grad_blocks, out_blocks = tail[:, :rows], tail[:, rows : 2 * rows]
-    sums = jnp.sum(tail[:, 2 * rows : 2 * rows + SUM_ROWS].astype(f32), axis=0)
-    sums2 = jnp.sum(tail[:, 2 * rows + SUM_ROWS : 2 * rows + 2 * SUM_ROWS].astype(f32), axis=0)
-    sums = batch_total(jnp.concatenate([sums, sums2], axis=0))
+    grad_blocks, out_blocks = tail[:, :rows], tail[:, rows + SUM_ROWS : 2 * rows + SUM_ROWS]
+    sums = jnp.concatenate([tail[:, 2 * rows + SUM_ROWS :], tail[:, rows : rows + SUM_ROWS]], axis=1)
+    sums = batch_total(jnp.sum(sums.astype(f32), axis=0))
     sums = sums[0::2] + sums[1::2]
     g_gain2, g_shift2, g_out_b, g_down_b = (sums[i, :chans] for i in range(4))
     g_up_b = sums[4, :hid]
@@ -1185,10 +1449,6 @@
     short = jnp.concatenate([short0, short], axis=1)
     g_in_bias, g_short_bias, g_short_weight = short[0], short[1], short[2:]
     g_gain1, g_shift1 = (sums[at + 1 + pieces + i, :chans] for i in range(2))
-    total = jnp.sum(tail[:, 2 * rows + 2 * SUM_ROWS :].astype(f32), axis=0).reshape(-1)
-    cut[0] = 0
-    g_filt_in, g_filt_in_bias = take(EMB, ford), take(ford)
-    g_filt_mid, g_filt_mid_bias, g_sine = take(ford, ford), take(ford), take(ford)
 
     return (
         from_blocks(out_blocks),

time: 491 us -> 456 us (0.929); the launches traced: 481 us -> 454 us
  waiting for transfers between devices: 183 us -> 128 us
  Pallas kernels: 129 us -> 152 us
  matrix products: 31.8 us -> 14.7 us
  starting transfers between devices: 73.5 us -> 89.7 us
  other arithmetic: 15.5 us -> 23.2 us
    all_to_all x6 -> x7, waiting for transfers between devices: 123 us -> 24.6 us  [exchange(): lax.all_to_all(values, 'chan', split_axis=0, concat_axis=0, tiled=True)]
    ppermute x1 -> x23, waiting for transfers between devices: 0.01 us -> 55.4 us  [the longest x1 22.1 us: on_device(): far_across = lax.ppermute(far, 'batch', swap)]
    ppermute x1 -> x23, starting transfers between devices: 0.26 us -> 27.4 us  [the longest x8 13.9 us: ring_hop(): return lax.ppermute(values, 'chan', moves)]
    all_gather x2 -> x1, waiting for transfers between devices: 28.8 us -> 2.46 us  [on_device(): near = lax.all_gather(late, 'chan', axis=0, axis_index_groups=along)]
    dot_general x8 -> x3, matrix products: 31.8 us -> 14.7 us  [mm(): lax.dot_general(a, b, (dims, ((), ())), precision=highest, preferred_elem...]
    all_to_all x1, waiting for transfers between devices: 23.6 us -> 37.2 us  [over_chips(): lax.all_to_all(both, 'chan', split_axis=0, concat_axis=0, tiled=True, axi...]
    convert_element_type x0 -> x5, other arithmetic: none -> 12.5 us  [the longest x3 11 us: added(): return sum((v.astype(f32) for v in values)).astype(bf16)]
    pallas_call x3 -> x5, Pallas kernels: 34.9 us -> 46.8 us  [whole_call(): pl.pallas_call(body, cost_estimate=takes(us), out_shape=out_shape, in_spe...]
  transfers between devices with their start and end apart: 18 -> 40, of which waited for: 10 -> 16; matrix products, arithmetic and copies ran while one was open for 15% -> 12% of each run, Pallas kernels for 18% -> 22%
where the time goes in v3:
time: 456 us; the launch traced here: 454 us
  Pallas kernels  152 us (33%)
  waiting for transfers between devices  128 us (28%)
  starting transfers between devices  89.7 us (20%)
  local copies, waits for them, and re-layouts  31.4 us (7%)
  other arithmetic  23.2 us (5%)
  between operations  14.9 us (3%)
  matrix products  14.7 us (3%)
    pallas_call x4, Pallas kernels, chip_call(): pl.pallas_call(body, cost_estimate=takes(us), out_shape=out, grid_spec=pl...  105 us
    all_to_all x7, starting transfers between devices, exchange(): lax.all_to_all(values, 'chan', split_axis=0, concat_axis=0, tiled=True)  48.7 us
    pallas_call x5, Pallas kernels, whole_call(): pl.pallas_call(body, cost_estimate=takes(us), out_shape=out_shape, in_spe...  46.8 us
    all_to_all x1, waiting for transfers between devices, over_chips(): lax.all_to_all(both, 'chan', split_axis=0, concat_axis=0, tiled=True, axi...  37.2 us
    all_to_all x7, waiting for transfers between devices, exchange(): lax.all_to_all(values, 'chan', split_axis=0, concat_axis=0, tiled=True)  24.6 us
    ppermute x1, waiting for transfers between devices, on_device(): far_across = lax.ppermute(far, 'batch', swap)  22.1 us
    dot_general x3, matrix products, mm(): lax.dot_general(a, b, (dims, ((), ())), precision=highest, preferred_elem...  14.7 us
    ppermute x8, starting transfers between devices, ring_hop(): return lax.ppermute(values, 'chan', moves)  13.9 us
  transfers between devices with their start and end apart: 40, of which 16 were waited for; matrix products, arithmetic and copies ran while one was open for 12% of the time, Pallas kernels for 22%

profile of v3, /device:TPU:0, one launch (start us, length us, event | category | flops | bytes accessed | tf_op | source)
XLA Modules:
  0.0 454.1 jit_solution(3226143511820737640)
XLA Ops:
  9.6 7.4 %all-to-all-start = ((bf16[16,96,256]{2,1,0:T(8,128)(2,1)}), bf16[16,96,256]{2,1,0:T(8,128)(2,1)S(1)}, u32[]{:S(2)}, u32[]{:S(2)}) async-start(bf16[16,96,256]{2,1,0:T(8,128)(2,1)} %bitcast.5), calls=%async_computation | async-start | bytes 1572864 | tf_op jit(solution)/shard_map/all_to_all | solution.py:1163
  19.6 6.2 %multiply_cosine_fusion.1 = (f32[64,4096]{1,0:T(8,128)}, f32[64,4096]{1,0:T(8,128)S(1)}, f32[64,4096]{1,0:T(8,128)}) fusion(f32[64]{0:T(128)S(1)} %copy-done.29, f32[64]{0:T(128)S(1)} %copy-done.36, f32[33,4096]{1,0:T(8,128)S(1)} %copy-done.6, f32[33,64]{1,0:T(8,128)S(1)} %copy-done), kind=kOutput, calls=%fused_computation.24 | convolution fusion | flops 104333312 | bytes 3695360 | tf_op jit(solution)/shard_map/dot_general | solution.py:1055
  25.9 6.2 %multiply_cosine_fusion = (f32[64,4096]{1,0:T(8,128)}, f32[64,4096]{1,0:T(8,128)S(1)}, f32[64,4096]{1,0:T(8,128)}) fusion(f32[64]{0:T(128)S(1)} %copy-done.29, f32[64]{0:T(128)S(1)} %copy-done.37, f32[64,4096]{1,0:T(8,128)S(1)} %get-tuple-element.161.h1_ref, f32[64,64]{1,0:T(8,128)S(1)} %copy-done.23), kind=kOutput, calls=%fused_computation.22 | convolution fusion | flops 201850880 | bytes 4211200 | tf_op jit(solution)/shard_map/dot_general | solution.py:1055
  32.0 4.5 collective-permute-done.1.refs_1_
  36.5 5.9 %collective-permute-start.2 = (bf16[176,768]{1,0:T(8,128)(2,1)S(1)}, bf16[176,768]{1,0:T(8,128)(2,1)S(1)}, u32[]{:S(2)}, u32[]{:S(2)}) collective-permute-start(bf16[176,768]{1,0:T(8,128)(2,1)S(1)} %collective-permute-done.1.refs_1_), channel_id=1, source_target_pairs={{0,4},{1,5},{4,8},{5,9},{8,12},{9,13},{12,14},{13,15},{14,10},{15,... | collective-permute-start | bytes 811016 | tf_op jit(solution)/shard_map/ppermute | solution.py:1111
  52.2 5.4 %shard_map.469.refs_7_.refs_1_.refs_3_ = f32[33,48,256]{2,1,0:T(8,128)} custom-call(f32[48,4096]{1,0:T(8,128)} %get-tuple-element.170.filter_ref, f32[33,1,256]{2,1,0:T(1,128)} %constant.86.clone.twist_ref.refs_3_.refs_5_, bf16[2,256,256]{2,1,0:T(8,128)(2,1)} %constant.87.clone.ahead_ref.refs_4_.refs_6_), custom_call_target="tpu_custom_call" | custom-call | flops 8000000000 | bytes 24000000 | tf_op jit(solution)/shard_map/pallas_call | solution.py:336
  60.2 4.4 collective-permute-done.7
  76.4 16.9 %shard_map.471 = (f32[768,32]{1,0:T(8,128)}, bf16[768,512]{1,0:T(8,128)(2,1)}, f32[16,512]{1,0:T(8,128)}, f32[16,48,512]{2,1,0:T(8,128)}, f32[16,96,512]{2,1,0:T...) custom-call(s32[13]{0:T(128)} %concatenate.35.refs_0_, ...), custom_call_target="tpu_custom_call" | custom-call | flops 99999997952 | bytes 300000000 | tf_op jit(solution)/shard_map/pallas_call | solution.py:574
  93.3 7.7 %all-to-all-start.1 = ((bf16[16,96,256]{2,1,0:T(8,128)(2,1)}), bf16[16,96,256]{2,1,0:T(8,128)(2,1)S(1)}, u32[]{:S(2)}, u32[]{:S(2)}) async-start(bf16[16,96,256]{2,1,0:T(8,128)(2,1)} %get-tuple-element.82), calls=%async_computation.1 | async-start | bytes 1572864 | tf_op jit(solution)/shard_map/all_to_all | solution.py:1163
  108.1 11.6 %all-to-all-done.1.refs_0_.refs_1_ = bf16[16,96,256]{2,1,0:T(8,128)(2,1)S(1)} async-done(((bf16[16,96,256]{2,1,0:T(8,128)(2,1)}), bf16[16,96,256]{2,1,0:T(8,128)(2,1)S(1)}, u32[]{:S(2)}, u32[]{:S(2)}) %all-to-all-start.1) | async-done | bytes 786464 | tf_op jit(solution)/shard_map/all_to_all | solution.py:1163
  119.7 5.5 %all-to-all-start.2 = ((bf16[16,96,256]{2,1,0:T(8,128)(2,1)}), bf16[16,96,256]{2,1,0:T(8,128)(2,1)S(1)}, u32[]{:S(2)}, u32[]{:S(2)}) async-start(bf16[16,96,256]{2,1,0:T(8,128)(2,1)} %bitcast.20), calls=%async_computation.2 | async-start | bytes 1572864 | tf_op jit(solution)/shard_map/all_to_all | solution.py:1163
  125.3 13.3 %shard_map.472 = (bf16[16,96,256]{2,1,0:T(8,128)(2,1)}, f32[33,96,256]{2,1,0:T(8,128)}) custom-call(bf16[16,96,256]{2,1,0:T(8,128)(2,1)} %copy-done.11, f32[33,48,256]{2,1,0:T(8,128)} %shard_map.469.refs_7_.refs_1_.refs_3_, f32[48,1]{1,0:T(8,128)} %copy.64.refs_2_.refs_4_, f32[33,1,256]{2,1,0:T(1,128)} %constant.86.clone.twist_ref.refs_3_.refs_5_, ...), custom_call_target="tpu_custom_call" | custom-call | flops 99999997952 | bytes 300000000 | tf_op jit(solution)/shard_map/pallas_call | solution.py:336
  138.6 10.4 %collective-permute-done.11.refs_8_.refs_9_ = bf16[4,432,384]{2,1,0:T(8,128)(2,1)} collective-permute-done((bf16[4,432,384]{2,1,0:T(8,128)(2,1)}, bf16[4,432,384]{2,1,0:T(8,128)(2,1)}, u32[]{:S(2)}, u32[]{:S(2)}) %collective-permute-start.11) | collective-permute-done | bytes 1327136 | tf_op jit(solution)/shard_map/ppermute | solution.py:1283
  151.0 4.1 all-to-all-start.3
  156.1 22.1 %collective-permute-done.14.refs_16_.refs_17_ = bf16[4,432,384]{2,1,0:T(8,128)(2,1)S(1)} collective-permute-done((bf16[4,432,384]{2,1,0:T(8,128)(2,1)}, bf16[4,432,384]{2,1,0:T(8,128)(2,1)S(1)}, u32[]{:S(2)}, u32[]{:S(2)}) %collective-permute-start.14) | collective-permute-done | bytes 1327136 | tf_op jit(solution)/shard_map/ppermute | solution.py:1292
  182.3 48.9 %shard_map.473 = (bf16[16,112,256]{2,1,0:T(8,128)(2,1)}, bf16[16,96,256]{2,1,0:T(8,128)(2,1)}, f32[768,512]{1,0:T(8,128)}, f32[768,512]{1,0:T(8,128)}, f32[768,1...) custom-call(s32[13]{0:T(128)} %concatenate.36.refs_0_, ...), custom_call_target="tpu_custom_call" | custom-call | flops 35999997952 | bytes 108000000 | tf_op jit(solution)/shard_map/pallas_call | solution.py:574
  231.4 4.8 %all-to-all-start.4 = ((bf16[16,96,256]{2,1,0:T(8,128)(2,1)}), bf16[16,96,256]{2,1,0:T(8,128)(2,1)S(1)}, u32[]{:S(2)}, u32[]{:S(2)}) async-start(bf16[16,96,256]{2,1,0:T(8,128)(2,1)} %get-tuple-element.91), calls=%async_computation.4 | async-start | bytes 1572864 | tf_op jit(solution)/shard_map/all_to_all | solution.py:1163
  236.7 3.9 add_convert_fusion.2
  242.0 12.9 %all-to-all-done.4.refs_0_ = bf16[16,96,256]{2,1,0:T(8,128)(2,1)S(1)} async-done(((bf16[16,96,256]{2,1,0:T(8,128)(2,1)}), bf16[16,96,256]{2,1,0:T(8,128)(2,1)S(1)}, u32[]{:S(2)}, u32[]{:S(2)}) %all-to-all-start.4) | async-done | bytes 786464 | tf_op jit(solution)/shard_map/all_to_all | solution.py:1163
  255.9 16.3 %shard_map.474 = (bf16[16,112,256]{2,1,0:T(8,128)(2,1)}, f32[48,4096]{1,0:T(8,128)}, f32[48,1]{1,0:T(8,128)}) custom-call(bf16[16,96,256]{2,1,0:T(8,128)(2,1)} %copy-done.14, bf16[16,96,256]{2,1,0:T(8,128)(2,1)} %copy-done.11, f32[33,96,256]{2,1,0:T(8,128)} %get-tuple-element.95.refs_2_, f32[33,48,256]{2,1,0:T(8,128)} %shard_map.469.refs_7_.refs_1_.refs_3_, ...), custom_call_target="tpu_custom_call" | custom-call | flops 99999997952 | bytes 300000000 | tf_op jit(solution)/shard_map/pallas_call | solution.py:336
  272.2 5.9 %all-to-all-start.5 = ((bf16[16,112,256]{2,1,0:T(8,128)(2,1)}), bf16[16,112,256]{2,1,0:T(8,128)(2,1)}, u32[]{:S(2)}, u32[]{:S(2)}) async-start(bf16[16,112,256]{2,1,0:T(8,128)(2,1)} %get-tuple-element.97), calls=%async_computation.5 | async-start | bytes 1835008 | tf_op jit(solution)/shard_map/all_to_all | solution.py:1163
  282.2 3.3 add_convert_fusion.1
  285.5 3.4 collective-permute-start.23
  289.7 13.8 %shard_map.475 = (bf16[16,48,768]{2,1,0:T(8,128)(2,1)}, f32[16,8,256]{2,1,0:T(8,128)}, f32[768,512]{1,0:T(8,128)}) custom-call(s32[13]{0:T(128)} %concatenate.35.refs_0_, f32[16,48,512]{2,1,0:T(8,128)} %bitcast.101, f32[16,48,128]{2,1,0:T(8,128)} %bitcast.110, bf16[16,48,640]{2,1,0:T(8,128)(2,1)} %get-tuple-element.111.refs_3_, ...), custom_call_target="tpu_custom_call" | custom-call | flops 2000000000 | bytes 6000000 | tf_op jit(solution)/shard_map/pallas_call | solution.py:574
  303.5 6.4 %collective-permute-done.19 = bf16[4,432,384]{2,1,0:T(8,128)(2,1)} collective-permute-done((bf16[4,432,384]{2,1,0:T(8,128)(2,1)}, bf16[4,432,384]{2,1,0:T(8,128)(2,1)}, u32[]{:S(2)}, u32[]{:S(2)}) %collective-permute-start.19) | collective-permute-done | bytes 1327136 | tf_op jit(solution)/shard_map/ppermute | solution.py:1323
  309.8 25.5 %shard_map.476 = (bf16[16,224,256]{2,1,0:T(8,128)(2,1)}, bf16[16,96,768]{2,1,0:T(8,128)(2,1)}) custom-call(s32[13]{0:T(128)} %concatenate.35.refs_0_, bf16[16,112,256]{2,1,0:T(8,128)(2,1)} %all-to-all-done.5.refs_1_, f32[16,96,512]{2,1,0:T(8,128)} %get-tuple-element.100.refs_2_, bf16[16,96,128]{2,1,0:T(8,128)(2,1)} %collective-permute-done.20.refs_3_, ...), custom_call_target="tpu_custom_call" | custom-call | flops 99999997952 | bytes 300000000 | tf_op jit(solution)/shard_map/pallas_call | solution.py:574
  335.3 13.3 %all-to-all-start.6 = ((bf16[16,224,256]{2,1,0:T(8,128)(2,1)}), bf16[16,224,256]{2,1,0:T(8,128)(2,1)S(1)}, u32[]{:S(2)}, u32[]{:S(2)}) async-start(bf16[16,224,256]{2,1,0:T(8,128)(2,1)} %get-tuple-element.116), calls=%async_computation.6 | async-start | bytes 3670016 | tf_op jit(solution)/shard_map/all_to_all | solution.py:1163
  348.7 3.8 add_convert_fusion
  366.1 8.7 %shard_map.477 = (f32[33,64]{1,0:T(8,128)}, f32[64,64]{1,0:T(8,128)}, f32[64,48]{1,0:T(8,128)}, f32[8,256]{1,0:T(8,128)}, f32[48,1]{1,0:T(8,128)}) custom-call(f32[48,4096]{1,0:T(8,128)} %get-tuple-element.120.d_ref, f32[48,4096]{1,0:T(8,128)} %get-tuple-element.181.raw_ref, f32[48,4096]{1,0:T(8,128)} %get-tuple-element.169.fall_ref, f32[64,4096]{1,0:T(8,128)} %copy-done.2, ...), custom_call_target="tpu_custom_call" | custom-call | flops 10000000 | bytes 30000 | tf_op jit(solution)/shard_map/pallas_call | solution.py:336
  379.7 6.3 %collective-permute-done.28 = f32[9568]{0:T(1024)S(1)} collective-permute-done((f32[9568]{0:T(1024)S(1)}, f32[9568]{0:T(1024)S(1)}, u32[]{:S(2)}, u32[]{:S(2)}) %collective-permute-start.28) | collective-permute-done | bytes 38304 | tf_op jit(solution)/shard_map/ppermute | solution.py:1333
  389.9 5.9 %all-to-all-start.7 = ((bf16[8,176,384]{2,1,0:T(8,128)(2,1)}), bf16[8,176,384]{2,1,0:T(8,128)(2,1)S(1)}, u32[]{:S(2)}, u32[]{:S(2)}) async-start(bf16[8,176,384]{2,1,0:T(8,128)(2,1)} %pad_maximum_fusion), calls=%async_computation.7 | async-start | bytes 2162688 | tf_op jit(solution)/shard_map/all_to_all | solution.py:1357
  404.0 37.2 %all-to-all-done.7 = bf16[8,176,384]{2,1,0:T(8,128)(2,1)S(1)} async-done(((bf16[8,176,384]{2,1,0:T(8,128)(2,1)}), bf16[8,176,384]{2,1,0:T(8,128)(2,1)S(1)}, u32[]{:S(2)}, u32[]{:S(2)}) %all-to-all-start.7) | async-done | bytes 1081376 | tf_op jit(solution)/shard_map/all_to_all | solution.py:1357
  (236 shorter events, 87.3 us)
Async XLA Ops:
  9.6 38.4 %all-to-all-start = ((bf16[16,96,256]{2,1,0:T(8,128)(2,1)}), bf16[16,96,256]{2,1,0:T(8,128)(2,1)S(1)}, u32[]{:S(2)}, u32[]{:S(2)}) async-start(bf16[16,96,256]{2,1,0:T(8,128)(2,1)} %bitcast.5), calls=%async_computation | async-start | bytes 1572864 | tf_op jit(solution)/shard_map/all_to_all | solution.py:1163
  17.0 88.2 %all-gather.3.cloned.1.call-start = ((), (), s32[]{:S(2)}) async-start(), calls=%async_computation.10 | async-start | bytes 1658880 | tf_op jit(solution)/shard_map/all_gather | solution.py:1273
  17.6 18.9 %collective-permute-start.1 = (bf16[176,768]{1,0:T(8,128)(2,1)S(1)}, bf16[176,768]{1,0:T(8,128)(2,1)S(1)}, u32[]{:S(2)}, u32[]{:S(2)}) collective-permute-start(bf16[176,768]{1,0:T(8,128)(2,1)S(1)} %fusion.9.refs_0_), channel_id=1, source_target_pairs={{0,4},{1,5},{4,8},{5,9},{8,12},{9,13},{12,14},{13,15},{14,10},{15,... | collective-permute-start | bytes 811016 | tf_op jit(solution)/shard_map/ppermute | solution.py:1111
  19.5 22.9 %collective-permute-start.4 = (bf16[176,768]{1,0:T(8,128)(2,1)S(1)}, bf16[176,768]{1,0:T(8,128)(2,1)S(1)}, u32[]{:S(2)}, u32[]{:S(2)}) collective-permute-start(bf16[176,768]{1,0:T(8,128)(2,1)S(1)} %fusion.9.refs_0_), channel_id=1, source_target_pairs={{0,2},{1,3},{4,0},{5,1},{8,4},{9,5},{12,8},{13,9},{14,12},{15,13},... | collective-permute-start | bytes 811016 | tf_op jit(solution)/shard_map/ppermute | solution.py:1111
  36.5 11.5 %collective-permute-start.2 = (bf16[176,768]{1,0:T(8,128)(2,1)S(1)}, bf16[176,768]{1,0:T(8,128)(2,1)S(1)}, u32[]{:S(2)}, u32[]{:S(2)}) collective-permute-start(bf16[176,768]{1,0:T(8,128)(2,1)S(1)} %collective-permute-done.1.refs_1_), channel_id=1, source_target_pairs={{0,4},{1,5},{4,8},{5,9},{8,12},{9,13},{12,14},{13,15},{14,10},{15,... | collective-permute-start | bytes 811016 | tf_op jit(solution)/shard_map/ppermute | solution.py:1111
  42.4 8.5 %collective-permute-start.5 = (bf16[176,768]{1,0:T(8,128)(2,1)S(1)}, bf16[176,768]{1,0:T(8,128)(2,1)S(1)}, u32[]{:S(2)}, u32[]{:S(2)}) collective-permute-start(bf16[176,768]{1,0:T(8,128)(2,1)S(1)} %collective-permute-done.4.refs_4_), channel_id=1, source_target_pairs={{0,2},{1,3},{4,0},{5,1},{8,4},{9,5},{12,8},{13,9},{14,12},{15,13},... | collective-permute-start | bytes 811016 | tf_op jit(solution)/shard_map/ppermute | solution.py:1111
  48.0 11.7 %collective-permute-start.3 = (bf16[176,768]{1,0:T(8,128)(2,1)S(1)}, bf16[176,768]{1,0:T(8,128)(2,1)S(1)}, u32[]{:S(2)}, u32[]{:S(2)}) collective-permute-start(bf16[176,768]{1,0:T(8,128)(2,1)S(1)} %collective-permute-done.2.refs_2_), channel_id=1, source_target_pairs={{0,4},{1,5},{4,8},{5,9},{8,12},{9,13},{12,14},{13,15},{14,10},{15,... | collective-permute-start | bytes 811016 | tf_op jit(solution)/shard_map/ppermute | solution.py:1111
  50.9 7.2 %collective-permute-start.6 = (bf16[176,768]{1,0:T(8,128)(2,1)S(1)}, bf16[176,768]{1,0:T(8,128)(2,1)S(1)}, u32[]{:S(2)}, u32[]{:S(2)}) collective-permute-start(bf16[176,768]{1,0:T(8,128)(2,1)S(1)} %collective-permute-done.5.refs_5_), channel_id=1, source_target_pairs={{0,2},{1,3},{4,0},{5,1},{8,4},{9,5},{12,8},{13,9},{14,12},{15,13},... | collective-permute-start | bytes 811016 | tf_op jit(solution)/shard_map/ppermute | solution.py:1111
  58.1 6.6 %collective-permute-start.8 = (bf16[96,768]{1,0:T(8,128)(2,1)S(1)}, bf16[96,768]{1,0:T(8,128)(2,1)S(1)}, u32[]{:S(2)}, u32[]{:S(2)}) collective-permute-start(bf16[96,768]{1,0:T(8,128)(2,1)S(1)} %slice.193), channel_id=1, source_target_pairs={{0,2},{1,3},{4,0},{5,1},{8,4},{9,5},{12,8},{13,9},{14,12},{15,13},... | collective-permute-start | bytes 442376 | tf_op jit(solution)/shard_map/ppermute | solution.py:1111
  93.3 26.4 %all-to-all-start.1 = ((bf16[16,96,256]{2,1,0:T(8,128)(2,1)}), bf16[16,96,256]{2,1,0:T(8,128)(2,1)S(1)}, u32[]{:S(2)}, u32[]{:S(2)}) async-start(bf16[16,96,256]{2,1,0:T(8,128)(2,1)} %get-tuple-element.82), calls=%async_computation.1 | async-start | bytes 1572864 | tf_op jit(solution)/shard_map/all_to_all | solution.py:1163
  105.2 44.7 %collective-permute-start.10 = (bf16[4,432,384]{2,1,0:T(8,128)(2,1)}, bf16[4,432,384]{2,1,0:T(8,128)(2,1)S(1)}, u32[]{:S(2)}, u32[]{:S(2)}) collective-permute-start(bf16[4,432,384]{2,1,0:T(8,128)(2,1)} %bitcast.124), channel_id=1, source_target_pairs={{0,16},{16,0},{1,17},{17,1},{2,18},{18,2},{3,19},{19,3},{4,20},{20... | collective-permute-start | bytes 3981320 | tf_op jit(solution)/shard_map/ppermute | solution.py:1284
  106.7 42.2 %collective-permute-start.11 = (bf16[4,432,384]{2,1,0:T(8,128)(2,1)}, bf16[4,432,384]{2,1,0:T(8,128)(2,1)}, u32[]{:S(2)}, u32[]{:S(2)}) collective-permute-start(bf16[4,432,384]{2,1,0:T(8,128)(2,1)} %bitcast.125), channel_id=1, source_target_pairs={{0,2},{1,3},{2,0},{3,1},{4,6},{5,7},{6,4},{7,5},{8,10},{9,11},{10,... | collective-permute-start | bytes 3981320 | tf_op jit(solution)/shard_map/ppermute | solution.py:1283
  119.7 30.2 %all-to-all-start.2 = ((bf16[16,96,256]{2,1,0:T(8,128)(2,1)}), bf16[16,96,256]{2,1,0:T(8,128)(2,1)S(1)}, u32[]{:S(2)}, u32[]{:S(2)}) async-start(bf16[16,96,256]{2,1,0:T(8,128)(2,1)} %bitcast.20), calls=%async_computation.2 | async-start | bytes 1572864 | tf_op jit(solution)/shard_map/all_to_all | solution.py:1163
  149.0 29.3 %collective-permute-start.14 = (bf16[4,432,384]{2,1,0:T(8,128)(2,1)}, bf16[4,432,384]{2,1,0:T(8,128)(2,1)S(1)}, u32[]{:S(2)}, u32[]{:S(2)}) collective-permute-start(bf16[4,432,384]{2,1,0:T(8,128)(2,1)} %collective-permute-done.11.refs_8_.refs_9_), channel_id=1, source_target_pairs={{0,16},{16,0},{1,17},{17,1},{2,18},{18,2},{3,19},{19,3},{4,20},{20... | collective-permute-start | bytes 3981320 | tf_op jit(solution)/shard_map/ppermute | solution.py:1292
  151.0 30.4 %all-to-all-start.3 = ((bf16[16,96,256]{2,1,0:T(8,128)(2,1)}), bf16[16,96,256]{2,1,0:T(8,128)(2,1)S(1)}, u32[]{:S(2)}, u32[]{:S(2)}) async-start(bf16[16,96,256]{2,1,0:T(8,128)(2,1)} %get-tuple-element.86), calls=%async_computation.3 | async-start | bytes 1572864 | tf_op jit(solution)/shard_map/all_to_all | solution.py:1163
  155.1 23.8 %collective-permute-start.12 = (bf16[4,432,384]{2,1,0:T(8,128)(2,1)}, bf16[4,432,384]{2,1,0:T(8,128)(2,1)}, u32[]{:S(2)}, u32[]{:S(2)}) collective-permute-start(bf16[4,432,384]{2,1,0:T(8,128)(2,1)} %bitcast.126), channel_id=1, source_target_pairs={{0,1},{1,0},{2,3},{3,2},{4,5},{5,4},{6,7},{7,6},{8,9},{9,8},{10,11... | collective-permute-start | bytes 3981320 | tf_op jit(solution)/shard_map/ppermute | solution.py:1268
  155.6 23.4 %collective-permute-start.13 = (bf16[4,432,384]{2,1,0:T(8,128)(2,1)}, bf16[4,432,384]{2,1,0:T(8,128)(2,1)}, u32[]{:S(2)}, u32[]{:S(2)}) collective-permute-start(bf16[4,432,384]{2,1,0:T(8,128)(2,1)} %collective-permute-done.11.refs_8_.refs_9_), channel_id=1, source_target_pairs={{0,1},{1,0},{2,3},{3,2},{4,5},{5,4},{6,7},{7,6},{8,9},{9,8},{10,11... | collective-permute-start | bytes 3981320 | tf_op jit(solution)/shard_map/ppermute | solution.py:1268
  155.7 23.3 %collective-permute-start.15 = (bf16[4,432,384]{2,1,0:T(8,128)(2,1)}, bf16[4,432,384]{2,1,0:T(8,128)(2,1)}, u32[]{:S(2)}, u32[]{:S(2)}) collective-permute-start(bf16[4,432,384]{2,1,0:T(8,128)(2,1)} %copy-done.46), channel_id=1, source_target_pairs={{0,1},{1,0},{2,3},{3,2},{4,5},{5,4},{6,7},{7,6},{8,9},{9,8},{10,11... | collective-permute-start | bytes 3981320 | tf_op jit(solution)/shard_map/ppermute | solution.py:1268
  231.4 23.5 %all-to-all-start.4 = ((bf16[16,96,256]{2,1,0:T(8,128)(2,1)}), bf16[16,96,256]{2,1,0:T(8,128)(2,1)S(1)}, u32[]{:S(2)}, u32[]{:S(2)}) async-start(bf16[16,96,256]{2,1,0:T(8,128)(2,1)} %get-tuple-element.91), calls=%async_computation.4 | async-start | bytes 1572864 | tf_op jit(solution)/shard_map/all_to_all | solution.py:1163
  236.3 46.0 %collective-permute-start.22 = (bf16[8,432,384]{2,1,0:T(8,128)(2,1)}, bf16[8,432,384]{2,1,0:T(8,128)(2,1)}, u32[]{:S(2)}, u32[]{:S(2)}) collective-permute-start(bf16[8,432,384]{2,1,0:T(8,128)(2,1)} %get-tuple-element.109), channel_id=1, source_target_pairs={{0,1},{1,0},{2,3},{3,2},{4,5},{5,4},{6,7},{7,6},{8,9},{9,8},{10,11... | collective-permute-start | bytes 7962632 | tf_op jit(solution)/shard_map/ppermute | solution.py:1268
  240.6 31.6 %collective-permute-start.18 = (bf16[4,432,384]{2,1,0:T(8,128)(2,1)}, bf16[4,432,384]{2,1,0:T(8,128)(2,1)}, u32[]{:S(2)}, u32[]{:S(2)}) collective-permute-start(bf16[4,432,384]{2,1,0:T(8,128)(2,1)} %get-tuple-element.153), channel_id=1, source_target_pairs={{0,16},{16,0},{1,17},{17,1},{2,18},{18,2},{3,19},{19,3},{4,20},{20... | collective-permute-start | bytes 3981320 | tf_op jit(solution)/shard_map/ppermute | solution.py:1322
  272.2 37.6 %all-to-all-start.5 = ((bf16[16,112,256]{2,1,0:T(8,128)(2,1)}), bf16[16,112,256]{2,1,0:T(8,128)(2,1)}, u32[]{:S(2)}, u32[]{:S(2)}) async-start(bf16[16,112,256]{2,1,0:T(8,128)(2,1)} %get-tuple-element.97), calls=%async_computation.5 | async-start | bytes 1835008 | tf_op jit(solution)/shard_map/all_to_all | solution.py:1163
  278.1 31.7 %collective-permute-start.19 = (bf16[4,432,384]{2,1,0:T(8,128)(2,1)}, bf16[4,432,384]{2,1,0:T(8,128)(2,1)}, u32[]{:S(2)}, u32[]{:S(2)}) collective-permute-start(bf16[4,432,384]{2,1,0:T(8,128)(2,1)} %get-tuple-element.98), channel_id=1, source_target_pairs={{0,16},{16,0},{1,17},{17,1},{2,18},{18,2},{3,19},{19,3},{4,20},{20... | collective-permute-start | bytes 3981320 | tf_op jit(solution)/shard_map/ppermute | solution.py:1323
  279.6 9.3 %collective-permute-start.21 = (f32[768,128]{1,0:T(8,128)}, f32[768,128]{1,0:T(8,128)S(1)}, u32[]{:S(2)}, u32[]{:S(2)}) collective-permute-start(f32[768,128]{1,0:T(8,128)} %get-tuple-element.107), channel_id=1, source_target_pairs={{1,0},{2,1},{3,2},{4,3},{5,4},{6,5},{7,6},{8,7},{9,8},{10,9},{11,1... | collective-permute-start | bytes 1179656 | tf_op jit(solution)/shard_map/ppermute | solution.py:1310
  280.9 28.9 %collective-permute-start.20 = (bf16[16,96,128]{2,1,0:T(8,128)(2,1)}, bf16[16,96,128]{2,1,0:T(8,128)(2,1)}, u32[]{:S(2)}, u32[]{:S(2)}) collective-permute-start(bf16[16,96,128]{2,1,0:T(8,128)(2,1)} %get-tuple-element.101), channel_id=1, source_target_pairs={{1,0},{2,1},{3,2},{4,3},{5,4},{6,5},{7,6},{8,7},{9,8},{10,9},{11,1... | collective-permute-start | bytes 1179656 | tf_op jit(solution)/shard_map/ppermute | solution.py:1287
  285.5 49.8 %collective-permute-start.23 = (bf16[4,432,384]{2,1,0:T(8,128)(2,1)}, bf16[4,432,384]{2,1,0:T(8,128)(2,1)S(1)}, u32[]{:S(2)}, u32[]{:S(2)}) collective-permute-start(bf16[4,432,384]{2,1,0:T(8,128)(2,1)} %add_convert_fusion.1), channel_id=1, source_target_pairs={{0,2},{1,3},{2,0},{3,1},{4,6},{5,7},{6,4},{7,5},{8,10},{9,11},{10,... | collective-permute-start | bytes 3981320 | tf_op jit(solution)/shard_map/ppermute | solution.py:1389
  335.3 54.6 %all-to-all-start.6 = ((bf16[16,224,256]{2,1,0:T(8,128)(2,1)}), bf16[16,224,256]{2,1,0:T(8,128)(2,1)S(1)}, u32[]{:S(2)}, u32[]{:S(2)}) async-start(bf16[16,224,256]{2,1,0:T(8,128)(2,1)} %get-tuple-element.116), calls=%async_computation.6 | async-start | bytes 3670016 | tf_op jit(solution)/shard_map/all_to_all | solution.py:1163
  348.6 93.5 %reduce-scatter.2.cloned.1.call-start = ((), (), s32[]{:S(2)}) async-start(), calls=%async_computation.9 | async-start | bytes 1658880 | tf_op jit(solution)/shard_map/reduce_scatter | solution.py:1404
  353.9 6.1 %collective-permute-start.26 = (bf16[8,96,768]{2,1,0:T(8,128)(2,1)S(1)}, bf16[8,96,768]{2,1,0:T(8,128)(2,1)}, u32[]{:S(2)}, u32[]{:S(2)}) collective-permute-start(bf16[8,96,768]{2,1,0:T(8,128)(2,1)S(1)} %dynamic-slice_bitcast_fusion), channel_id=1, source_target_pairs={{0,1},{1,0},{2,3},{3,2},{4,5},{5,4},{6,7},{7,6},{8,9},{9,8},{10,11... | collective-permute-start | bytes 3538952 | tf_op jit(solution)/shard_map/ppermute | solution.py:1349
  363.2 24.1 %collective-permute-start.27 = (bf16[8,144,384]{2,1,0:T(8,128)(2,1)}, bf16[8,144,384]{2,1,0:T(8,128)(2,1)}, u32[]{:S(2)}, u32[]{:S(2)}) collective-permute-start(bf16[8,144,384]{2,1,0:T(8,128)(2,1)} %fusion.4), channel_id=1, source_target_pairs={{0,16},{16,0},{1,17},{17,1},{2,18},{18,2},{3,19},{19,3},{4,20},{20... | collective-permute-start | bytes 2654216 | tf_op jit(solution)/shard_map/ppermute | solution.py:1343
  379.0 7.0 %collective-permute-start.28 = (f32[9568]{0:T(1024)S(1)}, f32[9568]{0:T(1024)S(1)}, u32[]{:S(2)}, u32[]{:S(2)}) collective-permute-start(f32[9568]{0:T(1024)S(1)} %concatenate.43), channel_id=1, source_target_pairs={{0,16},{16,0},{1,17},{17,1},{2,18},{18,2},{3,19},{19,3},{4,20},{20... | collective-permute-start | bytes 114824 | tf_op jit(solution)/shard_map/ppermute | solution.py:1333
  389.9 51.3 %all-to-all-start.7 = ((bf16[8,176,384]{2,1,0:T(8,128)(2,1)}), bf16[8,176,384]{2,1,0:T(8,128)(2,1)S(1)}, u32[]{:S(2)}, u32[]{:S(2)}) async-start(bf16[8,176,384]{2,1,0:T(8,128)(2,1)} %pad_maximum_fusion), calls=%async_computation.7 | async-start | bytes 2162688 | tf_op jit(solution)/shard_map/all_to_all | solution.py:1357
  (58 other events, 603.8 us)
Sparse Core Ops, SparseCore 0:
  72.9 32.2 all-gather.2
  386.2 50.4 reduce-scatter.1

commit v4 on v3

--- a/solution.py
+++ b/solution.py
@@ -549,9 +549,18 @@
 
 
 def first_tokens(values, seqs):
-    width = values.shape[1] // seqs
-    second = pltpu.roll(values[:, width : width + LANE], LANE // 2, 1)
-    return jnp.where(lanes_of((values.shape[0], LANE)) < LANE // 2, values[:, :LANE], second)
+    rows, width = values.shape[0], values.shape[1] // seqs
+    pad = jnp.zeros((LANE - rows, LANE), f32)
+    heads = []
+    for s in range(seqs):
+        tile = values[:, s * width : s * width + LANE]
+        heads.append((jnp.concatenate([tile, pad], axis=0) if rows < LANE else tile).T[:8])
+    return jnp.concatenate(heads, axis=0)
+
+
+def token_columns(heads, rows):
+    gap = jnp.zeros((LANE // 2 - 8, LANE), f32)
+    return jnp.concatenate([heads[:8], gap, heads[8:], gap], axis=0).T[:rows]
 
 
 def whole(a):
@@ -608,7 +617,7 @@
         sd((devices, chans, cols + LANE), bf16),
         sd((devices, 2 * chans, cols + LANE), bf16),
         sd((devices, rows, width), bf16),
-        sd((devices, 2 * chans, LANE), bf16),
+        sd((devices, 8 * seqs, LANE), bf16),
     )
     small = pl.BlockSpec((turns, PRM, LANE), lambda i, t: (0, 0, 0), pipeline_mode=pl.Buffered(1))
     return chip_call(
@@ -631,16 +640,16 @@
         refs = refs[4 * segments :]
     layer_ref, d_conv_ref, d_res_ref, p0_ref, p0h_ref = refs[:5]
     grads, refs = [refs[5 + 2 * p : 7 + 2 * p] for p in range(pieces)], refs[5 + 2 * pieces :]
-    cs, res, ds, xb, db, gb, acc_out, acc_in, folds, up_folds, stats, out_w32 = refs[:12]
-    out_w_refs = refs[12:]
+    cs, res, ds, xb, db, gb, acc_out, acc_in, folds, up_folds, stats, out_w32, out_w_ref, gs = refs
     devices, _, width = x_ref.shape
     dim, cols = d_res_ref.shape
     chans = dim // devices
-    hid = weights[0][0][0][0].shape[1] // 2
+    hid = weights[0][0][0][0].shape[1] // 2 * pieces
     turns = devices // 2
-    part = dim // pieces
+    part, some_hid, some_out = dim // pieces, hid // pieces, chans // pieces
     group = table_ref[turns + 2 + seqs] if pieces == 2 else 0
-    columns = [pl.ds(pl.multiple_of((group if p == 0 else 1 - group) * part, LANE), part) for p in range(pieces)]
+    halves = [group, 1 - group][:pieces]
+    columns = [pl.ds(pl.multiple_of(h * part, LANE), part) for h in halves]
     step = pl.program_id(0)
     last = pl.num_programs(0) - 1
     lane = lanes_of((1, cols))
@@ -663,24 +672,19 @@
             return carry
 
         lax.fori_loop(0, devices, gather, 0)
-        for piece, out_w_ref in zip(weights, out_w_refs):
+        for piece, h in zip(weights, halves):
             for core, parts in enumerate(piece):
                 turn = 0
                 for _, out_rows in parts:
                     for n in range(out_rows.shape[0]):
                         device, _ = slots(table_ref, turns, turn)[core]
-                        out_w32[device_rows(device), :] = out_rows[n].astype(f32)
+                        at = pl.ds(pl.multiple_of(device * chans + h * some_out, 8), some_out)
+                        out_w32[at, :] = out_rows[n].astype(f32)
                         turn += 1
-
-            def narrow(i, carry):
-                at = chunk_rows(i)
-                out_w_ref[at, :] = out_w32[at, :].astype(bf16)
-                return carry
-
-            lax.fori_loop(0, dim // CHUNK, narrow, 0)
 
         def gated(i, carry):
             at = chunk_rows(i)
+            out_w_ref[at, :] = out_w32[at, :].astype(bf16)
             gb[at, :] = (cs[at, :] * gate_ref[at, :]).astype(bf16)
             d = ds[at, :]
             db[at, :] = d.astype(bf16)
@@ -689,8 +693,7 @@
             return carry
 
         lax.fori_loop(0, dim // CHUNK, gated, 0)
-        for at, out_w_ref in zip(columns, out_w_refs):
-            acc_out[at, :] = mm16(out_w_ref[...], gb[...], TN)
+        acc_out[...] = mm16(out_w_ref[...], gb[...], TN)
 
         def add(i, carry):
             at = chunk_rows(i)
@@ -716,17 +719,20 @@
     up_b = []
     for device, _ in pair:
         prm = prm_ref[device_rows(device), :]
-        up_b += [prm[:, 21 + m : 22 + m] for m in range(hid // chans)]
+        for h in halves:
+            for m in range(some_hid // chans):
+                first, second = 21 + m, 21 + m + (pieces - 1) * some_hid // chans
+                up_b.append(jnp.where(h == 0, prm[:, first : first + 1], prm[:, second : second + 1]))
     up_b = jnp.concatenate(up_b, axis=0)
 
     def now(parts, rows):
         blocks = [ref[0, rows, :] for ref, _ in parts]
         return blocks[0] if len(blocks) == 1 else jnp.where(step < turns // 2, blocks[0], blocks[1])
 
-    ups = [jnp.concatenate([now(parts, slice(0, hid)) for parts in piece], axis=0) for piece in weights]
-    downs = [jnp.concatenate([now(parts, slice(hid, 2 * hid)) for parts in piece], axis=0) for piece in weights]
-    u = sum(mm16(up, xb[at, :], NN) for up, at in zip(ups, columns)) + up_b
-    d_act = sum(mm16(down, db[at, :], NN) for down, at in zip(downs, columns))
+    up = jnp.concatenate([now(piece[core], slice(0, some_hid)) for core in range(2) for piece in weights], axis=0)
+    down = jnp.concatenate([now(piece[core], slice(some_hid, 2 * some_hid)) for core in range(2) for piece in weights], axis=0)
+    u = mm16(up, xb[...], NN) + up_b
+    d_act = mm16(down, db[...], NN)
     a, k = 0.044715, math.sqrt(2.0 / math.pi)
     sq = u * u
     t = jnp.tanh(u * (k + (k * a) * sq))
@@ -735,17 +741,19 @@
     d_u = d_act * (half + 0.5 * u * (1.0 - t * t) * (k + (3.0 * k * a) * sq))
     d_low = d_u.astype(bf16)
     fold = folded(d_u)
-    for n, (device, _) in enumerate(pair):
-        up_folds[pl.ds(pl.multiple_of(device * hid, 8), hid), :] = fold[n * hid : (n + 1) * hid]
-    for up, down, at, g_refs in zip(ups, downs, columns, grads):
-        g_up = mm16(d_low, xb[at, :], NT).astype(bf16)
-        g_down = mm16(act, db[at, :], NT).astype(bf16)
-        for n, g_ref in enumerate(g_refs):
-            mine = slice(n * hid, (n + 1) * hid)
-            g_ref[step, :hid, :] = g_up[mine]
-            g_ref[step, hid : 2 * hid, :] = g_down[mine]
-        acc_out[at, :] += mm16(down, act, TN)
-        acc_in[at, :] += mm16(up, d_low, TN)
+    acc_out[...] += mm16(down, act, TN)
+    acc_in[...] += mm16(up, d_low, TN)
+    spots = [(n, p, h) for n in range(2) for p, h in enumerate(halves)]
+    for n, p, h in spots:
+        rows = slice((n * pieces + p) * some_hid, (n * pieces + p + 1) * some_hid)
+        up_folds[pl.ds(pl.multiple_of(pair[n][0] * hid + h * some_hid, 8), some_hid), :] = fold[rows]
+    for left, right, first in ((d_low, xb, 0), (act, db, hid)):
+        gs[...] = mm16(left, right[...], NT).astype(bf16)
+        for n, p, h in spots:
+            rows = slice((n * pieces + p) * some_hid, (n * pieces + p + 1) * some_hid)
+            at = pl.ds(pl.multiple_of(first + h * some_hid, some_hid), some_hid)
+            for g_refs, some in zip(grads, columns):
+                g_refs[n][step, at, :] = gs[rows, some]
 
     @pl.when(step == last)
     def _():
@@ -780,21 +788,18 @@
         lax.fori_loop(0, dim // CHUNK, residual, 0)
         for n in range(dim // 256):
             some = slice(n * 256, (n + 1) * 256)
-            acc_in[some, :] = sum(mm16(w[some, :], db[at, :], NN) for w, at in zip(out_w_refs, columns))
-        for at, g_refs in zip(columns, grads):
-            for n in range(dim // 256):
-                some = slice(n * 256, (n + 1) * 256)
-                out_w32[some, :] = mm16(gb[some, :], db[at, :], NT)
+            acc_in[some, :] = mm16(out_w_ref[some, :], db[...], NN)
+            out_w32[some, :] = mm16(gb[some, :], db[...], NT)
+        for g_refs, at in zip(grads, columns):
             for turn in range(turns):
                 for g_ref, (device, _) in zip(g_refs, slots(table_ref, turns, turn)):
-                    g_ref[turn, 2 * hid :, :] = out_w32[device_rows(device), :].astype(bf16)
+                    g_ref[turn, 2 * hid :, :] = out_w32[device_rows(device), at].astype(bf16)
 
         def products(i, carry):
             at = chunk_rows(i)
             d = acc_in[at, :]
             p0 = d * cs[at, :]
             p0_ref[at, :] = p0
-            p0h_ref[at, :] = first_tokens(p0, seqs)
             acc_in[at, :] = d * gate_ref[at, :]
             return carry
 
@@ -802,6 +807,7 @@
 
         def scatter(d, carry):
             at = device_rows(d)
+            p0h_ref[d] = first_tokens(p0_ref[at, :], seqs).astype(bf16)
             layer_ref[d, : seqs * chans, :] = stacked(acc_out[at, :], seqs).astype(bf16)
             d_conv_ref[d] = stacked(acc_in[at, :], seqs).astype(bf16)
             totals = [padded_totals(folds[q, at, :], width)[0] for q in range(4)]
@@ -818,14 +824,14 @@
     chans = dim // devices
     turns = devices // 2
     pieces = len(matrices)
-    part = dim // pieces
+    part, some_hid, some_out = dim // pieces, hid // pieces, chans // pieces
     sd = jax.ShapeDtypeStruct
     out = (
         sd((devices, rows + SUM_ROWS, width), bf16),
         sd((devices, rows, width), bf16),
         sd((dim, cols), f32),
         sd((dim, cols), f32),
-        sd((dim, LANE), f32),
+        sd((devices, 8 * seqs, LANE), bf16),
     ) + (sd((turns, 2 * hid + chans, part), bf16),) * (2 * pieces)
     big = pltpu.VMEM((dim, cols), f32)
     low = pltpu.VMEM((dim, cols), bf16)
@@ -838,9 +844,9 @@
                 count = a.shape[0]
                 args += [a, a]
                 specs += [
-                    pl.BlockSpec((1, 2 * hid, part), lambda i, t, f=first, c=count: (jnp.clip(i - f, 0, c - 1), 0, 0)),
+                    pl.BlockSpec((1, 2 * some_hid, dim), lambda i, t, f=first, c=count: (jnp.clip(i - f, 0, c - 1), 0, 0)),
                     pl.BlockSpec(
-                        (count, chans, part), lambda i, t: (0, 2 * hid // chans, 0), pipeline_mode=pl.Buffered(1)
+                        (count, some_out, dim), lambda i, t: (0, 2 * some_hid // some_out, 0), pipeline_mode=pl.Buffered(1)
                     ),
                 ]
                 first += count
@@ -855,9 +861,9 @@
         tuple(whole(o) for o in out),
         [
             big, big, big, low, low, low, big, big, pltpu.VMEM((4, dim, LANE), f32),
-            pltpu.VMEM((devices * hid, LANE), f32), pltpu.VMEM((16, cols), f32), pltpu.VMEM((dim, part), f32),
-        ]
-        + [pltpu.VMEM((dim, part), bf16)] * pieces,
+            pltpu.VMEM((devices * hid, LANE), f32), pltpu.VMEM((16, cols), f32), pltpu.VMEM((dim, dim), f32),
+            pltpu.VMEM((dim, dim), bf16), pltpu.VMEM((2 * hid, dim), bf16),
+        ],
     )
 
 
@@ -905,7 +911,7 @@
     for w_ref, (device, g) in zip((own_ref, other_ref), slots(table_ref, turns, step)):
         prm = prm_ref[pl.ds(pl.multiple_of(device * chans, 8), chans), :]
         d_low, totals = short_back(
-            seqs, prm, (0,), (p0_ref[g],), (p0h_ref[g],), projx_ref[g].astype(f32), cols // seqs, cols
+            seqs, prm, (0,), (p0_ref[g],), (token_columns(p0h_ref[g].astype(f32), chans),), projx_ref[g].astype(f32), cols // seqs, cols
         )
         sums_ref[g] = totals[0]
         acc[...] += mm16(w_ref[0, PRM : PRM + chans, :], d_low, TN)
@@ -957,7 +963,7 @@
         second = pltpu.roll(square[chans : 2 * chans], LANE // 2, 1)
         d_head = jnp.where(lanes_of((chans, LANE)) < LANE // 2, square[:chans], second)
         pair = pair_ref[g]
-        pair_head = heads_ref[g].astype(f32)
+        pair_head = token_columns(heads_ref[g].astype(f32), 2 * chans)
         d_short = (d_mixed * pair[chans:], d_mixed * pair[:chans])
         head = (d_head * pair_head[chans:], d_head * pair_head[:chans])
         d_low, totals = short_back(seqs, prm, (1, 2), d_short, head, projx_ref[g].astype(f32), width, cols)
@@ -1236,7 +1242,22 @@
     table = jnp.concatenate(
         [turns, jnp.stack([core, place]).astype(jnp.int32), seq_lengths, batch.astype(jnp.int32).reshape(1)]
     )
-    first = RingGather(jnp.concatenate([small, in_rows], axis=0), ring)
+    late = [up_weight, down_weight, out_weight]
+    stepped = groups == 2 and chips == 8 and dim % (2 * LANE) == 0
+    beside = [(i, i ^ 2) for i in range(devices)]
+    along = [list(range(k, devices, 4)) for k in range(4)]
+
+    def to_partner(values):
+        return lax.ppermute(values, "chan", partner)
+
+    if stepped:
+        late = [lax.dynamic_slice_in_dim(a, batch * (a.shape[0] // 2), a.shape[0] // 2, 0) for a in late]
+        late = jnp.concatenate(late, axis=0)
+        near = lax.all_gather(late, "chan", axis=0, axis_index_groups=along)
+    else:
+        late = jnp.concatenate(late, axis=0)
+        late = lax.all_gather(late, "chan", axis=0).reshape((chips, 2) + late.shape)
+    first = RingGather(after(jnp.concatenate([small, in_rows], axis=0), late) if stepped else jnp.concatenate([small, in_rows], axis=0), ring)
     first.advance(chips // 8)
     x = exchange(to_blocks(layer_in))
     rows = seqs * chans
@@ -1259,20 +1280,6 @@
     in_own, in_other = both_cores(first.shards())
     bias_col = conv_bias[:, None]
 
-    late = jnp.concatenate([up_weight, down_weight, out_weight], axis=0)
-    stepped = groups == 2 and chips == 8 and dim % (2 * LANE) == 0
-    beside = [(i, i ^ 2) for i in range(devices)]
-    along = [list(range(k, devices, 4)) for k in range(4)]
-
-    def to_partner(values):
-        return lax.ppermute(values, "chan", partner)
-
-    if stepped:
-        part = dim // 2
-        late = lax.dynamic_slice_in_dim(late, batch * part, part, 1)
-        near = lax.all_gather(late, "chan", axis=0, axis_index_groups=along)
-    else:
-        late = lax.all_gather(late, "chan", axis=0).reshape((chips, 2) + late.shape)
     prm, xn1, stat1, gate, pair, projx0, projx, mixed, heads = front(
         table, x, xh, in_own, in_other, filt_spec, seqs
     )
@@ -1286,7 +1293,7 @@
     backward_hop = [(i + 1, i) for i in range(devices - 1)]
     heads = lax.ppermute(heads, "chan", backward_hop)
     conv_chan, mixed_spec = conv_forward(mixed_chan, filt_spec, bias_col, seqs)
-    conv = exchange(after(conv_chan, near_across, cot) if stepped else conv_chan)
+    conv = exchange(after(conv_chan, near_across, cot, heads) if stepped else conv_chan)
     if stepped:
         far, near_across = after(far, conv_chan), after(near_across, conv_chan)
         far_across = lax.ppermute(far, "batch", swap)
@@ -1369,11 +1376,11 @@
         d_conv_chan, mixed_chan, mixed_spec, filt_spec, bias_col, seqs
     )
     if stepped:
-        d_mixed_chan = after(d_mixed_chan, far_theirs)
+        d_mixed_chan = after(d_mixed_chan, far_theirs, p0h)
         far_mine = added(mine[half:], mine_in[half:], far_theirs)
         p0h = after(p0h, far_mine)
     g_in0, sums0, acc0 = back_gate(
-        table, p0.reshape(devices, chans, cols), p0h.reshape(devices, chans, LANE), projx0, in_own, in_other, prm, xn1, seqs
+        table, p0.reshape(devices, chans, cols), p0h, projx0, in_own, in_other, prm, xn1, seqs
     )
     g_in0 = over_chip(g_in0)
     d_mixed = exchange(d_mixed_chan)
@@ -1385,7 +1392,6 @@
         jnp.concatenate(shared + [g_conv_bias[:, 0], g_decay[:, 0], g_filt_out.reshape(-1)])
     )
     if stepped:
-        d_mixed = after(d_mixed, near_theirs)
         far_mine = lax.ppermute(far_mine, "chan", beside)
     else:
         chan_groups = [list(range(q, devices, 2)) for q in range(2)]
@@ -1395,7 +1401,7 @@
         table, d_mixed, pair, heads, projx, in_own, in_other, prm, xn1, x, stat1, d_res, acc0, sums0, layer, seqs
     )
     if stepped:
-        tail = after(tail, far_mine)
+        tail = after(tail, far_mine, near_theirs)
         early = added(mine[:half], mine_in[:half], near_theirs, far_mine)
         g_in = after(g_in, early)
     tail = exchange(tail)
@@ -1418,7 +1424,7 @@
     if groups != 2:
         shared = shared / groups
     line = g_in.shape[2]
-    shared = jnp.pad(shared.astype(bf16), (0, -n_shared % (16 * line))).reshape(1, -1, line)
+    shared = jnp.pad(shared.astype(bf16), (0, -n_shared % (8 * line))).reshape(1, -1, line)
     shared = jnp.broadcast_to(shared, (devices // 2,) + shared.shape[1:])
     mine = 3 * chans
     in_grad = over_chips(jnp.concatenate([g_in, shared], axis=1))

time: 456 us -> 431 us (0.945)
  waiting for transfers between devices: 128 us -> 108 us
  Pallas kernels: 152 us -> 147 us
    all_to_all x1, waiting for transfers between devices: 37.2 us -> 27.7 us  [over_chips(): lax.all_to_all(both, 'chan', split_axis=0, concat_axis=0, tiled=True, axi...]
    ppermute x1, waiting for transfers between devices: 6.35 us -> 0.01 us  [on_device(): near_theirs = lax.ppermute(after(near_theirs, far_theirs), 'batch', swap)]
    ppermute x1, waiting for transfers between devices: 22.1 us -> 16.9 us  [on_device(): far_across = lax.ppermute(far, 'batch', swap)]
    pallas_call x4, Pallas kernels: 105 us -> 101 us  [chip_call(): pl.pallas_call(body, cost_estimate=takes(us), out_shape=out, grid_spec=pl...]
  transfers between devices with their start and end apart: 40 -> 40, of which waited for: 16 -> 19; matrix products, arithmetic and copies ran while one was open for 12% -> 13% of each run, Pallas kernels for 22% -> 23%
where the time goes in v4:
time: 431 us; the launch traced here: 429 us
  Pallas kernels  147 us (34%)
  waiting for transfers between devices  108 us (25%)
  starting transfers between devices  89.8 us (21%)
  local copies, waits for them, and re-layouts  31.8 us (7%)
  other arithmetic  22.6 us (5%)
  between operations  14.9 us (3%)
  matrix products  14.8 us (3%)
    pallas_call x4, Pallas kernels, chip_call(): pl.pallas_call(body, cost_estimate=takes(us), out_shape=out, grid_spec=pl...  101 us
    pallas_call x5, Pallas kernels, whole_call(): pl.pallas_call(body, cost_estimate=takes(us), out_shape=out_shape, in_spe...  46.9 us
    all_to_all x7, starting transfers between devices, exchange(): lax.all_to_all(values, 'chan', split_axis=0, concat_axis=0, tiled=True)  45.8 us
    all_to_all x1, waiting for transfers between devices, over_chips(): lax.all_to_all(both, 'chan', split_axis=0, concat_axis=0, tiled=True, axi...  27.7 us
    all_to_all x7, waiting for transfers between devices, exchange(): lax.all_to_all(values, 'chan', split_axis=0, concat_axis=0, tiled=True)  25.3 us
    ppermute x1, waiting for transfers between devices, on_device(): far_across = lax.ppermute(far, 'batch', swap)  16.9 us
    dot_general x3, matrix products, mm(): lax.dot_general(a, b, (dims, ((), ())), precision=highest, preferred_elem...  14.8 us
    ppermute x8, starting transfers between devices, ring_hop(): return lax.ppermute(values, 'chan', moves)  13.9 us
  transfers between devices with their start and end apart: 40, of which 19 were waited for; matrix products, arithmetic and copies ran while one was open for 13% of the time, Pallas kernels for 23%

profile of v4, /device:TPU:0, one launch (start us, length us, event | category | flops | bytes accessed | tf_op | source)
XLA Modules:
  0.0 429.3 jit_solution(15386781753406067678)
XLA Ops:
  9.6 7.5 %all-to-all-start = ((bf16[16,96,256]{2,1,0:T(8,128)(2,1)}), bf16[16,96,256]{2,1,0:T(8,128)(2,1)S(1)}, u32[]{:S(2)}, u32[]{:S(2)}) async-start(bf16[16,96,256]{2,1,0:T(8,128)(2,1)} %bitcast.5), calls=%async_computation | async-start | bytes 1572864 | tf_op jit(solution)/shard_map/all_to_all | solution.py:1169
  20.6 6.2 %multiply_cosine_fusion.1 = (f32[64,4096]{1,0:T(8,128)}, f32[64,4096]{1,0:T(8,128)S(1)}, f32[64,4096]{1,0:T(8,128)}) fusion(f32[64]{0:T(128)S(1)} %copy-done.32, f32[64]{0:T(128)S(1)} %copy-done.39, f32[33,4096]{1,0:T(8,128)S(1)} %copy-done.6, f32[33,64]{1,0:T(8,128)S(1)} %copy-done.30), kind=kOutput, calls=%fused_computation.24 | convolution fusion | flops 104333312 | bytes 3695360 | tf_op jit(solution)/shard_map/dot_general | solution.py:1061
  26.9 6.2 %multiply_cosine_fusion = (f32[64,4096]{1,0:T(8,128)}, f32[64,4096]{1,0:T(8,128)S(1)}, f32[64,4096]{1,0:T(8,128)}) fusion(f32[64]{0:T(128)S(1)} %copy-done.32, f32[64]{0:T(128)S(1)} %copy-done.40, f32[64,4096]{1,0:T(8,128)S(1)} %get-tuple-element.161.h1_ref, f32[64,64]{1,0:T(8,128)S(1)} %copy-done.23), kind=kOutput, calls=%fused_computation.22 | convolution fusion | flops 201850880 | bytes 4211200 | tf_op jit(solution)/shard_map/dot_general | solution.py:1061
  33.1 3.6 collective-permute-done.1.refs_1_
  36.6 5.9 %collective-permute-start.2 = (bf16[176,768]{1,0:T(8,128)(2,1)S(1)}, bf16[176,768]{1,0:T(8,128)(2,1)S(1)}, u32[]{:S(2)}, u32[]{:S(2)}) collective-permute-start(bf16[176,768]{1,0:T(8,128)(2,1)S(1)} %collective-permute-done.1.refs_1_), channel_id=1, source_target_pairs={{0,4},{1,5},{4,8},{5,9},{8,12},{9,13},{12,14},{13,15},{14,10},{15,... | collective-permute-start | bytes 811016 | tf_op jit(solution)/shard_map/ppermute | solution.py:1117
  45.0 3.1 collective-permute-done.2.refs_2_
  52.3 5.4 %shard_map.469.refs_7_.refs_1_.refs_3_ = f32[33,48,256]{2,1,0:T(8,128)} custom-call(f32[48,4096]{1,0:T(8,128)} %get-tuple-element.170.filter_ref, f32[33,1,256]{2,1,0:T(1,128)} %constant.94.clone.twist_ref.refs_3_.refs_5_, bf16[2,256,256]{2,1,0:T(8,128)(2,1)} %constant.95.clone.ahead_ref.refs_4_.refs_6_), custom_call_target="tpu_custom_call" | custom-call | flops 8000000000 | bytes 24000000 | tf_op jit(solution)/shard_map/pallas_call | solution.py:336
  60.4 4.4 %collective-permute-done.7 = bf16[80,768]{1,0:T(8,128)(2,1)S(1)} collective-permute-done((bf16[80,768]{1,0:T(8,128)(2,1)S(1)}, bf16[80,768]{1,0:T(8,128)(2,1)S(1)}, u32[]{:S(2)}, u32[]{:S(2)}) %collective-permute-start.7) | collective-permute-done | bytes 122912 | tf_op jit(solution)/shard_map/ppermute | solution.py:1117
  65.5 3.1 shard_map.470.refs_3_.refs_5_.refs_4_
  75.3 16.9 %shard_map.471 = (f32[768,32]{1,0:T(8,128)}, bf16[768,512]{1,0:T(8,128)(2,1)}, f32[16,512]{1,0:T(8,128)}, f32[16,48,512]{2,1,0:T(8,128)}, f32[16,96,512]{2,1,0:T...) custom-call(s32[13]{0:T(128)} %concatenate.35.refs_0_, ...), custom_call_target="tpu_custom_call" | custom-call | flops 99999997952 | bytes 300000000 | tf_op jit(solution)/shard_map/pallas_call | solution.py:583
  92.2 8.8 %all-to-all-start.1 = ((bf16[16,96,256]{2,1,0:T(8,128)(2,1)}), bf16[16,96,256]{2,1,0:T(8,128)(2,1)S(1)}, u32[]{:S(2)}, u32[]{:S(2)}) async-start(bf16[16,96,256]{2,1,0:T(8,128)(2,1)} %get-tuple-element.83), calls=%async_computation.1 | async-start | bytes 1572864 | tf_op jit(solution)/shard_map/all_to_all | solution.py:1169
  106.1 13.6 %all-to-all-done.1.refs_0_.refs_1_ = bf16[16,96,256]{2,1,0:T(8,128)(2,1)S(1)} async-done(((bf16[16,96,256]{2,1,0:T(8,128)(2,1)}), bf16[16,96,256]{2,1,0:T(8,128)(2,1)S(1)}, u32[]{:S(2)}, u32[]{:S(2)}) %all-to-all-start.1) | async-done | bytes 786464 | tf_op jit(solution)/shard_map/all_to_all | solution.py:1169
  119.8 5.5 %all-to-all-start.2 = ((bf16[16,96,256]{2,1,0:T(8,128)(2,1)}), bf16[16,96,256]{2,1,0:T(8,128)(2,1)S(1)}, u32[]{:S(2)}, u32[]{:S(2)}) async-start(bf16[16,96,256]{2,1,0:T(8,128)(2,1)} %bitcast.20), calls=%async_computation.2 | async-start | bytes 1572864 | tf_op jit(solution)/shard_map/all_to_all | solution.py:1169
  125.3 13.3 %shard_map.472 = (bf16[16,96,256]{2,1,0:T(8,128)(2,1)}, f32[33,96,256]{2,1,0:T(8,128)}) custom-call(bf16[16,96,256]{2,1,0:T(8,128)(2,1)} %copy-done.12, f32[33,48,256]{2,1,0:T(8,128)} %shard_map.469.refs_7_.refs_1_.refs_3_, f32[48,1]{1,0:T(8,128)} %copy.64.refs_2_.refs_4_, f32[33,1,256]{2,1,0:T(1,128)} %constant.94.clone.twist_ref.refs_3_.refs_5_, ...), custom_call_target="tpu_custom_call" | custom-call | flops 99999997952 | bytes 300000000 | tf_op jit(solution)/shard_map/pallas_call | solution.py:336
  138.6 9.5 %collective-permute-done.12.refs_8_.refs_9_ = bf16[4,216,768]{2,1,0:T(8,128)(2,1)} collective-permute-done((bf16[4,216,768]{2,1,0:T(8,128)(2,1)}, bf16[4,216,768]{2,1,0:T(8,128)(2,1)}, u32[]{:S(2)}, u32[]{:S(2)}) %collective-permute-start.12) | collective-permute-done | bytes 1327136 | tf_op jit(solution)/shard_map/ppermute | solution.py:1290
  153.6 6.5 %all-to-all-start.3 = ((bf16[16,96,256]{2,1,0:T(8,128)(2,1)}), bf16[16,96,256]{2,1,0:T(8,128)(2,1)S(1)}, u32[]{:S(2)}, u32[]{:S(2)}) async-start(bf16[16,96,256]{2,1,0:T(8,128)(2,1)} %get-tuple-element.88), calls=%async_computation.3 | async-start | bytes 1572864 | tf_op jit(solution)/shard_map/all_to_all | solution.py:1169
  161.1 16.9 %collective-permute-done.15.refs_16_.refs_17_ = bf16[4,216,768]{2,1,0:T(8,128)(2,1)S(1)} collective-permute-done((bf16[4,216,768]{2,1,0:T(8,128)(2,1)}, bf16[4,216,768]{2,1,0:T(8,128)(2,1)S(1)}, u32[]{:S(2)}, u32[]{:S(2)}) %collective-permute-start.15) | collective-permute-done | bytes 1327136 | tf_op jit(solution)/shard_map/ppermute | solution.py:1299
  182.1 44.2 %shard_map.473 = (bf16[16,112,256]{2,1,0:T(8,128)(2,1)}, bf16[16,96,256]{2,1,0:T(8,128)(2,1)}, f32[768,512]{1,0:T(8,128)}, f32[768,512]{1,0:T(8,128)}, bf16[16,1...) custom-call(s32[13]{0:T(128)} %concatenate.36.refs_0_, ...), custom_call_target="tpu_custom_call" | custom-call | flops 35999997952 | bytes 108000000 | tf_op jit(solution)/shard_map/pallas_call | solution.py:583
  226.5 5.0 %all-to-all-start.4 = ((bf16[16,96,256]{2,1,0:T(8,128)(2,1)}), bf16[16,96,256]{2,1,0:T(8,128)(2,1)S(1)}, u32[]{:S(2)}, u32[]{:S(2)}) async-start(bf16[16,96,256]{2,1,0:T(8,128)(2,1)} %get-tuple-element.93), calls=%async_computation.4 | async-start | bytes 1572864 | tf_op jit(solution)/shard_map/all_to_all | solution.py:1169
  233.2 4.0 add_convert_fusion.2
  238.8 11.5 %all-to-all-done.4.refs_0_ = bf16[16,96,256]{2,1,0:T(8,128)(2,1)S(1)} async-done(((bf16[16,96,256]{2,1,0:T(8,128)(2,1)}), bf16[16,96,256]{2,1,0:T(8,128)(2,1)S(1)}, u32[]{:S(2)}, u32[]{:S(2)}) %all-to-all-start.4) | async-done | bytes 786464 | tf_op jit(solution)/shard_map/all_to_all | solution.py:1169
  251.1 16.4 %shard_map.474 = (bf16[16,112,256]{2,1,0:T(8,128)(2,1)}, f32[48,4096]{1,0:T(8,128)}, f32[48,1]{1,0:T(8,128)}) custom-call(bf16[16,96,256]{2,1,0:T(8,128)(2,1)} %copy-done.15, bf16[16,96,256]{2,1,0:T(8,128)(2,1)} %copy-done.12, f32[33,96,256]{2,1,0:T(8,128)} %get-tuple-element.97.refs_2_, f32[33,48,256]{2,1,0:T(8,128)} %shard_map.469.refs_7_.refs_1_.refs_3_, ...), custom_call_target="tpu_custom_call" | custom-call | flops 99999997952 | bytes 300000000 | tf_op jit(solution)/shard_map/pallas_call | solution.py:336
  269.4 6.1 %all-to-all-start.5 = ((bf16[16,112,256]{2,1,0:T(8,128)(2,1)}), bf16[16,112,256]{2,1,0:T(8,128)(2,1)}, u32[]{:S(2)}, u32[]{:S(2)}) async-start(bf16[16,112,256]{2,1,0:T(8,128)(2,1)} %get-tuple-element.100), calls=%async_computation.5 | async-start | bytes 1835008 | tf_op jit(solution)/shard_map/all_to_all | solution.py:1169
  275.6 3.4 add_convert_fusion.1
  282.3 13.9 %shard_map.475 = (bf16[16,48,768]{2,1,0:T(8,128)(2,1)}, f32[16,8,256]{2,1,0:T(8,128)}, f32[768,512]{1,0:T(8,128)}) custom-call(s32[13]{0:T(128)} %concatenate.35.refs_0_, f32[16,48,512]{2,1,0:T(8,128)} %bitcast.100, bf16[16,16,128]{2,1,0:T(8,128)(2,1)} %copy-done.28, bf16[16,48,640]{2,1,0:T(8,128)(2,1)} %get-tuple-element.110.refs_3_, ...), custom_call_target="tpu_custom_call" | custom-call | flops 2000000000 | bytes 6000000 | tf_op jit(solution)/shard_map/pallas_call | solution.py:583
  296.5 25.6 %shard_map.476 = (bf16[16,224,256]{2,1,0:T(8,128)(2,1)}, bf16[16,96,768]{2,1,0:T(8,128)(2,1)}) custom-call(s32[13]{0:T(128)} %concatenate.35.refs_0_, bf16[16,112,256]{2,1,0:T(8,128)(2,1)} %all-to-all-done.5.refs_1_, f32[16,96,512]{2,1,0:T(8,128)} %get-tuple-element.101.refs_2_, bf16[16,16,128]{2,1,0:T(8,128)(2,1)} %copy-done.52, ...), custom_call_target="tpu_custom_call" | custom-call | flops 99999997952 | bytes 300000000 | tf_op jit(solution)/shard_map/pallas_call | solution.py:583
  323.1 6.2 %all-to-all-start.6 = ((bf16[16,224,256]{2,1,0:T(8,128)(2,1)}), bf16[16,224,256]{2,1,0:T(8,128)(2,1)S(1)}, u32[]{:S(2)}, u32[]{:S(2)}) async-start(bf16[16,224,256]{2,1,0:T(8,128)(2,1)} %get-tuple-element.116), calls=%async_computation.6 | async-start | bytes 3670016 | tf_op jit(solution)/shard_map/all_to_all | solution.py:1169
  329.7 4.0 add_convert_fusion
  347.2 8.7 %shard_map.477 = (f32[33,64]{1,0:T(8,128)}, f32[64,64]{1,0:T(8,128)}, f32[64,48]{1,0:T(8,128)}, f32[8,256]{1,0:T(8,128)}, f32[48,1]{1,0:T(8,128)}) custom-call(f32[48,4096]{1,0:T(8,128)} %get-tuple-element.120.d_ref, f32[48,4096]{1,0:T(8,128)} %get-tuple-element.181.raw_ref, f32[48,4096]{1,0:T(8,128)} %get-tuple-element.169.fall_ref, f32[64,4096]{1,0:T(8,128)} %copy-done.2, ...), custom_call_target="tpu_custom_call" | custom-call | flops 10000000 | bytes 30000 | tf_op jit(solution)/shard_map/pallas_call | solution.py:336
  360.8 6.3 %collective-permute-done.28 = f32[9568]{0:T(1024)S(1)} collective-permute-done((f32[9568]{0:T(1024)S(1)}, f32[9568]{0:T(1024)S(1)}, u32[]{:S(2)}, u32[]{:S(2)}) %collective-permute-start.28) | collective-permute-done | bytes 38304 | tf_op jit(solution)/shard_map/ppermute | solution.py:1340
  371.0 10.3 %all-to-all-start.7 = ((bf16[8,168,384]{2,1,0:T(8,128)(2,1)}), bf16[8,168,384]{2,1,0:T(8,128)(2,1)S(1)}, u32[]{:S(2)}, u32[]{:S(2)}) async-start(bf16[8,168,384]{2,1,0:T(8,128)(2,1)} %pad_maximum_fusion), calls=%async_computation.7 | async-start | bytes 2064384 | tf_op jit(solution)/shard_map/all_to_all | solution.py:1364
  388.7 27.7 %all-to-all-done.7 = bf16[8,168,384]{2,1,0:T(8,128)(2,1)S(1)} async-done(((bf16[8,168,384]{2,1,0:T(8,128)(2,1)}), bf16[8,168,384]{2,1,0:T(8,128)(2,1)S(1)}, u32[]{:S(2)}, u32[]{:S(2)}) %all-to-all-start.7) | async-done | bytes 1032224 | tf_op jit(solution)/shard_map/all_to_all | solution.py:1364
  (248 shorter events, 84.5 us)
Async XLA Ops:
  9.6 38.5 %all-to-all-start = ((bf16[16,96,256]{2,1,0:T(8,128)(2,1)}), bf16[16,96,256]{2,1,0:T(8,128)(2,1)S(1)}, u32[]{:S(2)}, u32[]{:S(2)}) async-start(bf16[16,96,256]{2,1,0:T(8,128)(2,1)} %bitcast.5), calls=%async_computation | async-start | bytes 1572864 | tf_op jit(solution)/shard_map/all_to_all | solution.py:1169
  17.1 86.4 %all-gather.3.cloned.1.call-start = ((), (), s32[]{:S(2)}) async-start(), calls=%async_computation.10 | async-start | bytes 1658880 | tf_op jit(solution)/shard_map/all_gather | solution.py:1256
  18.6 18.1 %collective-permute-start.1 = (bf16[176,768]{1,0:T(8,128)(2,1)S(1)}, bf16[176,768]{1,0:T(8,128)(2,1)S(1)}, u32[]{:S(2)}, u32[]{:S(2)}) collective-permute-start(bf16[176,768]{1,0:T(8,128)(2,1)S(1)} %fusion.7.refs_0_), channel_id=1, source_target_pairs={{0,4},{1,5},{4,8},{5,9},{8,12},{9,13},{12,14},{13,15},{14,10},{15,... | collective-permute-start | bytes 811016 | tf_op jit(solution)/shard_map/ppermute | solution.py:1117
  20.5 22.1 %collective-permute-start.4 = (bf16[176,768]{1,0:T(8,128)(2,1)S(1)}, bf16[176,768]{1,0:T(8,128)(2,1)S(1)}, u32[]{:S(2)}, u32[]{:S(2)}) collective-permute-start(bf16[176,768]{1,0:T(8,128)(2,1)S(1)} %fusion.7.refs_0_), channel_id=1, source_target_pairs={{0,2},{1,3},{4,0},{5,1},{8,4},{9,5},{12,8},{13,9},{14,12},{15,13},... | collective-permute-start | bytes 811016 | tf_op jit(solution)/shard_map/ppermute | solution.py:1117
  36.6 11.5 %collective-permute-start.2 = (bf16[176,768]{1,0:T(8,128)(2,1)S(1)}, bf16[176,768]{1,0:T(8,128)(2,1)S(1)}, u32[]{:S(2)}, u32[]{:S(2)}) collective-permute-start(bf16[176,768]{1,0:T(8,128)(2,1)S(1)} %collective-permute-done.1.refs_1_), channel_id=1, source_target_pairs={{0,4},{1,5},{4,8},{5,9},{8,12},{9,13},{12,14},{13,15},{14,10},{15,... | collective-permute-start | bytes 811016 | tf_op jit(solution)/shard_map/ppermute | solution.py:1117
  42.6 8.5 %collective-permute-start.5 = (bf16[176,768]{1,0:T(8,128)(2,1)S(1)}, bf16[176,768]{1,0:T(8,128)(2,1)S(1)}, u32[]{:S(2)}, u32[]{:S(2)}) collective-permute-start(bf16[176,768]{1,0:T(8,128)(2,1)S(1)} %collective-permute-done.4.refs_4_), channel_id=1, source_target_pairs={{0,2},{1,3},{4,0},{5,1},{8,4},{9,5},{12,8},{13,9},{14,12},{15,13},... | collective-permute-start | bytes 811016 | tf_op jit(solution)/shard_map/ppermute | solution.py:1117
  48.1 11.7 %collective-permute-start.3 = (bf16[176,768]{1,0:T(8,128)(2,1)S(1)}, bf16[176,768]{1,0:T(8,128)(2,1)S(1)}, u32[]{:S(2)}, u32[]{:S(2)}) collective-permute-start(bf16[176,768]{1,0:T(8,128)(2,1)S(1)} %collective-permute-done.2.refs_2_), channel_id=1, source_target_pairs={{0,4},{1,5},{4,8},{5,9},{8,12},{9,13},{12,14},{13,15},{14,10},{15,... | collective-permute-start | bytes 811016 | tf_op jit(solution)/shard_map/ppermute | solution.py:1117
  51.1 7.2 %collective-permute-start.6 = (bf16[176,768]{1,0:T(8,128)(2,1)S(1)}, bf16[176,768]{1,0:T(8,128)(2,1)S(1)}, u32[]{:S(2)}, u32[]{:S(2)}) collective-permute-start(bf16[176,768]{1,0:T(8,128)(2,1)S(1)} %collective-permute-done.5.refs_5_), channel_id=1, source_target_pairs={{0,2},{1,3},{4,0},{5,1},{8,4},{9,5},{12,8},{13,9},{14,12},{15,13},... | collective-permute-start | bytes 811016 | tf_op jit(solution)/shard_map/ppermute | solution.py:1117
  58.2 6.6 %collective-permute-start.8 = (bf16[96,768]{1,0:T(8,128)(2,1)S(1)}, bf16[96,768]{1,0:T(8,128)(2,1)S(1)}, u32[]{:S(2)}, u32[]{:S(2)}) collective-permute-start(bf16[96,768]{1,0:T(8,128)(2,1)S(1)} %slice.193), channel_id=1, source_target_pairs={{0,2},{1,3},{4,0},{5,1},{8,4},{9,5},{12,8},{13,9},{14,12},{15,13},... | collective-permute-start | bytes 442376 | tf_op jit(solution)/shard_map/ppermute | solution.py:1117
  92.2 27.6 %all-to-all-start.1 = ((bf16[16,96,256]{2,1,0:T(8,128)(2,1)}), bf16[16,96,256]{2,1,0:T(8,128)(2,1)S(1)}, u32[]{:S(2)}, u32[]{:S(2)}) async-start(bf16[16,96,256]{2,1,0:T(8,128)(2,1)} %get-tuple-element.83), calls=%async_computation.1 | async-start | bytes 1572864 | tf_op jit(solution)/shard_map/all_to_all | solution.py:1169
  103.5 49.0 %collective-permute-start.10 = (bf16[4,216,768]{2,1,0:T(8,128)(2,1)}, bf16[4,216,768]{2,1,0:T(8,128)(2,1)S(1)}, u32[]{:S(2)}, u32[]{:S(2)}) collective-permute-start(bf16[4,216,768]{2,1,0:T(8,128)(2,1)} %bitcast.122), channel_id=1, source_target_pairs={{0,16},{16,0},{1,17},{17,1},{2,18},{18,2},{3,19},{19,3},{4,20},{20... | collective-permute-start | bytes 3981320 | tf_op jit(solution)/shard_map/ppermute | solution.py:1291
  105.0 43.2 %collective-permute-start.12 = (bf16[4,216,768]{2,1,0:T(8,128)(2,1)}, bf16[4,216,768]{2,1,0:T(8,128)(2,1)}, u32[]{:S(2)}, u32[]{:S(2)}) collective-permute-start(bf16[4,216,768]{2,1,0:T(8,128)(2,1)} %bitcast.123), channel_id=1, source_target_pairs={{0,2},{1,3},{2,0},{3,1},{4,6},{5,7},{6,4},{7,5},{8,10},{9,11},{10,... | collective-permute-start | bytes 3981320 | tf_op jit(solution)/shard_map/ppermute | solution.py:1290
  119.8 32.8 %all-to-all-start.2 = ((bf16[16,96,256]{2,1,0:T(8,128)(2,1)}), bf16[16,96,256]{2,1,0:T(8,128)(2,1)S(1)}, u32[]{:S(2)}, u32[]{:S(2)}) async-start(bf16[16,96,256]{2,1,0:T(8,128)(2,1)} %bitcast.20), calls=%async_computation.2 | async-start | bytes 1572864 | tf_op jit(solution)/shard_map/all_to_all | solution.py:1169
  148.1 29.9 %collective-permute-start.15 = (bf16[4,216,768]{2,1,0:T(8,128)(2,1)}, bf16[4,216,768]{2,1,0:T(8,128)(2,1)S(1)}, u32[]{:S(2)}, u32[]{:S(2)}) collective-permute-start(bf16[4,216,768]{2,1,0:T(8,128)(2,1)} %collective-permute-done.12.refs_8_.refs_9_), channel_id=1, source_target_pairs={{0,16},{16,0},{1,17},{17,1},{2,18},{18,2},{3,19},{19,3},{4,20},{20... | collective-permute-start | bytes 3981320 | tf_op jit(solution)/shard_map/ppermute | solution.py:1299
  153.6 27.6 %all-to-all-start.3 = ((bf16[16,96,256]{2,1,0:T(8,128)(2,1)}), bf16[16,96,256]{2,1,0:T(8,128)(2,1)S(1)}, u32[]{:S(2)}, u32[]{:S(2)}) async-start(bf16[16,96,256]{2,1,0:T(8,128)(2,1)} %get-tuple-element.88), calls=%async_computation.3 | async-start | bytes 1572864 | tf_op jit(solution)/shard_map/all_to_all | solution.py:1169
  160.1 18.7 %collective-permute-start.13 = (bf16[4,216,768]{2,1,0:T(8,128)(2,1)}, bf16[4,216,768]{2,1,0:T(8,128)(2,1)}, u32[]{:S(2)}, u32[]{:S(2)}) collective-permute-start(bf16[4,216,768]{2,1,0:T(8,128)(2,1)} %bitcast.124), channel_id=1, source_target_pairs={{0,1},{1,0},{2,3},{3,2},{4,5},{5,4},{6,7},{7,6},{8,9},{9,8},{10,11... | collective-permute-start | bytes 3981320 | tf_op jit(solution)/shard_map/ppermute | solution.py:1251
  160.6 18.2 %collective-permute-start.14 = (bf16[4,216,768]{2,1,0:T(8,128)(2,1)}, bf16[4,216,768]{2,1,0:T(8,128)(2,1)}, u32[]{:S(2)}, u32[]{:S(2)}) collective-permute-start(bf16[4,216,768]{2,1,0:T(8,128)(2,1)} %collective-permute-done.12.refs_8_.refs_9_), channel_id=1, source_target_pairs={{0,1},{1,0},{2,3},{3,2},{4,5},{5,4},{6,7},{7,6},{8,9},{9,8},{10,11... | collective-permute-start | bytes 3981320 | tf_op jit(solution)/shard_map/ppermute | solution.py:1251
  160.7 18.1 %collective-permute-start.16 = (bf16[4,216,768]{2,1,0:T(8,128)(2,1)}, bf16[4,216,768]{2,1,0:T(8,128)(2,1)}, u32[]{:S(2)}, u32[]{:S(2)}) collective-permute-start(bf16[4,216,768]{2,1,0:T(8,128)(2,1)} %copy-done.49), channel_id=1, source_target_pairs={{0,1},{1,0},{2,3},{3,2},{4,5},{5,4},{6,7},{7,6},{8,9},{9,8},{10,11... | collective-permute-start | bytes 3981320 | tf_op jit(solution)/shard_map/ppermute | solution.py:1251
  226.3 6.9 %collective-permute-start.18 = (bf16[8,432,384]{2,1,0:T(8,128)(2,1)}, bf16[8,432,384]{2,1,0:T(8,128)(2,1)S(1)}, u32[]{:S(2)}, u32[]{:S(2)}) collective-permute-start(bf16[8,432,384]{2,1,0:T(8,128)(2,1)} %get-tuple-element.95), channel_id=1, source_target_pairs={{0,1},{1,0},{2,3},{3,2},{4,5},{5,4},{6,7},{7,6},{8,9},{9,8},{10,11... | collective-permute-start | bytes 7962632 | tf_op jit(solution)/shard_map/ppermute | solution.py:1251
  226.5 23.7 %all-to-all-start.4 = ((bf16[16,96,256]{2,1,0:T(8,128)(2,1)}), bf16[16,96,256]{2,1,0:T(8,128)(2,1)S(1)}, u32[]{:S(2)}, u32[]{:S(2)}) async-start(bf16[16,96,256]{2,1,0:T(8,128)(2,1)} %get-tuple-element.93), calls=%async_computation.4 | async-start | bytes 1572864 | tf_op jit(solution)/shard_map/all_to_all | solution.py:1169
  231.5 44.0 %collective-permute-start.21 = (bf16[8,432,384]{2,1,0:T(8,128)(2,1)}, bf16[8,432,384]{2,1,0:T(8,128)(2,1)}, u32[]{:S(2)}, u32[]{:S(2)}) collective-permute-start(bf16[8,432,384]{2,1,0:T(8,128)(2,1)} %get-tuple-element.108), channel_id=1, source_target_pairs={{0,1},{1,0},{2,3},{3,2},{4,5},{5,4},{6,7},{7,6},{8,9},{9,8},{10,11... | collective-permute-start | bytes 7962632 | tf_op jit(solution)/shard_map/ppermute | solution.py:1251
  231.9 35.6 %collective-permute-start.20 = (bf16[16,16,128]{2,1,0:T(8,128)(2,1)}, bf16[16,16,128]{2,1,0:T(8,128)(2,1)S(1)}, u32[]{:S(2)}, u32[]{:S(2)}) collective-permute-start(bf16[16,16,128]{2,1,0:T(8,128)(2,1)} %get-tuple-element.99), channel_id=1, source_target_pairs={{1,0},{2,1},{3,2},{4,3},{5,4},{6,5},{7,6},{8,7},{9,8},{10,9},{11,1... | collective-permute-start | bytes 196616 | tf_op jit(solution)/shard_map/ppermute | solution.py:1317
  237.3 32.2 %collective-permute-start.19 = (bf16[4,432,384]{2,1,0:T(8,128)(2,1)}, bf16[4,432,384]{2,1,0:T(8,128)(2,1)}, u32[]{:S(2)}, u32[]{:S(2)}) collective-permute-start(bf16[4,432,384]{2,1,0:T(8,128)(2,1)} %get-tuple-element.153), channel_id=1, source_target_pairs={{0,16},{16,0},{1,17},{17,1},{2,18},{18,2},{3,19},{19,3},{4,20},{20... | collective-permute-start | bytes 3981320 | tf_op jit(solution)/shard_map/ppermute | solution.py:1329
  269.4 27.0 %all-to-all-start.5 = ((bf16[16,112,256]{2,1,0:T(8,128)(2,1)}), bf16[16,112,256]{2,1,0:T(8,128)(2,1)}, u32[]{:S(2)}, u32[]{:S(2)}) async-start(bf16[16,112,256]{2,1,0:T(8,128)(2,1)} %get-tuple-element.100), calls=%async_computation.5 | async-start | bytes 1835008 | tf_op jit(solution)/shard_map/all_to_all | solution.py:1169
  279.0 43.1 %collective-permute-start.22 = (bf16[4,432,384]{2,1,0:T(8,128)(2,1)}, bf16[4,432,384]{2,1,0:T(8,128)(2,1)S(1)}, u32[]{:S(2)}, u32[]{:S(2)}) collective-permute-start(bf16[4,432,384]{2,1,0:T(8,128)(2,1)} %add_convert_fusion.1), channel_id=1, source_target_pairs={{0,2},{1,3},{2,0},{3,1},{4,6},{5,7},{6,4},{7,5},{8,10},{9,11},{10,... | collective-permute-start | bytes 3981320 | tf_op jit(solution)/shard_map/ppermute | solution.py:1395
  280.8 41.2 %collective-permute-start.23 = (bf16[4,432,384]{2,1,0:T(8,128)(2,1)}, bf16[4,432,384]{2,1,0:T(8,128)(2,1)S(1)}, u32[]{:S(2)}, u32[]{:S(2)}) collective-permute-start(bf16[4,432,384]{2,1,0:T(8,128)(2,1)} %get-tuple-element.115), channel_id=1, source_target_pairs={{0,16},{16,0},{1,17},{17,1},{2,18},{18,2},{3,19},{19,3},{4,20},{20... | collective-permute-start | bytes 3981320 | tf_op jit(solution)/shard_map/ppermute | solution.py:1330
  323.1 47.9 %all-to-all-start.6 = ((bf16[16,224,256]{2,1,0:T(8,128)(2,1)}), bf16[16,224,256]{2,1,0:T(8,128)(2,1)S(1)}, u32[]{:S(2)}, u32[]{:S(2)}) async-start(bf16[16,224,256]{2,1,0:T(8,128)(2,1)} %get-tuple-element.116), calls=%async_computation.6 | async-start | bytes 3670016 | tf_op jit(solution)/shard_map/all_to_all | solution.py:1169
  329.4 87.9 %reduce-scatter.2.cloned.1.call-start = ((), (), s32[]{:S(2)}) async-start(), calls=%async_computation.9 | async-start | bytes 1658880 | tf_op jit(solution)/shard_map/reduce_scatter | solution.py:1410
  335.0 6.1 %collective-permute-start.26 = (bf16[8,96,768]{2,1,0:T(8,128)(2,1)S(1)}, bf16[8,96,768]{2,1,0:T(8,128)(2,1)}, u32[]{:S(2)}, u32[]{:S(2)}) collective-permute-start(bf16[8,96,768]{2,1,0:T(8,128)(2,1)S(1)} %dynamic-slice_bitcast_fusion), channel_id=1, source_target_pairs={{0,1},{1,0},{2,3},{3,2},{4,5},{5,4},{6,7},{7,6},{8,9},{9,8},{10,11... | collective-permute-start | bytes 3538952 | tf_op jit(solution)/shard_map/ppermute | solution.py:1356
  344.3 24.1 %collective-permute-start.27 = (bf16[8,144,384]{2,1,0:T(8,128)(2,1)}, bf16[8,144,384]{2,1,0:T(8,128)(2,1)}, u32[]{:S(2)}, u32[]{:S(2)}) collective-permute-start(bf16[8,144,384]{2,1,0:T(8,128)(2,1)} %fusion.4), channel_id=1, source_target_pairs={{0,16},{16,0},{1,17},{17,1},{2,18},{18,2},{3,19},{19,3},{4,20},{20... | collective-permute-start | bytes 2654216 | tf_op jit(solution)/shard_map/ppermute | solution.py:1350
  360.2 6.9 %collective-permute-start.28 = (f32[9568]{0:T(1024)S(1)}, f32[9568]{0:T(1024)S(1)}, u32[]{:S(2)}, u32[]{:S(2)}) collective-permute-start(f32[9568]{0:T(1024)S(1)} %concatenate.43), channel_id=1, source_target_pairs={{0,16},{16,0},{1,17},{17,1},{2,18},{18,2},{3,19},{19,3},{4,20},{20... | collective-permute-start | bytes 114824 | tf_op jit(solution)/shard_map/ppermute | solution.py:1340
  371.0 45.4 %all-to-all-start.7 = ((bf16[8,168,384]{2,1,0:T(8,128)(2,1)}), bf16[8,168,384]{2,1,0:T(8,128)(2,1)S(1)}, u32[]{:S(2)}, u32[]{:S(2)}) async-start(bf16[8,168,384]{2,1,0:T(8,128)(2,1)} %pad_maximum_fusion), calls=%async_computation.7 | async-start | bytes 2064384 | tf_op jit(solution)/shard_map/all_to_all | solution.py:1364
  (63 other events, 671.8 us)
Sparse Core Ops, SparseCore 0:
  71.3 32.1 all-gather.2
  360.9 39.2 reduce-scatter.1

commit v5 on v4

--- a/solution.py
+++ b/solution.py
@@ -1,3 +1,4 @@
+import functools
 import math
 
 import jax
@@ -23,7 +24,7 @@
 vmem_limit = 56 * 1024 * 1024
 HEAD_ROWS = 16
 SUM_ROWS = 16
-BATCH = 3
+BATCH = 11
 PRM = 32
 
 
@@ -621,7 +622,7 @@
     )
     small = pl.BlockSpec((turns, PRM, LANE), lambda i, t: (0, 0, 0), pipeline_mode=pl.Buffered(1))
     return chip_call(
-        100,
+        2,
         lambda *refs: front_body(seqs, *refs),
         table,
         turns,
@@ -633,13 +634,14 @@
     )
 
 
-def middle_body(seqs, pieces, segments, table_ref, conv_ref, x_ref, cot_ref, gate_ref, prm_ref, *refs):
+def middle_body(seqs, pieces, segments, per, table_ref, conv_ref, x_ref, cot_ref, gate_ref, prm_ref, *refs):
     weights = []
     for _ in range(pieces):
         weights.append([[refs[2 * (segments * core + n) : 2 * (segments * core + n) + 2] for n in range(segments)] for core in range(2)])
         refs = refs[4 * segments :]
     layer_ref, d_conv_ref, d_res_ref, p0_ref, p0h_ref = refs[:5]
-    grads, refs = [refs[5 + 2 * p : 7 + 2 * p] for p in range(pieces)], refs[5 + 2 * pieces :]
+    grads = [[refs[5 + segments * (2 * p + n) : 5 + segments * (2 * p + n + 1)] for n in range(2)] for p in range(pieces)]
+    refs = refs[5 + 2 * pieces * segments :]
     cs, res, ds, xb, db, gb, acc_out, acc_in, folds, up_folds, stats, out_w32, out_w_ref, gs = refs
     devices, _, width = x_ref.shape
     dim, cols = d_res_ref.shape
@@ -715,9 +717,9 @@
         stats[0:8, :] = jnp.broadcast_to(mean, (8, cols))
         stats[8:16, :] = jnp.broadcast_to(inverse, (8, cols))
 
-    pair = slots(table_ref, turns, step)
+    pair = [device for j in range(per) for device, _ in slots(table_ref, turns, step * per + j)]
     up_b = []
-    for device, _ in pair:
+    for device in pair:
         prm = prm_ref[device_rows(device), :]
         for h in halves:
             for m in range(some_hid // chans):
@@ -725,12 +727,16 @@
                 up_b.append(jnp.where(h == 0, prm[:, first : first + 1], prm[:, second : second + 1]))
     up_b = jnp.concatenate(up_b, axis=0)
 
-    def now(parts, rows):
-        blocks = [ref[0, rows, :] for ref, _ in parts]
-        return blocks[0] if len(blocks) == 1 else jnp.where(step < turns // 2, blocks[0], blocks[1])
-
-    up = jnp.concatenate([now(piece[core], slice(0, some_hid)) for core in range(2) for piece in weights], axis=0)
-    down = jnp.concatenate([now(piece[core], slice(some_hid, 2 * some_hid)) for core in range(2) for piece in weights], axis=0)
+    def now(parts, rows, j):
+        blocks = [ref[j, rows, :] for ref, _ in parts]
+        return blocks[0] if len(blocks) == 1 else jnp.where(step * per < turns // 2, blocks[0], blocks[1])
+
+    def rows_now(rows):
+        return jnp.concatenate(
+            [now(piece[core], rows, j) for j in range(per) for core in range(2) for piece in weights], axis=0
+        )
+
+    up, down = rows_now(slice(0, some_hid)), rows_now(slice(some_hid, 2 * some_hid))
     u = mm16(up, xb[...], NN) + up_b
     d_act = mm16(down, db[...], NN)
     a, k = 0.044715, math.sqrt(2.0 / math.pi)
@@ -743,17 +749,24 @@
     fold = folded(d_u)
     acc_out[...] += mm16(down, act, TN)
     acc_in[...] += mm16(up, d_low, TN)
-    spots = [(n, p, h) for n in range(2) for p, h in enumerate(halves)]
+    spots = [(n, p, h) for n in range(2 * per) for p, h in enumerate(halves)]
     for n, p, h in spots:
         rows = slice((n * pieces + p) * some_hid, (n * pieces + p + 1) * some_hid)
-        up_folds[pl.ds(pl.multiple_of(pair[n][0] * hid + h * some_hid, 8), some_hid), :] = fold[rows]
-    for left, right, first in ((d_low, xb, 0), (act, db, hid)):
-        gs[...] = mm16(left, right[...], NT).astype(bf16)
+        up_folds[pl.ds(pl.multiple_of(pair[n] * hid + h * some_hid, 8), some_hid), :] = fold[rows]
+    gs[0] = mm16(d_low, xb[...], NT).astype(bf16)
+    gs[1] = mm16(act, db[...], NT).astype(bf16)
+
+    def hand_out(k):
         for n, p, h in spots:
             rows = slice((n * pieces + p) * some_hid, (n * pieces + p + 1) * some_hid)
-            at = pl.ds(pl.multiple_of(first + h * some_hid, some_hid), some_hid)
-            for g_refs, some in zip(grads, columns):
-                g_refs[n][step, at, :] = gs[rows, some]
+            for which in range(2):
+                at = pl.ds(pl.multiple_of(which * hid + h * some_hid, some_hid), some_hid)
+                for g_refs, some in zip(grads, columns):
+                    g_refs[n % 2][k][step * per + n // 2 - k * (turns // segments), at, :] = gs[which, rows, some]
+
+    for k in range(segments):
+        count = turns // segments
+        pl.when((step * per >= k * count) & (step * per < (k + 1) * count))(functools.partial(hand_out, k))
 
     @pl.when(step == last)
     def _():
@@ -793,7 +806,8 @@
         for g_refs, at in zip(grads, columns):
             for turn in range(turns):
                 for g_ref, (device, _) in zip(g_refs, slots(table_ref, turns, turn)):
-                    g_ref[turn, 2 * hid :, :] = out_w32[device_rows(device), at].astype(bf16)
+                    count = turns // segments
+                    g_ref[turn // count][turn % count, 2 * hid :, :] = out_w32[device_rows(device), at].astype(bf16)
 
         def products(i, carry):
             at = chunk_rows(i)
@@ -823,7 +837,7 @@
     dim, cols = gate.shape
     chans = dim // devices
     turns = devices // 2
-    pieces = len(matrices)
+    pieces, segments = len(matrices), len(matrices[0][0])
     part, some_hid, some_out = dim // pieces, hid // pieces, chans // pieces
     sd = jax.ShapeDtypeStruct
     out = (
@@ -832,11 +846,11 @@
         sd((dim, cols), f32),
         sd((dim, cols), f32),
         sd((devices, 8 * seqs, LANE), bf16),
-    ) + (sd((turns, 2 * hid + chans, part), bf16),) * (2 * pieces)
+    ) + (sd((turns // segments, 2 * hid + chans, part), bf16),) * (2 * pieces * segments)
     big = pltpu.VMEM((dim, cols), f32)
     low = pltpu.VMEM((dim, cols), bf16)
     args, specs = [conv, x, cot, gate, prm], [whole(conv), whole(x), whole(cot), whole(gate), whole(prm)]
-    segments = len(matrices[0][0])
+    per = 2
     for piece in matrices:
         for parts in piece:
             first = 0
@@ -844,7 +858,10 @@
                 count = a.shape[0]
                 args += [a, a]
                 specs += [
-                    pl.BlockSpec((1, 2 * some_hid, dim), lambda i, t, f=first, c=count: (jnp.clip(i - f, 0, c - 1), 0, 0)),
+                    pl.BlockSpec(
+                        (per, 2 * some_hid, dim),
+                        lambda i, t, f=first // per, c=count // per: (jnp.clip(i - f, 0, c - 1), 0, 0),
+                    ),
                     pl.BlockSpec(
                         (count, some_out, dim), lambda i, t: (0, 2 * some_hid // some_out, 0), pipeline_mode=pl.Buffered(1)
                     ),
@@ -852,9 +869,9 @@
                 first += count
     return chip_call(
         36,
-        lambda *refs: middle_body(seqs, pieces, segments, *refs),
+        lambda *refs: middle_body(seqs, pieces, segments, per, *refs),
         table,
-        turns,
+        turns // per,
         args,
         specs,
         out,
@@ -862,7 +879,7 @@
         [
             big, big, big, low, low, low, big, big, pltpu.VMEM((4, dim, LANE), f32),
             pltpu.VMEM((devices * hid, LANE), f32), pltpu.VMEM((16, cols), f32), pltpu.VMEM((dim, dim), f32),
-            pltpu.VMEM((dim, dim), bf16), pltpu.VMEM((2 * hid, dim), bf16),
+            pltpu.VMEM((dim, dim), bf16), pltpu.VMEM((2, 2 * per * hid, dim), bf16),
         ],
     )
 
@@ -942,7 +959,7 @@
 
 def back_body(
     seqs, table_ref, d_mixed_ref, pair_ref, heads_ref, projx_ref, own_ref, other_ref, prm_ref, xn_ref, x_ref, stat_ref, d_res_ref,
-    acc0_ref, sums0_ref, layer_ref, tail_ref, g_ref, acc, xs, folds, sums,
+    acc0_ref, sums0_ref, tail_ref, g_ref, acc, xs, folds, sums,
 ):
     devices, _, width = x_ref.shape
     dim, cols = xn_ref.shape
@@ -1012,20 +1029,19 @@
             totals = [sums0_ref[d]] + [sums[n, d] for n in range(sums.shape[0])]
             totals += [padded_totals(folds[q, at, :], width)[0] for q in range(2)]
             tail_ref[d, rows : rows + SUM_ROWS, :] = as_rows(totals, SUM_ROWS)
-            tail_ref[d, rows + SUM_ROWS :, :] = layer_ref[d]
             return carry
 
         lax.fori_loop(0, devices, scatter, 0)
 
 
-def back(table, d_mixed, pair, heads, projx, own, other, prm, xn, x, stat, d_res, acc0, sums0, layer, seqs):
+def back(table, d_mixed, pair, heads, projx, own, other, prm, xn, x, stat, d_res, acc0, sums0, seqs):
     devices, rows, width = x.shape
     dim, cols = xn.shape
     chans = dim // devices
     sd = jax.ShapeDtypeStruct
     pieces = -(-2 * (2 + KS) * chans // width)
     out = (
-        sd((devices, 2 * rows + 2 * SUM_ROWS, width), bf16),
+        sd((devices, rows + SUM_ROWS, width), bf16),
         sd((devices, 2 * chans, dim), bf16),
     )
     return chip_call(
@@ -1033,10 +1049,10 @@
         lambda *refs: back_body(seqs, *refs),
         table,
         devices // 2,
-        (d_mixed, pair, heads, projx, own, other, prm, xn, x, stat, d_res, acc0, sums0, layer),
+        (d_mixed, pair, heads, projx, own, other, prm, xn, x, stat, d_res, acc0, sums0),
         [by_chip(a) for a in (d_mixed, pair, heads, projx)]
         + [by_turn(own), by_turn(other), whole(prm), whole(xn), whole(x)]
-        + [whole(a) for a in (stat, d_res, acc0, sums0, layer)],
+        + [whole(a) for a in (stat, d_res, acc0, sums0)],
         out,
         (whole(out[0]), by_chip(out[1])),
         [
@@ -1066,21 +1082,27 @@
 NT = ((1,), (1,))
 
 
+def mm_split(a, b, dims):
+    a_upper, b_upper = a.astype(bf16), b.astype(bf16)
+    a_lower, b_lower = (a - a_upper.astype(f32)).astype(bf16), (b - b_upper.astype(f32)).astype(bf16)
+    return mm16(a_upper, b_upper, dims) + mm16(a_lower, b_upper, dims) + mm16(a_upper, b_lower, dims)
+
+
 def filter_back_body(d_ref, raw_ref, fall_ref, h1_ref, h2_ref, c1_ref, c2_ref, pre1_ref, pre2_ref, feat_ref, mid_ref, last_ref, rate_ref,
                      g_in_ref, g_mid_ref, g_last_ref, g_rows_ref, g_decay_ref):
     chans = d_ref.shape[0]
     d = d_ref[...]
     q = d * (fall_ref[...] + decay_floor)
-    g_last_ref[...] = mm(h2_ref[...], q, NT)
+    g_last_ref[...] = mm_split(h2_ref[...], q, NT)
     decay = folded(d * raw_ref[...] * fall_ref[...] * feat_ref[0:1, :])
     g_decay_ref[...] = -jnp.sum(decay, axis=1, keepdims=True)
-    u2 = mm(last_ref[...], q, NN) * c2_ref[...]
+    u2 = mm_split(last_ref[...], q, NN) * c2_ref[...]
     rate = rate_ref[...]
     fu2 = rate * u2
-    u1 = mm(mid_ref[...], fu2, NN) * c1_ref[...]
+    u1 = mm_split(mid_ref[...], fu2, NN) * c1_ref[...]
     fu1 = rate * u1
-    g_in_ref[...] = mm(feat_ref[...], fu1, NT)
-    g_mid_ref[...] = mm(h1_ref[...], fu2, NT)
+    g_in_ref[...] = mm_split(feat_ref[...], fu1, NT)
+    g_mid_ref[...] = mm_split(h1_ref[...], fu2, NT)
     rows = jnp.concatenate([folded(fu1), folded(fu2), folded(u2 * pre2_ref[...] + u1 * pre1_ref[...])], axis=0)
     extra = jnp.zeros((-rows.shape[0] % LANE, LANE), f32)
     g_rows_ref[...] = row_totals(jnp.concatenate([rows, extra], axis=0))
@@ -1320,14 +1342,15 @@
         return sum(v.astype(f32) for v in values).astype(bf16)
 
     if stepped:
-        mine, mine_in = results[5], to_partner(results[6])
-        theirs, theirs_in = results[7], to_partner(results[8])
-        half = chips // 2
-        far_theirs = added(theirs[half:], theirs_in[half:])
-        near_theirs = added(theirs[:half], theirs_in[:half])
-        d_conv_chan = after(d_conv_chan, far_theirs, near_theirs)
+        near_mine, far_mine = (results[5], results[7]), (results[6], results[8])
+        near_theirs, far_theirs = (results[9], results[11]), (results[10], results[12])
+        far_theirs = added(far_theirs[0], to_partner(far_theirs[1]))
+        d_conv_chan = after(d_conv_chan, far_theirs)
         far_theirs = lax.ppermute(far_theirs, "batch", swap)
+        near_theirs = added(near_theirs[0], to_partner(after(near_theirs[1], d_conv_chan)))
         near_theirs = lax.ppermute(after(near_theirs, far_theirs), "batch", swap)
+        far_mine = far_mine[0], to_partner(after(far_mine[1], d_conv_chan))
+        near_mine = near_mine[0], to_partner(after(near_mine[1], d_conv_chan))
     else:
         early = added(results[5], to_partner(results[6]))
 
@@ -1377,20 +1400,14 @@
     )
     if stepped:
         d_mixed_chan = after(d_mixed_chan, far_theirs, p0h)
-        far_mine = added(mine[half:], mine_in[half:], far_theirs)
+        far_mine = added(*far_mine, far_theirs)
         p0h = after(p0h, far_mine)
     g_in0, sums0, acc0 = back_gate(
         table, p0.reshape(devices, chans, cols), p0h, projx0, in_own, in_other, prm, xn1, seqs
     )
     g_in0 = over_chip(g_in0)
     d_mixed = exchange(d_mixed_chan)
-    g_filt_in, g_filt_mid, g_filt_out, g_rows, g_decay = filter_back(
-        d_filter, raw, falling, h1, h2, c1, c2, pre1, pre2, feat, filt_mid, filt_out, rate
-    )
-    shared = [g_filt_in.reshape(-1), g_filt_mid.reshape(-1), g_rows[0, : 3 * ford]]
-    total = batch_total(
-        jnp.concatenate(shared + [g_conv_bias[:, 0], g_decay[:, 0], g_filt_out.reshape(-1)])
-    )
+    layer = exchange(after(layer, d_mixed))
     if stepped:
         far_mine = lax.ppermute(far_mine, "chan", beside)
     else:
@@ -1398,13 +1415,21 @@
         early = lax.psum_scatter(early, "chan", scatter_dimension=0, tiled=True, axis_index_groups=chan_groups)[0]
 
     tail, g_in = back(
-        table, d_mixed, pair, heads, projx, in_own, in_other, prm, xn1, x, stat1, d_res, acc0, sums0, layer, seqs
+        table, d_mixed, pair, heads, projx, in_own, in_other, prm, xn1, x, stat1, d_res, acc0, sums0, seqs
     )
     if stepped:
-        tail = after(tail, far_mine, near_theirs)
-        early = added(mine[:half], mine_in[:half], near_theirs, far_mine)
-        g_in = after(g_in, early)
+        tail = after(tail, far_mine, near_theirs, layer)
+        early = added(*near_mine, near_theirs, far_mine)
+        early = after(early, g_in)
+        d_filter = after(d_filter, early)
     tail = exchange(tail)
+    g_filt_in, g_filt_mid, g_filt_out, g_rows, g_decay = filter_back(
+        d_filter, raw, falling, h1, h2, c1, c2, pre1, pre2, feat, filt_mid, filt_out, rate
+    )
+    shared = [g_filt_in.reshape(-1), g_filt_mid.reshape(-1), g_rows[0, : 3 * ford]]
+    total = batch_total(
+        jnp.concatenate(shared + [g_conv_bias[:, 0], g_decay[:, 0], g_filt_out.reshape(-1)])
+    )
     g_in = over_groups(jnp.concatenate([g_in0, over_chip(g_in)], axis=1))
     if stepped:
         early = lax.psum_scatter(early, "chan", scatter_dimension=0, tiled=True, axis_index_groups=along)[0]
@@ -1441,8 +1466,8 @@
     early = early.astype(f32) if stepped else over_batch(early)
     up_grad, down_grad, out_grad = early[:hid], early[hid : 2 * hid], early[2 * hid :]
 
-    grad_blocks, out_blocks = tail[:, :rows], tail[:, rows + SUM_ROWS : 2 * rows + SUM_ROWS]
-    sums = jnp.concatenate([tail[:, 2 * rows + SUM_ROWS :], tail[:, rows : rows + SUM_ROWS]], axis=1)
+    grad_blocks, out_blocks = tail[:, :rows], layer[:, :rows]
+    sums = jnp.concatenate([layer[:, rows:], tail[:, rows:]], axis=1)
     sums = batch_total(jnp.sum(sums.astype(f32), axis=0))
     sums = sums[0::2] + sums[1::2]
     g_gain2, g_shift2, g_out_b, g_down_b = (sums[i, :chans] for i in range(4))

time: 431 us -> 424 us (0.984)
  Pallas kernels: 147 us -> 137 us
  waiting for transfers between devices: 108 us -> 114 us
    pallas_call x5, Pallas kernels: 46.9 us -> 39.2 us  [whole_call(): pl.pallas_call(body, cost_estimate=takes(us), out_shape=out_shape, in_spe...]
    all_to_all x1, starting transfers between devices: 10.3 us -> 5.6 us  [over_chips(): lax.all_to_all(both, 'chan', split_axis=0, concat_axis=0, tiled=True, axi...]
    all_to_all x7 -> x8, starting transfers between devices: 45.8 us -> 50.4 us  [exchange(): lax.all_to_all(values, 'chan', split_axis=0, concat_axis=0, tiled=True)]
    all_to_all x7 -> x8, waiting for transfers between devices: 25.3 us -> 28.1 us  [exchange(): lax.all_to_all(values, 'chan', split_axis=0, concat_axis=0, tiled=True)]
    convert_element_type x3 -> x4, other arithmetic: 11.4 us -> 11.6 us  [added(): return sum((v.astype(f32) for v in values)).astype(bf16)]
  transfers between devices with their start and end apart: 40 -> 43, of which waited for: 19 -> 18; matrix products, arithmetic and copies ran while one was open for 13% -> 13% of each run, Pallas kernels for 23% -> 22%
where the time goes in v5:
time: 424 us; the launch traced here: 422 us
  Pallas kernels  137 us (32%)
  waiting for transfers between devices  114 us (27%)
  starting transfers between devices  89 us (21%)
  local copies, waits for them, and re-layouts  29.9 us (7%)
  other arithmetic  22.6 us (5%)
  between operations  14.9 us (4%)
  matrix products  14.7 us (3%)
    pallas_call x4, Pallas kernels, chip_call(): pl.pallas_call(body, cost_estimate=takes(us), out_shape=out, grid_spec=pl...  97.8 us
    all_to_all x8, starting transfers between devices, exchange(): lax.all_to_all(values, 'chan', split_axis=0, concat_axis=0, tiled=True)  50.4 us
    pallas_call x5, Pallas kernels, whole_call(): pl.pallas_call(body, cost_estimate=takes(us), out_shape=out_shape, in_spe...  39.2 us
    all_to_all x1, waiting for transfers between devices, over_chips(): lax.all_to_all(both, 'chan', split_axis=0, concat_axis=0, tiled=True, axi...  29.5 us
    all_to_all x8, waiting for transfers between devices, exchange(): lax.all_to_all(values, 'chan', split_axis=0, concat_axis=0, tiled=True)  28.1 us
    ppermute x1, waiting for transfers between devices, on_device(): far_across = lax.ppermute(far, 'batch', swap)  18.1 us
    dot_general x3, matrix products, mm(): lax.dot_general(a, b, (dims, ((), ())), precision=highest, preferred_elem...  14.7 us
    ppermute x8, starting transfers between devices, ring_hop(): return lax.ppermute(values, 'chan', moves)  13.9 us
  transfers between devices with their start and end apart: 43, of which 18 were waited for; matrix products, arithmetic and copies ran while one was open for 13% of the time, Pallas kernels for 22%

profile of v5, /device:TPU:0, one launch (start us, length us, event | category | flops | bytes accessed | tf_op | source)
XLA Modules:
  0.0 422.1 jit_solution(4544468762799889085)
XLA Ops:
  9.5 7.5 %all-to-all-start = ((bf16[16,96,256]{2,1,0:T(8,128)(2,1)}), bf16[16,96,256]{2,1,0:T(8,128)(2,1)S(1)}, u32[]{:S(2)}, u32[]{:S(2)}) async-start(bf16[16,96,256]{2,1,0:T(8,128)(2,1)} %bitcast.5), calls=%async_computation | async-start | bytes 1572864 | tf_op jit(solution)/shard_map/all_to_all | solution.py:1191
  20.6 6.1 %multiply_cosine_fusion.1 = (f32[64,4096]{1,0:T(8,128)}, f32[64,4096]{1,0:T(8,128)S(1)}, f32[64,4096]{1,0:T(8,128)}) fusion(f32[64]{0:T(128)S(1)} %copy-done.35, f32[64]{0:T(128)S(1)} %copy-done.41, f32[33,4096]{1,0:T(8,128)S(1)} %copy-done.6, f32[33,64]{1,0:T(8,128)S(1)} %copy-done.33), kind=kOutput, calls=%fused_computation.24 | convolution fusion | flops 104333312 | bytes 3695360 | tf_op jit(solution)/shard_map/dot_general | solution.py:1077
  26.8 6.2 %multiply_cosine_fusion = (f32[64,4096]{1,0:T(8,128)}, f32[64,4096]{1,0:T(8,128)S(1)}, f32[64,4096]{1,0:T(8,128)}) fusion(f32[64]{0:T(128)S(1)} %copy-done.35, f32[64]{0:T(128)S(1)} %copy-done.42, f32[64,4096]{1,0:T(8,128)S(1)} %get-tuple-element.173.h1_ref, f32[64,64]{1,0:T(8,128)S(1)} %copy-done.26), kind=kOutput, calls=%fused_computation.22 | convolution fusion | flops 201850880 | bytes 4211200 | tf_op jit(solution)/shard_map/dot_general | solution.py:1077
  32.9 3.6 collective-permute-done.1.refs_1_
  36.6 5.9 %collective-permute-start.2 = (bf16[176,768]{1,0:T(8,128)(2,1)S(1)}, bf16[176,768]{1,0:T(8,128)(2,1)S(1)}, u32[]{:S(2)}, u32[]{:S(2)}) collective-permute-start(bf16[176,768]{1,0:T(8,128)(2,1)S(1)} %collective-permute-done.1.refs_1_), channel_id=1, source_target_pairs={{0,4},{1,5},{4,8},{5,9},{8,12},{9,13},{12,14},{13,15},{14,10},{15,... | collective-permute-start | bytes 811016 | tf_op jit(solution)/shard_map/ppermute | solution.py:1139
  44.9 3.1 collective-permute-done.2.refs_2_
  52.2 4.1 shard_map.469.refs_7_.refs_1_.refs_3_
  60.3 4.4 %collective-permute-done.7 = bf16[80,768]{1,0:T(8,128)(2,1)S(1)} collective-permute-done((bf16[80,768]{1,0:T(8,128)(2,1)S(1)}, bf16[80,768]{1,0:T(8,128)(2,1)S(1)}, u32[]{:S(2)}, u32[]{:S(2)}) %collective-permute-start.7) | collective-permute-done | bytes 122912 | tf_op jit(solution)/shard_map/ppermute | solution.py:1139
  65.5 3.1 shard_map.470.refs_3_.refs_5_.refs_4_
  75.1 16.9 %shard_map.471 = (f32[768,32]{1,0:T(8,128)}, bf16[768,512]{1,0:T(8,128)(2,1)}, f32[16,512]{1,0:T(8,128)}, f32[16,48,512]{2,1,0:T(8,128)}, f32[16,96,512]{2,1,0:T...) custom-call(s32[13]{0:T(128)} %concatenate.36.refs_0_, ...), custom_call_target="tpu_custom_call" | custom-call | flops 2000000000 | bytes 6000000 | tf_op jit(solution)/shard_map/pallas_call | solution.py:584
  91.9 8.8 %all-to-all-start.1 = ((bf16[16,96,256]{2,1,0:T(8,128)(2,1)}), bf16[16,96,256]{2,1,0:T(8,128)(2,1)S(1)}, u32[]{:S(2)}, u32[]{:S(2)}) async-start(bf16[16,96,256]{2,1,0:T(8,128)(2,1)} %get-tuple-element.92), calls=%async_computation.1 | async-start | bytes 1572864 | tf_op jit(solution)/shard_map/all_to_all | solution.py:1191
  105.8 13.7 %all-to-all-done.1.refs_0_.refs_1_ = bf16[16,96,256]{2,1,0:T(8,128)(2,1)S(1)} async-done(((bf16[16,96,256]{2,1,0:T(8,128)(2,1)}), bf16[16,96,256]{2,1,0:T(8,128)(2,1)S(1)}, u32[]{:S(2)}, u32[]{:S(2)}) %all-to-all-start.1) | async-done | bytes 786464 | tf_op jit(solution)/shard_map/all_to_all | solution.py:1191
  119.5 5.5 %all-to-all-start.2 = ((bf16[16,96,256]{2,1,0:T(8,128)(2,1)}), bf16[16,96,256]{2,1,0:T(8,128)(2,1)S(1)}, u32[]{:S(2)}, u32[]{:S(2)}) async-start(bf16[16,96,256]{2,1,0:T(8,128)(2,1)} %bitcast.20), calls=%async_computation.2 | async-start | bytes 1572864 | tf_op jit(solution)/shard_map/all_to_all | solution.py:1191
  125.1 11.1 %shard_map.472 = (bf16[16,96,256]{2,1,0:T(8,128)(2,1)}, f32[33,96,256]{2,1,0:T(8,128)}) custom-call(bf16[16,96,256]{2,1,0:T(8,128)(2,1)} %copy-done.14, f32[33,48,256]{2,1,0:T(8,128)} %shard_map.469.refs_7_.refs_1_.refs_3_, f32[48,1]{1,0:T(8,128)} %copy.64.refs_2_.refs_4_, f32[33,1,256]{2,1,0:T(1,128)} %constant.94.clone.twist_ref.refs_3_.refs_5_, ...), custom_call_target="tpu_custom_call" | custom-call | flops 99999997952 | bytes 300000000 | tf_op jit(solution)/shard_map/pallas_call | solution.py:337
  136.2 11.8 %collective-permute-done.12.refs_8_.refs_9_ = bf16[4,216,768]{2,1,0:T(8,128)(2,1)} collective-permute-done((bf16[4,216,768]{2,1,0:T(8,128)(2,1)}, bf16[4,216,768]{2,1,0:T(8,128)(2,1)}, u32[]{:S(2)}, u32[]{:S(2)}) %collective-permute-start.12) | collective-permute-done | bytes 1327136 | tf_op jit(solution)/shard_map/ppermute | solution.py:1312
  152.3 6.5 %all-to-all-start.3 = ((bf16[16,96,256]{2,1,0:T(8,128)(2,1)}), bf16[16,96,256]{2,1,0:T(8,128)(2,1)S(1)}, u32[]{:S(2)}, u32[]{:S(2)}) async-start(bf16[16,96,256]{2,1,0:T(8,128)(2,1)} %get-tuple-element.97), calls=%async_computation.3 | async-start | bytes 1572864 | tf_op jit(solution)/shard_map/all_to_all | solution.py:1191
  159.8 18.1 %collective-permute-done.15.refs_16_.refs_17_ = bf16[4,216,768]{2,1,0:T(8,128)(2,1)} collective-permute-done((bf16[4,216,768]{2,1,0:T(8,128)(2,1)}, bf16[4,216,768]{2,1,0:T(8,128)(2,1)}, u32[]{:S(2)}, u32[]{:S(2)}) %collective-permute-start.15) | collective-permute-done | bytes 1327136 | tf_op jit(solution)/shard_map/ppermute | solution.py:1321
  182.2 42.0 %shard_map.473 = (bf16[16,112,256]{2,1,0:T(8,128)(2,1)}, bf16[16,96,256]{2,1,0:T(8,128)(2,1)}, f32[768,512]{1,0:T(8,128)}, f32[768,512]{1,0:T(8,128)}, bf16[16,1...) custom-call(s32[13]{0:T(128)} %concatenate.35.refs_0_, ...), custom_call_target="tpu_custom_call" | custom-call | flops 35999997952 | bytes 108000000 | tf_op jit(solution)/shard_map/pallas_call | solution.py:584
  224.4 5.1 %all-to-all-start.4 = ((bf16[16,96,256]{2,1,0:T(8,128)(2,1)}), bf16[16,96,256]{2,1,0:T(8,128)(2,1)S(1)}, u32[]{:S(2)}, u32[]{:S(2)}) async-start(bf16[16,96,256]{2,1,0:T(8,128)(2,1)} %get-tuple-element.103), calls=%async_computation.4 | async-start | bytes 1572864 | tf_op jit(solution)/shard_map/all_to_all | solution.py:1191
  233.8 14.4 %all-to-all-done.4.refs_0_ = bf16[16,96,256]{2,1,0:T(8,128)(2,1)S(1)} async-done(((bf16[16,96,256]{2,1,0:T(8,128)(2,1)}), bf16[16,96,256]{2,1,0:T(8,128)(2,1)S(1)}, u32[]{:S(2)}, u32[]{:S(2)}) %all-to-all-start.4) | async-done | bytes 786464 | tf_op jit(solution)/shard_map/all_to_all | solution.py:1191
  249.1 14.1 %shard_map.474 = (bf16[16,112,256]{2,1,0:T(8,128)(2,1)}, f32[48,4096]{1,0:T(8,128)}, f32[48,1]{1,0:T(8,128)}) custom-call(bf16[16,96,256]{2,1,0:T(8,128)(2,1)} %copy-done.17, bf16[16,96,256]{2,1,0:T(8,128)(2,1)} %copy-done.14, f32[33,96,256]{2,1,0:T(8,128)} %get-tuple-element.107.refs_2_, f32[33,48,256]{2,1,0:T(8,128)} %shard_map.469.refs_7_.refs_1_.refs_3_, ...), custom_call_target="tpu_custom_call" | custom-call | flops 99999997952 | bytes 300000000 | tf_op jit(solution)/shard_map/pallas_call | solution.py:337
  264.3 6.4 %all-to-all-start.5 = ((bf16[16,112,256]{2,1,0:T(8,128)(2,1)}), bf16[16,112,256]{2,1,0:T(8,128)(2,1)}, u32[]{:S(2)}, u32[]{:S(2)}) async-start(bf16[16,112,256]{2,1,0:T(8,128)(2,1)} %get-tuple-element.110), calls=%async_computation.5 | async-start | bytes 1835008 | tf_op jit(solution)/shard_map/all_to_all | solution.py:1191
  270.7 3.2 add_convert_fusion.2
  280.0 13.9 %shard_map.475 = (bf16[16,48,768]{2,1,0:T(8,128)(2,1)}, f32[16,8,256]{2,1,0:T(8,128)}, f32[768,512]{1,0:T(8,128)}) custom-call(s32[13]{0:T(128)} %concatenate.36.refs_0_, f32[16,48,512]{2,1,0:T(8,128)} %bitcast.100, bf16[16,16,128]{2,1,0:T(8,128)(2,1)} %copy-done.31, bf16[16,48,640]{2,1,0:T(8,128)(2,1)} %get-tuple-element.122.refs_3_, ...), custom_call_target="tpu_custom_call" | custom-call | flops 2000000000 | bytes 6000000 | tf_op jit(solution)/shard_map/pallas_call | solution.py:584
  293.9 4.7 %all-to-all-start.6 = ((bf16[16,112,256]{2,1,0:T(8,128)(2,1)}), bf16[16,112,256]{2,1,0:T(8,128)(2,1)S(1)}, u32[]{:S(2)}, u32[]{:S(2)}) async-start(bf16[16,112,256]{2,1,0:T(8,128)(2,1)} %get-tuple-element.111), calls=%async_computation.6 | async-start | bytes 1835008 | tf_op jit(solution)/shard_map/all_to_all | solution.py:1191
  298.6 25.0 %shard_map.476 = (bf16[16,112,256]{2,1,0:T(8,128)(2,1)}, bf16[16,96,768]{2,1,0:T(8,128)(2,1)}) custom-call(s32[13]{0:T(128)} %concatenate.36.refs_0_, bf16[16,112,256]{2,1,0:T(8,128)(2,1)} %all-to-all-done.5.refs_1_, f32[16,96,512]{2,1,0:T(8,128)} %get-tuple-element.112.refs_2_, bf16[16,16,128]{2,1,0:T(8,128)(2,1)} %copy-done.52, ...), custom_call_target="tpu_custom_call" | custom-call | flops 99999997952 | bytes 300000000 | tf_op jit(solution)/shard_map/pallas_call | solution.py:584
  327.0 5.8 %all-to-all-start.7 = ((bf16[16,112,256]{2,1,0:T(8,128)(2,1)}), bf16[16,112,256]{2,1,0:T(8,128)(2,1)}, u32[]{:S(2)}, u32[]{:S(2)}) async-start(bf16[16,112,256]{2,1,0:T(8,128)(2,1)} %get-tuple-element.130), calls=%async_computation.7 | async-start | bytes 1835008 | tf_op jit(solution)/shard_map/all_to_all | solution.py:1191
  339.5 4.2 %add_convert_fusion = bf16[4,432,384]{2,1,0:T(8,128)(2,1)} fusion(bf16[4,432,384]{2,1,0:T(8,128)(2,1)} %copy-done.7, bf16[4,432,384]{2,1,0:T(8,128)(2,1)} %collective-permute-done.24, bf16[4,432,384]{2,1,0:T(8,128)(2,1)} %collective-permute-done.29, bf16[4,432,384]{2,1,0:T(8,128)(2,1)} %get-tuple-element.134), kind=kLoop, calls=%fused_computation.5 | loop fusion | flops 5308416 | bytes 6635520 | tf_op jit(solution)/shard_map/convert_element_type | solution.py:1342
  343.8 6.8 %shard_map.477 = (f32[33,64]{1,0:T(8,128)}, f32[64,64]{1,0:T(8,128)}, f32[64,48]{1,0:T(8,128)}, f32[8,256]{1,0:T(8,128)}, f32[48,1]{1,0:T(8,128)}) custom-call(f32[48,4096]{1,0:T(8,128)} %get-tuple-element.138.d_ref, f32[48,4096]{1,0:T(8,128)} %get-tuple-element.193.raw_ref, f32[48,4096]{1,0:T(8,128)} %get-tuple-element.181.fall_ref, f32[64,4096]{1,0:T(8,128)} %copy-done.3, ...), custom_call_target="tpu_custom_call" | custom-call | flops 10000000 | bytes 30000 | tf_op jit(solution)/shard_map/pallas_call | solution.py:337
  356.1 4.2 collective-permute-done.30
  364.2 5.6 %all-to-all-start.8 = ((bf16[8,168,384]{2,1,0:T(8,128)(2,1)}), bf16[8,168,384]{2,1,0:T(8,128)(2,1)S(1)}, u32[]{:S(2)}, u32[]{:S(2)}) async-start(bf16[8,168,384]{2,1,0:T(8,128)(2,1)} %pad_maximum_fusion), calls=%async_computation.8 | async-start | bytes 2064384 | tf_op jit(solution)/shard_map/all_to_all | solution.py:1387
  379.8 29.5 %all-to-all-done.8 = bf16[8,168,384]{2,1,0:T(8,128)(2,1)S(1)} async-done(((bf16[8,168,384]{2,1,0:T(8,128)(2,1)}), bf16[8,168,384]{2,1,0:T(8,128)(2,1)S(1)}, u32[]{:S(2)}, u32[]{:S(2)}) %all-to-all-start.8) | async-done | bytes 1032224 | tf_op jit(solution)/shard_map/all_to_all | solution.py:1387
  (257 shorter events, 85.8 us)
Async XLA Ops:
  9.5 38.5 %all-to-all-start = ((bf16[16,96,256]{2,1,0:T(8,128)(2,1)}), bf16[16,96,256]{2,1,0:T(8,128)(2,1)S(1)}, u32[]{:S(2)}, u32[]{:S(2)}) async-start(bf16[16,96,256]{2,1,0:T(8,128)(2,1)} %bitcast.5), calls=%async_computation | async-start | bytes 1572864 | tf_op jit(solution)/shard_map/all_to_all | solution.py:1191
  17.1 86.4 %all-gather.3.cloned.1.call-start = ((), (), s32[]{:S(2)}) async-start(), calls=%async_computation.11 | async-start | bytes 1658880 | tf_op jit(solution)/shard_map/all_gather | solution.py:1278
  18.5 18.0 %collective-permute-start.1 = (bf16[176,768]{1,0:T(8,128)(2,1)S(1)}, bf16[176,768]{1,0:T(8,128)(2,1)S(1)}, u32[]{:S(2)}, u32[]{:S(2)}) collective-permute-start(bf16[176,768]{1,0:T(8,128)(2,1)S(1)} %fusion.7.refs_0_), channel_id=1, source_target_pairs={{0,4},{1,5},{4,8},{5,9},{8,12},{9,13},{12,14},{13,15},{14,10},{15,... | collective-permute-start | bytes 811016 | tf_op jit(solution)/shard_map/ppermute | solution.py:1139
  20.4 22.0 %collective-permute-start.4 = (bf16[176,768]{1,0:T(8,128)(2,1)S(1)}, bf16[176,768]{1,0:T(8,128)(2,1)S(1)}, u32[]{:S(2)}, u32[]{:S(2)}) collective-permute-start(bf16[176,768]{1,0:T(8,128)(2,1)S(1)} %fusion.7.refs_0_), channel_id=1, source_target_pairs={{0,2},{1,3},{4,0},{5,1},{8,4},{9,5},{12,8},{13,9},{14,12},{15,13},... | collective-permute-start | bytes 811016 | tf_op jit(solution)/shard_map/ppermute | solution.py:1139
  36.6 11.5 %collective-permute-start.2 = (bf16[176,768]{1,0:T(8,128)(2,1)S(1)}, bf16[176,768]{1,0:T(8,128)(2,1)S(1)}, u32[]{:S(2)}, u32[]{:S(2)}) collective-permute-start(bf16[176,768]{1,0:T(8,128)(2,1)S(1)} %collective-permute-done.1.refs_1_), channel_id=1, source_target_pairs={{0,4},{1,5},{4,8},{5,9},{8,12},{9,13},{12,14},{13,15},{14,10},{15,... | collective-permute-start | bytes 811016 | tf_op jit(solution)/shard_map/ppermute | solution.py:1139
  42.5 8.5 %collective-permute-start.5 = (bf16[176,768]{1,0:T(8,128)(2,1)S(1)}, bf16[176,768]{1,0:T(8,128)(2,1)S(1)}, u32[]{:S(2)}, u32[]{:S(2)}) collective-permute-start(bf16[176,768]{1,0:T(8,128)(2,1)S(1)} %collective-permute-done.4.refs_4_), channel_id=1, source_target_pairs={{0,2},{1,3},{4,0},{5,1},{8,4},{9,5},{12,8},{13,9},{14,12},{15,13},... | collective-permute-start | bytes 811016 | tf_op jit(solution)/shard_map/ppermute | solution.py:1139
  48.0 11.7 %collective-permute-start.3 = (bf16[176,768]{1,0:T(8,128)(2,1)S(1)}, bf16[176,768]{1,0:T(8,128)(2,1)S(1)}, u32[]{:S(2)}, u32[]{:S(2)}) collective-permute-start(bf16[176,768]{1,0:T(8,128)(2,1)S(1)} %collective-permute-done.2.refs_2_), channel_id=1, source_target_pairs={{0,4},{1,5},{4,8},{5,9},{8,12},{9,13},{12,14},{13,15},{14,10},{15,... | collective-permute-start | bytes 811016 | tf_op jit(solution)/shard_map/ppermute | solution.py:1139
  51.0 7.2 %collective-permute-start.6 = (bf16[176,768]{1,0:T(8,128)(2,1)S(1)}, bf16[176,768]{1,0:T(8,128)(2,1)S(1)}, u32[]{:S(2)}, u32[]{:S(2)}) collective-permute-start(bf16[176,768]{1,0:T(8,128)(2,1)S(1)} %collective-permute-done.5.refs_5_), channel_id=1, source_target_pairs={{0,2},{1,3},{4,0},{5,1},{8,4},{9,5},{12,8},{13,9},{14,12},{15,13},... | collective-permute-start | bytes 811016 | tf_op jit(solution)/shard_map/ppermute | solution.py:1139
  91.9 27.6 %all-to-all-start.1 = ((bf16[16,96,256]{2,1,0:T(8,128)(2,1)}), bf16[16,96,256]{2,1,0:T(8,128)(2,1)S(1)}, u32[]{:S(2)}, u32[]{:S(2)}) async-start(bf16[16,96,256]{2,1,0:T(8,128)(2,1)} %get-tuple-element.92), calls=%async_computation.1 | async-start | bytes 1572864 | tf_op jit(solution)/shard_map/all_to_all | solution.py:1191
  103.4 48.8 %collective-permute-start.10 = (bf16[4,216,768]{2,1,0:T(8,128)(2,1)}, bf16[4,216,768]{2,1,0:T(8,128)(2,1)}, u32[]{:S(2)}, u32[]{:S(2)}) collective-permute-start(bf16[4,216,768]{2,1,0:T(8,128)(2,1)} %bitcast.123), channel_id=1, source_target_pairs={{0,16},{16,0},{1,17},{17,1},{2,18},{18,2},{3,19},{19,3},{4,20},{20... | collective-permute-start | bytes 3981320 | tf_op jit(solution)/shard_map/ppermute | solution.py:1313
  104.9 43.1 %collective-permute-start.12 = (bf16[4,216,768]{2,1,0:T(8,128)(2,1)}, bf16[4,216,768]{2,1,0:T(8,128)(2,1)}, u32[]{:S(2)}, u32[]{:S(2)}) collective-permute-start(bf16[4,216,768]{2,1,0:T(8,128)(2,1)} %bitcast.124), channel_id=1, source_target_pairs={{0,2},{1,3},{2,0},{3,1},{4,6},{5,7},{6,4},{7,5},{8,10},{9,11},{10,... | collective-permute-start | bytes 3981320 | tf_op jit(solution)/shard_map/ppermute | solution.py:1312
  119.5 32.8 %all-to-all-start.2 = ((bf16[16,96,256]{2,1,0:T(8,128)(2,1)}), bf16[16,96,256]{2,1,0:T(8,128)(2,1)S(1)}, u32[]{:S(2)}, u32[]{:S(2)}) async-start(bf16[16,96,256]{2,1,0:T(8,128)(2,1)} %bitcast.20), calls=%async_computation.2 | async-start | bytes 1572864 | tf_op jit(solution)/shard_map/all_to_all | solution.py:1191
  148.0 29.9 %collective-permute-start.15 = (bf16[4,216,768]{2,1,0:T(8,128)(2,1)}, bf16[4,216,768]{2,1,0:T(8,128)(2,1)}, u32[]{:S(2)}, u32[]{:S(2)}) collective-permute-start(bf16[4,216,768]{2,1,0:T(8,128)(2,1)} %collective-permute-done.12.refs_8_.refs_9_), channel_id=1, source_target_pairs={{0,16},{16,0},{1,17},{17,1},{2,18},{18,2},{3,19},{19,3},{4,20},{20... | collective-permute-start | bytes 3981320 | tf_op jit(solution)/shard_map/ppermute | solution.py:1321
  152.3 29.0 %all-to-all-start.3 = ((bf16[16,96,256]{2,1,0:T(8,128)(2,1)}), bf16[16,96,256]{2,1,0:T(8,128)(2,1)S(1)}, u32[]{:S(2)}, u32[]{:S(2)}) async-start(bf16[16,96,256]{2,1,0:T(8,128)(2,1)} %get-tuple-element.97), calls=%async_computation.3 | async-start | bytes 1572864 | tf_op jit(solution)/shard_map/all_to_all | solution.py:1191
  158.8 19.7 %collective-permute-start.13 = (bf16[4,216,768]{2,1,0:T(8,128)(2,1)S(1)}, bf16[4,216,768]{2,1,0:T(8,128)(2,1)}, u32[]{:S(2)}, u32[]{:S(2)}) collective-permute-start(bf16[4,216,768]{2,1,0:T(8,128)(2,1)S(1)} %bitcast.127), channel_id=1, source_target_pairs={{0,1},{1,0},{2,3},{3,2},{4,5},{5,4},{6,7},{7,6},{8,9},{9,8},{10,11... | collective-permute-start | bytes 3981320 | tf_op jit(solution)/shard_map/ppermute | solution.py:1273
  159.3 19.2 %collective-permute-start.14 = (bf16[4,216,768]{2,1,0:T(8,128)(2,1)}, bf16[4,216,768]{2,1,0:T(8,128)(2,1)}, u32[]{:S(2)}, u32[]{:S(2)}) collective-permute-start(bf16[4,216,768]{2,1,0:T(8,128)(2,1)} %collective-permute-done.12.refs_8_.refs_9_), channel_id=1, source_target_pairs={{0,1},{1,0},{2,3},{3,2},{4,5},{5,4},{6,7},{7,6},{8,9},{9,8},{10,11... | collective-permute-start | bytes 3981320 | tf_op jit(solution)/shard_map/ppermute | solution.py:1273
  159.4 19.1 %collective-permute-start.16 = (bf16[4,216,768]{2,1,0:T(8,128)(2,1)}, bf16[4,216,768]{2,1,0:T(8,128)(2,1)}, u32[]{:S(2)}, u32[]{:S(2)}) collective-permute-start(bf16[4,216,768]{2,1,0:T(8,128)(2,1)} %collective-permute-done.10.refs_14_.refs_15_), channel_id=1, source_target_pairs={{0,1},{1,0},{2,3},{3,2},{4,5},{5,4},{6,7},{7,6},{8,9},{9,8},{10,11... | collective-permute-start | bytes 3981320 | tf_op jit(solution)/shard_map/ppermute | solution.py:1273
  224.4 23.8 %all-to-all-start.4 = ((bf16[16,96,256]{2,1,0:T(8,128)(2,1)}), bf16[16,96,256]{2,1,0:T(8,128)(2,1)S(1)}, u32[]{:S(2)}, u32[]{:S(2)}) async-start(bf16[16,96,256]{2,1,0:T(8,128)(2,1)} %get-tuple-element.103), calls=%async_computation.4 | async-start | bytes 1572864 | tf_op jit(solution)/shard_map/all_to_all | solution.py:1191
  229.5 33.7 %collective-permute-start.20 = (bf16[16,16,128]{2,1,0:T(8,128)(2,1)}, bf16[16,16,128]{2,1,0:T(8,128)(2,1)S(1)}, u32[]{:S(2)}, u32[]{:S(2)}) collective-permute-start(bf16[16,16,128]{2,1,0:T(8,128)(2,1)} %get-tuple-element.109), channel_id=1, source_target_pairs={{1,0},{2,1},{3,2},{4,3},{5,4},{6,5},{7,6},{8,7},{9,8},{10,9},{11,1... | collective-permute-start | bytes 196616 | tf_op jit(solution)/shard_map/ppermute | solution.py:1339
  232.2 32.1 %collective-permute-start.19 = (bf16[4,432,384]{2,1,0:T(8,128)(2,1)}, bf16[4,432,384]{2,1,0:T(8,128)(2,1)S(1)}, u32[]{:S(2)}, u32[]{:S(2)}) collective-permute-start(bf16[4,432,384]{2,1,0:T(8,128)(2,1)} %add_convert_fusion.3), channel_id=1, source_target_pairs={{0,16},{16,0},{1,17},{17,1},{2,18},{18,2},{3,19},{19,3},{4,20},{20... | collective-permute-start | bytes 3981320 | tf_op jit(solution)/shard_map/ppermute | solution.py:1349
  248.2 22.5 %collective-permute-start.21 = (bf16[4,432,384]{2,1,0:T(8,128)(2,1)}, bf16[4,432,384]{2,1,0:T(8,128)(2,1)}, u32[]{:S(2)}, u32[]{:S(2)}) collective-permute-start(bf16[4,432,384]{2,1,0:T(8,128)(2,1)} %get-tuple-element.120), channel_id=1, source_target_pairs={{0,1},{1,0},{2,3},{3,2},{4,5},{5,4},{6,7},{7,6},{8,9},{9,8},{10,11... | collective-permute-start | bytes 3981320 | tf_op jit(solution)/shard_map/ppermute | solution.py:1273
  248.5 27.3 %collective-permute-start.23 = (bf16[4,432,384]{2,1,0:T(8,128)(2,1)}, bf16[4,432,384]{2,1,0:T(8,128)(2,1)}, u32[]{:S(2)}, u32[]{:S(2)}) collective-permute-start(bf16[4,432,384]{2,1,0:T(8,128)(2,1)} %get-tuple-element.128), channel_id=1, source_target_pairs={{0,1},{1,0},{2,3},{3,2},{4,5},{5,4},{6,7},{7,6},{8,9},{9,8},{10,11... | collective-permute-start | bytes 3981320 | tf_op jit(solution)/shard_map/ppermute | solution.py:1273
  264.3 29.6 %all-to-all-start.5 = ((bf16[16,112,256]{2,1,0:T(8,128)(2,1)}), bf16[16,112,256]{2,1,0:T(8,128)(2,1)}, u32[]{:S(2)}, u32[]{:S(2)}) async-start(bf16[16,112,256]{2,1,0:T(8,128)(2,1)} %get-tuple-element.110), calls=%async_computation.5 | async-start | bytes 1835008 | tf_op jit(solution)/shard_map/all_to_all | solution.py:1191
  273.9 53.1 %collective-permute-start.22 = (bf16[4,432,384]{2,1,0:T(8,128)(2,1)}, bf16[4,432,384]{2,1,0:T(8,128)(2,1)S(1)}, u32[]{:S(2)}, u32[]{:S(2)}) collective-permute-start(bf16[4,432,384]{2,1,0:T(8,128)(2,1)} %add_convert_fusion.2), channel_id=1, source_target_pairs={{0,2},{1,3},{2,0},{3,1},{4,6},{5,7},{6,4},{7,5},{8,10},{9,11},{10,... | collective-permute-start | bytes 3981320 | tf_op jit(solution)/shard_map/ppermute | solution.py:1412
  278.5 48.5 %collective-permute-start.24 = (bf16[4,432,384]{2,1,0:T(8,128)(2,1)}, bf16[4,432,384]{2,1,0:T(8,128)(2,1)}, u32[]{:S(2)}, u32[]{:S(2)}) collective-permute-start(bf16[4,432,384]{2,1,0:T(8,128)(2,1)} %add_convert_fusion.1), channel_id=1, source_target_pairs={{0,16},{16,0},{1,17},{17,1},{2,18},{18,2},{3,19},{19,3},{4,20},{20... | collective-permute-start | bytes 3981320 | tf_op jit(solution)/shard_map/ppermute | solution.py:1351
  293.9 33.1 %all-to-all-start.6 = ((bf16[16,112,256]{2,1,0:T(8,128)(2,1)}), bf16[16,112,256]{2,1,0:T(8,128)(2,1)S(1)}, u32[]{:S(2)}, u32[]{:S(2)}) async-start(bf16[16,112,256]{2,1,0:T(8,128)(2,1)} %get-tuple-element.111), calls=%async_computation.6 | async-start | bytes 1835008 | tf_op jit(solution)/shard_map/all_to_all | solution.py:1191
  325.1 9.2 %collective-permute-start.27 = (bf16[8,96,768]{2,1,0:T(8,128)(2,1)S(1)}, bf16[8,96,768]{2,1,0:T(8,128)(2,1)}, u32[]{:S(2)}, u32[]{:S(2)}) collective-permute-start(bf16[8,96,768]{2,1,0:T(8,128)(2,1)S(1)} %dynamic-slice_bitcast_fusion), channel_id=1, source_target_pairs={{0,1},{1,0},{2,3},{3,2},{4,5},{5,4},{6,7},{7,6},{8,9},{9,8},{10,11... | collective-permute-start | bytes 3538952 | tf_op jit(solution)/shard_map/ppermute | solution.py:1379
  326.6 12.9 %collective-permute-start.29 = (bf16[4,432,384]{2,1,0:T(8,128)(2,1)}, bf16[4,432,384]{2,1,0:T(8,128)(2,1)}, u32[]{:S(2)}, u32[]{:S(2)}) collective-permute-start(bf16[4,432,384]{2,1,0:T(8,128)(2,1)} %get-tuple-element.136), channel_id=1, source_target_pairs={{0,1},{1,0},{2,3},{3,2},{4,5},{5,4},{6,7},{7,6},{8,9},{9,8},{10,11... | collective-permute-start | bytes 3981320 | tf_op jit(solution)/shard_map/ppermute | solution.py:1273
  327.0 37.1 %all-to-all-start.7 = ((bf16[16,112,256]{2,1,0:T(8,128)(2,1)}), bf16[16,112,256]{2,1,0:T(8,128)(2,1)}, u32[]{:S(2)}, u32[]{:S(2)}) async-start(bf16[16,112,256]{2,1,0:T(8,128)(2,1)} %get-tuple-element.130), calls=%async_computation.7 | async-start | bytes 1835008 | tf_op jit(solution)/shard_map/all_to_all | solution.py:1191
  332.9 77.3 %reduce-scatter.2.cloned.1.call-start = ((), (), s32[]{:S(2)}) async-start(), calls=%async_computation.10 | async-start | bytes 1658880 | tf_op jit(solution)/shard_map/reduce_scatter | solution.py:1435
  337.3 24.3 %collective-permute-start.28 = (bf16[8,144,384]{2,1,0:T(8,128)(2,1)}, bf16[8,144,384]{2,1,0:T(8,128)(2,1)}, u32[]{:S(2)}, u32[]{:S(2)}) collective-permute-start(bf16[8,144,384]{2,1,0:T(8,128)(2,1)} %fusion.4), channel_id=1, source_target_pairs={{0,16},{16,0},{1,17},{17,1},{2,18},{18,2},{3,19},{19,3},{4,20},{20... | collective-permute-start | bytes 2654216 | tf_op jit(solution)/shard_map/ppermute | solution.py:1373
  364.2 45.1 %all-to-all-start.8 = ((bf16[8,168,384]{2,1,0:T(8,128)(2,1)}), bf16[8,168,384]{2,1,0:T(8,128)(2,1)S(1)}, u32[]{:S(2)}, u32[]{:S(2)}) async-start(bf16[8,168,384]{2,1,0:T(8,128)(2,1)} %pad_maximum_fusion), calls=%async_computation.8 | async-start | bytes 2064384 | tf_op jit(solution)/shard_map/all_to_all | solution.py:1387
  (66 other events, 537.2 us)
Sparse Core Ops, SparseCore 0:
  71.2 32.1 all-gather.2
  356.3 44.7 reduce-scatter.1

commit v6 on v5

--- a/solution.py
+++ b/solution.py
@@ -26,6 +26,7 @@
 SUM_ROWS = 16
 BATCH = 11
 PRM = 32
+SMALL = PRM // 2
 
 
 def unit(turns):
@@ -491,7 +492,8 @@
     def _():
         for turn in range(turns):
             for ref, (device, _) in zip((own_small, other_small), slots(table_ref, turns, turn)):
-                small = jnp.concatenate([ref[turn].astype(f32), jnp.zeros((LANE - PRM, LANE), f32)], axis=0)
+                small = ref[turn].astype(f32)
+                small = jnp.concatenate([small[:, :LANE], small[:, LANE:], jnp.zeros((LANE - PRM, LANE), f32)], axis=0)
                 prm_ref[pl.ds(pl.multiple_of(device * chans, 8), chans), :] = small.T[:chans, :PRM]
 
         def gather(d, carry):
@@ -522,7 +524,7 @@
     keep = (table_ref[turns + 1] > 0).astype(f32)
     for w_ref, (device, g) in zip((own_ref, other_ref), slots(table_ref, turns, step)):
         prm = prm_ref[pl.ds(pl.multiple_of(device * chans, 8), chans), :]
-        proj = mm16(w_ref[0, PRM:, :], xb[...], NN)
+        proj = mm16(w_ref[0, SMALL:, :], xb[...], NN)
         ys = []
         px = []
         for i in range(3):
@@ -620,7 +622,7 @@
         sd((devices, rows, width), bf16),
         sd((devices, 8 * seqs, LANE), bf16),
     )
-    small = pl.BlockSpec((turns, PRM, LANE), lambda i, t: (0, 0, 0), pipeline_mode=pl.Buffered(1))
+    small = pl.BlockSpec((turns, SMALL, 2 * LANE), lambda i, t: (0, 0, 0), pipeline_mode=pl.Buffered(1))
     return chip_call(
         2,
         lambda *refs: front_body(seqs, *refs),
@@ -931,7 +933,7 @@
             seqs, prm, (0,), (p0_ref[g],), (token_columns(p0h_ref[g].astype(f32), chans),), projx_ref[g].astype(f32), cols // seqs, cols
         )
         sums_ref[g] = totals[0]
-        acc[...] += mm16(w_ref[0, PRM : PRM + chans, :], d_low, TN)
+        acc[...] += mm16(w_ref[0, SMALL : SMALL + chans, :], d_low, TN)
         g_ref[g] = mm16(d_low, xn_ref[...], NT).astype(bf16)
 
 
@@ -986,7 +988,7 @@
         d_low, totals = short_back(seqs, prm, (1, 2), d_short, head, projx_ref[g].astype(f32), width, cols)
         for n, t in enumerate(totals):
             sums[n, device] = t
-        acc[...] += mm16(w_ref[0, PRM + chans :, :], d_low, TN)
+        acc[...] += mm16(w_ref[0, SMALL + chans :, :], d_low, TN)
         g_ref[g] = mm16(d_low, xn_ref[...], NT).astype(bf16)
 
     @pl.when(step == last)
@@ -1252,7 +1254,8 @@
         ],
         axis=0,
     )
-    small = jnp.pad(small, ((0, PRM - small.shape[0]), (0, dim - chans)))
+    small = jnp.pad(small, ((0, PRM - small.shape[0]), (0, LANE - chans)))
+    small = jnp.concatenate([small[:SMALL], small[SMALL:], jnp.zeros((SMALL, dim - 2 * LANE), bf16)], axis=1)
     in_rows = in_weight.transpose(1, 2, 0).reshape(3 * chans, dim)
     ring = ring_of(devices // 2)
     chips = devices // 2

time: 424 us -> 422 us (level)
  transfers between devices with their start and end apart: 43 -> 43, of which waited for: 18 -> 20; matrix products, arithmetic and copies ran while one was open for 13% -> 13% of each run, Pallas kernels for 22% -> 22%
where the time goes in v6:
time: 422 us; the launch traced here: 420 us
  Pallas kernels  137 us (32%)
  waiting for transfers between devices  111 us (26%)
  starting transfers between devices  90.3 us (21%)
  local copies, waits for them, and re-layouts  29.9 us (7%)
  other arithmetic  22.7 us (5%)
  between operations  14.9 us (4%)
  matrix products  14.8 us (4%)
    pallas_call x4, Pallas kernels, chip_call(): pl.pallas_call(body, cost_estimate=takes(us), out_shape=out, grid_spec=pl...  97.9 us
    all_to_all x8, starting transfers between devices, exchange(): lax.all_to_all(values, 'chan', split_axis=0, concat_axis=0, tiled=True)  51.6 us
    pallas_call x5, Pallas kernels, whole_call(): pl.pallas_call(body, cost_estimate=takes(us), out_shape=out_shape, in_spe...  39.3 us
    all_to_all x1, waiting for transfers between devices, over_chips(): lax.all_to_all(both, 'chan', split_axis=0, concat_axis=0, tiled=True, axi...  29.4 us
    all_to_all x8, waiting for transfers between devices, exchange(): lax.all_to_all(values, 'chan', split_axis=0, concat_axis=0, tiled=True)  28.1 us
    ppermute x1, waiting for transfers between devices, on_device(): far_across = lax.ppermute(far, 'batch', swap)  18.3 us
    dot_general x3, matrix products, mm(): lax.dot_general(a, b, (dims, ((), ())), precision=highest, preferred_elem...  14.8 us
    ppermute x8, starting transfers between devices, ring_hop(): return lax.ppermute(values, 'chan', moves)  13.7 us
  transfers between devices with their start and end apart: 43, of which 20 were waited for; matrix products, arithmetic and copies ran while one was open for 13% of the time, Pallas kernels for 22%

profile of v6, /device:TPU:0, one launch (start us, length us, event | category | flops | bytes accessed | tf_op | source)
XLA Modules:
  0.0 420.3 jit_solution(5425156616139768576)
XLA Ops:
  9.5 7.5 %all-to-all-start = ((bf16[16,96,256]{2,1,0:T(8,128)(2,1)}), bf16[16,96,256]{2,1,0:T(8,128)(2,1)S(1)}, u32[]{:S(2)}, u32[]{:S(2)}) async-start(bf16[16,96,256]{2,1,0:T(8,128)(2,1)} %bitcast.5), calls=%async_computation | async-start | bytes 1572864 | tf_op jit(solution)/shard_map/all_to_all | solution.py:1193
  20.6 6.2 %multiply_cosine_fusion.1 = (f32[64,4096]{1,0:T(8,128)}, f32[64,4096]{1,0:T(8,128)S(1)}, f32[64,4096]{1,0:T(8,128)}) fusion(f32[64]{0:T(128)S(1)} %copy-done.35, f32[64]{0:T(128)S(1)} %copy-done.41, f32[33,4096]{1,0:T(8,128)S(1)} %copy-done.6, f32[33,64]{1,0:T(8,128)S(1)} %copy-done.33), kind=kOutput, calls=%fused_computation.24 | convolution fusion | flops 104333312 | bytes 3695360 | tf_op jit(solution)/shard_map/dot_general | solution.py:1079
  26.9 6.2 %multiply_cosine_fusion = (f32[64,4096]{1,0:T(8,128)}, f32[64,4096]{1,0:T(8,128)S(1)}, f32[64,4096]{1,0:T(8,128)}) fusion(f32[64]{0:T(128)S(1)} %copy-done.35, f32[64]{0:T(128)S(1)} %copy-done.42, f32[64,4096]{1,0:T(8,128)S(1)} %get-tuple-element.173.h1_ref, f32[64,64]{1,0:T(8,128)S(1)} %copy-done.26), kind=kOutput, calls=%fused_computation.22 | convolution fusion | flops 201850880 | bytes 4211200 | tf_op jit(solution)/shard_map/dot_general | solution.py:1079
  33.1 2.9 collective-permute-done.1.refs_1_
  36.0 5.9 %collective-permute-start.2 = (bf16[160,768]{1,0:T(8,128)(2,1)S(1)}, bf16[160,768]{1,0:T(8,128)(2,1)S(1)}, u32[]{:S(2)}, u32[]{:S(2)}) collective-permute-start(bf16[160,768]{1,0:T(8,128)(2,1)S(1)} %collective-permute-done.1.refs_1_), channel_id=1, source_target_pairs={{0,4},{1,5},{4,8},{5,9},{8,12},{9,13},{12,14},{13,15},{14,10},{15,... | collective-permute-start | bytes 737288 | tf_op jit(solution)/shard_map/ppermute | solution.py:1141
  51.2 4.1 shard_map.469.refs_7_.refs_1_.refs_3_
  58.4 2.8 collective-permute-done.7
  62.3 3.1 shard_map.470.refs_3_.refs_5_.refs_4_
  71.6 16.9 %shard_map.471 = (f32[768,32]{1,0:T(8,128)}, bf16[768,512]{1,0:T(8,128)(2,1)}, f32[16,512]{1,0:T(8,128)}, f32[16,48,512]{2,1,0:T(8,128)}, f32[16,96,512]{2,1,0:T...) custom-call(s32[13]{0:T(128)} %concatenate.39.refs_0_, ...), custom_call_target="tpu_custom_call" | custom-call | flops 2000000000 | bytes 6000000 | tf_op jit(solution)/shard_map/pallas_call | solution.py:586
  88.5 10.3 %all-to-all-start.1 = ((bf16[16,96,256]{2,1,0:T(8,128)(2,1)}), bf16[16,96,256]{2,1,0:T(8,128)(2,1)S(1)}, u32[]{:S(2)}, u32[]{:S(2)}) async-start(bf16[16,96,256]{2,1,0:T(8,128)(2,1)} %get-tuple-element.92), calls=%async_computation.1 | async-start | bytes 1572864 | tf_op jit(solution)/shard_map/all_to_all | solution.py:1193
  103.9 13.7 %all-to-all-done.1.refs_0_.refs_1_ = bf16[16,96,256]{2,1,0:T(8,128)(2,1)S(1)} async-done(((bf16[16,96,256]{2,1,0:T(8,128)(2,1)}), bf16[16,96,256]{2,1,0:T(8,128)(2,1)S(1)}, u32[]{:S(2)}, u32[]{:S(2)}) %all-to-all-start.1) | async-done | bytes 786464 | tf_op jit(solution)/shard_map/all_to_all | solution.py:1193
  117.6 5.5 %all-to-all-start.2 = ((bf16[16,96,256]{2,1,0:T(8,128)(2,1)}), bf16[16,96,256]{2,1,0:T(8,128)(2,1)S(1)}, u32[]{:S(2)}, u32[]{:S(2)}) async-start(bf16[16,96,256]{2,1,0:T(8,128)(2,1)} %bitcast.20), calls=%async_computation.2 | async-start | bytes 1572864 | tf_op jit(solution)/shard_map/all_to_all | solution.py:1193
  123.1 11.1 %shard_map.472 = (bf16[16,96,256]{2,1,0:T(8,128)(2,1)}, f32[33,96,256]{2,1,0:T(8,128)}) custom-call(bf16[16,96,256]{2,1,0:T(8,128)(2,1)} %copy-done.14, f32[33,48,256]{2,1,0:T(8,128)} %shard_map.469.refs_7_.refs_1_.refs_3_, f32[48,1]{1,0:T(8,128)} %copy.64.refs_2_.refs_4_, f32[33,1,256]{2,1,0:T(1,128)} %constant.95.clone.twist_ref.refs_3_.refs_5_, ...), custom_call_target="tpu_custom_call" | custom-call | flops 99999997952 | bytes 300000000 | tf_op jit(solution)/shard_map/pallas_call | solution.py:338
  134.2 11.5 %collective-permute-done.12.refs_8_.refs_9_ = bf16[4,216,768]{2,1,0:T(8,128)(2,1)} collective-permute-done((bf16[4,216,768]{2,1,0:T(8,128)(2,1)}, bf16[4,216,768]{2,1,0:T(8,128)(2,1)}, u32[]{:S(2)}, u32[]{:S(2)}) %collective-permute-start.12) | collective-permute-done | bytes 1327136 | tf_op jit(solution)/shard_map/ppermute | solution.py:1315
  150.3 6.5 %all-to-all-start.3 = ((bf16[16,96,256]{2,1,0:T(8,128)(2,1)}), bf16[16,96,256]{2,1,0:T(8,128)(2,1)S(1)}, u32[]{:S(2)}, u32[]{:S(2)}) async-start(bf16[16,96,256]{2,1,0:T(8,128)(2,1)} %get-tuple-element.97), calls=%async_computation.3 | async-start | bytes 1572864 | tf_op jit(solution)/shard_map/all_to_all | solution.py:1193
  157.9 18.3 %collective-permute-done.15.refs_16_.refs_17_ = bf16[4,216,768]{2,1,0:T(8,128)(2,1)} collective-permute-done((bf16[4,216,768]{2,1,0:T(8,128)(2,1)}, bf16[4,216,768]{2,1,0:T(8,128)(2,1)}, u32[]{:S(2)}, u32[]{:S(2)}) %collective-permute-start.15) | collective-permute-done | bytes 1327136 | tf_op jit(solution)/shard_map/ppermute | solution.py:1324
  180.5 42.0 %shard_map.473 = (bf16[16,112,256]{2,1,0:T(8,128)(2,1)}, bf16[16,96,256]{2,1,0:T(8,128)(2,1)}, f32[768,512]{1,0:T(8,128)}, f32[768,512]{1,0:T(8,128)}, bf16[16,1...) custom-call(s32[13]{0:T(128)} %concatenate.38.refs_0_, ...), custom_call_target="tpu_custom_call" | custom-call | flops 35999997952 | bytes 108000000 | tf_op jit(solution)/shard_map/pallas_call | solution.py:586
  222.7 4.9 %all-to-all-start.4 = ((bf16[16,96,256]{2,1,0:T(8,128)(2,1)}), bf16[16,96,256]{2,1,0:T(8,128)(2,1)S(1)}, u32[]{:S(2)}, u32[]{:S(2)}) async-start(bf16[16,96,256]{2,1,0:T(8,128)(2,1)} %get-tuple-element.103), calls=%async_computation.4 | async-start | bytes 1572864 | tf_op jit(solution)/shard_map/all_to_all | solution.py:1193
  231.9 14.4 %all-to-all-done.4.refs_0_ = bf16[16,96,256]{2,1,0:T(8,128)(2,1)S(1)} async-done(((bf16[16,96,256]{2,1,0:T(8,128)(2,1)}), bf16[16,96,256]{2,1,0:T(8,128)(2,1)S(1)}, u32[]{:S(2)}, u32[]{:S(2)}) %all-to-all-start.4) | async-done | bytes 786464 | tf_op jit(solution)/shard_map/all_to_all | solution.py:1193
  247.2 14.1 %shard_map.474 = (bf16[16,112,256]{2,1,0:T(8,128)(2,1)}, f32[48,4096]{1,0:T(8,128)}, f32[48,1]{1,0:T(8,128)}) custom-call(bf16[16,96,256]{2,1,0:T(8,128)(2,1)} %copy-done.17, bf16[16,96,256]{2,1,0:T(8,128)(2,1)} %copy-done.14, f32[33,96,256]{2,1,0:T(8,128)} %get-tuple-element.107.refs_2_, f32[33,48,256]{2,1,0:T(8,128)} %shard_map.469.refs_7_.refs_1_.refs_3_, ...), custom_call_target="tpu_custom_call" | custom-call | flops 99999997952 | bytes 300000000 | tf_op jit(solution)/shard_map/pallas_call | solution.py:338
  262.4 6.4 %all-to-all-start.5 = ((bf16[16,112,256]{2,1,0:T(8,128)(2,1)}), bf16[16,112,256]{2,1,0:T(8,128)(2,1)}, u32[]{:S(2)}, u32[]{:S(2)}) async-start(bf16[16,112,256]{2,1,0:T(8,128)(2,1)} %get-tuple-element.110), calls=%async_computation.5 | async-start | bytes 1835008 | tf_op jit(solution)/shard_map/all_to_all | solution.py:1193
  268.8 3.2 add_convert_fusion.2
  273.9 2.8 add_convert_fusion.1
  278.2 14.0 %shard_map.475 = (bf16[16,48,768]{2,1,0:T(8,128)(2,1)}, f32[16,8,256]{2,1,0:T(8,128)}, f32[768,512]{1,0:T(8,128)}) custom-call(s32[13]{0:T(128)} %concatenate.39.refs_0_, f32[16,48,512]{2,1,0:T(8,128)} %bitcast.101, bf16[16,16,128]{2,1,0:T(8,128)(2,1)} %copy-done.31, bf16[16,48,640]{2,1,0:T(8,128)(2,1)} %get-tuple-element.122.refs_3_, ...), custom_call_target="tpu_custom_call" | custom-call | flops 2000000000 | bytes 6000000 | tf_op jit(solution)/shard_map/pallas_call | solution.py:586
  292.2 4.7 %all-to-all-start.6 = ((bf16[16,112,256]{2,1,0:T(8,128)(2,1)}), bf16[16,112,256]{2,1,0:T(8,128)(2,1)S(1)}, u32[]{:S(2)}, u32[]{:S(2)}) async-start(bf16[16,112,256]{2,1,0:T(8,128)(2,1)} %get-tuple-element.111), calls=%async_computation.6 | async-start | bytes 1835008 | tf_op jit(solution)/shard_map/all_to_all | solution.py:1193
  296.9 25.0 %shard_map.476 = (bf16[16,112,256]{2,1,0:T(8,128)(2,1)}, bf16[16,96,768]{2,1,0:T(8,128)(2,1)}) custom-call(s32[13]{0:T(128)} %concatenate.39.refs_0_, bf16[16,112,256]{2,1,0:T(8,128)(2,1)} %all-to-all-done.5.refs_1_, f32[16,96,512]{2,1,0:T(8,128)} %get-tuple-element.112.refs_2_, bf16[16,16,128]{2,1,0:T(8,128)(2,1)} %copy-done.52, ...), custom_call_target="tpu_custom_call" | custom-call | flops 99999997952 | bytes 300000000 | tf_op jit(solution)/shard_map/pallas_call | solution.py:586
  325.3 5.8 %all-to-all-start.7 = ((bf16[16,112,256]{2,1,0:T(8,128)(2,1)}), bf16[16,112,256]{2,1,0:T(8,128)(2,1)}, u32[]{:S(2)}, u32[]{:S(2)}) async-start(bf16[16,112,256]{2,1,0:T(8,128)(2,1)} %get-tuple-element.130), calls=%async_computation.7 | async-start | bytes 1835008 | tf_op jit(solution)/shard_map/all_to_all | solution.py:1193
  337.6 4.3 %add_convert_fusion = bf16[4,432,384]{2,1,0:T(8,128)(2,1)} fusion(bf16[4,432,384]{2,1,0:T(8,128)(2,1)} %copy-done.7, bf16[4,432,384]{2,1,0:T(8,128)(2,1)} %collective-permute-done.24, bf16[4,432,384]{2,1,0:T(8,128)(2,1)} %collective-permute-done.29, bf16[4,432,384]{2,1,0:T(8,128)(2,1)} %get-tuple-element.134), kind=kLoop, calls=%fused_computation.5 | loop fusion | flops 5308416 | bytes 6635520 | tf_op jit(solution)/shard_map/convert_element_type | solution.py:1345
  341.9 6.8 %shard_map.477 = (f32[33,64]{1,0:T(8,128)}, f32[64,64]{1,0:T(8,128)}, f32[64,48]{1,0:T(8,128)}, f32[8,256]{1,0:T(8,128)}, f32[48,1]{1,0:T(8,128)}) custom-call(f32[48,4096]{1,0:T(8,128)} %get-tuple-element.138.d_ref, f32[48,4096]{1,0:T(8,128)} %get-tuple-element.195.raw_ref, f32[48,4096]{1,0:T(8,128)} %get-tuple-element.181.fall_ref, f32[64,4096]{1,0:T(8,128)} %copy-done.3, ...), custom_call_target="tpu_custom_call" | custom-call | flops 10000000 | bytes 30000 | tf_op jit(solution)/shard_map/pallas_call | solution.py:338
  354.4 4.1 collective-permute-done.30
  362.5 5.6 %all-to-all-start.8 = ((bf16[8,168,384]{2,1,0:T(8,128)(2,1)}), bf16[8,168,384]{2,1,0:T(8,128)(2,1)S(1)}, u32[]{:S(2)}, u32[]{:S(2)}) async-start(bf16[8,168,384]{2,1,0:T(8,128)(2,1)} %pad_maximum_fusion), calls=%async_computation.8 | async-start | bytes 2064384 | tf_op jit(solution)/shard_map/all_to_all | solution.py:1390
  378.0 29.4 %all-to-all-done.8 = bf16[8,168,384]{2,1,0:T(8,128)(2,1)S(1)} async-done(((bf16[8,168,384]{2,1,0:T(8,128)(2,1)}), bf16[8,168,384]{2,1,0:T(8,128)(2,1)S(1)}, u32[]{:S(2)}, u32[]{:S(2)}) %all-to-all-start.8) | async-done | bytes 1032224 | tf_op jit(solution)/shard_map/all_to_all | solution.py:1390
  (259 shorter events, 85.3 us)
Async XLA Ops:
  9.5 37.5 %all-to-all-start = ((bf16[16,96,256]{2,1,0:T(8,128)(2,1)}), bf16[16,96,256]{2,1,0:T(8,128)(2,1)S(1)}, u32[]{:S(2)}, u32[]{:S(2)}) async-start(bf16[16,96,256]{2,1,0:T(8,128)(2,1)} %bitcast.5), calls=%async_computation | async-start | bytes 1572864 | tf_op jit(solution)/shard_map/all_to_all | solution.py:1193
  17.1 84.5 %all-gather.3.cloned.1.call-start = ((), (), s32[]{:S(2)}) async-start(), calls=%async_computation.11 | async-start | bytes 1658880 | tf_op jit(solution)/shard_map/all_gather | solution.py:1281
  18.5 17.5 %collective-permute-start.1 = (bf16[160,768]{1,0:T(8,128)(2,1)S(1)}, bf16[160,768]{1,0:T(8,128)(2,1)S(1)}, u32[]{:S(2)}, u32[]{:S(2)}) collective-permute-start(bf16[160,768]{1,0:T(8,128)(2,1)S(1)} %pad_maximum_fusion.2.refs_0_), channel_id=1, source_target_pairs={{0,4},{1,5},{4,8},{5,9},{8,12},{9,13},{12,14},{13,15},{14,10},{15,... | collective-permute-start | bytes 737288 | tf_op jit(solution)/shard_map/ppermute | solution.py:1141
  20.5 21.5 %collective-permute-start.4 = (bf16[160,768]{1,0:T(8,128)(2,1)S(1)}, bf16[160,768]{1,0:T(8,128)(2,1)S(1)}, u32[]{:S(2)}, u32[]{:S(2)}) collective-permute-start(bf16[160,768]{1,0:T(8,128)(2,1)S(1)} %pad_maximum_fusion.2.refs_0_), channel_id=1, source_target_pairs={{0,2},{1,3},{4,0},{5,1},{8,4},{9,5},{12,8},{13,9},{14,12},{15,13},... | collective-permute-start | bytes 737288 | tf_op jit(solution)/shard_map/ppermute | solution.py:1141
  36.0 10.9 %collective-permute-start.2 = (bf16[160,768]{1,0:T(8,128)(2,1)S(1)}, bf16[160,768]{1,0:T(8,128)(2,1)S(1)}, u32[]{:S(2)}, u32[]{:S(2)}) collective-permute-start(bf16[160,768]{1,0:T(8,128)(2,1)S(1)} %collective-permute-done.1.refs_1_), channel_id=1, source_target_pairs={{0,4},{1,5},{4,8},{5,9},{8,12},{9,13},{12,14},{13,15},{14,10},{15,... | collective-permute-start | bytes 737288 | tf_op jit(solution)/shard_map/ppermute | solution.py:1141
  41.9 8.0 %collective-permute-start.5 = (bf16[160,768]{1,0:T(8,128)(2,1)S(1)}, bf16[160,768]{1,0:T(8,128)(2,1)S(1)}, u32[]{:S(2)}, u32[]{:S(2)}) collective-permute-start(bf16[160,768]{1,0:T(8,128)(2,1)S(1)} %collective-permute-done.4.refs_4_), channel_id=1, source_target_pairs={{0,2},{1,3},{4,0},{5,1},{8,4},{9,5},{12,8},{13,9},{14,12},{15,13},... | collective-permute-start | bytes 737288 | tf_op jit(solution)/shard_map/ppermute | solution.py:1141
  47.0 9.3 %collective-permute-start.3 = (bf16[160,768]{1,0:T(8,128)(2,1)S(1)}, bf16[160,768]{1,0:T(8,128)(2,1)S(1)}, u32[]{:S(2)}, u32[]{:S(2)}) collective-permute-start(bf16[160,768]{1,0:T(8,128)(2,1)S(1)} %collective-permute-done.2.refs_2_), channel_id=1, source_target_pairs={{0,4},{1,5},{4,8},{5,9},{8,12},{9,13},{12,14},{13,15},{14,10},{15,... | collective-permute-start | bytes 737288 | tf_op jit(solution)/shard_map/ppermute | solution.py:1141
  49.9 6.7 %collective-permute-start.6 = (bf16[160,768]{1,0:T(8,128)(2,1)S(1)}, bf16[160,768]{1,0:T(8,128)(2,1)S(1)}, u32[]{:S(2)}, u32[]{:S(2)}) collective-permute-start(bf16[160,768]{1,0:T(8,128)(2,1)S(1)} %collective-permute-done.5.refs_5_), channel_id=1, source_target_pairs={{0,2},{1,3},{4,0},{5,1},{8,4},{9,5},{12,8},{13,9},{14,12},{15,13},... | collective-permute-start | bytes 737288 | tf_op jit(solution)/shard_map/ppermute | solution.py:1141
  88.5 29.1 %all-to-all-start.1 = ((bf16[16,96,256]{2,1,0:T(8,128)(2,1)}), bf16[16,96,256]{2,1,0:T(8,128)(2,1)S(1)}, u32[]{:S(2)}, u32[]{:S(2)}) async-start(bf16[16,96,256]{2,1,0:T(8,128)(2,1)} %get-tuple-element.92), calls=%async_computation.1 | async-start | bytes 1572864 | tf_op jit(solution)/shard_map/all_to_all | solution.py:1193
  101.5 48.8 %collective-permute-start.10 = (bf16[4,216,768]{2,1,0:T(8,128)(2,1)}, bf16[4,216,768]{2,1,0:T(8,128)(2,1)}, u32[]{:S(2)}, u32[]{:S(2)}) collective-permute-start(bf16[4,216,768]{2,1,0:T(8,128)(2,1)} %bitcast.123), channel_id=1, source_target_pairs={{0,16},{16,0},{1,17},{17,1},{2,18},{18,2},{3,19},{19,3},{4,20},{20... | collective-permute-start | bytes 3981320 | tf_op jit(solution)/shard_map/ppermute | solution.py:1316
  102.4 43.3 %collective-permute-start.12 = (bf16[4,216,768]{2,1,0:T(8,128)(2,1)}, bf16[4,216,768]{2,1,0:T(8,128)(2,1)}, u32[]{:S(2)}, u32[]{:S(2)}) collective-permute-start(bf16[4,216,768]{2,1,0:T(8,128)(2,1)} %bitcast.124), channel_id=1, source_target_pairs={{0,2},{1,3},{2,0},{3,1},{4,6},{5,7},{6,4},{7,5},{8,10},{9,11},{10,... | collective-permute-start | bytes 3981320 | tf_op jit(solution)/shard_map/ppermute | solution.py:1315
  117.6 32.8 %all-to-all-start.2 = ((bf16[16,96,256]{2,1,0:T(8,128)(2,1)}), bf16[16,96,256]{2,1,0:T(8,128)(2,1)S(1)}, u32[]{:S(2)}, u32[]{:S(2)}) async-start(bf16[16,96,256]{2,1,0:T(8,128)(2,1)} %bitcast.20), calls=%async_computation.2 | async-start | bytes 1572864 | tf_op jit(solution)/shard_map/all_to_all | solution.py:1193
  145.7 30.5 %collective-permute-start.15 = (bf16[4,216,768]{2,1,0:T(8,128)(2,1)}, bf16[4,216,768]{2,1,0:T(8,128)(2,1)}, u32[]{:S(2)}, u32[]{:S(2)}) collective-permute-start(bf16[4,216,768]{2,1,0:T(8,128)(2,1)} %collective-permute-done.12.refs_8_.refs_9_), channel_id=1, source_target_pairs={{0,16},{16,0},{1,17},{17,1},{2,18},{18,2},{3,19},{19,3},{4,20},{20... | collective-permute-start | bytes 3981320 | tf_op jit(solution)/shard_map/ppermute | solution.py:1324
  150.3 29.3 %all-to-all-start.3 = ((bf16[16,96,256]{2,1,0:T(8,128)(2,1)}), bf16[16,96,256]{2,1,0:T(8,128)(2,1)S(1)}, u32[]{:S(2)}, u32[]{:S(2)}) async-start(bf16[16,96,256]{2,1,0:T(8,128)(2,1)} %get-tuple-element.97), calls=%async_computation.3 | async-start | bytes 1572864 | tf_op jit(solution)/shard_map/all_to_all | solution.py:1193
  156.9 19.9 %collective-permute-start.13 = (bf16[4,216,768]{2,1,0:T(8,128)(2,1)S(1)}, bf16[4,216,768]{2,1,0:T(8,128)(2,1)}, u32[]{:S(2)}, u32[]{:S(2)}) collective-permute-start(bf16[4,216,768]{2,1,0:T(8,128)(2,1)S(1)} %bitcast.127), channel_id=1, source_target_pairs={{0,1},{1,0},{2,3},{3,2},{4,5},{5,4},{6,7},{7,6},{8,9},{9,8},{10,11... | collective-permute-start | bytes 3981320 | tf_op jit(solution)/shard_map/ppermute | solution.py:1276
  157.4 19.5 %collective-permute-start.14 = (bf16[4,216,768]{2,1,0:T(8,128)(2,1)}, bf16[4,216,768]{2,1,0:T(8,128)(2,1)}, u32[]{:S(2)}, u32[]{:S(2)}) collective-permute-start(bf16[4,216,768]{2,1,0:T(8,128)(2,1)} %collective-permute-done.12.refs_8_.refs_9_), channel_id=1, source_target_pairs={{0,1},{1,0},{2,3},{3,2},{4,5},{5,4},{6,7},{7,6},{8,9},{9,8},{10,11... | collective-permute-start | bytes 3981320 | tf_op jit(solution)/shard_map/ppermute | solution.py:1276
  157.5 19.3 %collective-permute-start.16 = (bf16[4,216,768]{2,1,0:T(8,128)(2,1)}, bf16[4,216,768]{2,1,0:T(8,128)(2,1)}, u32[]{:S(2)}, u32[]{:S(2)}) collective-permute-start(bf16[4,216,768]{2,1,0:T(8,128)(2,1)} %collective-permute-done.10.refs_14_.refs_15_), channel_id=1, source_target_pairs={{0,1},{1,0},{2,3},{3,2},{4,5},{5,4},{6,7},{7,6},{8,9},{9,8},{10,11... | collective-permute-start | bytes 3981320 | tf_op jit(solution)/shard_map/ppermute | solution.py:1276
  222.7 23.6 %all-to-all-start.4 = ((bf16[16,96,256]{2,1,0:T(8,128)(2,1)}), bf16[16,96,256]{2,1,0:T(8,128)(2,1)S(1)}, u32[]{:S(2)}, u32[]{:S(2)}) async-start(bf16[16,96,256]{2,1,0:T(8,128)(2,1)} %get-tuple-element.103), calls=%async_computation.4 | async-start | bytes 1572864 | tf_op jit(solution)/shard_map/all_to_all | solution.py:1193
  227.6 33.7 %collective-permute-start.20 = (bf16[16,16,128]{2,1,0:T(8,128)(2,1)}, bf16[16,16,128]{2,1,0:T(8,128)(2,1)S(1)}, u32[]{:S(2)}, u32[]{:S(2)}) collective-permute-start(bf16[16,16,128]{2,1,0:T(8,128)(2,1)} %get-tuple-element.109), channel_id=1, source_target_pairs={{1,0},{2,1},{3,2},{4,3},{5,4},{6,5},{7,6},{8,7},{9,8},{10,9},{11,1... | collective-permute-start | bytes 196616 | tf_op jit(solution)/shard_map/ppermute | solution.py:1342
  230.3 32.1 %collective-permute-start.19 = (bf16[4,432,384]{2,1,0:T(8,128)(2,1)}, bf16[4,432,384]{2,1,0:T(8,128)(2,1)S(1)}, u32[]{:S(2)}, u32[]{:S(2)}) collective-permute-start(bf16[4,432,384]{2,1,0:T(8,128)(2,1)} %add_convert_fusion.3), channel_id=1, source_target_pairs={{0,16},{16,0},{1,17},{17,1},{2,18},{18,2},{3,19},{19,3},{4,20},{20... | collective-permute-start | bytes 3981320 | tf_op jit(solution)/shard_map/ppermute | solution.py:1352
  246.3 22.5 %collective-permute-start.21 = (bf16[4,432,384]{2,1,0:T(8,128)(2,1)}, bf16[4,432,384]{2,1,0:T(8,128)(2,1)}, u32[]{:S(2)}, u32[]{:S(2)}) collective-permute-start(bf16[4,432,384]{2,1,0:T(8,128)(2,1)} %get-tuple-element.120), channel_id=1, source_target_pairs={{0,1},{1,0},{2,3},{3,2},{4,5},{5,4},{6,7},{7,6},{8,9},{9,8},{10,11... | collective-permute-start | bytes 3981320 | tf_op jit(solution)/shard_map/ppermute | solution.py:1276
  246.5 27.3 %collective-permute-start.23 = (bf16[4,432,384]{2,1,0:T(8,128)(2,1)}, bf16[4,432,384]{2,1,0:T(8,128)(2,1)}, u32[]{:S(2)}, u32[]{:S(2)}) collective-permute-start(bf16[4,432,384]{2,1,0:T(8,128)(2,1)} %get-tuple-element.128), channel_id=1, source_target_pairs={{0,1},{1,0},{2,3},{3,2},{4,5},{5,4},{6,7},{7,6},{8,9},{9,8},{10,11... | collective-permute-start | bytes 3981320 | tf_op jit(solution)/shard_map/ppermute | solution.py:1276
  262.4 29.8 %all-to-all-start.5 = ((bf16[16,112,256]{2,1,0:T(8,128)(2,1)}), bf16[16,112,256]{2,1,0:T(8,128)(2,1)}, u32[]{:S(2)}, u32[]{:S(2)}) async-start(bf16[16,112,256]{2,1,0:T(8,128)(2,1)} %get-tuple-element.110), calls=%async_computation.5 | async-start | bytes 1835008 | tf_op jit(solution)/shard_map/all_to_all | solution.py:1193
  272.0 53.3 %collective-permute-start.22 = (bf16[4,432,384]{2,1,0:T(8,128)(2,1)}, bf16[4,432,384]{2,1,0:T(8,128)(2,1)S(1)}, u32[]{:S(2)}, u32[]{:S(2)}) collective-permute-start(bf16[4,432,384]{2,1,0:T(8,128)(2,1)} %add_convert_fusion.2), channel_id=1, source_target_pairs={{0,2},{1,3},{2,0},{3,1},{4,6},{5,7},{6,4},{7,5},{8,10},{9,11},{10,... | collective-permute-start | bytes 3981320 | tf_op jit(solution)/shard_map/ppermute | solution.py:1415
  276.7 48.6 %collective-permute-start.24 = (bf16[4,432,384]{2,1,0:T(8,128)(2,1)}, bf16[4,432,384]{2,1,0:T(8,128)(2,1)}, u32[]{:S(2)}, u32[]{:S(2)}) collective-permute-start(bf16[4,432,384]{2,1,0:T(8,128)(2,1)} %add_convert_fusion.1), channel_id=1, source_target_pairs={{0,16},{16,0},{1,17},{17,1},{2,18},{18,2},{3,19},{19,3},{4,20},{20... | collective-permute-start | bytes 3981320 | tf_op jit(solution)/shard_map/ppermute | solution.py:1354
  292.2 33.1 %all-to-all-start.6 = ((bf16[16,112,256]{2,1,0:T(8,128)(2,1)}), bf16[16,112,256]{2,1,0:T(8,128)(2,1)S(1)}, u32[]{:S(2)}, u32[]{:S(2)}) async-start(bf16[16,112,256]{2,1,0:T(8,128)(2,1)} %get-tuple-element.111), calls=%async_computation.6 | async-start | bytes 1835008 | tf_op jit(solution)/shard_map/all_to_all | solution.py:1193
  323.3 9.2 %collective-permute-start.27 = (bf16[8,96,768]{2,1,0:T(8,128)(2,1)S(1)}, bf16[8,96,768]{2,1,0:T(8,128)(2,1)}, u32[]{:S(2)}, u32[]{:S(2)}) collective-permute-start(bf16[8,96,768]{2,1,0:T(8,128)(2,1)S(1)} %dynamic-slice_bitcast_fusion), channel_id=1, source_target_pairs={{0,1},{1,0},{2,3},{3,2},{4,5},{5,4},{6,7},{7,6},{8,9},{9,8},{10,11... | collective-permute-start | bytes 3538952 | tf_op jit(solution)/shard_map/ppermute | solution.py:1382
  324.8 12.8 %collective-permute-start.29 = (bf16[4,432,384]{2,1,0:T(8,128)(2,1)}, bf16[4,432,384]{2,1,0:T(8,128)(2,1)}, u32[]{:S(2)}, u32[]{:S(2)}) collective-permute-start(bf16[4,432,384]{2,1,0:T(8,128)(2,1)} %get-tuple-element.136), channel_id=1, source_target_pairs={{0,1},{1,0},{2,3},{3,2},{4,5},{5,4},{6,7},{7,6},{8,9},{9,8},{10,11... | collective-permute-start | bytes 3981320 | tf_op jit(solution)/shard_map/ppermute | solution.py:1276
  325.3 37.2 %all-to-all-start.7 = ((bf16[16,112,256]{2,1,0:T(8,128)(2,1)}), bf16[16,112,256]{2,1,0:T(8,128)(2,1)}, u32[]{:S(2)}, u32[]{:S(2)}) async-start(bf16[16,112,256]{2,1,0:T(8,128)(2,1)} %get-tuple-element.130), calls=%async_computation.7 | async-start | bytes 1835008 | tf_op jit(solution)/shard_map/all_to_all | solution.py:1193
  331.1 77.2 %reduce-scatter.2.cloned.1.call-start = ((), (), s32[]{:S(2)}) async-start(), calls=%async_computation.10 | async-start | bytes 1658880 | tf_op jit(solution)/shard_map/reduce_scatter | solution.py:1438
  335.5 24.3 %collective-permute-start.28 = (bf16[8,144,384]{2,1,0:T(8,128)(2,1)}, bf16[8,144,384]{2,1,0:T(8,128)(2,1)}, u32[]{:S(2)}, u32[]{:S(2)}) collective-permute-start(bf16[8,144,384]{2,1,0:T(8,128)(2,1)} %fusion.4), channel_id=1, source_target_pairs={{0,16},{16,0},{1,17},{17,1},{2,18},{18,2},{3,19},{19,3},{4,20},{20... | collective-permute-start | bytes 2654216 | tf_op jit(solution)/shard_map/ppermute | solution.py:1376
  362.5 45.0 %all-to-all-start.8 = ((bf16[8,168,384]{2,1,0:T(8,128)(2,1)}), bf16[8,168,384]{2,1,0:T(8,128)(2,1)S(1)}, u32[]{:S(2)}, u32[]{:S(2)}) async-start(bf16[8,168,384]{2,1,0:T(8,128)(2,1)} %pad_maximum_fusion), calls=%async_computation.8 | async-start | bytes 2064384 | tf_op jit(solution)/shard_map/all_to_all | solution.py:1390
  (66 other events, 532.2 us)
Sparse Core Ops, SparseCore 0:
  68.0 33.4 all-gather.2
  354.5 44.5 reduce-scatter.1

commit v7 on v6

--- a/solution.py
+++ b/solution.py
@@ -263,13 +263,13 @@
 def conv_forward_body(seqs, mixed_ref, filt_ref, bias_ref, twist_ref, ahead_ref, back_ref, out_ref, spec_ref, xs_ref, work_ref):
     rows = mixed_ref.shape[1]
     spread(mixed_ref, xs_ref)
-    rows_forward(xs_ref, spec_ref, rows)
+    rows_forward(xs_ref, work_ref, rows)
 
     def step(i, carry):
         at = pl.ds(i * BATCH, BATCH)
         twist = twists(twist_ref, at, rows)
-        z = fine_forward(together(spec_ref[at]), twist, ahead_ref)
-        spec_ref[at] = apart(z)
+        z = fine_forward(together(work_ref[at]), twist, ahead_ref)
+        spec_ref[at] = apart(z).astype(bf16)
         k = together(jnp.concatenate([filt_ref[at]] * seqs, axis=1))
         work_ref[at] = apart(fine_inverse(times(z, k), twist, back_ref))
         return carry
@@ -305,7 +305,7 @@
         at = pl.ds(i * BATCH, BATCH)
         z = fine_forward(together(spec_ref[at]), twists(twist_ref, at, rows), ahead_ref)
         k = together(jnp.concatenate([filt_ref[at]] * seqs, axis=1))
-        cross = apart(times_conj(z, together(mixed_spec_ref[at])))
+        cross = apart(times_conj(z, together(mixed_spec_ref[at].astype(f32))))
         cross = sum(cross[:, s * chans : (s + 1) * chans] for s in range(seqs))
         both = together(jnp.concatenate([apart(times_conj(z, k)), cross], axis=1))
         work_ref[at] = apart(fine_inverse(both, twists(twist_ref, at, rows + chans), back_ref))
@@ -365,7 +365,7 @@
     return whole_call(
         100,
         lambda *refs: conv_forward_body(seqs, *refs),
-        (jax.ShapeDtypeStruct(mixed.shape, bf16), jax.ShapeDtypeStruct((n, rows, 2 * LANE), f32)),
+        (jax.ShapeDtypeStruct(mixed.shape, bf16), jax.ShapeDtypeStruct((n, rows, 2 * LANE), bf16)),
         [pltpu.VMEM((COARSE, rows, LANE), f32), pltpu.VMEM((n, rows, 2 * LANE), f32)],
         mixed,
         filt_spec,
@@ -546,7 +546,7 @@
         projx_ref[g] = jnp.concatenate(px[1:], axis=0).astype(bf16)
         gate_ref[g] = ys[0]
         pair = jnp.concatenate(ys[1:], axis=0)
-        pair_ref[g] = pair
+        pair_ref[g] = pair.astype(bf16)
         mixed_ref[g] = stacked(ys[1] * ys[2], seqs).astype(bf16)
         heads_ref[g] = first_tokens(pair, seqs).astype(bf16)
 
@@ -616,7 +616,7 @@
         sd((dim, cols), bf16),
         sd((16, cols), f32),
         sd((devices, chans, cols), f32),
-        sd((devices, 2 * chans, cols), f32),
+        sd((devices, 2 * chans, cols), bf16),
         sd((devices, chans, cols + LANE), bf16),
         sd((devices, 2 * chans, cols + LANE), bf16),
         sd((devices, rows, width), bf16),
@@ -981,7 +981,7 @@
         square = jnp.concatenate([block[seqs * chans :, :LANE], jnp.zeros((LANE - HEAD_ROWS, LANE), f32)], axis=0).T
         second = pltpu.roll(square[chans : 2 * chans], LANE // 2, 1)
         d_head = jnp.where(lanes_of((chans, LANE)) < LANE // 2, square[:chans], second)
-        pair = pair_ref[g]
+        pair = pair_ref[g].astype(f32)
         pair_head = token_columns(heads_ref[g].astype(f32), 2 * chans)
         d_short = (d_mixed * pair[chans:], d_mixed * pair[:chans])
         head = (d_head * pair_head[chans:], d_head * pair_head[:chans])

time: 422 us -> 422 us (level)
  no operation moved by 1% of the time
where the time goes in v7:
time: 422 us; the launch traced here: 420 us
  Pallas kernels  136 us (32%)
  waiting for transfers between devices  112 us (27%)
  starting transfers between devices  90.4 us (21%)
  local copies, waits for them, and re-layouts  30 us (7%)
  other arithmetic  22.6 us (5%)
  between operations  14.9 us (4%)
  matrix products  14.7 us (3%)
    pallas_call x4, Pallas kernels, chip_call(): pl.pallas_call(body, cost_estimate=takes(us), out_shape=out, grid_spec=pl...  97.7 us
    all_to_all x8, starting transfers between devices, exchange(): lax.all_to_all(values, 'chan', split_axis=0, concat_axis=0, tiled=True)  51.9 us
    pallas_call x5, Pallas kernels, whole_call(): pl.pallas_call(body, cost_estimate=takes(us), out_shape=out_shape, in_spe...  38.4 us
    all_to_all x1, waiting for transfers between devices, over_chips(): lax.all_to_all(both, 'chan', split_axis=0, concat_axis=0, tiled=True, axi...  29.5 us
    all_to_all x8, waiting for transfers between devices, exchange(): lax.all_to_all(values, 'chan', split_axis=0, concat_axis=0, tiled=True)  28.1 us
    ppermute x1, waiting for transfers between devices, on_device(): far_across = lax.ppermute(far, 'batch', swap)  18.1 us
    dot_general x3, matrix products, mm(): lax.dot_general(a, b, (dims, ((), ())), precision=highest, preferred_elem...  14.7 us
    ppermute x8, starting transfers between devices, ring_hop(): return lax.ppermute(values, 'chan', moves)  13.7 us
  transfers between devices with their start and end apart: 43, of which 20 were waited for; matrix products, arithmetic and copies ran while one was open for 13% of the time, Pallas kernels for 22%

profile of v7, /device:TPU:0, one launch (start us, length us, event | category | flops | bytes accessed | tf_op | source)
XLA Modules:
  0.0 420.2 jit_solution(6994451628208382168)
XLA Ops:
  9.5 7.5 %all-to-all-start = ((bf16[16,96,256]{2,1,0:T(8,128)(2,1)}), bf16[16,96,256]{2,1,0:T(8,128)(2,1)S(1)}, u32[]{:S(2)}, u32[]{:S(2)}) async-start(bf16[16,96,256]{2,1,0:T(8,128)(2,1)} %bitcast.5), calls=%async_computation | async-start | bytes 1572864 | tf_op jit(solution)/shard_map/all_to_all | solution.py:1193
  20.5 6.1 %multiply_cosine_fusion.1 = (f32[64,4096]{1,0:T(8,128)}, f32[64,4096]{1,0:T(8,128)S(1)}, f32[64,4096]{1,0:T(8,128)}) fusion(f32[64]{0:T(128)S(1)} %copy-done.35, f32[64]{0:T(128)S(1)} %copy-done.41, f32[33,4096]{1,0:T(8,128)S(1)} %copy-done.6, f32[33,64]{1,0:T(8,128)S(1)} %copy-done.33), kind=kOutput, calls=%fused_computation.24 | convolution fusion | flops 104333312 | bytes 3695360 | tf_op jit(solution)/shard_map/dot_general | solution.py:1079
  26.7 6.2 %multiply_cosine_fusion = (f32[64,4096]{1,0:T(8,128)}, f32[64,4096]{1,0:T(8,128)S(1)}, f32[64,4096]{1,0:T(8,128)}) fusion(f32[64]{0:T(128)S(1)} %copy-done.35, f32[64]{0:T(128)S(1)} %copy-done.42, f32[64,4096]{1,0:T(8,128)S(1)} %get-tuple-element.173.h1_ref, f32[64,64]{1,0:T(8,128)S(1)} %copy-done.26), kind=kOutput, calls=%fused_computation.22 | convolution fusion | flops 201850880 | bytes 4211200 | tf_op jit(solution)/shard_map/dot_general | solution.py:1079
  32.9 3.1 collective-permute-done.1.refs_1_
  36.0 5.9 %collective-permute-start.2 = (bf16[160,768]{1,0:T(8,128)(2,1)S(1)}, bf16[160,768]{1,0:T(8,128)(2,1)S(1)}, u32[]{:S(2)}, u32[]{:S(2)}) collective-permute-start(bf16[160,768]{1,0:T(8,128)(2,1)S(1)} %collective-permute-done.1.refs_1_), channel_id=1, source_target_pairs={{0,4},{1,5},{4,8},{5,9},{8,12},{9,13},{12,14},{13,15},{14,10},{15,... | collective-permute-start | bytes 737288 | tf_op jit(solution)/shard_map/ppermute | solution.py:1141
  51.2 4.1 shard_map.469.refs_7_.refs_1_.refs_3_
  58.4 2.8 collective-permute-done.7
  62.3 3.0 shard_map.470.refs_3_.refs_5_.refs_4_
  71.6 16.8 %shard_map.471 = (f32[768,32]{1,0:T(8,128)}, bf16[768,512]{1,0:T(8,128)(2,1)}, f32[16,512]{1,0:T(8,128)}, f32[16,48,512]{2,1,0:T(8,128)}, bf16[16,96,512]{2,1,0:...) custom-call(s32[13]{0:T(128)} %concatenate.39.refs_0_, ...), custom_call_target="tpu_custom_call" | custom-call | flops 2000000000 | bytes 6000000 | tf_op jit(solution)/shard_map/pallas_call | solution.py:586
  88.5 10.3 %all-to-all-start.1 = ((bf16[16,96,256]{2,1,0:T(8,128)(2,1)}), bf16[16,96,256]{2,1,0:T(8,128)(2,1)S(1)}, u32[]{:S(2)}, u32[]{:S(2)}) async-start(bf16[16,96,256]{2,1,0:T(8,128)(2,1)} %get-tuple-element.92), calls=%async_computation.1 | async-start | bytes 1572864 | tf_op jit(solution)/shard_map/all_to_all | solution.py:1193
  103.9 13.6 %all-to-all-done.1.refs_0_.refs_1_ = bf16[16,96,256]{2,1,0:T(8,128)(2,1)S(1)} async-done(((bf16[16,96,256]{2,1,0:T(8,128)(2,1)}), bf16[16,96,256]{2,1,0:T(8,128)(2,1)S(1)}, u32[]{:S(2)}, u32[]{:S(2)}) %all-to-all-start.1) | async-done | bytes 786464 | tf_op jit(solution)/shard_map/all_to_all | solution.py:1193
  117.6 5.5 %all-to-all-start.2 = ((bf16[16,96,256]{2,1,0:T(8,128)(2,1)}), bf16[16,96,256]{2,1,0:T(8,128)(2,1)S(1)}, u32[]{:S(2)}, u32[]{:S(2)}) async-start(bf16[16,96,256]{2,1,0:T(8,128)(2,1)} %bitcast.20), calls=%async_computation.2 | async-start | bytes 1572864 | tf_op jit(solution)/shard_map/all_to_all | solution.py:1193
  123.1 10.7 %shard_map.472 = (bf16[16,96,256]{2,1,0:T(8,128)(2,1)}, bf16[33,96,256]{2,1,0:T(8,128)(2,1)}) custom-call(bf16[16,96,256]{2,1,0:T(8,128)(2,1)} %copy-done.14, f32[33,48,256]{2,1,0:T(8,128)} %shard_map.469.refs_7_.refs_1_.refs_3_, f32[48,1]{1,0:T(8,128)} %copy.64.refs_2_.refs_4_, f32[33,1,256]{2,1,0:T(1,128)} %constant.95.clone.twist_ref.refs_3_.refs_5_, ...), custom_call_target="tpu_custom_call" | custom-call | flops 99999997952 | bytes 300000000 | tf_op jit(solution)/shard_map/pallas_call | solution.py:338
  133.8 12.2 %collective-permute-done.12.refs_8_.refs_9_ = bf16[4,216,768]{2,1,0:T(8,128)(2,1)} collective-permute-done((bf16[4,216,768]{2,1,0:T(8,128)(2,1)}, bf16[4,216,768]{2,1,0:T(8,128)(2,1)}, u32[]{:S(2)}, u32[]{:S(2)}) %collective-permute-start.12) | collective-permute-done | bytes 1327136 | tf_op jit(solution)/shard_map/ppermute | solution.py:1315
  150.3 6.5 %all-to-all-start.3 = ((bf16[16,96,256]{2,1,0:T(8,128)(2,1)}), bf16[16,96,256]{2,1,0:T(8,128)(2,1)S(1)}, u32[]{:S(2)}, u32[]{:S(2)}) async-start(bf16[16,96,256]{2,1,0:T(8,128)(2,1)} %get-tuple-element.97), calls=%async_computation.3 | async-start | bytes 1572864 | tf_op jit(solution)/shard_map/all_to_all | solution.py:1193
  157.9 18.1 %collective-permute-done.15.refs_16_.refs_17_ = bf16[4,216,768]{2,1,0:T(8,128)(2,1)} collective-permute-done((bf16[4,216,768]{2,1,0:T(8,128)(2,1)}, bf16[4,216,768]{2,1,0:T(8,128)(2,1)}, u32[]{:S(2)}, u32[]{:S(2)}) %collective-permute-start.15) | collective-permute-done | bytes 1327136 | tf_op jit(solution)/shard_map/ppermute | solution.py:1324
  180.3 42.0 %shard_map.473 = (bf16[16,112,256]{2,1,0:T(8,128)(2,1)}, bf16[16,96,256]{2,1,0:T(8,128)(2,1)}, f32[768,512]{1,0:T(8,128)}, f32[768,512]{1,0:T(8,128)}, bf16[16,1...) custom-call(s32[13]{0:T(128)} %concatenate.38.refs_0_, ...), custom_call_target="tpu_custom_call" | custom-call | flops 35999997952 | bytes 108000000 | tf_op jit(solution)/shard_map/pallas_call | solution.py:586
  222.5 5.1 %all-to-all-start.4 = ((bf16[16,96,256]{2,1,0:T(8,128)(2,1)}), bf16[16,96,256]{2,1,0:T(8,128)(2,1)S(1)}, u32[]{:S(2)}, u32[]{:S(2)}) async-start(bf16[16,96,256]{2,1,0:T(8,128)(2,1)} %get-tuple-element.103), calls=%async_computation.4 | async-start | bytes 1572864 | tf_op jit(solution)/shard_map/all_to_all | solution.py:1193
  231.9 14.4 %all-to-all-done.4.refs_0_ = bf16[16,96,256]{2,1,0:T(8,128)(2,1)S(1)} async-done(((bf16[16,96,256]{2,1,0:T(8,128)(2,1)}), bf16[16,96,256]{2,1,0:T(8,128)(2,1)S(1)}, u32[]{:S(2)}, u32[]{:S(2)}) %all-to-all-start.4) | async-done | bytes 786464 | tf_op jit(solution)/shard_map/all_to_all | solution.py:1193
  247.2 13.8 %shard_map.474 = (bf16[16,112,256]{2,1,0:T(8,128)(2,1)}, f32[48,4096]{1,0:T(8,128)}, f32[48,1]{1,0:T(8,128)}) custom-call(bf16[16,96,256]{2,1,0:T(8,128)(2,1)} %copy-done.17, bf16[16,96,256]{2,1,0:T(8,128)(2,1)} %copy-done.14, bf16[33,96,256]{2,1,0:T(8,128)(2,1)} %get-tuple-element.107.refs_2_, f32[33,48,256]{2,1,0:T(8,128)} %shard_map.469.refs_7_.refs_1_.refs_3_, ...), custom_call_target="tpu_custom_call" | custom-call | flops 99999997952 | bytes 300000000 | tf_op jit(solution)/shard_map/pallas_call | solution.py:338
  262.4 6.4 %all-to-all-start.5 = ((bf16[16,112,256]{2,1,0:T(8,128)(2,1)}), bf16[16,112,256]{2,1,0:T(8,128)(2,1)}, u32[]{:S(2)}, u32[]{:S(2)}) async-start(bf16[16,112,256]{2,1,0:T(8,128)(2,1)} %get-tuple-element.110), calls=%async_computation.5 | async-start | bytes 1835008 | tf_op jit(solution)/shard_map/all_to_all | solution.py:1193
  268.8 3.1 add_convert_fusion.2
  273.8 2.8 add_convert_fusion.1
  278.2 14.0 %shard_map.475 = (bf16[16,48,768]{2,1,0:T(8,128)(2,1)}, f32[16,8,256]{2,1,0:T(8,128)}, f32[768,512]{1,0:T(8,128)}) custom-call(s32[13]{0:T(128)} %concatenate.39.refs_0_, f32[16,48,512]{2,1,0:T(8,128)} %bitcast.101, bf16[16,16,128]{2,1,0:T(8,128)(2,1)} %copy-done.31, bf16[16,48,640]{2,1,0:T(8,128)(2,1)} %get-tuple-element.122.refs_3_, ...), custom_call_target="tpu_custom_call" | custom-call | flops 2000000000 | bytes 6000000 | tf_op jit(solution)/shard_map/pallas_call | solution.py:586
  292.2 4.7 %all-to-all-start.6 = ((bf16[16,112,256]{2,1,0:T(8,128)(2,1)}), bf16[16,112,256]{2,1,0:T(8,128)(2,1)S(1)}, u32[]{:S(2)}, u32[]{:S(2)}) async-start(bf16[16,112,256]{2,1,0:T(8,128)(2,1)} %get-tuple-element.111), calls=%async_computation.6 | async-start | bytes 1835008 | tf_op jit(solution)/shard_map/all_to_all | solution.py:1193
  296.8 24.9 %shard_map.476 = (bf16[16,112,256]{2,1,0:T(8,128)(2,1)}, bf16[16,96,768]{2,1,0:T(8,128)(2,1)}) custom-call(s32[13]{0:T(128)} %concatenate.39.refs_0_, bf16[16,112,256]{2,1,0:T(8,128)(2,1)} %all-to-all-done.5.refs_1_, bf16[16,96,512]{2,1,0:T(8,128)(2,1)} %get-tuple-element.112.refs_2_, bf16[16,16,128]{2,1,0:T(8,128)(2,1)} %copy-done.52, ...), custom_call_target="tpu_custom_call" | custom-call | flops 99999997952 | bytes 300000000 | tf_op jit(solution)/shard_map/pallas_call | solution.py:586
  325.1 5.8 %all-to-all-start.7 = ((bf16[16,112,256]{2,1,0:T(8,128)(2,1)}), bf16[16,112,256]{2,1,0:T(8,128)(2,1)}, u32[]{:S(2)}, u32[]{:S(2)}) async-start(bf16[16,112,256]{2,1,0:T(8,128)(2,1)} %get-tuple-element.130), calls=%async_computation.7 | async-start | bytes 1835008 | tf_op jit(solution)/shard_map/all_to_all | solution.py:1193
  337.6 4.3 %add_convert_fusion = bf16[4,432,384]{2,1,0:T(8,128)(2,1)} fusion(bf16[4,432,384]{2,1,0:T(8,128)(2,1)} %copy-done.7, bf16[4,432,384]{2,1,0:T(8,128)(2,1)} %collective-permute-done.24, bf16[4,432,384]{2,1,0:T(8,128)(2,1)} %collective-permute-done.29, bf16[4,432,384]{2,1,0:T(8,128)(2,1)} %get-tuple-element.134), kind=kLoop, calls=%fused_computation.5 | loop fusion | flops 5308416 | bytes 6635520 | tf_op jit(solution)/shard_map/convert_element_type | solution.py:1345
  341.9 6.8 %shard_map.477 = (f32[33,64]{1,0:T(8,128)}, f32[64,64]{1,0:T(8,128)}, f32[64,48]{1,0:T(8,128)}, f32[8,256]{1,0:T(8,128)}, f32[48,1]{1,0:T(8,128)}) custom-call(f32[48,4096]{1,0:T(8,128)} %get-tuple-element.138.d_ref, f32[48,4096]{1,0:T(8,128)} %get-tuple-element.195.raw_ref, f32[48,4096]{1,0:T(8,128)} %get-tuple-element.181.fall_ref, f32[64,4096]{1,0:T(8,128)} %copy-done.3, ...), custom_call_target="tpu_custom_call" | custom-call | flops 10000000 | bytes 30000 | tf_op jit(solution)/shard_map/pallas_call | solution.py:338
  354.3 4.1 collective-permute-done.30
  362.3 5.6 %all-to-all-start.8 = ((bf16[8,168,384]{2,1,0:T(8,128)(2,1)}), bf16[8,168,384]{2,1,0:T(8,128)(2,1)S(1)}, u32[]{:S(2)}, u32[]{:S(2)}) async-start(bf16[8,168,384]{2,1,0:T(8,128)(2,1)} %pad_maximum_fusion), calls=%async_computation.8 | async-start | bytes 2064384 | tf_op jit(solution)/shard_map/all_to_all | solution.py:1390
  377.9 29.5 %all-to-all-done.8 = bf16[8,168,384]{2,1,0:T(8,128)(2,1)S(1)} async-done(((bf16[8,168,384]{2,1,0:T(8,128)(2,1)}), bf16[8,168,384]{2,1,0:T(8,128)(2,1)S(1)}, u32[]{:S(2)}, u32[]{:S(2)}) %all-to-all-start.8) | async-done | bytes 1032224 | tf_op jit(solution)/shard_map/all_to_all | solution.py:1390
  (259 shorter events, 85.4 us)
Async XLA Ops:
  9.5 37.5 %all-to-all-start = ((bf16[16,96,256]{2,1,0:T(8,128)(2,1)}), bf16[16,96,256]{2,1,0:T(8,128)(2,1)S(1)}, u32[]{:S(2)}, u32[]{:S(2)}) async-start(bf16[16,96,256]{2,1,0:T(8,128)(2,1)} %bitcast.5), calls=%async_computation | async-start | bytes 1572864 | tf_op jit(solution)/shard_map/all_to_all | solution.py:1193
  17.1 84.4 %all-gather.3.cloned.1.call-start = ((), (), s32[]{:S(2)}) async-start(), calls=%async_computation.11 | async-start | bytes 1658880 | tf_op jit(solution)/shard_map/all_gather | solution.py:1281
  18.5 17.5 %collective-permute-start.1 = (bf16[160,768]{1,0:T(8,128)(2,1)S(1)}, bf16[160,768]{1,0:T(8,128)(2,1)S(1)}, u32[]{:S(2)}, u32[]{:S(2)}) collective-permute-start(bf16[160,768]{1,0:T(8,128)(2,1)S(1)} %pad_maximum_fusion.2.refs_0_), channel_id=1, source_target_pairs={{0,4},{1,5},{4,8},{5,9},{8,12},{9,13},{12,14},{13,15},{14,10},{15,... | collective-permute-start | bytes 737288 | tf_op jit(solution)/shard_map/ppermute | solution.py:1141
  20.4 21.5 %collective-permute-start.4 = (bf16[160,768]{1,0:T(8,128)(2,1)S(1)}, bf16[160,768]{1,0:T(8,128)(2,1)S(1)}, u32[]{:S(2)}, u32[]{:S(2)}) collective-permute-start(bf16[160,768]{1,0:T(8,128)(2,1)S(1)} %pad_maximum_fusion.2.refs_0_), channel_id=1, source_target_pairs={{0,2},{1,3},{4,0},{5,1},{8,4},{9,5},{12,8},{13,9},{14,12},{15,13},... | collective-permute-start | bytes 737288 | tf_op jit(solution)/shard_map/ppermute | solution.py:1141
  36.0 10.9 %collective-permute-start.2 = (bf16[160,768]{1,0:T(8,128)(2,1)S(1)}, bf16[160,768]{1,0:T(8,128)(2,1)S(1)}, u32[]{:S(2)}, u32[]{:S(2)}) collective-permute-start(bf16[160,768]{1,0:T(8,128)(2,1)S(1)} %collective-permute-done.1.refs_1_), channel_id=1, source_target_pairs={{0,4},{1,5},{4,8},{5,9},{8,12},{9,13},{12,14},{13,15},{14,10},{15,... | collective-permute-start | bytes 737288 | tf_op jit(solution)/shard_map/ppermute | solution.py:1141
  41.9 8.0 %collective-permute-start.5 = (bf16[160,768]{1,0:T(8,128)(2,1)S(1)}, bf16[160,768]{1,0:T(8,128)(2,1)S(1)}, u32[]{:S(2)}, u32[]{:S(2)}) collective-permute-start(bf16[160,768]{1,0:T(8,128)(2,1)S(1)} %collective-permute-done.4.refs_4_), channel_id=1, source_target_pairs={{0,2},{1,3},{4,0},{5,1},{8,4},{9,5},{12,8},{13,9},{14,12},{15,13},... | collective-permute-start | bytes 737288 | tf_op jit(solution)/shard_map/ppermute | solution.py:1141
  47.0 9.3 %collective-permute-start.3 = (bf16[160,768]{1,0:T(8,128)(2,1)S(1)}, bf16[160,768]{1,0:T(8,128)(2,1)S(1)}, u32[]{:S(2)}, u32[]{:S(2)}) collective-permute-start(bf16[160,768]{1,0:T(8,128)(2,1)S(1)} %collective-permute-done.2.refs_2_), channel_id=1, source_target_pairs={{0,4},{1,5},{4,8},{5,9},{8,12},{9,13},{12,14},{13,15},{14,10},{15,... | collective-permute-start | bytes 737288 | tf_op jit(solution)/shard_map/ppermute | solution.py:1141
  49.9 6.7 %collective-permute-start.6 = (bf16[160,768]{1,0:T(8,128)(2,1)S(1)}, bf16[160,768]{1,0:T(8,128)(2,1)S(1)}, u32[]{:S(2)}, u32[]{:S(2)}) collective-permute-start(bf16[160,768]{1,0:T(8,128)(2,1)S(1)} %collective-permute-done.5.refs_5_), channel_id=1, source_target_pairs={{0,2},{1,3},{4,0},{5,1},{8,4},{9,5},{12,8},{13,9},{14,12},{15,13},... | collective-permute-start | bytes 737288 | tf_op jit(solution)/shard_map/ppermute | solution.py:1141
  88.5 29.1 %all-to-all-start.1 = ((bf16[16,96,256]{2,1,0:T(8,128)(2,1)}), bf16[16,96,256]{2,1,0:T(8,128)(2,1)S(1)}, u32[]{:S(2)}, u32[]{:S(2)}) async-start(bf16[16,96,256]{2,1,0:T(8,128)(2,1)} %get-tuple-element.92), calls=%async_computation.1 | async-start | bytes 1572864 | tf_op jit(solution)/shard_map/all_to_all | solution.py:1193
  101.5 48.9 %collective-permute-start.10 = (bf16[4,216,768]{2,1,0:T(8,128)(2,1)}, bf16[4,216,768]{2,1,0:T(8,128)(2,1)}, u32[]{:S(2)}, u32[]{:S(2)}) collective-permute-start(bf16[4,216,768]{2,1,0:T(8,128)(2,1)} %bitcast.123), channel_id=1, source_target_pairs={{0,16},{16,0},{1,17},{17,1},{2,18},{18,2},{3,19},{19,3},{4,20},{20... | collective-permute-start | bytes 3981320 | tf_op jit(solution)/shard_map/ppermute | solution.py:1316
  102.9 43.1 %collective-permute-start.12 = (bf16[4,216,768]{2,1,0:T(8,128)(2,1)}, bf16[4,216,768]{2,1,0:T(8,128)(2,1)}, u32[]{:S(2)}, u32[]{:S(2)}) collective-permute-start(bf16[4,216,768]{2,1,0:T(8,128)(2,1)} %bitcast.124), channel_id=1, source_target_pairs={{0,2},{1,3},{2,0},{3,1},{4,6},{5,7},{6,4},{7,5},{8,10},{9,11},{10,... | collective-permute-start | bytes 3981320 | tf_op jit(solution)/shard_map/ppermute | solution.py:1315
  117.6 32.8 %all-to-all-start.2 = ((bf16[16,96,256]{2,1,0:T(8,128)(2,1)}), bf16[16,96,256]{2,1,0:T(8,128)(2,1)S(1)}, u32[]{:S(2)}, u32[]{:S(2)}) async-start(bf16[16,96,256]{2,1,0:T(8,128)(2,1)} %bitcast.20), calls=%async_computation.2 | async-start | bytes 1572864 | tf_op jit(solution)/shard_map/all_to_all | solution.py:1193
  146.0 29.9 %collective-permute-start.15 = (bf16[4,216,768]{2,1,0:T(8,128)(2,1)}, bf16[4,216,768]{2,1,0:T(8,128)(2,1)}, u32[]{:S(2)}, u32[]{:S(2)}) collective-permute-start(bf16[4,216,768]{2,1,0:T(8,128)(2,1)} %collective-permute-done.12.refs_8_.refs_9_), channel_id=1, source_target_pairs={{0,16},{16,0},{1,17},{17,1},{2,18},{18,2},{3,19},{19,3},{4,20},{20... | collective-permute-start | bytes 3981320 | tf_op jit(solution)/shard_map/ppermute | solution.py:1324
  150.3 29.0 %all-to-all-start.3 = ((bf16[16,96,256]{2,1,0:T(8,128)(2,1)}), bf16[16,96,256]{2,1,0:T(8,128)(2,1)S(1)}, u32[]{:S(2)}, u32[]{:S(2)}) async-start(bf16[16,96,256]{2,1,0:T(8,128)(2,1)} %get-tuple-element.97), calls=%async_computation.3 | async-start | bytes 1572864 | tf_op jit(solution)/shard_map/all_to_all | solution.py:1193
  156.9 19.7 %collective-permute-start.13 = (bf16[4,216,768]{2,1,0:T(8,128)(2,1)S(1)}, bf16[4,216,768]{2,1,0:T(8,128)(2,1)}, u32[]{:S(2)}, u32[]{:S(2)}) collective-permute-start(bf16[4,216,768]{2,1,0:T(8,128)(2,1)S(1)} %bitcast.127), channel_id=1, source_target_pairs={{0,1},{1,0},{2,3},{3,2},{4,5},{5,4},{6,7},{7,6},{8,9},{9,8},{10,11... | collective-permute-start | bytes 3981320 | tf_op jit(solution)/shard_map/ppermute | solution.py:1276
  157.4 19.2 %collective-permute-start.14 = (bf16[4,216,768]{2,1,0:T(8,128)(2,1)}, bf16[4,216,768]{2,1,0:T(8,128)(2,1)}, u32[]{:S(2)}, u32[]{:S(2)}) collective-permute-start(bf16[4,216,768]{2,1,0:T(8,128)(2,1)} %collective-permute-done.12.refs_8_.refs_9_), channel_id=1, source_target_pairs={{0,1},{1,0},{2,3},{3,2},{4,5},{5,4},{6,7},{7,6},{8,9},{9,8},{10,11... | collective-permute-start | bytes 3981320 | tf_op jit(solution)/shard_map/ppermute | solution.py:1276
  157.5 19.1 %collective-permute-start.16 = (bf16[4,216,768]{2,1,0:T(8,128)(2,1)}, bf16[4,216,768]{2,1,0:T(8,128)(2,1)}, u32[]{:S(2)}, u32[]{:S(2)}) collective-permute-start(bf16[4,216,768]{2,1,0:T(8,128)(2,1)} %collective-permute-done.10.refs_14_.refs_15_), channel_id=1, source_target_pairs={{0,1},{1,0},{2,3},{3,2},{4,5},{5,4},{6,7},{7,6},{8,9},{9,8},{10,11... | collective-permute-start | bytes 3981320 | tf_op jit(solution)/shard_map/ppermute | solution.py:1276
  222.5 23.8 %all-to-all-start.4 = ((bf16[16,96,256]{2,1,0:T(8,128)(2,1)}), bf16[16,96,256]{2,1,0:T(8,128)(2,1)S(1)}, u32[]{:S(2)}, u32[]{:S(2)}) async-start(bf16[16,96,256]{2,1,0:T(8,128)(2,1)} %get-tuple-element.103), calls=%async_computation.4 | async-start | bytes 1572864 | tf_op jit(solution)/shard_map/all_to_all | solution.py:1193
  227.6 33.4 %collective-permute-start.20 = (bf16[16,16,128]{2,1,0:T(8,128)(2,1)}, bf16[16,16,128]{2,1,0:T(8,128)(2,1)S(1)}, u32[]{:S(2)}, u32[]{:S(2)}) collective-permute-start(bf16[16,16,128]{2,1,0:T(8,128)(2,1)} %get-tuple-element.109), channel_id=1, source_target_pairs={{1,0},{2,1},{3,2},{4,3},{5,4},{6,5},{7,6},{8,7},{9,8},{10,9},{11,1... | collective-permute-start | bytes 196616 | tf_op jit(solution)/shard_map/ppermute | solution.py:1342
  230.3 32.1 %collective-permute-start.19 = (bf16[4,432,384]{2,1,0:T(8,128)(2,1)}, bf16[4,432,384]{2,1,0:T(8,128)(2,1)S(1)}, u32[]{:S(2)}, u32[]{:S(2)}) collective-permute-start(bf16[4,432,384]{2,1,0:T(8,128)(2,1)} %add_convert_fusion.3), channel_id=1, source_target_pairs={{0,16},{16,0},{1,17},{17,1},{2,18},{18,2},{3,19},{19,3},{4,20},{20... | collective-permute-start | bytes 3981320 | tf_op jit(solution)/shard_map/ppermute | solution.py:1352
  246.3 22.5 %collective-permute-start.21 = (bf16[4,432,384]{2,1,0:T(8,128)(2,1)}, bf16[4,432,384]{2,1,0:T(8,128)(2,1)}, u32[]{:S(2)}, u32[]{:S(2)}) collective-permute-start(bf16[4,432,384]{2,1,0:T(8,128)(2,1)} %get-tuple-element.120), channel_id=1, source_target_pairs={{0,1},{1,0},{2,3},{3,2},{4,5},{5,4},{6,7},{7,6},{8,9},{9,8},{10,11... | collective-permute-start | bytes 3981320 | tf_op jit(solution)/shard_map/ppermute | solution.py:1276
  246.6 27.3 %collective-permute-start.23 = (bf16[4,432,384]{2,1,0:T(8,128)(2,1)}, bf16[4,432,384]{2,1,0:T(8,128)(2,1)}, u32[]{:S(2)}, u32[]{:S(2)}) collective-permute-start(bf16[4,432,384]{2,1,0:T(8,128)(2,1)} %get-tuple-element.128), channel_id=1, source_target_pairs={{0,1},{1,0},{2,3},{3,2},{4,5},{5,4},{6,7},{7,6},{8,9},{9,8},{10,11... | collective-permute-start | bytes 3981320 | tf_op jit(solution)/shard_map/ppermute | solution.py:1276
  262.4 29.8 %all-to-all-start.5 = ((bf16[16,112,256]{2,1,0:T(8,128)(2,1)}), bf16[16,112,256]{2,1,0:T(8,128)(2,1)}, u32[]{:S(2)}, u32[]{:S(2)}) async-start(bf16[16,112,256]{2,1,0:T(8,128)(2,1)} %get-tuple-element.110), calls=%async_computation.5 | async-start | bytes 1835008 | tf_op jit(solution)/shard_map/all_to_all | solution.py:1193
  272.0 53.1 %collective-permute-start.22 = (bf16[4,432,384]{2,1,0:T(8,128)(2,1)}, bf16[4,432,384]{2,1,0:T(8,128)(2,1)S(1)}, u32[]{:S(2)}, u32[]{:S(2)}) collective-permute-start(bf16[4,432,384]{2,1,0:T(8,128)(2,1)} %add_convert_fusion.2), channel_id=1, source_target_pairs={{0,2},{1,3},{2,0},{3,1},{4,6},{5,7},{6,4},{7,5},{8,10},{9,11},{10,... | collective-permute-start | bytes 3981320 | tf_op jit(solution)/shard_map/ppermute | solution.py:1415
  276.6 48.5 %collective-permute-start.24 = (bf16[4,432,384]{2,1,0:T(8,128)(2,1)}, bf16[4,432,384]{2,1,0:T(8,128)(2,1)}, u32[]{:S(2)}, u32[]{:S(2)}) collective-permute-start(bf16[4,432,384]{2,1,0:T(8,128)(2,1)} %add_convert_fusion.1), channel_id=1, source_target_pairs={{0,16},{16,0},{1,17},{17,1},{2,18},{18,2},{3,19},{19,3},{4,20},{20... | collective-permute-start | bytes 3981320 | tf_op jit(solution)/shard_map/ppermute | solution.py:1354
  292.2 32.9 %all-to-all-start.6 = ((bf16[16,112,256]{2,1,0:T(8,128)(2,1)}), bf16[16,112,256]{2,1,0:T(8,128)(2,1)S(1)}, u32[]{:S(2)}, u32[]{:S(2)}) async-start(bf16[16,112,256]{2,1,0:T(8,128)(2,1)} %get-tuple-element.111), calls=%async_computation.6 | async-start | bytes 1835008 | tf_op jit(solution)/shard_map/all_to_all | solution.py:1193
  323.2 9.2 %collective-permute-start.27 = (bf16[8,96,768]{2,1,0:T(8,128)(2,1)S(1)}, bf16[8,96,768]{2,1,0:T(8,128)(2,1)}, u32[]{:S(2)}, u32[]{:S(2)}) collective-permute-start(bf16[8,96,768]{2,1,0:T(8,128)(2,1)S(1)} %dynamic-slice_bitcast_fusion), channel_id=1, source_target_pairs={{0,1},{1,0},{2,3},{3,2},{4,5},{5,4},{6,7},{7,6},{8,9},{9,8},{10,11... | collective-permute-start | bytes 3538952 | tf_op jit(solution)/shard_map/ppermute | solution.py:1382
  324.7 12.9 %collective-permute-start.29 = (bf16[4,432,384]{2,1,0:T(8,128)(2,1)}, bf16[4,432,384]{2,1,0:T(8,128)(2,1)}, u32[]{:S(2)}, u32[]{:S(2)}) collective-permute-start(bf16[4,432,384]{2,1,0:T(8,128)(2,1)} %get-tuple-element.136), channel_id=1, source_target_pairs={{0,1},{1,0},{2,3},{3,2},{4,5},{5,4},{6,7},{7,6},{8,9},{9,8},{10,11... | collective-permute-start | bytes 3981320 | tf_op jit(solution)/shard_map/ppermute | solution.py:1276
  325.1 37.2 %all-to-all-start.7 = ((bf16[16,112,256]{2,1,0:T(8,128)(2,1)}), bf16[16,112,256]{2,1,0:T(8,128)(2,1)}, u32[]{:S(2)}, u32[]{:S(2)}) async-start(bf16[16,112,256]{2,1,0:T(8,128)(2,1)} %get-tuple-element.130), calls=%async_computation.7 | async-start | bytes 1835008 | tf_op jit(solution)/shard_map/all_to_all | solution.py:1193
  330.9 77.3 %reduce-scatter.2.cloned.1.call-start = ((), (), s32[]{:S(2)}) async-start(), calls=%async_computation.10 | async-start | bytes 1658880 | tf_op jit(solution)/shard_map/reduce_scatter | solution.py:1438
  335.4 24.3 %collective-permute-start.28 = (bf16[8,144,384]{2,1,0:T(8,128)(2,1)}, bf16[8,144,384]{2,1,0:T(8,128)(2,1)}, u32[]{:S(2)}, u32[]{:S(2)}) collective-permute-start(bf16[8,144,384]{2,1,0:T(8,128)(2,1)} %fusion.4), channel_id=1, source_target_pairs={{0,16},{16,0},{1,17},{17,1},{2,18},{18,2},{3,19},{19,3},{4,20},{20... | collective-permute-start | bytes 2654216 | tf_op jit(solution)/shard_map/ppermute | solution.py:1376
  362.3 45.1 %all-to-all-start.8 = ((bf16[8,168,384]{2,1,0:T(8,128)(2,1)}), bf16[8,168,384]{2,1,0:T(8,128)(2,1)S(1)}, u32[]{:S(2)}, u32[]{:S(2)}) async-start(bf16[8,168,384]{2,1,0:T(8,128)(2,1)} %pad_maximum_fusion), calls=%async_computation.8 | async-start | bytes 2064384 | tf_op jit(solution)/shard_map/all_to_all | solution.py:1390
  (66 other events, 533.5 us)
Sparse Core Ops, SparseCore 0:
  68.0 33.4 all-gather.2
  354.4 44.6 reduce-scatter.1
